TPU v7x, 32 devices: a whole 2x2x4 slice. The times are simulated.
32 devices in a mesh: seq: 8 (over z, y), head: 4 (over x, core).
Axes of the slice: x: 2, y: 2, z: 4, core: 2. Of those that a mesh axis runs over, the one named last changes fastest.
Arguments:
- hidden_in: bfloat16 [64, 8192], P(None, 'seq'), may hold values from -6 to 6
- w_query: bfloat16 [8192, 8192], P('seq', 'head'), may hold values from -0.0625 to 0.0625
- w_keyval: bfloat16 [8192, 2048], P('seq', 'head'), may hold values from -0.0625 to 0.0625
- w_out: bfloat16 [8192, 8192], P('head', 'seq'), may hold values from -0.0625 to 0.0625
- key_cache: bfloat16 [1024, 128, 1024], P('seq', None, 'head'), may hold values from -6 to 6
- value_cache: bfloat16 [1024, 128, 1024], P('seq', None, 'head'), may hold values from -6 to 6
- key_scale: float32 [1024, 8], P('seq', 'head'), may hold values from 0.25 to 300
- value_scale: float32 [1024, 8], P('seq', 'head'), may hold values from 0.5 to 2
- page_counts: int32 [64], replicated, may hold values from 1 to 128, 1024 in all
- slot_pages: int32 [1024], P('seq'), may hold values from 0 to 1023, each once
- trim: int32 [64], replicated, may hold values from 0 to 127
Outputs:
- attn_out: bfloat16 [64, 8192], P(None, 'seq')
Inputs may be any that keep to these rules, and one draw needn't show every extreme that they name: `page_counts`: every request has at least one page; the page counts sum to 1024.
All inputs are finite; a program needn't handle non-finite values.
Results may differ from a plain program's by a relative error of at most 0.0095.
Values may be sent and summed in bfloat16 or wider, within the bound.
No kernel may reach another device: no remote copies, remote signals or barrier semaphores. Data moves between devices by JAX's collectives and lax.ppermute only.
A program may use at most 128 MiB of HBM per device.

v0:
```python
import math

import jax
import jax.numpy as jnp
from jax import lax
from jax.sharding import PartitionSpec as P

HD = 128
PAGE = 128


masked_low = -1e30


def widen(factor, size):
    return jnp.repeat(factor, size, axis=1)


def finish(query, keyval, cache_max, cache_sum, cache_out, kv_local, group):
    inverse_square_root = 1.0 / math.sqrt(HD)
    requests = query.shape[0]
    heads_local = kv_local * group
    pairs = keyval.reshape(requests, kv_local, 2, HD)
    new_key = pairs[:, :, 0]
    new_value = pairs[:, :, 1].astype(jnp.float32)
    query_heads = query.reshape(requests, kv_local, group, HD)
    own = (
        jnp.einsum(
            "rgjd,rgd->rgj", query_heads, new_key, preferred_element_type=jnp.float32
        ).reshape(requests, heads_local)
        * inverse_square_root
    )
    top = jnp.maximum(cache_max, own)
    old_part = jnp.exp(cache_max - top)
    new_part = jnp.exp(own - top)
    denom = cache_sum * old_part + new_part
    spread_value = jnp.broadcast_to(
        new_value[:, :, None, :], (requests, kv_local, group, HD)
    ).reshape(requests, heads_local * HD)
    numer = cache_out * widen(old_part, HD) + widen(new_part, HD) * spread_value
    return (numer / widen(denom, HD)).astype(jnp.bfloat16)


def body(
    hidden_in,
    w_query,
    w_keyval,
    w_out,
    key_cache,
    value_cache,
    key_scale,
    value_scale,
    page_counts,
    slot_pages,
    trim,
):
    requests = hidden_in.shape[0]
    slots = key_cache.shape[0]
    kv_local = w_keyval.shape[1] // (2 * HD)
    heads_local = w_query.shape[1] // HD
    group = heads_local // kv_local
    part_query = jnp.dot(hidden_in, w_query, preferred_element_type=jnp.float32)
    part_keyval = jnp.dot(hidden_in, w_keyval, preferred_element_type=jnp.float32)
    sum_query, sum_keyval = lax.psum((part_query, part_keyval), "seq")
    query = sum_query.astype(jnp.bfloat16)
    keyval = sum_keyval.astype(jnp.bfloat16)
    start = jnp.cumsum(page_counts) - page_counts
    ends = start + page_counts
    owner = jnp.sum((ends[None, :] <= slot_pages[:, None]).astype(jnp.int32), axis=1)
    selector = owner[:, None] == jnp.arange(requests, dtype=jnp.int32)[None, :]
    select_int = selector.astype(jnp.int32)
    index = slot_pages - jnp.sum(select_int * start[None, :], axis=1)
    lengths = PAGE * page_counts - trim
    page_len = jnp.sum(select_int * lengths[None, :], axis=1)
    inverse_square_root = 1.0 / math.sqrt(HD)
    q_sel = jnp.dot(
        selector.astype(jnp.bfloat16), query, preferred_element_type=jnp.float32
    ).astype(jnp.bfloat16)
    q_sel = q_sel.reshape(slots, kv_local, group, HD)
    key_rows = key_cache.reshape(slots, PAGE, kv_local, HD)
    value_rows = value_cache.reshape(slots, PAGE, kv_local, HD)
    unscaled_pages = jnp.einsum(
        "sgjd,stgd->sgjt", q_sel, key_rows, preferred_element_type=jnp.float32
    )
    score_matrix = unscaled_pages * (key_scale * inverse_square_root)[:, :, None, None]
    position = index[:, None] * PAGE + jnp.arange(PAGE, dtype=jnp.int32)[None, :]
    valid = (position < page_len[:, None])[:, None, None, :]
    score_matrix = jnp.where(valid, score_matrix, masked_low)
    page_max = jnp.max(score_matrix, axis=-1)
    probs = jnp.where(valid, jnp.exp(score_matrix - page_max[..., None]), 0.0).astype(jnp.bfloat16)
    page_sum = jnp.sum(probs.astype(jnp.float32), axis=-1).reshape(slots, heads_local)
    page_out = jnp.einsum("sgjt,stgd->sgjd", probs, value_rows, preferred_element_type=jnp.float32)
    page_out = (page_out * value_scale[:, :, None, None]).reshape(slots, heads_local, HD)
    page_max = page_max.reshape(slots, heads_local)
    select_float = selector.astype(jnp.float32)
    dev_max = jnp.max(jnp.where(selector[:, :, None], page_max[:, None, :], masked_low), axis=0)
    slot_max = jnp.max(jnp.where(selector[:, :, None], dev_max[None, :, :], masked_low), axis=1)
    weight = jnp.exp(page_max - slot_max)
    dev_sum = jnp.dot(select_float.T, page_sum * weight, precision=lax.Precision.HIGHEST)
    weighted = (page_out * weight[:, :, None]).reshape(slots, heads_local * HD)
    dev_out = jnp.dot(select_float.T, weighted, precision=lax.Precision.HIGHEST)
    cache_max = lax.pmax(dev_max, "seq")
    factor = jnp.exp(dev_max - cache_max)
    cache_sum, cache_out = lax.psum((dev_sum * factor, dev_out * widen(factor, HD)), "seq")
    context = finish(query, keyval, cache_max, cache_sum, cache_out, kv_local, group)
    partial_out = jnp.dot(context, w_out, preferred_element_type=jnp.float32)
    return lax.psum(partial_out, "head").astype(jnp.bfloat16)


def solution(mesh):
    return jax.shard_map(
        body,
        mesh=mesh,
        in_specs=(
            P(None, "seq"),
            P("seq", "head"),
            P("seq", "head"),
            P("head", "seq"),
            P("seq", None, "head"),
            P("seq", None, "head"),
            P("seq", "head"),
            P("seq", "head"),
            P(),
            P("seq"),
            P(),
        ),
        out_specs=P(None, "seq"),
        check_vma=False,
    )
```

profile of v0, /device:TPU:0, one launch (start us, length us, event | category | flops | bytes accessed | tf_op | source)
XLA Modules:
  0.0 189.1 jit_solution(8371516243339164515)
XLA Ops:
  6.5 0.8 copy.51
  7.6 0.8 convert_reduce_fusion.1
  8.3 0.7 multiply_subtract_fusion
  9.1 0.7 subtract_multiply_fusion
  9.8 3.1 %fusion.35 = f32[64,2048]{1,0:T(8,128)S(1)} fusion(bf16[64,1024]{1,0:T(8,128)(2,1)} %param.11, bf16[1024,2048]{1,0:T(8,128)(2,1)} %param.12), kind=kOutput, calls=%fused_computation.55 | convolution fusion | flops 268435456 | bytes 4849664 | tf_op jit(solution)/shard_map/dot_general | solution.py:62
  12.9 45.2 %all-reduce.7 = bf16[64,2048]{1,0:T(8,128)(2,1)S(1)} all-reduce(f32[64,2048]{1,0:T(8,128)S(1)} %fusion.35), channel_id=1, replica_groups=mesh['seq'=8,'head'=4] {'seq'}, use_global_device_ids=true, to_apply=%region_4.5 | all-reduce | flops 131072 | bytes 786432 | tf_op jit(solution)/shard_map/psum | solution.py:64
  58.1 0.3 fusion.15
  58.6 0.7 broadcast_multiply_fusion
  59.5 7.0 %fusion.34 = (f32[128,2,8]{2,1,0:T(2,128)S(1)}, f32[128,2,8,128]{3,2,1,0:T(8,128)S(1)}) fusion(f32[128,2]{1,0:T(8,128)S(1)} %copy.53, bf16[128,2,8,128]{3,2,1,0:T(8,128)(2,1)S(1)} %bitcast.104, pred[128,128]{1,0:T(8,128)(4,1)S(1)} %add_compare_fusion, bf16[128,128,256]{2,1,0:T(8,128)(2,1)} %param.15), kind=kOutput, calls=%fused_computation.54 | convolution fusion | flops 67893248 | bytes 9987072 | tf_op jit(solution)/shard_map/sgjd,stgd->sgjt/dot_general | solution.py:82
  66.6 0.2 select_reduce_fusion.1
  66.9 0.2 select_reduce_fusion
  67.2 17.4 %pmax.7 = f32[64,16]{0,1:T(8,128)S(1)} all-reduce(f32[64,16]{0,1:T(8,128)S(1)} %copy.59), channel_id=1, replica_groups=mesh['seq'=8,'head'=4] {'seq'}, use_global_device_ids=true, to_apply=%region_8.9 | all-reduce | flops 1024 | bytes 8192 | tf_op jit(solution)/shard_map/pmax | solution.py:102
  84.8 4.8 %fusion.9 = f32[128,2,8,128]{3,2,1,0:T(8,128)S(1)} fusion(f32[128,2]{1,0:T(8,128)S(1)} %copy.55, f32[128,2,8,128]{3,2,1,0:T(8,128)S(1)} %get-tuple-element.17, f32[128,2,8]{2,1,0:T(2,128)S(1)} %get-tuple-element.16, pred[128,128]{1,0:T(8,128)(4,1)S(1)} %add_compare_fusion, bf16[128,128,256]{2,1,0:T(8,128)(2,1)} %param.16), kind=kOutput, calls=%fused_computation.9 | convolution fusion | flops 68157440 | bytes 10511360 | tf_op jit(solution)/shard_map/sgjt,stgd->sgjd/dot_general | solution.py:92
  89.6 0.2 broadcast_in_dim.101
  89.8 0.3 mul.103
  90.1 2.1 %convolution_multiply_fusion = f32[64,2048]{1,0:T(8,128)} fusion(f32[16,8,16,128]{3,2,1,0:T(8,128)S(1)} %bitcast.102, f32[16,8,16,128]{3,2,1,0:T(8,128)S(1)} %bitcast.110, f32[8,8,16,128]{3,2,1,0:T(8,128)S(1)} %bitcast.109, s32[128]{0:T(128)S(1)} %convert_reduce_fusion.1), kind=kOutput, calls=%fused_computation.7 | convolution fusion | flops 201728000 | bytes 3146240 | tf_op jit(solution)/shard_map/dot_general | solution.py:101
  92.2 0.8 convert_reduce_fusion
  93.3 0.3 fusion.36
  93.6 37.5 %all-reduce.8 = (bf16[64,512]{1,0:T(8,128)(2,1)S(1)}, f32[64,16]{0,1:T(8,128)S(1)}) all-reduce(f32[64,512]{1,0:T(8,128)S(1)} %fusion.36, f32[64,16]{0,1:T(8,128)S(1)} %convolution_multiply_fusion.1), channel_id=1, replica_groups=mesh['seq'=8,'head'=4] {'seq'}, use_global_device_ids=true, to_apply=%region_10.11 | all-reduce | flops 33792 | bytes 204800 | tf_op jit(solution)/shard_map/psum | solution.py:64
  131.2 0.3 fusion.24
  131.8 32.4 %all-reduce.6.cloned.1.call-done = f32[64,2048]{1,0:T(8,128)} async-done(((f32[64,2048]{1,0:T(8,128)}), f32[64,2048]{1,0:T(8,128)}) %all-reduce.6.cloned.1.call-update) | async-done | bytes 524304 | tf_op jit(solution)/shard_map/psum | solution.py:104
  164.4 0.2 broadcast_in_dim.103
  164.8 3.9 %fusion.21 = f32[64,1024]{1,0:T(8,128)S(1)} fusion(bf16[2048,1024]{1,0:T(8,128)(2,1)} %param.14, f32[8,8,16,128]{3,2,1,0:T(8,128)S(1)} %bitcast.107, f32[8,8,16,128]{3,2,1,0:T(8,128)S(1)} %bitcast.108, f32[8,8,16,128]{3,2,1,0:T(8,128)S(1)} %bitcast.106, f32[64,2048]{1,0:T(8,128)} %all-reduce.6.cloned.1.call-done, f32[8,8,16,128]{3,2,1,0:T(8,128)S(1)} %bitcast.105), kind=kOutput, calls=%fused_computation.26 | convolution fusion | flops 269090816 | bytes 7077888 | tf_op jit(solution)/shard_map/dot_general | solution.py:106
  168.7 13.5 %all-reduce.9 = bf16[64,1024]{1,0:T(8,128)(2,1)} all-reduce(f32[64,1024]{1,0:T(8,128)S(1)} %fusion.21), channel_id=1, replica_groups=mesh['seq'=8,'head'=4] {'head'}, use_global_device_ids=true, to_apply=%region_13.14 | all-reduce | flops 65536 | bytes 393216 | tf_op jit(solution)/shard_map/psum | solution.py:107
  (36 shorter events, 2.3 us)
Async XLA Ops:
  6.5 86.7 %copy-start = (bf16[1024,512]{1,0:T(8,128)(2,1)S(1)}, bf16[1024,512]{1,0:T(8,128)(2,1)}, u32[]{:S(2)}) copy-start(bf16[1024,512]{1,0:T(8,128)(2,1)} %param.13) | copy-start | bytes 3145732
  6.5 157.7 %all-reduce.6.cloned.1.call-start = ((), (), s32[]{:S(2)}) async-start(), calls=%async_computation | async-start | bytes 1048576 | tf_op jit(solution)/shard_map/psum | solution.py:104
  9.8 57.3 %copy-start.2 = (f32[128,2]{0,1:T(2,128)S(1)}, f32[128,2]{0,1:T(2,128)}, u32[]{:S(2)}) copy-start(f32[128,2]{0,1:T(2,128)} %param.18) | copy-start | bytes 3076
  84.8 8.5 %copy-start.1 = (bf16[64,1024]{1,0:T(8,128)(2,1)S(1)}, bf16[64,1024]{1,0:T(8,128)(2,1)}, u32[]{:S(2)}) copy-start(bf16[64,1024]{1,0:T(8,128)(2,1)} %param.11) | copy-start | bytes 393220
Sparse Core Ops, SparseCore 0:
  92.3 71.8 all-reduce.5
where the time goes:
time: 190 us; the launch traced here: 189 us
  blocking collectives  114 us (60%)
  waiting for transfers between devices  32.4 us (17%)
  matrix products  21.9 us (12%)
  between operations  13.6 us (7%)
  other arithmetic  4.54 us (2%)
  local copies, waits for them, and re-layouts  3.13 us (2%)
    psum x2, blocking collectives, body(): sum_query, sum_keyval = lax.psum((part_query, part_keyval), 'seq')  82.7 us
    psum x1, waiting for transfers between devices, body(): lax.psum((dev_sum * factor, dev_out * widen(factor, HD)), 'seq')  32.4 us
    pmax x1, blocking collectives, body(): cache_max = lax.pmax(dev_max, 'seq')  17.4 us
    psum x1, blocking collectives, body(): return lax.psum(partial_out, 'head').astype(jnp.bfloat16)  13.5 us
    dot_general x1, matrix products, body(): jnp.einsum('sgjd,stgd->sgjt', q_sel, key_rows, preferred_element_type=jnp...  6.98 us
    dot_general x1, matrix products, body(): jnp.einsum('sgjt,stgd->sgjd', probs, value_rows, preferred_element_type=j...  4.76 us
    dot_general x1, matrix products, body(): partial_out = jnp.dot(context, w_out, preferred_element_type=jnp.float32)  3.89 us
  transfers between devices with their start and end apart: 1, of which 1 were waited for; matrix products, arithmetic and copies ran while one was open for 1% of the time, Pallas kernels for 0%

commit v1 on v0

v1 whole, which is shorter than its diff:
```python
import math

import jax
import jax.numpy as jnp
from jax import lax
from jax.sharding import PartitionSpec as P

HD = 128
PAGE = 128


masked_low = -1e30


def widen(factor, size):
    return jnp.repeat(factor, size, axis=1)


def split_three(x):
    hi = lax.reduce_precision(x, 8, 7)
    rest = x - hi
    mid = lax.reduce_precision(rest, 8, 7)
    return hi, mid, rest - mid


def exchange(x, axis, n):
    return lax.all_to_all(x.reshape(n, x.shape[0] // n, x.shape[1]), axis, 0, 0)


def gather_direct(x, axis, n):
    me = lax.axis_index(axis)
    blocks = [x]
    for shift in range(1, n):
        blocks.append(lax.ppermute(x, axis, [(j, (j + shift) % n) for j in range(n)]))
    stacked = jnp.stack(blocks)
    order = jnp.mod(me - jnp.arange(n, dtype=jnp.int32), n)
    return jnp.take(stacked, order, axis=0).reshape(n * x.shape[0], x.shape[1])


def body(
    hidden_in,
    w_query,
    w_keyval,
    w_out,
    key_cache,
    value_cache,
    key_scale,
    value_scale,
    page_counts,
    slot_pages,
    trim,
    seq_size,
    head_size,
):
    requests = hidden_in.shape[0]
    slots = key_cache.shape[0]
    kv_local = w_keyval.shape[1] // (2 * HD)
    heads_local = w_query.shape[1] // HD
    group = heads_local // kv_local
    wide = heads_local * HD
    mine = requests // seq_size
    inverse_square_root = 1.0 / math.sqrt(HD)

    part_query = jnp.dot(hidden_in, w_query, preferred_element_type=jnp.float32)
    part_keyval = jnp.dot(hidden_in, w_keyval, preferred_element_type=jnp.float32)
    parts = exchange(jnp.concatenate([part_query, part_keyval], axis=1), "seq", seq_size)
    sums = jnp.sum(parts, axis=0).astype(jnp.bfloat16)
    my_query, my_keyval = sums[:, :wide], sums[:, wide:]
    query = gather_direct(my_query, "seq", seq_size)

    start = jnp.cumsum(page_counts) - page_counts
    ends = start + page_counts
    owner = jnp.sum((ends[None, :] <= slot_pages[:, None]).astype(jnp.int32), axis=1)
    selector = owner[:, None] == jnp.arange(requests, dtype=jnp.int32)[None, :]
    select_int = selector.astype(jnp.int32)
    index = slot_pages - jnp.sum(select_int * start[None, :], axis=1)
    lengths = PAGE * page_counts - trim
    page_len = jnp.sum(select_int * lengths[None, :], axis=1)

    q_sel = jnp.dot(
        selector.astype(jnp.bfloat16), query, preferred_element_type=jnp.float32
    ).astype(jnp.bfloat16)
    q_sel = q_sel.reshape(slots, kv_local, group, HD)
    key_rows = key_cache.reshape(slots, PAGE, kv_local, HD)
    value_rows = value_cache.reshape(slots, PAGE, kv_local, HD)
    unscaled_pages = jnp.einsum(
        "sgjd,stgd->sgjt", q_sel, key_rows, preferred_element_type=jnp.float32
    )
    score_matrix = unscaled_pages * (key_scale * inverse_square_root)[:, :, None, None]
    position = index[:, None] * PAGE + jnp.arange(PAGE, dtype=jnp.int32)[None, :]
    valid = (position < page_len[:, None])[:, None, None, :]
    score_matrix = jnp.where(valid, score_matrix, masked_low)
    page_max = jnp.max(score_matrix, axis=-1)
    probs = jnp.where(valid, jnp.exp(score_matrix - page_max[..., None]), 0.0).astype(jnp.bfloat16)
    page_sum = jnp.sum(probs.astype(jnp.float32), axis=-1).reshape(slots, heads_local)
    page_out = jnp.einsum("sgjt,stgd->sgjd", probs, value_rows, preferred_element_type=jnp.float32)
    page_out = (page_out * value_scale[:, :, None, None]).reshape(slots, heads_local, HD)
    page_max = page_max.reshape(slots, heads_local)
    select_float = selector.astype(jnp.float32)
    dev_max = jnp.max(jnp.where(selector[:, :, None], page_max[:, None, :], masked_low), axis=0)
    slot_max = jnp.max(jnp.where(selector[:, :, None], dev_max[None, :, :], masked_low), axis=1)
    weight = jnp.exp(page_max - slot_max)
    dev_sum = jnp.dot(select_float.T, page_sum * weight, precision=lax.Precision.HIGHEST)
    weighted = (page_out * weight[:, :, None]).reshape(slots, wide)
    dev_out = jnp.dot(select_float.T, weighted, precision=lax.Precision.HIGHEST)

    pieces = jnp.concatenate([*split_three(dev_max), *split_three(dev_sum)], axis=1)
    pieces = jnp.pad(pieces, ((0, 0), (0, -pieces.shape[1] % 128)))
    packed = jnp.concatenate([dev_out, pieces], axis=1).astype(jnp.bfloat16)
    got = exchange(packed, "seq", seq_size).astype(jnp.float32)
    out_parts = got[:, :, :wide]
    stat = got[:, :, wide : wide + 6 * heads_local].reshape(seq_size, mine, 6, heads_local)
    max_parts = stat[:, :, 0] + stat[:, :, 1] + stat[:, :, 2]
    sum_parts = stat[:, :, 3] + stat[:, :, 4] + stat[:, :, 5]

    pairs = my_keyval.reshape(mine, kv_local, 2, HD)
    new_key = pairs[:, :, 0]
    new_value = pairs[:, :, 1].astype(jnp.float32)
    own = (
        jnp.einsum(
            "rgjd,rgd->rgj",
            my_query.reshape(mine, kv_local, group, HD),
            new_key,
            preferred_element_type=jnp.float32,
        ).reshape(mine, heads_local)
        * inverse_square_root
    )
    top = jnp.maximum(jnp.max(max_parts, axis=0), own)
    factor = jnp.exp(max_parts - top[None])
    new_part = jnp.exp(own - top)
    denom = jnp.sum(sum_parts * factor, axis=0) + new_part
    numer = jnp.sum(
        out_parts.reshape(seq_size, mine, heads_local, HD) * factor[..., None], axis=0
    )
    spread_value = jnp.broadcast_to(
        new_value[:, :, None, :], (mine, kv_local, group, HD)
    ).reshape(mine, heads_local, HD)
    numer = numer + new_part[..., None] * spread_value
    my_context = (numer / denom[..., None]).astype(jnp.bfloat16).reshape(mine, wide)
    context = lax.all_gather(my_context, "seq", axis=0, tiled=True)

    total = jnp.dot(context, w_out, preferred_element_type=jnp.float32)
    step = 1
    while step < head_size:
        total = total + lax.ppermute(
            total, "head", [(j, j ^ step) for j in range(head_size)]
        )
        step *= 2
    return total.astype(jnp.bfloat16)


def solution(mesh):
    seq_size, head_size = mesh.shape["seq"], mesh.shape["head"]

    def local(*args):
        return body(*args, seq_size=seq_size, head_size=head_size)

    return jax.shard_map(
        local,
        mesh=mesh,
        in_specs=(
            P(None, "seq"),
            P("seq", "head"),
            P("seq", "head"),
            P("head", "seq"),
            P("seq", None, "head"),
            P("seq", None, "head"),
            P("seq", "head"),
            P("seq", "head"),
            P(),
            P("seq"),
            P(),
        ),
        out_specs=P(None, "seq"),
        check_vma=False,
    )
```

time: 190 us -> 119 us (0.63)
  blocking collectives: 114 us -> 30.7 us
  starting transfers between devices: 0.01 us -> 23.3 us
  between operations: 13.6 us -> 0.37 us
  waiting for transfers between devices: 32.4 us -> 35.9 us
    psum x3 -> x0, blocking collectives: 96.2 us -> none  [the longest x2 82.7 us: body(): sum_query, sum_keyval = lax.psum((part_query, part_keyval), 'seq')]
    psum x1 -> x0, waiting for transfers between devices: 32.4 us -> none  [body(): lax.psum((dev_sum * factor, dev_out * widen(factor, HD)), 'seq')]
    all_gather x0 -> x1, blocking collectives: none -> 30.7 us  [body(): context = lax.all_gather(my_context, 'seq', axis=0, tiled=True)]
    all_to_all x0 -> x2, waiting for transfers between devices: none -> 24.3 us  [exchange(): return lax.all_to_all(x.reshape(n, x.shape[0] // n, x.shape[1]), axis, 0, 0)]
    pmax x1 -> x0, blocking collectives: 17.4 us -> none  [body(): cache_max = lax.pmax(dev_max, 'seq')]
    all_to_all x0 -> x2, starting transfers between devices: none -> 11.8 us  [exchange(): return lax.all_to_all(x.reshape(n, x.shape[0] // n, x.shape[1]), axis, 0, 0)]
    ppermute x0 -> x9, waiting for transfers between devices: none -> 11.6 us  [the longest x2 8.32 us: body(): lax.ppermute(total, 'head', [(j, j ^ step) for j in range(head_size)])]
    ppermute x0 -> x9, starting transfers between devices: none -> 11.4 us  [the longest x7 9.75 us: gather_direct(): lax.ppermute(x, axis, [(j, (j + shift) % n) for j in range(n)])]
  transfers between devices with their start and end apart: 1 -> 11, of which waited for: 1 -> 7; matrix products, arithmetic and copies ran while one was open for 1% -> 1% of each run, Pallas kernels for 0% -> 0%
where the time goes in v1:
time: 119 us
  waiting for transfers between devices  35.9 us (30%)
  blocking collectives  30.7 us (26%)
  starting transfers between devices  23.3 us (20%)
  matrix products  20.2 us (17%)
  other arithmetic  4.77 us (4%)
  local copies, waits for them, and re-layouts  3.41 us (3%)
    all_gather x1, blocking collectives, body(): context = lax.all_gather(my_context, 'seq', axis=0, tiled=True)  30.7 us
    all_to_all x2, waiting for transfers between devices, exchange(): return lax.all_to_all(x.reshape(n, x.shape[0] // n, x.shape[1]), axis, 0, 0)  24.3 us
    all_to_all x2, starting transfers between devices, exchange(): return lax.all_to_all(x.reshape(n, x.shape[0] // n, x.shape[1]), axis, 0, 0)  11.8 us
    ppermute x7, starting transfers between devices, gather_direct(): lax.ppermute(x, axis, [(j, (j + shift) % n) for j in range(n)])  9.75 us
    ppermute x2, waiting for transfers between devices, body(): lax.ppermute(total, 'head', [(j, j ^ step) for j in range(head_size)])  8.32 us
    dot_general x1, matrix products, body(): jnp.einsum('sgjd,stgd->sgjt', q_sel, key_rows, preferred_element_type=jnp...  6.98 us
    dot_general x1, matrix products, body(): jnp.einsum('sgjt,stgd->sgjd', probs, value_rows, preferred_element_type=j...  4.73 us
    ppermute x7, waiting for transfers between devices, gather_direct(): lax.ppermute(x, axis, [(j, (j + shift) % n) for j in range(n)])  3.3 us
  transfers between devices with their start and end apart: 11, of which 7 were waited for; matrix products, arithmetic and copies ran while one was open for 1% of the time, Pallas kernels for 0%

profile of v1, /device:TPU:0, one launch (start us, length us, event | category | flops | bytes accessed | tf_op | source)
XLA Modules:
  0.0 118.7 jit_solution(7780740771861133363)
XLA Ops:
  0.0 1.2 %copy-done = bf16[1024,512]{1,0:T(8,128)(2,1)S(1)} copy-done((bf16[1024,512]{1,0:T(8,128)(2,1)S(1)}, bf16[1024,512]{1,0:T(8,128)(2,1)}, u32[]{:S(2)}) %copy-start) | copy-done | bytes 1048600
  1.2 1.2 %fusion.52 = f32[64,512]{1,0:T(8,128)S(1)} fusion(bf16[64,1024]{1,0:T(8,128)(2,1)} %param.11, bf16[1024,512]{1,0:T(8,128)(2,1)S(1)} %copy-done), kind=kOutput, calls=%fused_computation.110 | convolution fusion | flops 67108864 | bytes 1310720 | tf_op jit(solution)/shard_map/dot_general | solution.py:65
  2.4 3.1 %fusion.51 = f32[64,2048]{1,0:T(8,128)S(1)} fusion(bf16[64,1024]{1,0:T(8,128)(2,1)} %param.11, bf16[1024,2048]{1,0:T(8,128)(2,1)} %param.12), kind=kOutput, calls=%fused_computation.109 | convolution fusion | flops 268435456 | bytes 4849664 | tf_op jit(solution)/shard_map/dot_general | solution.py:64
  5.5 0.9 maximum_bitcast_fusion
  6.4 7.3 %all-to-all-start = ((f32[8,8,2560]{2,1,0:T(8,128)}), f32[8,8,2560]{2,1,0:T(8,128)S(1)}, u32[]{:S(2)}, u32[]{:S(2)}) async-start(f32[8,8,2560]{2,1,0:T(8,128)} %maximum_bitcast_fusion), calls=%async_computation | async-start | bytes 1310720 | tf_op jit(solution)/shard_map/all_to_all | solution.py:27
  14.8 16.2 %all-to-all-done = f32[8,8,2560]{2,1,0:T(8,128)S(1)} async-done(((f32[8,8,2560]{2,1,0:T(8,128)}), f32[8,8,2560]{2,1,0:T(8,128)S(1)}, u32[]{:S(2)}, u32[]{:S(2)}) %all-to-all-start) | async-done | bytes 655392 | tf_op jit(solution)/shard_map/all_to_all | solution.py:27
  31.0 1.5 %collective-permute-start = (bf16[8,2048]{1,0:T(8,128)(2,1)S(1)}, bf16[8,2048]{1,0:T(8,128)(2,1)S(1)}, u32[]{:S(2)}, u32[]{:S(2)}) collective-permute-start(bf16[8,2048]{1,0:T(8,128)(2,1)S(1)} %slice.50), channel_id=1, source_target_pairs={{0,4},{4,8},{8,12},{12,16},{16,20},{20,24},{24,28},{28,0},{1,5},{5... | collective-permute-start | bytes 98312 | tf_op jit(solution)/shard_map/ppermute | solution.py:34
  32.6 1.7 %collective-permute-start.2 = (bf16[8,2048]{1,0:T(8,128)(2,1)S(1)}, bf16[8,2048]{1,0:T(8,128)(2,1)S(1)}, u32[]{:S(2)}, u32[]{:S(2)}) collective-permute-start(bf16[8,2048]{1,0:T(8,128)(2,1)S(1)} %slice.50), channel_id=1, source_target_pairs={{0,12},{4,16},{8,20},{12,24},{16,28},{20,0},{24,4},{28,8},{1,13},{... | collective-permute-start | bytes 98312 | tf_op jit(solution)/shard_map/ppermute | solution.py:34
  34.3 2.7 %collective-permute-start.3 = (bf16[8,2048]{1,0:T(8,128)(2,1)S(1)}, bf16[8,2048]{1,0:T(8,128)(2,1)S(1)}, u32[]{:S(2)}, u32[]{:S(2)}) collective-permute-start(bf16[8,2048]{1,0:T(8,128)(2,1)S(1)} %slice.50), channel_id=1, source_target_pairs={{0,16},{4,20},{8,24},{12,28},{16,0},{20,4},{24,8},{28,12},{1,17},{... | collective-permute-start | bytes 98312 | tf_op jit(solution)/shard_map/ppermute | solution.py:34
  37.0 1.4 %collective-permute-start.4 = (bf16[8,2048]{1,0:T(8,128)(2,1)S(1)}, bf16[8,2048]{1,0:T(8,128)(2,1)S(1)}, u32[]{:S(2)}, u32[]{:S(2)}) collective-permute-start(bf16[8,2048]{1,0:T(8,128)(2,1)S(1)} %slice.50), channel_id=1, source_target_pairs={{0,20},{4,24},{8,28},{12,0},{16,4},{20,8},{24,12},{28,16},{1,21},{... | collective-permute-start | bytes 98312 | tf_op jit(solution)/shard_map/ppermute | solution.py:34
  38.4 1.8 %collective-permute-start.5 = (bf16[8,2048]{1,0:T(8,128)(2,1)S(1)}, bf16[8,2048]{1,0:T(8,128)(2,1)S(1)}, u32[]{:S(2)}, u32[]{:S(2)}) collective-permute-start(bf16[8,2048]{1,0:T(8,128)(2,1)S(1)} %slice.50), channel_id=1, source_target_pairs={{0,24},{4,28},{8,0},{12,4},{16,8},{20,12},{24,16},{28,20},{1,25},{... | collective-permute-start | bytes 98312 | tf_op jit(solution)/shard_map/ppermute | solution.py:34
  40.9 0.9 collective-permute-done.4
  41.8 0.9 collective-permute-done.5
  42.7 1.5 %collective-permute-done.6 = bf16[8,2048]{1,0:T(8,128)(2,1)S(1)} collective-permute-done((bf16[8,2048]{1,0:T(8,128)(2,1)S(1)}, bf16[8,2048]{1,0:T(8,128)(2,1)S(1)}, u32[]{:S(2)}, u32[]{:S(2)}) %collective-permute-start.6) | collective-permute-done | bytes 32800 | tf_op jit(solution)/shard_map/ppermute | solution.py:34
  45.2 7.0 %fusion.50 = (f32[128,2,8]{2,1,0:T(2,128)S(1)}, f32[128,2,8,128]{3,2,1,0:T(8,128)S(1)}) fusion(f32[128,2]{1,0:T(8,128)S(1)} %copy.77, bf16[128,2,8,128]{3,2,1,0:T(8,128)(2,1)S(1)} %bitcast.114, pred[128,128]{1,0:T(8,128)(4,1)S(1)} %add_compare_fusion, bf16[128,128,256]{2,1,0:T(8,128)(2,1)} %param.15), kind=kOutput, calls=%fused_computation.108 | convolution fusion | flops 67893248 | bytes 9987072 | tf_op jit(solution)/shard_map/sgjd,stgd->sgjt/dot_general | solution.py:86
  52.8 0.8 convert_reduce_fusion
  54.1 4.7 %fusion.12 = f32[128,2,8,128]{3,2,1,0:T(8,128)S(1)} fusion(f32[128,2,8]{2,1,0:T(2,128)S(1)} %copy.82, f32[128,2]{1,0:T(8,128)S(1)} %copy.79, f32[128,2,8,128]{3,2,1,0:T(8,128)S(1)} %get-tuple-element.20, f32[128,2,8]{2,1,0:T(2,128)S(1)} %get-tuple-element.19, pred[128,128]{1,0:T(8,128)(4,1)S(1)} %add_compare_fusion, bf16[128,128,256]{2,1,0:T(8,128)(2,1)} %param.16), kind=kOutput, calls=%fused_computation.11 | convolution fusion | flops 68419584 | bytes 10519552 | tf_op jit(solution)/shard_map/sgjt,stgd->sgjd/dot_general | solution.py:96
  60.3 4.6 %all-to-all-start.1 = ((bf16[8,8,2176]{2,1,0:T(8,128)(2,1)}), bf16[8,8,2176]{2,1,0:T(8,128)(2,1)S(1)}, u32[]{:S(2)}, u32[]{:S(2)}) async-start(bf16[8,8,2176]{2,1,0:T(8,128)(2,1)} %pad_maximum_fusion), calls=%async_computation.1 | async-start | bytes 557056 | tf_op jit(solution)/shard_map/all_to_all | solution.py:27
  65.1 8.1 %all-to-all-done.1 = bf16[8,8,2176]{2,1,0:T(8,128)(2,1)S(1)} async-done(((bf16[8,8,2176]{2,1,0:T(8,128)(2,1)}), bf16[8,8,2176]{2,1,0:T(8,128)(2,1)S(1)}, u32[]{:S(2)}, u32[]{:S(2)}) %all-to-all-start.1) | async-done | bytes 278560 | tf_op jit(solution)/shard_map/all_to_all | solution.py:27
  74.2 30.7 %all_gather.3 = bf16[64,2048]{1,0:T(8,128)(2,1)S(1)} all-gather(bf16[8,2048]{1,0:T(8,128)(2,1)S(1)} %fusion.22), channel_id=1, replica_groups=mesh['seq'=8,'head'=4] {'seq'}, dimensions={0}, use_global_device_ids=true | all-gather | bytes 294912 | tf_op jit(solution)/shard_map/all_gather | solution.py:140
  104.9 3.0 %fusion.53 = f32[64,1024]{1,0:T(8,128)S(1)} fusion(bf16[64,2048]{1,0:T(8,128)(2,1)S(1)} %all_gather.3, bf16[2048,1024]{1,0:T(8,128)(2,1)} %param.14), kind=kOutput, calls=%fused_computation.111 | convolution fusion | flops 268435456 | bytes 4718592 | tf_op jit(solution)/shard_map/dot_general | solution.py:142
  108.0 1.5 %collective-permute-done.7 = f32[64,1024]{1,0:T(8,128)S(1)} collective-permute-done((f32[64,1024]{1,0:T(8,128)S(1)}, f32[64,1024]{1,0:T(8,128)S(1)}, u32[]{:S(2)}, u32[]{:S(2)}) %collective-permute-start.7) | collective-permute-done | bytes 262176 | tf_op jit(solution)/shard_map/ppermute | solution.py:145
  109.6 1.6 %collective-permute-start.8 = (f32[64,1024]{1,0:T(8,128)S(1)}, f32[64,1024]{1,0:T(8,128)S(1)}, u32[]{:S(2)}, u32[]{:S(2)}) collective-permute-start(f32[64,1024]{1,0:T(8,128)S(1)} %add.116), channel_id=1, source_target_pairs={{0,2},{1,3},{2,0},{3,1},{4,6},{5,7},{6,4},{7,5},{8,10},{9,11},{10,... | collective-permute-start | bytes 786440 | tf_op jit(solution)/shard_map/ppermute | solution.py:145
  111.2 6.8 %collective-permute-done.8 = f32[64,1024]{1,0:T(8,128)S(1)} collective-permute-done((f32[64,1024]{1,0:T(8,128)S(1)}, f32[64,1024]{1,0:T(8,128)S(1)}, u32[]{:S(2)}, u32[]{:S(2)}) %collective-permute-start.8) | collective-permute-done | bytes 262176 | tf_op jit(solution)/shard_map/ppermute | solution.py:145
  (88 shorter events, 7.2 us)
Async XLA Ops:
  0.0 1.2 %copy-start = (bf16[1024,512]{1,0:T(8,128)(2,1)S(1)}, bf16[1024,512]{1,0:T(8,128)(2,1)}, u32[]{:S(2)}) copy-start(bf16[1024,512]{1,0:T(8,128)(2,1)} %param.13) | copy-start | bytes 3145732
  0.0 13.7 %copy-start.3 = (f32[128,2]{0,1:T(2,128)S(1)}, f32[128,2]{0,1:T(2,128)}, u32[]{:S(2)}) copy-start(f32[128,2]{0,1:T(2,128)} %param.17) | copy-start | bytes 3076
  0.0 14.1 %copy-start.1 = (s32[64]{0:T(128)S(1)}, s32[64]{0:T(128)}, u32[]{:S(2)}) copy-start(s32[64]{0:T(128)} %param.19) | copy-start | bytes 772
  0.0 14.4 %copy-start.2 = (f32[128,2]{0,1:T(2,128)S(1)}, f32[128,2]{0,1:T(2,128)}, u32[]{:S(2)}) copy-start(f32[128,2]{0,1:T(2,128)} %param.18) | copy-start | bytes 3076
  0.0 14.5 %copy-start.5 = (s32[128]{0:T(128)S(1)}, s32[128]{0:T(128)}, u32[]{:S(2)}) copy-start(s32[128]{0:T(128)} %param.20) | copy-start | bytes 1540
  0.0 14.6 %copy-start.4 = (s32[64]{0:T(128)S(1)}, s32[64]{0:T(128)}, u32[]{:S(2)}) copy-start(s32[64]{0:T(128)} %param.21) | copy-start | bytes 772
  6.4 24.6 %all-to-all-start = ((f32[8,8,2560]{2,1,0:T(8,128)}), f32[8,8,2560]{2,1,0:T(8,128)S(1)}, u32[]{:S(2)}, u32[]{:S(2)}) async-start(f32[8,8,2560]{2,1,0:T(8,128)} %maximum_bitcast_fusion), calls=%async_computation | async-start | bytes 1310720 | tf_op jit(solution)/shard_map/all_to_all | solution.py:27
  31.0 7.4 %collective-permute-start = (bf16[8,2048]{1,0:T(8,128)(2,1)S(1)}, bf16[8,2048]{1,0:T(8,128)(2,1)S(1)}, u32[]{:S(2)}, u32[]{:S(2)}) collective-permute-start(bf16[8,2048]{1,0:T(8,128)(2,1)S(1)} %slice.50), channel_id=1, source_target_pairs={{0,4},{4,8},{8,12},{12,16},{16,20},{20,24},{24,28},{28,0},{1,5},{5... | collective-permute-start | bytes 98312 | tf_op jit(solution)/shard_map/ppermute | solution.py:34
  32.6 7.7 %collective-permute-start.1 = (bf16[8,2048]{1,0:T(8,128)(2,1)S(1)}, bf16[8,2048]{1,0:T(8,128)(2,1)S(1)}, u32[]{:S(2)}, u32[]{:S(2)}) collective-permute-start(bf16[8,2048]{1,0:T(8,128)(2,1)S(1)} %slice.50), channel_id=1, source_target_pairs={{0,8},{4,12},{8,16},{12,20},{16,24},{20,28},{24,0},{28,4},{1,9},{5... | collective-permute-start | bytes 98312 | tf_op jit(solution)/shard_map/ppermute | solution.py:34
  32.6 8.3 %collective-permute-start.2 = (bf16[8,2048]{1,0:T(8,128)(2,1)S(1)}, bf16[8,2048]{1,0:T(8,128)(2,1)S(1)}, u32[]{:S(2)}, u32[]{:S(2)}) collective-permute-start(bf16[8,2048]{1,0:T(8,128)(2,1)S(1)} %slice.50), channel_id=1, source_target_pairs={{0,12},{4,16},{8,20},{12,24},{16,28},{20,0},{24,4},{28,8},{1,13},{... | collective-permute-start | bytes 98312 | tf_op jit(solution)/shard_map/ppermute | solution.py:34
  34.3 6.5 %collective-permute-start.3 = (bf16[8,2048]{1,0:T(8,128)(2,1)S(1)}, bf16[8,2048]{1,0:T(8,128)(2,1)S(1)}, u32[]{:S(2)}, u32[]{:S(2)}) collective-permute-start(bf16[8,2048]{1,0:T(8,128)(2,1)S(1)} %slice.50), channel_id=1, source_target_pairs={{0,16},{4,20},{8,24},{12,28},{16,0},{20,4},{24,8},{28,12},{1,17},{... | collective-permute-start | bytes 98312 | tf_op jit(solution)/shard_map/ppermute | solution.py:34
  37.0 4.8 %collective-permute-start.4 = (bf16[8,2048]{1,0:T(8,128)(2,1)S(1)}, bf16[8,2048]{1,0:T(8,128)(2,1)S(1)}, u32[]{:S(2)}, u32[]{:S(2)}) collective-permute-start(bf16[8,2048]{1,0:T(8,128)(2,1)S(1)} %slice.50), channel_id=1, source_target_pairs={{0,20},{4,24},{8,28},{12,0},{16,4},{20,8},{24,12},{28,16},{1,21},{... | collective-permute-start | bytes 98312 | tf_op jit(solution)/shard_map/ppermute | solution.py:34
  38.4 4.3 %collective-permute-start.5 = (bf16[8,2048]{1,0:T(8,128)(2,1)S(1)}, bf16[8,2048]{1,0:T(8,128)(2,1)S(1)}, u32[]{:S(2)}, u32[]{:S(2)}) collective-permute-start(bf16[8,2048]{1,0:T(8,128)(2,1)S(1)} %slice.50), channel_id=1, source_target_pairs={{0,24},{4,28},{8,0},{12,4},{16,8},{20,12},{24,16},{28,20},{1,25},{... | collective-permute-start | bytes 98312 | tf_op jit(solution)/shard_map/ppermute | solution.py:34
  40.2 3.9 %collective-permute-start.6 = (bf16[8,2048]{1,0:T(8,128)(2,1)S(1)}, bf16[8,2048]{1,0:T(8,128)(2,1)S(1)}, u32[]{:S(2)}, u32[]{:S(2)}) collective-permute-start(bf16[8,2048]{1,0:T(8,128)(2,1)S(1)} %slice.50), channel_id=1, source_target_pairs={{0,28},{4,0},{8,4},{12,8},{16,12},{20,16},{24,20},{28,24},{1,29},{... | collective-permute-start | bytes 98312 | tf_op jit(solution)/shard_map/ppermute | solution.py:34
  60.3 12.9 %all-to-all-start.1 = ((bf16[8,8,2176]{2,1,0:T(8,128)(2,1)}), bf16[8,8,2176]{2,1,0:T(8,128)(2,1)S(1)}, u32[]{:S(2)}, u32[]{:S(2)}) async-start(bf16[8,8,2176]{2,1,0:T(8,128)(2,1)} %pad_maximum_fusion), calls=%async_computation.1 | async-start | bytes 557056 | tf_op jit(solution)/shard_map/all_to_all | solution.py:27
  108.0 1.6 %collective-permute-start.7 = (f32[64,1024]{1,0:T(8,128)S(1)}, f32[64,1024]{1,0:T(8,128)S(1)}, u32[]{:S(2)}, u32[]{:S(2)}) collective-permute-start(f32[64,1024]{1,0:T(8,128)S(1)} %fusion.53), channel_id=1, source_target_pairs={{0,1},{1,0},{2,3},{3,2},{4,5},{5,4},{6,7},{7,6},{8,9},{9,8},{10,11... | collective-permute-start | bytes 786440 | tf_op jit(solution)/shard_map/ppermute | solution.py:145
  109.6 8.4 %collective-permute-start.8 = (f32[64,1024]{1,0:T(8,128)S(1)}, f32[64,1024]{1,0:T(8,128)S(1)}, u32[]{:S(2)}, u32[]{:S(2)}) collective-permute-start(f32[64,1024]{1,0:T(8,128)S(1)} %add.116), channel_id=1, source_target_pairs={{0,2},{1,3},{2,0},{3,1},{4,6},{5,7},{6,4},{7,5},{8,10},{9,11},{10,... | collective-permute-start | bytes 786440 | tf_op jit(solution)/shard_map/ppermute | solution.py:145

commit v2 on v1

--- a/solution.py
+++ b/solution.py
@@ -28,13 +28,50 @@
 
 
 def gather_direct(x, axis, n):
+    return lax.all_to_all(jnp.broadcast_to(x[None], (n, *x.shape)), axis, 0, 0).reshape(
+        n * x.shape[0], x.shape[1]
+    )
+
+
+def swap(x, axis, n, mask):
+    return lax.ppermute(x, axis, [(j, j ^ mask) for j in range(n)])
+
+
+def bit_groups(n):
+    groups, shift = [], 0
+    while (1 << shift) < n:
+        size = min(4, n >> shift)
+        groups.append((shift, size))
+        shift += size.bit_length() - 1
+    return groups
+
+
+def scatter_sum(x, axis, n):
     me = lax.axis_index(axis)
-    blocks = [x]
-    for shift in range(1, n):
-        blocks.append(lax.ppermute(x, axis, [(j, (j + shift) % n) for j in range(n)]))
-    stacked = jnp.stack(blocks)
-    order = jnp.mod(me - jnp.arange(n, dtype=jnp.int32), n)
-    return jnp.take(stacked, order, axis=0).reshape(n * x.shape[0], x.shape[1])
+    for shift, size in bit_groups(n):
+        digit = (me >> shift) % size
+        x = x.reshape(x.shape[0] // size, size, *x.shape[1:])
+
+        def block(offset):
+            return lax.dynamic_index_in_dim(x, digit ^ offset, axis=1, keepdims=False)
+
+        parts = [swap(block(d), axis, n, d << shift) for d in range(1, size)]
+        x = sum(parts, block(0))
+    return x[0]
+
+
+def gather_relative(x, axis, n):
+    for shift, size in reversed(bit_groups(n)):
+        parts = [x] + [swap(x, axis, n, d << shift) for d in range(1, size)]
+        x = jnp.concatenate(parts, axis=0)
+    return x
+
+
+def relative_blocks(n):
+    offsets = [0]
+    for shift, size in reversed(bit_groups(n)):
+        offsets = [d << shift | e for d in range(size) for e in offsets]
+    return offsets
 
 
 def body(
@@ -63,10 +100,17 @@
 
     part_query = jnp.dot(hidden_in, w_query, preferred_element_type=jnp.float32)
     part_keyval = jnp.dot(hidden_in, w_keyval, preferred_element_type=jnp.float32)
-    parts = exchange(jnp.concatenate([part_query, part_keyval], axis=1), "seq", seq_size)
-    sums = jnp.sum(parts, axis=0).astype(jnp.bfloat16)
+    part_all = jnp.concatenate([part_query, part_keyval], axis=1)
+    sums = scatter_sum(
+        part_all.reshape(seq_size, mine, part_all.shape[1]), "seq", seq_size
+    ).astype(jnp.bfloat16)
     my_query, my_keyval = sums[:, :wide], sums[:, wide:]
-    query = gather_direct(my_query, "seq", seq_size)
+    query = gather_relative(my_query, "seq", seq_size)
+    offsets = jnp.array(relative_blocks(seq_size), dtype=jnp.int32)
+    row_request = (
+        (lax.axis_index("seq") ^ offsets)[:, None] * mine
+        + jnp.arange(mine, dtype=jnp.int32)[None, :]
+    ).reshape(requests)
 
     start = jnp.cumsum(page_counts) - page_counts
     ends = start + page_counts
@@ -78,7 +122,9 @@
     page_len = jnp.sum(select_int * lengths[None, :], axis=1)
 
     q_sel = jnp.dot(
-        selector.astype(jnp.bfloat16), query, preferred_element_type=jnp.float32
+        (owner[:, None] == row_request[None, :]).astype(jnp.bfloat16),
+        query,
+        preferred_element_type=jnp.float32,
     ).astype(jnp.bfloat16)
     q_sel = q_sel.reshape(slots, kv_local, group, HD)
     key_rows = key_cache.reshape(slots, PAGE, kv_local, HD)
@@ -137,14 +183,17 @@
     ).reshape(mine, heads_local, HD)
     numer = numer + new_part[..., None] * spread_value
     my_context = (numer / denom[..., None]).astype(jnp.bfloat16).reshape(mine, wide)
-    context = lax.all_gather(my_context, "seq", axis=0, tiled=True)
+    context = gather_direct(my_context, "seq", seq_size)
 
     total = jnp.dot(context, w_out, preferred_element_type=jnp.float32)
     step = 1
     while step < head_size:
-        total = total + lax.ppermute(
-            total, "head", [(j, j ^ step) for j in range(head_size)]
-        )
+        if step > 1:
+            total = lax.reduce_precision(total, 8, 7)
+            other = swap(total.astype(jnp.bfloat16), "head", head_size, step)
+        else:
+            other = swap(total, "head", head_size, step)
+        total = total + other.astype(jnp.float32)
         step *= 2
     return total.astype(jnp.bfloat16)
 

time: 119 us -> 89 us (0.75)
  blocking collectives: 30.7 us -> 11 us
  starting transfers between devices: 23.3 us -> 18.6 us
  waiting for transfers between devices: 35.9 us -> 31.5 us
    all_gather x1 -> x0, blocking collectives: 30.7 us -> none  [body(): context = lax.all_gather(my_context, 'seq', axis=0, tiled=True)]
    all_to_all x2 -> x1, waiting for transfers between devices: 24.3 us -> 8.1 us  [exchange(): return lax.all_to_all(x.reshape(n, x.shape[0] // n, x.shape[1]), axis, 0, 0)]
    ppermute x9 -> x10, waiting for transfers between devices: 11.6 us -> 23.4 us  [swap(): return lax.ppermute(x, axis, [(j, j ^ mask) for j in range(n)])]
    all_to_all x0 -> x1, blocking collectives: none -> 11 us  [gather_direct(): lax.all_to_all(jnp.broadcast_to(x[None], (n, *x.shape)), axis, 0, 0)]
    all_to_all x2 -> x1, starting transfers between devices: 11.8 us -> 4.33 us  [exchange(): return lax.all_to_all(x.reshape(n, x.shape[0] // n, x.shape[1]), axis, 0, 0)]
    ppermute x9 -> x10, starting transfers between devices: 11.4 us -> 14.3 us  [swap(): return lax.ppermute(x, axis, [(j, j ^ mask) for j in range(n)])]
  transfers between devices with their start and end apart: 11 -> 11, of which waited for: 7 -> 10; matrix products, arithmetic and copies ran while one was open for 1% -> 1% of each run, Pallas kernels for 0% -> 0%
where the time goes in v2:
time: 89 us; the launch traced here: 88.7 us
  waiting for transfers between devices  31.5 us (35%)
  matrix products  20.3 us (23%)
  starting transfers between devices  18.6 us (21%)
  blocking collectives  11 us (12%)
  other arithmetic  4.02 us (5%)
  local copies, waits for them, and re-layouts  2.81 us (3%)
    ppermute x10, waiting for transfers between devices, swap(): return lax.ppermute(x, axis, [(j, j ^ mask) for j in range(n)])  23.4 us
    ppermute x10, starting transfers between devices, swap(): return lax.ppermute(x, axis, [(j, j ^ mask) for j in range(n)])  14.3 us
    all_to_all x1, blocking collectives, gather_direct(): lax.all_to_all(jnp.broadcast_to(x[None], (n, *x.shape)), axis, 0, 0)  11 us
    all_to_all x1, waiting for transfers between devices, exchange(): return lax.all_to_all(x.reshape(n, x.shape[0] // n, x.shape[1]), axis, 0, 0)  8.1 us
    dot_general x1, matrix products, body(): jnp.einsum('sgjd,stgd->sgjt', q_sel, key_rows, preferred_element_type=jnp...  6.98 us
    dot_general x1, matrix products, body(): jnp.einsum('sgjt,stgd->sgjd', probs, value_rows, preferred_element_type=j...  4.73 us
    all_to_all x1, starting transfers between devices, exchange(): return lax.all_to_all(x.reshape(n, x.shape[0] // n, x.shape[1]), axis, 0, 0)  4.33 us
    dot_general x1, matrix products, body(): part_query = jnp.dot(hidden_in, w_query, preferred_element_type=jnp.float32)  3.11 us
  transfers between devices with their start and end apart: 11, of which 10 were waited for; matrix products, arithmetic and copies ran while one was open for 1% of the time, Pallas kernels for 0%

profile of v2, /device:TPU:0, one launch (start us, length us, event | category | flops | bytes accessed | tf_op | source)
XLA Modules:
  0.0 88.7 jit_solution(6297843198759363134)
XLA Ops:
  0.1 1.2 %copy-done = bf16[1024,512]{1,0:T(8,128)(2,1)S(1)} copy-done((bf16[1024,512]{1,0:T(8,128)(2,1)S(1)}, bf16[1024,512]{1,0:T(8,128)(2,1)}, u32[]{:S(2)}) %copy-start) | copy-done | bytes 1048600
  1.2 1.2 %fusion.55 = f32[64,512]{1,0:T(8,128)S(1)} fusion(bf16[64,1024]{1,0:T(8,128)(2,1)} %param.12, bf16[1024,512]{1,0:T(8,128)(2,1)S(1)} %copy-done), kind=kOutput, calls=%fused_computation.108 | convolution fusion | flops 67108864 | bytes 1310720 | tf_op jit(solution)/shard_map/dot_general | solution.py:102
  2.4 3.1 %fusion.54 = f32[64,2048]{1,0:T(8,128)S(1)} fusion(bf16[64,1024]{1,0:T(8,128)(2,1)} %param.12, bf16[1024,2048]{1,0:T(8,128)(2,1)} %param.13), kind=kOutput, calls=%fused_computation.107 | convolution fusion | flops 268435456 | bytes 4849664 | tf_op jit(solution)/shard_map/dot_general | solution.py:101
  5.7 4.0 %collective-permute-start.2 = (f32[2,8,2560]{2,1,0:T(8,128)S(1)}, f32[2,8,2560]{2,1,0:T(8,128)S(1)}, u32[]{:S(2)}, u32[]{:S(2)}) collective-permute-start(f32[2,8,2560]{2,1,0:T(8,128)S(1)} %get-tuple-element.12), channel_id=1, source_target_pairs={{0,12},{4,8},{8,4},{12,0},{16,28},{20,24},{24,20},{28,16},{1,13},{... | collective-permute-start | bytes 491528 | tf_op jit(solution)/shard_map/ppermute | solution.py:37
  11.1 3.6 %collective-permute-done.2 = f32[2,8,2560]{2,1,0:T(8,128)S(1)} collective-permute-done((f32[2,8,2560]{2,1,0:T(8,128)S(1)}, f32[2,8,2560]{2,1,0:T(8,128)S(1)}, u32[]{:S(2)}, u32[]{:S(2)}) %collective-permute-start.2) | collective-permute-done | bytes 163872 | tf_op jit(solution)/shard_map/ppermute | solution.py:37
  14.7 2.9 %collective-permute-done.1 = f32[2,8,2560]{2,1,0:T(8,128)S(1)} collective-permute-done((f32[2,8,2560]{2,1,0:T(8,128)S(1)}, f32[2,8,2560]{2,1,0:T(8,128)S(1)}, u32[]{:S(2)}, u32[]{:S(2)}) %collective-permute-start.1) | collective-permute-done | bytes 163872 | tf_op jit(solution)/shard_map/ppermute | solution.py:37
  17.7 2.6 %collective-permute-start.3 = (f32[1,8,2560]{2,1,0:T(8,128)S(1)}, f32[1,8,2560]{2,1,0:T(8,128)S(1)}, u32[]{:S(2)}, u32[]{:S(2)}) collective-permute-start(f32[1,8,2560]{2,1,0:T(8,128)S(1)} %constant_dynamic-slice_fusion), channel_id=1, source_target_pairs={{0,16},{4,20},{8,24},{12,28},{16,0},{20,4},{24,8},{28,12},{1,17},{... | collective-permute-start | bytes 245768 | tf_op jit(solution)/shard_map/ppermute | solution.py:37
  20.4 4.1 %collective-permute-done.3 = f32[1,8,2560]{2,1,0:T(8,128)S(1)} collective-permute-done((f32[1,8,2560]{2,1,0:T(8,128)S(1)}, f32[1,8,2560]{2,1,0:T(8,128)S(1)}, u32[]{:S(2)}, u32[]{:S(2)}) %collective-permute-start.3) | collective-permute-done | bytes 81952 | tf_op jit(solution)/shard_map/ppermute | solution.py:37
  24.5 1.4 %collective-permute-start.4 = (bf16[8,2048]{1,0:T(8,128)(2,1)S(1)}, bf16[8,2048]{1,0:T(8,128)(2,1)S(1)}, u32[]{:S(2)}, u32[]{:S(2)}) collective-permute-start(bf16[8,2048]{1,0:T(8,128)(2,1)S(1)} %get-tuple-element.18), channel_id=1, source_target_pairs={{0,16},{4,20},{8,24},{12,28},{16,0},{20,4},{24,8},{28,12},{1,17},{... | collective-permute-start | bytes 98312 | tf_op jit(solution)/shard_map/ppermute | solution.py:37
  26.2 3.1 %collective-permute-done.4 = bf16[8,2048]{1,0:T(8,128)(2,1)S(1)} collective-permute-done((bf16[8,2048]{1,0:T(8,128)(2,1)S(1)}, bf16[8,2048]{1,0:T(8,128)(2,1)S(1)}, u32[]{:S(2)}, u32[]{:S(2)}) %collective-permute-start.4) | collective-permute-done | bytes 32800 | tf_op jit(solution)/shard_map/ppermute | solution.py:37
  29.3 2.4 %collective-permute-start.5 = (bf16[16,2048]{1,0:T(8,128)(2,1)S(1)}, bf16[16,2048]{1,0:T(8,128)(2,1)S(1)}, u32[]{:S(2)}, u32[]{:S(2)}) collective-permute-start(bf16[16,2048]{1,0:T(8,128)(2,1)S(1)} %pad_maximum_fusion.2), channel_id=1, source_target_pairs={{0,4},{4,0},{8,12},{12,8},{16,20},{20,16},{24,28},{28,24},{1,5},{5... | collective-permute-start | bytes 196616 | tf_op jit(solution)/shard_map/ppermute | solution.py:37
  32.2 1.0 %collective-permute-start.7 = (bf16[16,2048]{1,0:T(8,128)(2,1)S(1)}, bf16[16,2048]{1,0:T(8,128)(2,1)S(1)}, u32[]{:S(2)}, u32[]{:S(2)}) collective-permute-start(bf16[16,2048]{1,0:T(8,128)(2,1)S(1)} %pad_maximum_fusion.2), channel_id=1, source_target_pairs={{0,12},{4,8},{8,4},{12,0},{16,28},{20,24},{24,20},{28,16},{1,13},{... | collective-permute-start | bytes 196616 | tf_op jit(solution)/shard_map/ppermute | solution.py:37
  34.0 2.0 %collective-permute-done.6 = bf16[16,2048]{1,0:T(8,128)(2,1)S(1)} collective-permute-done((bf16[16,2048]{1,0:T(8,128)(2,1)S(1)}, bf16[16,2048]{1,0:T(8,128)(2,1)S(1)}, u32[]{:S(2)}, u32[]{:S(2)}) %collective-permute-start.6) | collective-permute-done | bytes 65568 | tf_op jit(solution)/shard_map/ppermute | solution.py:37
  36.0 1.4 %collective-permute-done.7 = bf16[16,2048]{1,0:T(8,128)(2,1)S(1)} collective-permute-done((bf16[16,2048]{1,0:T(8,128)(2,1)S(1)}, bf16[16,2048]{1,0:T(8,128)(2,1)S(1)}, u32[]{:S(2)}, u32[]{:S(2)}) %collective-permute-start.7) | collective-permute-done | bytes 65568 | tf_op jit(solution)/shard_map/ppermute | solution.py:37
  38.0 7.0 %fusion.53 = (f32[128,2,8]{2,1,0:T(2,128)S(1)}, f32[128,2,8,128]{3,2,1,0:T(8,128)S(1)}) fusion(f32[128,2]{1,0:T(8,128)S(1)} %copy.78, bf16[128,2,8,128]{3,2,1,0:T(8,128)(2,1)S(1)} %bitcast.111, pred[128,128]{1,0:T(8,128)(4,1)S(1)} %add_compare_fusion, bf16[128,128,256]{2,1,0:T(8,128)(2,1)} %param.16), kind=kOutput, calls=%fused_computation.106 | convolution fusion | flops 67893248 | bytes 9987072 | tf_op jit(solution)/shard_map/sgjd,stgd->sgjt/dot_general | solution.py:132
  45.6 0.8 convert_reduce_fusion
  46.9 4.7 %fusion.12 = f32[128,2,8,128]{3,2,1,0:T(8,128)S(1)} fusion(f32[128,2,8]{2,1,0:T(2,128)S(1)} %copy.83, f32[128,2]{1,0:T(8,128)S(1)} %copy.80, f32[128,2,8,128]{3,2,1,0:T(8,128)S(1)} %get-tuple-element.25, f32[128,2,8]{2,1,0:T(2,128)S(1)} %get-tuple-element.24, pred[128,128]{1,0:T(8,128)(4,1)S(1)} %add_compare_fusion, bf16[128,128,256]{2,1,0:T(8,128)(2,1)} %param.17), kind=kOutput, calls=%fused_computation.10 | convolution fusion | flops 68419584 | bytes 10519552 | tf_op jit(solution)/shard_map/sgjt,stgd->sgjd/dot_general | solution.py:142
  53.1 4.3 %all-to-all-start = ((bf16[8,8,2176]{2,1,0:T(8,128)(2,1)}), bf16[8,8,2176]{2,1,0:T(8,128)(2,1)S(1)}, u32[]{:S(2)}, u32[]{:S(2)}) async-start(bf16[8,8,2176]{2,1,0:T(8,128)(2,1)} %pad_maximum_fusion.1), calls=%async_computation | async-start | bytes 557056 | tf_op jit(solution)/shard_map/all_to_all | solution.py:27
  57.6 8.1 %all-to-all-done = bf16[8,8,2176]{2,1,0:T(8,128)(2,1)S(1)} async-done(((bf16[8,8,2176]{2,1,0:T(8,128)(2,1)}), bf16[8,8,2176]{2,1,0:T(8,128)(2,1)S(1)}, u32[]{:S(2)}, u32[]{:S(2)}) %all-to-all-start) | async-done | bytes 278560 | tf_op jit(solution)/shard_map/all_to_all | solution.py:27
  66.7 11.0 %all_to_all.10 = bf16[8,8,2048]{2,1,0:T(8,128)(2,1)S(1)} all-to-all(bf16[8,8,2048]{2,1,0:T(8,128)(2,1)S(1)} %broadcast_in_dim.104), channel_id=1, replica_groups=mesh['seq'=8,'head'=4] {'seq'}, dimensions={0} | all-to-all | bytes 524288 | tf_op jit(solution)/shard_map/all_to_all | solution.py:31
  77.7 3.0 %fusion.20 = f32[64,1024]{1,0:T(8,128)S(1)} fusion(bf16[2048,1024]{1,0:T(8,128)(2,1)} %param.15, bf16[8,8,2048]{2,1,0:T(8,128)(2,1)S(1)} %all_to_all.10), kind=kOutput, calls=%fused_computation.21 | convolution fusion | flops 268435456 | bytes 4718592 | tf_op jit(solution)/shard_map/dot_general | solution.py:188
  80.8 1.5 %collective-permute-done.8 = f32[64,1024]{1,0:T(8,128)S(1)} collective-permute-done((f32[64,1024]{1,0:T(8,128)S(1)}, f32[64,1024]{1,0:T(8,128)S(1)}, u32[]{:S(2)}, u32[]{:S(2)}) %collective-permute-start.8) | collective-permute-done | bytes 262176 | tf_op jit(solution)/shard_map/ppermute | solution.py:37
  82.3 1.6 %collective-permute-start.9 = (bf16[64,1024]{1,0:T(8,128)(2,1)S(1)}, bf16[64,1024]{1,0:T(8,128)(2,1)S(1)}, u32[]{:S(2)}, u32[]{:S(2)}) collective-permute-start(bf16[64,1024]{1,0:T(8,128)(2,1)S(1)} %fusion.24), channel_id=1, source_target_pairs={{0,2},{1,3},{2,0},{3,1},{4,6},{5,7},{6,4},{7,5},{8,10},{9,11},{10,... | collective-permute-start | bytes 393224 | tf_op jit(solution)/shard_map/ppermute | solution.py:37
  83.9 4.1 %collective-permute-done.9 = bf16[64,1024]{1,0:T(8,128)(2,1)S(1)} collective-permute-done((bf16[64,1024]{1,0:T(8,128)(2,1)S(1)}, bf16[64,1024]{1,0:T(8,128)(2,1)S(1)}, u32[]{:S(2)}, u32[]{:S(2)}) %collective-permute-start.9) | collective-permute-done | bytes 131104 | tf_op jit(solution)/shard_map/ppermute | solution.py:37
  (88 shorter events, 8.1 us)
Async XLA Ops:
  0.0 1.2 %copy-start = (bf16[1024,512]{1,0:T(8,128)(2,1)S(1)}, bf16[1024,512]{1,0:T(8,128)(2,1)}, u32[]{:S(2)}) copy-start(bf16[1024,512]{1,0:T(8,128)(2,1)} %param.14) | copy-start | bytes 3145732
  0.0 10.7 %copy-start.6 = (s32[8]{0:T(128)S(1)}, s32[8]{0:T(128)}, u32[]{:S(2)}) copy-start(s32[8]{0:T(128)} %constant.73.clone) | copy-start | bytes 100
  0.0 10.4 %copy-start.1 = (s32[64]{0:T(128)S(1)}, s32[64]{0:T(128)}, u32[]{:S(2)}) copy-start(s32[64]{0:T(128)} %param.20) | copy-start | bytes 772
  0.0 10.7 %copy-start.5 = (s32[128]{0:T(128)S(1)}, s32[128]{0:T(128)}, u32[]{:S(2)}) copy-start(s32[128]{0:T(128)} %param.21) | copy-start | bytes 1540
  0.0 10.8 %copy-start.4 = (s32[64]{0:T(128)S(1)}, s32[64]{0:T(128)}, u32[]{:S(2)}) copy-start(s32[64]{0:T(128)} %param.22) | copy-start | bytes 772
  0.0 20.3 %copy-start.3 = (f32[128,2]{0,1:T(2,128)S(1)}, f32[128,2]{0,1:T(2,128)}, u32[]{:S(2)}) copy-start(f32[128,2]{0,1:T(2,128)} %param.18) | copy-start | bytes 3076
  0.0 26.1 %copy-start.2 = (f32[128,2]{0,1:T(2,128)S(1)}, f32[128,2]{0,1:T(2,128)}, u32[]{:S(2)}) copy-start(f32[128,2]{0,1:T(2,128)} %param.19) | copy-start | bytes 3076
  5.7 9.1 %collective-permute-start.2 = (f32[2,8,2560]{2,1,0:T(8,128)S(1)}, f32[2,8,2560]{2,1,0:T(8,128)S(1)}, u32[]{:S(2)}, u32[]{:S(2)}) collective-permute-start(f32[2,8,2560]{2,1,0:T(8,128)S(1)} %get-tuple-element.12), channel_id=1, source_target_pairs={{0,12},{4,8},{8,4},{12,0},{16,28},{20,24},{24,20},{28,16},{1,13},{... | collective-permute-start | bytes 491528 | tf_op jit(solution)/shard_map/ppermute | solution.py:37
  9.7 7.9 %collective-permute-start.1 = (f32[2,8,2560]{2,1,0:T(8,128)S(1)}, f32[2,8,2560]{2,1,0:T(8,128)S(1)}, u32[]{:S(2)}, u32[]{:S(2)}) collective-permute-start(f32[2,8,2560]{2,1,0:T(8,128)S(1)} %get-tuple-element.13), channel_id=1, source_target_pairs={{0,8},{4,12},{8,0},{12,4},{16,24},{20,28},{24,16},{28,20},{1,9},{5... | collective-permute-start | bytes 491528 | tf_op jit(solution)/shard_map/ppermute | solution.py:37
  10.2 7.5 %collective-permute-start = (f32[2,8,2560]{2,1,0:T(8,128)S(1)}, f32[2,8,2560]{2,1,0:T(8,128)S(1)}, u32[]{:S(2)}, u32[]{:S(2)}) collective-permute-start(f32[2,8,2560]{2,1,0:T(8,128)S(1)} %get-tuple-element.11), channel_id=1, source_target_pairs={{0,4},{4,0},{8,12},{12,8},{16,20},{20,16},{24,28},{28,24},{1,5},{5... | collective-permute-start | bytes 491528 | tf_op jit(solution)/shard_map/ppermute | solution.py:37
  17.7 6.7 %collective-permute-start.3 = (f32[1,8,2560]{2,1,0:T(8,128)S(1)}, f32[1,8,2560]{2,1,0:T(8,128)S(1)}, u32[]{:S(2)}, u32[]{:S(2)}) collective-permute-start(f32[1,8,2560]{2,1,0:T(8,128)S(1)} %constant_dynamic-slice_fusion), channel_id=1, source_target_pairs={{0,16},{4,20},{8,24},{12,28},{16,0},{20,4},{24,8},{28,12},{1,17},{... | collective-permute-start | bytes 245768 | tf_op jit(solution)/shard_map/ppermute | solution.py:37
  24.5 4.9 %collective-permute-start.4 = (bf16[8,2048]{1,0:T(8,128)(2,1)S(1)}, bf16[8,2048]{1,0:T(8,128)(2,1)S(1)}, u32[]{:S(2)}, u32[]{:S(2)}) collective-permute-start(bf16[8,2048]{1,0:T(8,128)(2,1)S(1)} %get-tuple-element.18), channel_id=1, source_target_pairs={{0,16},{4,20},{8,24},{12,28},{16,0},{20,4},{24,8},{28,12},{1,17},{... | collective-permute-start | bytes 98312 | tf_op jit(solution)/shard_map/ppermute | solution.py:37
  29.3 4.6 %collective-permute-start.5 = (bf16[16,2048]{1,0:T(8,128)(2,1)S(1)}, bf16[16,2048]{1,0:T(8,128)(2,1)S(1)}, u32[]{:S(2)}, u32[]{:S(2)}) collective-permute-start(bf16[16,2048]{1,0:T(8,128)(2,1)S(1)} %pad_maximum_fusion.2), channel_id=1, source_target_pairs={{0,4},{4,0},{8,12},{12,8},{16,20},{20,16},{24,28},{28,24},{1,5},{5... | collective-permute-start | bytes 196616 | tf_op jit(solution)/shard_map/ppermute | solution.py:37
  31.7 4.3 %collective-permute-start.6 = (bf16[16,2048]{1,0:T(8,128)(2,1)S(1)}, bf16[16,2048]{1,0:T(8,128)(2,1)S(1)}, u32[]{:S(2)}, u32[]{:S(2)}) collective-permute-start(bf16[16,2048]{1,0:T(8,128)(2,1)S(1)} %pad_maximum_fusion.2), channel_id=1, source_target_pairs={{0,8},{4,12},{8,0},{12,4},{16,24},{20,28},{24,16},{28,20},{1,9},{5... | collective-permute-start | bytes 196616 | tf_op jit(solution)/shard_map/ppermute | solution.py:37
  32.2 5.2 %collective-permute-start.7 = (bf16[16,2048]{1,0:T(8,128)(2,1)S(1)}, bf16[16,2048]{1,0:T(8,128)(2,1)S(1)}, u32[]{:S(2)}, u32[]{:S(2)}) collective-permute-start(bf16[16,2048]{1,0:T(8,128)(2,1)S(1)} %pad_maximum_fusion.2), channel_id=1, source_target_pairs={{0,12},{4,8},{8,4},{12,0},{16,28},{20,24},{24,20},{28,16},{1,13},{... | collective-permute-start | bytes 196616 | tf_op jit(solution)/shard_map/ppermute | solution.py:37
  53.1 12.7 %all-to-all-start = ((bf16[8,8,2176]{2,1,0:T(8,128)(2,1)}), bf16[8,8,2176]{2,1,0:T(8,128)(2,1)S(1)}, u32[]{:S(2)}, u32[]{:S(2)}) async-start(bf16[8,8,2176]{2,1,0:T(8,128)(2,1)} %pad_maximum_fusion.1), calls=%async_computation | async-start | bytes 557056 | tf_op jit(solution)/shard_map/all_to_all | solution.py:27
  80.7 1.6 %collective-permute-start.8 = (f32[64,1024]{1,0:T(8,128)S(1)}, f32[64,1024]{1,0:T(8,128)S(1)}, u32[]{:S(2)}, u32[]{:S(2)}) collective-permute-start(f32[64,1024]{1,0:T(8,128)S(1)} %fusion.20), channel_id=1, source_target_pairs={{0,1},{1,0},{2,3},{3,2},{4,5},{5,4},{6,7},{7,6},{8,9},{9,8},{10,11... | collective-permute-start | bytes 786440 | tf_op jit(solution)/shard_map/ppermute | solution.py:37
  82.3 5.6 %collective-permute-start.9 = (bf16[64,1024]{1,0:T(8,128)(2,1)S(1)}, bf16[64,1024]{1,0:T(8,128)(2,1)S(1)}, u32[]{:S(2)}, u32[]{:S(2)}) collective-permute-start(bf16[64,1024]{1,0:T(8,128)(2,1)S(1)} %fusion.24), channel_id=1, source_target_pairs={{0,2},{1,3},{2,0},{3,1},{4,6},{5,7},{6,4},{7,5},{8,10},{9,11},{10,... | collective-permute-start | bytes 393224 | tf_op jit(solution)/shard_map/ppermute | solution.py:37

commit v3 on v2

v3 whole, which is shorter than its diff:
```python
import functools
import math

import jax
import jax.numpy as jnp
from jax import lax
from jax.experimental import pallas as pl
from jax.experimental.pallas import tpu as pltpu
from jax.sharding import PartitionSpec as P

HD = 128
PAGE = 128
LANES = 128
CHUNK = 8
STAT = 16


masked_low = -1e30


def gather_direct(x, axis, n):
    return lax.all_to_all(jnp.broadcast_to(x[None], (n, *x.shape)), axis, 0, 0).reshape(
        n * x.shape[0], x.shape[1]
    )


def swap(x, axis, n, mask):
    return lax.ppermute(x, axis, [(j, j ^ mask) for j in range(n)])


def bit_groups(n):
    groups, shift = [], 0
    while (1 << shift) < n:
        size = min(4, n >> shift)
        groups.append((shift, size))
        shift += size.bit_length() - 1
    return groups


def scatter_sum(x, axis, n):
    me = lax.axis_index(axis)
    for shift, size in bit_groups(n):
        digit = (me >> shift) % size
        x = x.reshape(x.shape[0] // size, size, *x.shape[1:])

        def block(offset):
            return lax.dynamic_index_in_dim(x, digit ^ offset, axis=1, keepdims=False)

        parts = [swap(block(d), axis, n, d << shift) for d in range(1, size)]
        x = sum(parts, block(0))
    return x[0]


def gather_relative(x, axis, n):
    for shift, size in reversed(bit_groups(n)):
        parts = [x] + [swap(x, axis, n, d << shift) for d in range(1, size)]
        x = jnp.concatenate(parts, axis=0)
    return x


def relative_place(offset, n):
    place, weight = 0, n
    for shift, size in bit_groups(n):
        weight //= size
        place = place + ((offset >> shift) & (size - 1)) * weight
    return place


def attention_kernel(
    row_of,
    request_of,
    value_scale,
    query,
    key_factor,
    valid,
    owner,
    key_cache,
    value_cache,
    out,
    query_low,
    query_high,
    keys,
    values,
    scores,
    page_max,
    dev_max,
    total_out,
    total_sum,
    total_max,
    key_sem,
    value_sem,
):
    slots = key_cache.shape[0]
    heads = LANES // CHUNK
    group = heads // 2
    chunks = slots // CHUNK
    blocks, block_rows, _ = out.shape
    mine = block_rows // heads - 1

    def key_copy(c):
        part = pl.ds(c * CHUNK, CHUNK)
        return pltpu.make_async_copy(key_cache.at[part], keys.at[part], key_sem.at[c])

    def value_copy(c):
        part = pl.ds(c * CHUNK, CHUNK)
        return pltpu.make_async_copy(value_cache.at[part], values.at[part], value_sem.at[c])

    for c in range(chunks):
        key_copy(c).start()
    for c in range(chunks):
        value_copy(c).start()

    rows = query[...]
    low_head = lax.broadcasted_iota(jnp.int32, rows.shape, 0) % heads < group
    zero = jnp.zeros_like(rows)
    query_low[...] = jnp.where(low_head, rows, zero)
    query_high[...] = jnp.where(low_head, zero, rows)
    total_out[...] = jnp.zeros_like(total_out)
    total_sum[...] = jnp.zeros_like(total_sum)
    total_max[...] = jnp.full_like(total_max, masked_low)

    lane_slot = lax.broadcasted_iota(jnp.int32, (PAGE, LANES), 1) // heads
    token = lax.broadcasted_iota(jnp.int32, (PAGE, LANES), 0)

    @pl.loop(0, chunks)
    def _(c):
        places = [pl.multiple_of(row_of[c * CHUNK + s] * heads, heads) for s in range(CHUNK)]
        chosen = jnp.concatenate(
            [
                jnp.concatenate([ref[pl.ds(place, heads), :] for place in places], axis=0)
                for ref in (query_low, query_high)
            ],
            axis=1,
        )
        key_copy(c).wait()
        block = keys[pl.ds(c * CHUNK, CHUNK)].reshape(CHUNK * PAGE, 2 * HD)
        every = lax.dot_general(
            block, chosen, (((1,), (1,)), ((), ())), preferred_element_type=jnp.float32
        )
        score = every[:PAGE]
        for s in range(1, CHUNK):
            score = jnp.where(lane_slot == s, every[s * PAGE : (s + 1) * PAGE], score)
        score = jnp.where(
            token < valid[pl.ds(c, 1), :], score * key_factor[pl.ds(c, 1), :], masked_low
        )
        scores[c] = score
        page_max[pl.ds(c, 1), :] = jnp.max(score, axis=0, keepdims=True)

    biggest, who = page_max[...], owner[...]
    best = biggest
    for turn in range(CHUNK):
        other = pltpu.roll(biggest, turn * heads, 1) if turn else biggest
        other_who = pltpu.roll(who, turn * heads, 1) if turn else who
        for c in range(chunks):
            best = jnp.maximum(
                best, jnp.where(other_who[c : c + 1] == who, other[c : c + 1], masked_low)
            )
    dev_max[...] = best

    ones = jnp.ones((PAGE, LANES), jnp.bfloat16)

    @pl.loop(0, chunks)
    def _(c):
        top = dev_max[pl.ds(c, 1), :]
        prob = jnp.exp(scores[c] - top).T.astype(jnp.bfloat16)
        top_rows = jnp.broadcast_to(top, (PAGE, LANES)).T
        sums = jnp.dot(prob, ones, preferred_element_type=jnp.float32)
        empty = jnp.zeros((heads, PAGE), jnp.bfloat16)
        value_copy(c).wait()
        for s in range(0, CHUNK, 2):
            pair = jnp.concatenate(
                [
                    jnp.concatenate([prob[s * heads : (s + 1) * heads], empty], axis=1),
                    jnp.concatenate([empty, prob[(s + 1) * heads : (s + 2) * heads]], axis=1),
                ],
                axis=0,
            )
            block = values[pl.ds(c * CHUNK + s, 2)].reshape(2 * PAGE, 2 * HD)
            both = jnp.dot(pair, block, preferred_element_type=jnp.float32)
            for t in range(2):
                slot = c * CHUNK + s + t
                here = pl.ds(pl.multiple_of(request_of[slot] * heads, heads), heads)
                base = t * heads
                total_out[here, :] += jnp.concatenate(
                    [
                        both[base : base + group, :HD] * value_scale[2 * slot],
                        both[base + group : base + heads, HD:] * value_scale[2 * slot + 1],
                    ],
                    axis=0,
                )
                part = slice((s + t) * heads, (s + t + 1) * heads)
                total_sum[here, :] += sums[part]
                total_max[here, :] = top_rows[part]

    lane = lax.broadcasted_iota(jnp.int32, (heads, LANES), 1)
    for b in range(blocks):
        first = b * mine * heads
        out[b, : mine * heads, :] = total_out[first : first + mine * heads, :].astype(jnp.bfloat16)
        stat = jnp.zeros((heads, LANES), jnp.float32)
        for r in range(mine):
            part = slice(first + r * heads, first + (r + 1) * heads)
            both = jnp.where(lane % STAT < STAT // 2, total_max[part, :], total_sum[part, :])
            hi = both.astype(jnp.bfloat16).astype(jnp.float32)
            rest = both - hi
            mid = rest.astype(jnp.bfloat16).astype(jnp.float32)
            piece = jnp.where(lane < STAT, hi, jnp.where(lane < 2 * STAT, mid, rest - mid))
            stat = jnp.where(lane % (STAT // 2) == r, piece, stat)
        out[b, mine * heads :, :] = stat.astype(jnp.bfloat16)


def finish_kernel(got, query, keyval, out):
    sources, block_rows, _ = got.shape
    heads = LANES // CHUNK
    group = heads // 2
    mine = block_rows // heads - 1
    lane = lax.broadcasted_iota(jnp.int32, (heads, LANES), 1)
    low_head = lax.broadcasted_iota(jnp.int32, (heads, LANES), 0) < group
    new = keyval[...].astype(jnp.float32)

    def spread(r, which):
        low = jnp.broadcast_to(new[4 * r + which : 4 * r + which + 1], (heads, LANES))
        high = jnp.broadcast_to(new[4 * r + 2 + which : 4 * r + 3 + which], (heads, LANES))
        return jnp.where(low_head, low, high)

    own = jnp.zeros((heads, LANES), jnp.float32)
    for r in range(mine):
        rows = query[r * heads : (r + 1) * heads, :].astype(jnp.float32)
        dot = jnp.sum(rows * spread(r, 0), axis=1, keepdims=True) * (1.0 / math.sqrt(HD))
        own = jnp.where(lane == r, dot, own)
    maxima, sums = [], []
    for j in range(sources):
        stat = got[j, mine * heads :, :].astype(jnp.float32)
        whole = (stat + pltpu.roll(stat, LANES - STAT, 1)) + pltpu.roll(stat, LANES - 2 * STAT, 1)
        maxima.append(jnp.where(lane < mine, whole, 0.0))
        sums.append(jnp.where(lane < mine, pltpu.roll(whole, LANES - STAT // 2, 1), 0.0))
    top = functools.reduce(jnp.maximum, maxima, own)
    fresh = jnp.exp(own - top)
    factors = [jnp.exp(m - top) for m in maxima]
    denom = sum((s * f for s, f in zip(sums, factors)), fresh)
    fresh = fresh / denom
    factors = [f / denom for f in factors]
    for r in range(mine):
        numer = fresh[:, r : r + 1] * spread(r, 1)
        for j in range(sources):
            part = got[j, r * heads : (r + 1) * heads, :].astype(jnp.float32)
            numer = numer + factors[j][:, r : r + 1] * part
        out[r * heads : (r + 1) * heads, :] = numer.astype(jnp.bfloat16)


def body(
    hidden_in,
    w_query,
    w_keyval,
    w_out,
    key_cache,
    value_cache,
    key_scale,
    value_scale,
    page_counts,
    slot_pages,
    trim,
    seq_size,
    head_size,
):
    requests = hidden_in.shape[0]
    slots = key_cache.shape[0]
    kv_local = w_keyval.shape[1] // (2 * HD)
    heads_local = w_query.shape[1] // HD
    wide = heads_local * HD
    assert kv_local == 2 and heads_local * CHUNK == LANES
    assert slots % CHUNK == 0
    mine = requests // seq_size
    inverse_square_root = 1.0 / math.sqrt(HD)

    start = jnp.cumsum(page_counts) - page_counts
    ends = start + page_counts
    owner = jnp.sum((ends[None, :] <= slot_pages[:, None]).astype(jnp.int32), axis=1)
    selector = owner[:, None] == jnp.arange(requests, dtype=jnp.int32)[None, :]
    select_int = selector.astype(jnp.int32)
    index = slot_pages - jnp.sum(select_int * start[None, :], axis=1)
    lengths = PAGE * page_counts - trim
    page_valid = jnp.sum(select_int * lengths[None, :], axis=1) - index * PAGE
    block = owner // mine
    row_of = (
        relative_place(lax.axis_index("seq") ^ block, seq_size) * mine + owner - block * mine
    )

    def on_lanes(x):
        return jnp.broadcast_to(x, (slots, heads_local)).reshape(slots // CHUNK, LANES)

    key_factor = on_lanes(
        jnp.repeat(key_scale * inverse_square_root, heads_local // kv_local, axis=1)
    )
    valid = on_lanes(page_valid[:, None])
    owner_lanes = on_lanes(owner[:, None])

    part_query = jnp.dot(hidden_in, w_query, preferred_element_type=jnp.float32)
    part_keyval = jnp.dot(hidden_in, w_keyval, preferred_element_type=jnp.float32)
    part_all = jnp.concatenate([part_query, part_keyval], axis=1)
    sums = scatter_sum(
        part_all.reshape(seq_size, mine, part_all.shape[1]), "seq", seq_size
    ).astype(jnp.bfloat16)
    my_query = sums[:, :wide].reshape(mine * heads_local, HD)
    my_keyval = sums[:, wide:].reshape(mine * 2 * kv_local, HD)
    query = gather_relative(my_query, "seq", seq_size)

    smem = pl.BlockSpec(memory_space=pltpu.SMEM)
    vmem = pl.BlockSpec(memory_space=pltpu.VMEM)
    hbm = pl.BlockSpec(memory_space=pl.ANY)
    chunks = slots // CHUNK
    every_row = requests * heads_local
    block_rows = (mine + 1) * heads_local
    totals = pl.pallas_call(
        attention_kernel,
        out_shape=jax.ShapeDtypeStruct((seq_size, block_rows, HD), jnp.bfloat16),
        in_specs=[smem, smem, smem, vmem, vmem, vmem, vmem, hbm, hbm],
        out_specs=vmem,
        scratch_shapes=[
            pltpu.VMEM((every_row, HD), jnp.bfloat16),
            pltpu.VMEM((every_row, HD), jnp.bfloat16),
            pltpu.VMEM(key_cache.shape, jnp.bfloat16),
            pltpu.VMEM(value_cache.shape, jnp.bfloat16),
            pltpu.VMEM((chunks, PAGE, LANES), jnp.float32),
            pltpu.VMEM((chunks, LANES), jnp.float32),
            pltpu.VMEM((chunks, LANES), jnp.float32),
            pltpu.VMEM((every_row, HD), jnp.float32),
            pltpu.VMEM((every_row, HD), jnp.float32),
            pltpu.VMEM((every_row, HD), jnp.float32),
            pltpu.SemaphoreType.DMA((chunks,)),
            pltpu.SemaphoreType.DMA((chunks,)),
        ],
        compiler_params=pltpu.CompilerParams(vmem_limit_bytes=40 * 2**20),
        cost_estimate=pl.CostEstimate(
            flops=4 * slots * PAGE * wide,
            bytes_accessed=2 * (key_cache.size + value_cache.size),
            transcendentals=slots * PAGE * heads_local,
        ),
        name="paged_attention",
    )(
        row_of,
        owner,
        value_scale.reshape(slots * kv_local),
        query,
        key_factor,
        valid,
        owner_lanes,
        key_cache,
        value_cache,
    )

    got = lax.all_to_all(totals, "seq", 0, 0)
    my_context = pl.pallas_call(
        finish_kernel,
        out_shape=jax.ShapeDtypeStruct((mine * heads_local, HD), jnp.bfloat16),
        in_specs=[vmem, vmem, vmem],
        out_specs=vmem,
        name="finish",
    )(got, my_query, my_keyval).reshape(mine, wide)
    context = gather_direct(my_context, "seq", seq_size)

    total = jnp.dot(context, w_out, preferred_element_type=jnp.float32)
    step = 1
    while step < head_size:
        if step > 1:
            total = lax.reduce_precision(total, 8, 7)
            other = swap(total.astype(jnp.bfloat16), "head", head_size, step)
        else:
            other = swap(total, "head", head_size, step)
        total = total + other.astype(jnp.float32)
        step *= 2
    return total.astype(jnp.bfloat16)


def solution(mesh):
    seq_size, head_size = mesh.shape["seq"], mesh.shape["head"]

    def local(*args):
        return body(*args, seq_size=seq_size, head_size=head_size)

    return jax.shard_map(
        local,
        mesh=mesh,
        in_specs=(
            P(None, "seq"),
            P("seq", "head"),
            P("seq", "head"),
            P("head", "seq"),
            P("seq", None, "head"),
            P("seq", None, "head"),
            P("seq", "head"),
            P("seq", "head"),
            P(),
            P("seq"),
            P(),
        ),
        out_specs=P(None, "seq"),
        check_vma=False,
    )
```

time: 89 us -> 93.3 us (1.048)
  Pallas kernels: 0 us -> 16.7 us
  matrix products: 20.3 us -> 6.49 us
  local copies, waits for them, and re-layouts: 2.81 us -> 7.07 us
  other arithmetic: 4.02 us -> 1.26 us
  waiting for transfers between devices: 31.5 us -> 29.9 us
  starting transfers between devices: 18.6 us -> 20.1 us
    pallas_call x0 -> x2, Pallas kernels: none -> 16.7 us  [the longest x1 14.7 us: body(): pl.pallas_call(attention_kernel, out_shape=jax.ShapeDtypeStruct((seq_size...]
    dot_general x6 -> x0, matrix products: 12.9 us -> none  [the longest x1 6.98 us: body(): jnp.einsum('sgjd,stgd->sgjt', q_sel, key_rows, preferred_element_type=jnp...]
    unnamed x20 -> x24, local copies, waits for them, and re-layouts: 1.53 us -> 4.28 us
    ppermute x10, starting transfers between devices: 14.3 us -> 15.8 us  [swap(): return lax.ppermute(x, axis, [(j, j ^ mask) for j in range(n)])]
    ppermute x10, waiting for transfers between devices: 23.4 us -> 22.1 us  [swap(): return lax.ppermute(x, axis, [(j, j ^ mask) for j in range(n)])]
    reduce_sum x3 -> x0, other arithmetic: 1.01 us -> none  [the longest x1 0.78 us: body(): jnp.sum(probs.astype(jnp.float32), axis=-1).reshape(slots, heads_local)]
  transfers between devices with their start and end apart: 11 -> 11, of which waited for: 10 -> 10; matrix products, arithmetic and copies ran while one was open for 1% -> 3% of each run, Pallas kernels for 0% -> 0%
where the time goes in v3:
time: 93.3 us; the launch traced here: 92.9 us
  waiting for transfers between devices  29.9 us (32%)
  starting transfers between devices  20.1 us (22%)
  Pallas kernels  16.7 us (18%)
  blocking collectives  11 us (12%)
  local copies, waits for them, and re-layouts  7.07 us (8%)
  matrix products  6.49 us (7%)
  other arithmetic  1.26 us (1%)
    ppermute x10, waiting for transfers between devices, swap(): return lax.ppermute(x, axis, [(j, j ^ mask) for j in range(n)])  22.1 us
    ppermute x10, starting transfers between devices, swap(): return lax.ppermute(x, axis, [(j, j ^ mask) for j in range(n)])  15.8 us
    pallas_call x1, Pallas kernels, body(): pl.pallas_call(attention_kernel, out_shape=jax.ShapeDtypeStruct((seq_size...  14.7 us
    all_to_all x1, blocking collectives, gather_direct(): lax.all_to_all(jnp.broadcast_to(x[None], (n, *x.shape)), axis, 0, 0)  11 us
    all_to_all x1, waiting for transfers between devices, body(): got = lax.all_to_all(totals, 'seq', 0, 0)  7.83 us
    all_to_all x1, starting transfers between devices, body(): got = lax.all_to_all(totals, 'seq', 0, 0)  4.34 us
    unnamed x24, local copies, waits for them, and re-layouts  4.28 us
    dot_general x1, matrix products, body(): part_query = jnp.dot(hidden_in, w_query, preferred_element_type=jnp.float32)  3.18 us
  transfers between devices with their start and end apart: 11, of which 10 were waited for; matrix products, arithmetic and copies ran while one was open for 3% of the time, Pallas kernels for 0%

profile of v3, /device:TPU:0, one launch (start us, length us, event | category | flops | bytes accessed | tf_op | source)
XLA Modules:
  0.0 92.9 jit_solution(5052329842369046816)
XLA Ops:
  0.0 3.2 %fusion.6 = f32[64,2048]{1,0:T(8,128)S(1)} fusion(bf16[64,1024]{1,0:T(8,128)(2,1)} %param.11, bf16[1024,2048]{1,0:T(8,128)(2,1)} %param.12), kind=kOutput, calls=%fused_computation.34 | convolution fusion | flops 268435456 | bytes 4849664 | tf_op jit(solution)/shard_map/dot_general | solution.py:297
  3.7 3.0 %collective-permute-start = (f32[2,8,2560]{2,1,0:T(8,128)S(1)}, f32[2,8,2560]{2,1,0:T(8,128)S(1)}, u32[]{:S(2)}, u32[]{:S(2)}) collective-permute-start(f32[2,8,2560]{2,1,0:T(8,128)S(1)} %get-tuple-element.7), channel_id=1, source_target_pairs={{0,4},{4,0},{8,12},{12,8},{16,20},{20,16},{24,28},{28,24},{1,5},{5... | collective-permute-start | bytes 491528 | tf_op jit(solution)/shard_map/ppermute | solution.py:28
  6.7 1.6 %collective-permute-start.1 = (f32[2,8,2560]{2,1,0:T(8,128)S(1)}, f32[2,8,2560]{2,1,0:T(8,128)S(1)}, u32[]{:S(2)}, u32[]{:S(2)}) collective-permute-start(f32[2,8,2560]{2,1,0:T(8,128)S(1)} %get-tuple-element.9), channel_id=1, source_target_pairs={{0,8},{4,12},{8,0},{12,4},{16,24},{20,28},{24,16},{28,20},{1,9},{5... | collective-permute-start | bytes 491528 | tf_op jit(solution)/shard_map/ppermute | solution.py:28
  8.9 2.1 %collective-permute-done = f32[2,8,2560]{2,1,0:T(8,128)S(1)} collective-permute-done((f32[2,8,2560]{2,1,0:T(8,128)S(1)}, f32[2,8,2560]{2,1,0:T(8,128)S(1)}, u32[]{:S(2)}, u32[]{:S(2)}) %collective-permute-start) | collective-permute-done | bytes 163872 | tf_op jit(solution)/shard_map/ppermute | solution.py:28
  10.9 2.9 %collective-permute-done.1 = f32[2,8,2560]{2,1,0:T(8,128)S(1)} collective-permute-done((f32[2,8,2560]{2,1,0:T(8,128)S(1)}, f32[2,8,2560]{2,1,0:T(8,128)S(1)}, u32[]{:S(2)}, u32[]{:S(2)}) %collective-permute-start.1) | collective-permute-done | bytes 163872 | tf_op jit(solution)/shard_map/ppermute | solution.py:28
  13.8 1.8 %collective-permute-done.2 = f32[2,8,2560]{2,1,0:T(8,128)S(1)} collective-permute-done((f32[2,8,2560]{2,1,0:T(8,128)S(1)}, f32[2,8,2560]{2,1,0:T(8,128)S(1)}, u32[]{:S(2)}, u32[]{:S(2)}) %collective-permute-start.2) | collective-permute-done | bytes 163872 | tf_op jit(solution)/shard_map/ppermute | solution.py:28
  15.7 2.8 %collective-permute-start.3 = (f32[1,8,2560]{2,1,0:T(8,128)S(1)}, f32[1,8,2560]{2,1,0:T(8,128)S(1)}, u32[]{:S(2)}, u32[]{:S(2)}) collective-permute-start(f32[1,8,2560]{2,1,0:T(8,128)S(1)} %constant_dynamic-slice_fusion), channel_id=1, source_target_pairs={{0,16},{4,20},{8,24},{12,28},{16,0},{20,4},{24,8},{28,12},{1,17},{... | collective-permute-start | bytes 245768 | tf_op jit(solution)/shard_map/ppermute | solution.py:28
  18.5 2.6 %collective-permute-done.3 = f32[1,8,2560]{2,1,0:T(8,128)S(1)} collective-permute-done((f32[1,8,2560]{2,1,0:T(8,128)S(1)}, f32[1,8,2560]{2,1,0:T(8,128)S(1)}, u32[]{:S(2)}, u32[]{:S(2)}) %collective-permute-start.3) | collective-permute-done | bytes 81952 | tf_op jit(solution)/shard_map/ppermute | solution.py:28
  21.2 2.9 %collective-permute-start.4 = (bf16[128,128]{1,0:T(8,128)(2,1)S(1)}, bf16[128,128]{1,0:T(8,128)(2,1)S(1)}, u32[]{:S(2)}, u32[]{:S(2)}) collective-permute-start(bf16[128,128]{1,0:T(8,128)(2,1)S(1)} %reshape.57.query), channel_id=1, source_target_pairs={{0,16},{4,20},{8,24},{12,28},{16,0},{20,4},{24,8},{28,12},{1,17},{... | collective-permute-start | bytes 98312 | tf_op jit(solution)/shard_map/ppermute | solution.py:28
  24.1 2.0 %collective-permute-done.4 = bf16[128,128]{1,0:T(8,128)(2,1)S(1)} collective-permute-done((bf16[128,128]{1,0:T(8,128)(2,1)S(1)}, bf16[128,128]{1,0:T(8,128)(2,1)S(1)}, u32[]{:S(2)}, u32[]{:S(2)}) %collective-permute-start.4) | collective-permute-done | bytes 32800 | tf_op jit(solution)/shard_map/ppermute | solution.py:28
  26.1 1.7 %collective-permute-start.5 = (bf16[256,128]{1,0:T(8,128)(2,1)S(1)}, bf16[256,128]{1,0:T(8,128)(2,1)S(1)}, u32[]{:S(2)}, u32[]{:S(2)}) collective-permute-start(bf16[256,128]{1,0:T(8,128)(2,1)S(1)} %get-tuple-element.10), channel_id=1, source_target_pairs={{0,4},{4,0},{8,12},{12,8},{16,20},{20,16},{24,28},{28,24},{1,5},{5... | collective-permute-start | bytes 196616 | tf_op jit(solution)/shard_map/ppermute | solution.py:28
  29.2 2.1 %collective-permute-start.6 = (bf16[256,128]{1,0:T(8,128)(2,1)S(1)}, bf16[256,128]{1,0:T(8,128)(2,1)S(1)}, u32[]{:S(2)}, u32[]{:S(2)}) collective-permute-start(bf16[256,128]{1,0:T(8,128)(2,1)S(1)} %get-tuple-element.10), channel_id=1, source_target_pairs={{0,8},{4,12},{8,0},{12,4},{16,24},{20,28},{24,16},{28,20},{1,9},{5... | collective-permute-start | bytes 196616 | tf_op jit(solution)/shard_map/ppermute | solution.py:28
  31.3 2.2 %collective-permute-done.6 = bf16[256,128]{1,0:T(8,128)(2,1)S(1)} collective-permute-done((bf16[256,128]{1,0:T(8,128)(2,1)S(1)}, bf16[256,128]{1,0:T(8,128)(2,1)S(1)}, u32[]{:S(2)}, u32[]{:S(2)}) %collective-permute-start.6) | collective-permute-done | bytes 65568 | tf_op jit(solution)/shard_map/ppermute | solution.py:28
  33.5 2.9 %collective-permute-done.7 = bf16[256,128]{1,0:T(8,128)(2,1)S(1)} collective-permute-done((bf16[256,128]{1,0:T(8,128)(2,1)S(1)}, bf16[256,128]{1,0:T(8,128)(2,1)S(1)}, u32[]{:S(2)}, u32[]{:S(2)}) %collective-permute-start.7) | collective-permute-done | bytes 65568 | tf_op jit(solution)/shard_map/ppermute | solution.py:28
  36.4 3.4 %copy-done.1 = bf16[128,128,256]{2,1,0:T(8,128)(2,1)S(1)} copy-done((bf16[128,128,256]{2,1,0:T(8,128)(2,1)S(1)}, bf16[128,128,256]{2,1,0:T(8,128)(2,1)}, u32[]{:S(2)}) %copy-start.1) | copy-done | bytes 8388632
  39.8 14.7 %paged_attention.1 = bf16[8,144,128]{2,1,0:T(8,128)(2,1)} custom-call(s32[128]{0:T(128)S(1)} %multiply_subtract_fusion.2.row_of, s32[128]{0:T(128)S(1)} %convert_reduce_fusion.request_of, f32[256]{0:T(256)S(1)} %reshape.56.value_scale, bf16[1024,128]{1,0:T(8,128)(2,1)S(1)} %constant_dynamic-update-slice_fusion.2.query, ...), custom_call_target="tpu_custom_call" | custom-call | flops 134217728 | bytes 16777216 | tf_op jit(solution)/shard_map/paged_attention/pallas_call | solution.py:313
  54.5 4.3 %all-to-all-start = ((bf16[8,144,128]{2,1,0:T(8,128)(2,1)}), bf16[8,144,128]{2,1,0:T(8,128)(2,1)S(1)}, u32[]{:S(2)}, u32[]{:S(2)}) async-start(bf16[8,144,128]{2,1,0:T(8,128)(2,1)} %paged_attention.1), calls=%async_computation | async-start | bytes 589824 | tf_op jit(solution)/shard_map/all_to_all | solution.py:351
  59.5 7.8 %all-to-all-done.got = bf16[8,144,128]{2,1,0:T(8,128)(2,1)S(1)} async-done(((bf16[8,144,128]{2,1,0:T(8,128)(2,1)}), bf16[8,144,128]{2,1,0:T(8,128)(2,1)S(1)}, u32[]{:S(2)}, u32[]{:S(2)}) %all-to-all-start) | async-done | bytes 294944 | tf_op jit(solution)/shard_map/all_to_all | solution.py:351
  68.0 2.0 %finish.1 = bf16[128,128]{1,0:T(8,128)(2,1)} custom-call(bf16[8,144,128]{2,1,0:T(8,128)(2,1)} %copy-done.2, bf16[128,128]{1,0:T(8,128)(2,1)} %copy-done.4, bf16[32,128]{1,0:T(8,128)(2,1)} %reshape.58.keyval), custom_call_target="tpu_custom_call" | custom-call | tf_op jit(solution)/shard_map/finish/pallas_call | solution.py:352
  70.9 11.0 %all_to_all.10 = bf16[8,8,2048]{2,1,0:T(8,128)(2,1)S(1)} all-to-all(bf16[8,8,2048]{2,1,0:T(8,128)(2,1)S(1)} %broadcast_in_dim.44), channel_id=1, replica_groups=mesh['seq'=8,'head'=4] {'seq'}, dimensions={0} | all-to-all | bytes 524288 | tf_op jit(solution)/shard_map/all_to_all | solution.py:22
  81.9 3.0 %fusion = f32[64,1024]{1,0:T(8,128)S(1)} fusion(bf16[2048,1024]{1,0:T(8,128)(2,1)} %param.14, bf16[8,8,2048]{2,1,0:T(8,128)(2,1)S(1)} %all_to_all.10), kind=kOutput, calls=%fused_computation.1 | convolution fusion | flops 268435456 | bytes 4718592 | tf_op jit(solution)/shard_map/dot_general | solution.py:361
  85.0 1.5 %collective-permute-done.8 = f32[64,1024]{1,0:T(8,128)S(1)} collective-permute-done((f32[64,1024]{1,0:T(8,128)S(1)}, f32[64,1024]{1,0:T(8,128)S(1)}, u32[]{:S(2)}, u32[]{:S(2)}) %collective-permute-start.8) | collective-permute-done | bytes 262176 | tf_op jit(solution)/shard_map/ppermute | solution.py:28
  86.6 1.6 %collective-permute-start.9 = (bf16[64,1024]{1,0:T(8,128)(2,1)S(1)}, bf16[64,1024]{1,0:T(8,128)(2,1)S(1)}, u32[]{:S(2)}, u32[]{:S(2)}) collective-permute-start(bf16[64,1024]{1,0:T(8,128)(2,1)S(1)} %fusion.4), channel_id=1, source_target_pairs={{0,2},{1,3},{2,0},{3,1},{4,6},{5,7},{6,4},{7,5},{8,10},{9,11},{10,... | collective-permute-start | bytes 393224 | tf_op jit(solution)/shard_map/ppermute | solution.py:28
  88.1 4.0 %collective-permute-done.9 = bf16[64,1024]{1,0:T(8,128)(2,1)S(1)} collective-permute-done((bf16[64,1024]{1,0:T(8,128)(2,1)S(1)}, bf16[64,1024]{1,0:T(8,128)(2,1)S(1)}, u32[]{:S(2)}, u32[]{:S(2)}) %collective-permute-start.9) | collective-permute-done | bytes 131104 | tf_op jit(solution)/shard_map/ppermute | solution.py:28
  (62 shorter events, 5.3 us)
Async XLA Ops:
  0.0 3.2 %copy-start = (bf16[1024,512]{1,0:T(8,128)(2,1)S(1)}, bf16[1024,512]{1,0:T(8,128)(2,1)}, u32[]{:S(2)}) copy-start(bf16[1024,512]{1,0:T(8,128)(2,1)} %param.13) | copy-start | bytes 3145732
  0.0 3.2 %copy-start.3 = (bf16[64,1024]{1,0:T(8,128)(2,1)S(1)}, bf16[64,1024]{1,0:T(8,128)(2,1)}, u32[]{:S(2)}) copy-start(bf16[64,1024]{1,0:T(8,128)(2,1)} %param.11) | copy-start | bytes 393220
  0.0 8.3 %copy-start.5 = (s32[64]{0:T(128)S(1)}, s32[64]{0:T(128)}, u32[]{:S(2)}) copy-start(s32[64]{0:T(128)} %param.19) | copy-start | bytes 772
  0.0 8.6 %copy-start.7 = (f32[128,2]{0,1:T(2,128)S(1)}, f32[128,2]{0,1:T(2,128)}, u32[]{:S(2)}) copy-start(f32[128,2]{0,1:T(2,128)} %param.17) | copy-start | bytes 3076
  0.0 8.6 %copy-start.8 = (s32[64]{0:T(128)S(1)}, s32[64]{0:T(128)}, u32[]{:S(2)}) copy-start(s32[64]{0:T(128)} %param.21) | copy-start | bytes 772
  0.0 8.6 %copy-start.9 = (s32[128]{0:T(128)S(1)}, s32[128]{0:T(128)}, u32[]{:S(2)}) copy-start(s32[128]{0:T(128)} %param.20) | copy-start | bytes 1540
  3.2 25.7 %copy-start.6 = (f32[128,2]{0,1:T(2,128)S(1)}, f32[128,2]{0,1:T(2,128)}, u32[]{:S(2)}) copy-start(f32[128,2]{0,1:T(2,128)} %param.18) | copy-start | bytes 3076
  3.7 7.2 %collective-permute-start = (f32[2,8,2560]{2,1,0:T(8,128)S(1)}, f32[2,8,2560]{2,1,0:T(8,128)S(1)}, u32[]{:S(2)}, u32[]{:S(2)}) collective-permute-start(f32[2,8,2560]{2,1,0:T(8,128)S(1)} %get-tuple-element.7), channel_id=1, source_target_pairs={{0,4},{4,0},{8,12},{12,8},{16,20},{20,16},{24,28},{28,24},{1,5},{5... | collective-permute-start | bytes 491528 | tf_op jit(solution)/shard_map/ppermute | solution.py:28
  6.7 7.1 %collective-permute-start.1 = (f32[2,8,2560]{2,1,0:T(8,128)S(1)}, f32[2,8,2560]{2,1,0:T(8,128)S(1)}, u32[]{:S(2)}, u32[]{:S(2)}) collective-permute-start(f32[2,8,2560]{2,1,0:T(8,128)S(1)} %get-tuple-element.9), channel_id=1, source_target_pairs={{0,8},{4,12},{8,0},{12,4},{16,24},{20,28},{24,16},{28,20},{1,9},{5... | collective-permute-start | bytes 491528 | tf_op jit(solution)/shard_map/ppermute | solution.py:28
  8.3 7.4 %collective-permute-start.2 = (f32[2,8,2560]{2,1,0:T(8,128)S(1)}, f32[2,8,2560]{2,1,0:T(8,128)S(1)}, u32[]{:S(2)}, u32[]{:S(2)}) collective-permute-start(f32[2,8,2560]{2,1,0:T(8,128)S(1)} %get-tuple-element.8), channel_id=1, source_target_pairs={{0,12},{4,8},{8,4},{12,0},{16,28},{20,24},{24,20},{28,16},{1,13},{... | collective-permute-start | bytes 491528 | tf_op jit(solution)/shard_map/ppermute | solution.py:28
  15.7 5.4 %collective-permute-start.3 = (f32[1,8,2560]{2,1,0:T(8,128)S(1)}, f32[1,8,2560]{2,1,0:T(8,128)S(1)}, u32[]{:S(2)}, u32[]{:S(2)}) collective-permute-start(f32[1,8,2560]{2,1,0:T(8,128)S(1)} %constant_dynamic-slice_fusion), channel_id=1, source_target_pairs={{0,16},{4,20},{8,24},{12,28},{16,0},{20,4},{24,8},{28,12},{1,17},{... | collective-permute-start | bytes 245768 | tf_op jit(solution)/shard_map/ppermute | solution.py:28
  21.2 33.3 %copy-start.4 = (bf16[128,128]{1,0:T(8,128)(2,1)}, bf16[128,128]{1,0:T(8,128)(2,1)S(1)}, u32[]{:S(2)}) copy-start(bf16[128,128]{1,0:T(8,128)(2,1)S(1)} %reshape.57.query) | copy-start | bytes 98308
  21.2 4.9 %collective-permute-start.4 = (bf16[128,128]{1,0:T(8,128)(2,1)S(1)}, bf16[128,128]{1,0:T(8,128)(2,1)S(1)}, u32[]{:S(2)}, u32[]{:S(2)}) collective-permute-start(bf16[128,128]{1,0:T(8,128)(2,1)S(1)} %reshape.57.query), channel_id=1, source_target_pairs={{0,16},{4,20},{8,24},{12,28},{16,0},{20,4},{24,8},{28,12},{1,17},{... | collective-permute-start | bytes 98312 | tf_op jit(solution)/shard_map/ppermute | solution.py:28
  26.1 5.2 %collective-permute-start.5 = (bf16[256,128]{1,0:T(8,128)(2,1)S(1)}, bf16[256,128]{1,0:T(8,128)(2,1)S(1)}, u32[]{:S(2)}, u32[]{:S(2)}) collective-permute-start(bf16[256,128]{1,0:T(8,128)(2,1)S(1)} %get-tuple-element.10), channel_id=1, source_target_pairs={{0,4},{4,0},{8,12},{12,8},{16,20},{20,16},{24,28},{28,24},{1,5},{5... | collective-permute-start | bytes 196616 | tf_op jit(solution)/shard_map/ppermute | solution.py:28
  29.2 4.3 %collective-permute-start.6 = (bf16[256,128]{1,0:T(8,128)(2,1)S(1)}, bf16[256,128]{1,0:T(8,128)(2,1)S(1)}, u32[]{:S(2)}, u32[]{:S(2)}) collective-permute-start(bf16[256,128]{1,0:T(8,128)(2,1)S(1)} %get-tuple-element.10), channel_id=1, source_target_pairs={{0,8},{4,12},{8,0},{12,4},{16,24},{20,28},{24,16},{28,20},{1,9},{5... | collective-permute-start | bytes 196616 | tf_op jit(solution)/shard_map/ppermute | solution.py:28
  31.2 5.2 %collective-permute-start.7 = (bf16[256,128]{1,0:T(8,128)(2,1)S(1)}, bf16[256,128]{1,0:T(8,128)(2,1)S(1)}, u32[]{:S(2)}, u32[]{:S(2)}) collective-permute-start(bf16[256,128]{1,0:T(8,128)(2,1)S(1)} %get-tuple-element.10), channel_id=1, source_target_pairs={{0,12},{4,8},{8,4},{12,0},{16,28},{20,24},{24,20},{28,16},{1,13},{... | collective-permute-start | bytes 196616 | tf_op jit(solution)/shard_map/ppermute | solution.py:28
  36.4 3.4 %copy-start.1 = (bf16[128,128,256]{2,1,0:T(8,128)(2,1)S(1)}, bf16[128,128,256]{2,1,0:T(8,128)(2,1)}, u32[]{:S(2)}) copy-start(bf16[128,128,256]{2,1,0:T(8,128)(2,1)} %key_cache.1) | copy-start | bytes 25165828
  54.5 12.8 %all-to-all-start = ((bf16[8,144,128]{2,1,0:T(8,128)(2,1)}), bf16[8,144,128]{2,1,0:T(8,128)(2,1)S(1)}, u32[]{:S(2)}, u32[]{:S(2)}) async-start(bf16[8,144,128]{2,1,0:T(8,128)(2,1)} %paged_attention.1), calls=%async_computation | async-start | bytes 589824 | tf_op jit(solution)/shard_map/all_to_all | solution.py:351
  67.3 0.7 copy-start.2
  84.9 1.6 %collective-permute-start.8 = (f32[64,1024]{1,0:T(8,128)S(1)}, f32[64,1024]{1,0:T(8,128)S(1)}, u32[]{:S(2)}, u32[]{:S(2)}) collective-permute-start(f32[64,1024]{1,0:T(8,128)S(1)} %fusion), channel_id=1, source_target_pairs={{0,1},{1,0},{2,3},{3,2},{4,5},{5,4},{6,7},{7,6},{8,9},{9,8},{10,11... | collective-permute-start | bytes 786440 | tf_op jit(solution)/shard_map/ppermute | solution.py:28
  86.6 5.6 %collective-permute-start.9 = (bf16[64,1024]{1,0:T(8,128)(2,1)S(1)}, bf16[64,1024]{1,0:T(8,128)(2,1)S(1)}, u32[]{:S(2)}, u32[]{:S(2)}) collective-permute-start(bf16[64,1024]{1,0:T(8,128)(2,1)S(1)} %fusion.4), channel_id=1, source_target_pairs={{0,2},{1,3},{2,0},{3,1},{4,6},{5,7},{6,4},{7,5},{8,10},{9,11},{10,... | collective-permute-start | bytes 393224 | tf_op jit(solution)/shard_map/ppermute | solution.py:28

commit v4 on v3

--- a/solution.py
+++ b/solution.py
@@ -16,12 +16,6 @@
 
 
 masked_low = -1e30
-
-
-def gather_direct(x, axis, n):
-    return lax.all_to_all(jnp.broadcast_to(x[None], (n, *x.shape)), axis, 0, 0).reshape(
-        n * x.shape[0], x.shape[1]
-    )
 
 
 def swap(x, axis, n, mask):
@@ -37,7 +31,7 @@
     return groups
 
 
-def scatter_sum(x, axis, n):
+def scatter_sum(x, axis, n, beside):
     me = lax.axis_index(axis)
     for shift, size in bit_groups(n):
         digit = (me >> shift) % size
@@ -47,8 +41,10 @@
             return lax.dynamic_index_in_dim(x, digit ^ offset, axis=1, keepdims=False)
 
         parts = [swap(block(d), axis, n, d << shift) for d in range(1, size)]
+        if shift == 0:
+            parts, beside = lax.optimization_barrier((parts, beside))
         x = sum(parts, block(0))
-    return x[0]
+    return x[0], beside
 
 
 def gather_relative(x, axis, n):
@@ -56,6 +52,24 @@
         parts = [x] + [swap(x, axis, n, d << shift) for d in range(1, size)]
         x = jnp.concatenate(parts, axis=0)
     return x
+
+
+def gather_in_order(x, axis, n):
+    rows = x.shape[0]
+    me = lax.axis_index(axis)
+    held = [(0, x)]
+    out = jnp.zeros((n * rows, x.shape[1]), x.dtype)
+    for shift, size in reversed(bit_groups(n)):
+        stacked = jnp.concatenate([block for _, block in held], axis=0)
+        held = [
+            (d << shift | offset, part[i * rows : (i + 1) * rows])
+            for d in range(size)
+            for part in [swap(stacked, axis, n, d << shift) if d else stacked]
+            for i, (offset, _) in enumerate(held)
+        ]
+    for offset, block in held:
+        out = lax.dynamic_update_slice_in_dim(out, block, (me ^ offset) * rows, axis=0)
+    return out
 
 
 def relative_place(offset, n):
@@ -67,13 +81,9 @@
 
 
 def attention_kernel(
-    row_of,
-    request_of,
-    value_scale,
+    place_of,
     query,
-    key_factor,
-    valid,
-    owner,
+    tables,
     key_cache,
     value_cache,
     out,
@@ -81,12 +91,13 @@
     query_high,
     keys,
     values,
-    scores,
+    probs,
+    page_out,
+    page_sum,
     page_max,
     dev_max,
     total_out,
-    total_sum,
-    total_max,
+    total_stat,
     key_sem,
     value_sem,
 ):
@@ -96,6 +107,7 @@
     chunks = slots // CHUNK
     blocks, block_rows, _ = out.shape
     mine = block_rows // heads - 1
+    chunk_rows = CHUNK * heads
 
     def key_copy(c):
         part = pl.ds(c * CHUNK, CHUNK)
@@ -107,7 +119,6 @@
 
     for c in range(chunks):
         key_copy(c).start()
-    for c in range(chunks):
         value_copy(c).start()
 
     rows = query[...]
@@ -116,15 +127,20 @@
     query_low[...] = jnp.where(low_head, rows, zero)
     query_high[...] = jnp.where(low_head, zero, rows)
     total_out[...] = jnp.zeros_like(total_out)
-    total_sum[...] = jnp.zeros_like(total_sum)
-    total_max[...] = jnp.full_like(total_max, masked_low)
+    stat_lane = lax.broadcasted_iota(jnp.int32, total_stat.shape, 1) % STAT
+    total_stat[...] = jnp.where(stat_lane < STAT // 2, masked_low, 0.0)
+
+    def table(which, c):
+        return tables[pl.ds(which * chunks + c, 1), :]
 
     lane_slot = lax.broadcasted_iota(jnp.int32, (PAGE, LANES), 1) // heads
-    token = lax.broadcasted_iota(jnp.int32, (PAGE, LANES), 0)
-
-    @pl.loop(0, chunks)
-    def _(c):
-        places = [pl.multiple_of(row_of[c * CHUNK + s] * heads, heads) for s in range(CHUNK)]
+    token = lax.broadcasted_iota(jnp.int32, (PAGE, LANES), 0).astype(jnp.float32)
+
+    def score_chunk(c):
+        places = [
+            pl.multiple_of((place_of[c * CHUNK + s] >> 16) * heads, heads)
+            for s in range(CHUNK)
+        ]
         chosen = jnp.concatenate(
             [
                 jnp.concatenate([ref[pl.ds(place, heads), :] for place in places], axis=0)
@@ -132,7 +148,6 @@
             ],
             axis=1,
         )
-        key_copy(c).wait()
         block = keys[pl.ds(c * CHUNK, CHUNK)].reshape(CHUNK * PAGE, 2 * HD)
         every = lax.dot_general(
             block, chosen, (((1,), (1,)), ((), ())), preferred_element_type=jnp.float32
@@ -140,33 +155,19 @@
         score = every[:PAGE]
         for s in range(1, CHUNK):
             score = jnp.where(lane_slot == s, every[s * PAGE : (s + 1) * PAGE], score)
-        score = jnp.where(
-            token < valid[pl.ds(c, 1), :], score * key_factor[pl.ds(c, 1), :], masked_low
+        score = jnp.where(token < table(1, c), score * table(0, c), masked_low)
+        top = jnp.max(score, axis=0, keepdims=True)
+        page_max[pl.ds(c, 1), :] = top
+        probs[c] = jnp.exp(score - top).T.astype(jnp.bfloat16)
+
+    ones = jnp.ones((PAGE, LANES), jnp.bfloat16)
+    empty = jnp.zeros((heads, PAGE), jnp.bfloat16)
+
+    def value_chunk(c):
+        prob = probs[c]
+        page_sum[pl.ds(pl.multiple_of(c * chunk_rows, chunk_rows), chunk_rows), :] = jnp.dot(
+            prob, ones, preferred_element_type=jnp.float32
         )
-        scores[c] = score
-        page_max[pl.ds(c, 1), :] = jnp.max(score, axis=0, keepdims=True)
-
-    biggest, who = page_max[...], owner[...]
-    best = biggest
-    for turn in range(CHUNK):
-        other = pltpu.roll(biggest, turn * heads, 1) if turn else biggest
-        other_who = pltpu.roll(who, turn * heads, 1) if turn else who
-        for c in range(chunks):
-            best = jnp.maximum(
-                best, jnp.where(other_who[c : c + 1] == who, other[c : c + 1], masked_low)
-            )
-    dev_max[...] = best
-
-    ones = jnp.ones((PAGE, LANES), jnp.bfloat16)
-
-    @pl.loop(0, chunks)
-    def _(c):
-        top = dev_max[pl.ds(c, 1), :]
-        prob = jnp.exp(scores[c] - top).T.astype(jnp.bfloat16)
-        top_rows = jnp.broadcast_to(top, (PAGE, LANES)).T
-        sums = jnp.dot(prob, ones, preferred_element_type=jnp.float32)
-        empty = jnp.zeros((heads, PAGE), jnp.bfloat16)
-        value_copy(c).wait()
         for s in range(0, CHUNK, 2):
             pair = jnp.concatenate(
                 [
@@ -177,20 +178,63 @@
             )
             block = values[pl.ds(c * CHUNK + s, 2)].reshape(2 * PAGE, 2 * HD)
             both = jnp.dot(pair, block, preferred_element_type=jnp.float32)
-            for t in range(2):
-                slot = c * CHUNK + s + t
-                here = pl.ds(pl.multiple_of(request_of[slot] * heads, heads), heads)
-                base = t * heads
-                total_out[here, :] += jnp.concatenate(
+            page_out[pl.ds(pl.multiple_of((c * CHUNK + s) * heads, heads), 2 * heads), :] = (
+                jnp.concatenate(
                     [
-                        both[base : base + group, :HD] * value_scale[2 * slot],
-                        both[base + group : base + heads, HD:] * value_scale[2 * slot + 1],
+                        both[:group, :HD],
+                        both[group:heads, HD:],
+                        both[heads : heads + group, :HD],
+                        both[heads + group :, HD:],
                     ],
                     axis=0,
                 )
-                part = slice((s + t) * heads, (s + t + 1) * heads)
-                total_sum[here, :] += sums[part]
-                total_max[here, :] = top_rows[part]
+            )
+
+    key_copy(0).wait()
+    score_chunk(0)
+
+    @pl.loop(1, chunks)
+    def _(c):
+        key_copy(c).wait()
+        value_copy(c - 1).wait()
+        value_chunk(c - 1)
+        score_chunk(c)
+
+    value_copy(chunks - 1).wait()
+    value_chunk(chunks - 1)
+
+    biggest, who = page_max[...], tables[3 * chunks :, :]
+    best = biggest
+    for turn in range(CHUNK):
+        other = pltpu.roll(biggest, turn * heads, 1) if turn else biggest
+        other_who = pltpu.roll(who, turn * heads, 1) if turn else who
+        for c in range(chunks):
+            best = jnp.maximum(
+                best, jnp.where(other_who[c : c + 1] == who, other[c : c + 1], masked_low)
+            )
+    dev_max[...] = best
+
+    keep_max = lax.broadcasted_iota(jnp.int32, (heads, LANES), 1) % STAT < STAT // 2
+
+    @pl.loop(0, chunks)
+    def _(c):
+        top = dev_max[pl.ds(c, 1), :]
+        weight = jnp.exp(page_max[pl.ds(c, 1), :] - top)
+
+        def on_rows(x):
+            return jnp.broadcast_to(x, (PAGE, LANES)).T
+
+        out_weight, weight, top = on_rows(weight * table(2, c)), on_rows(weight), on_rows(top)
+        for s in range(CHUNK):
+            here = pl.ds(
+                pl.multiple_of((place_of[c * CHUNK + s] & 0xFFFF) * heads, heads), heads
+            )
+            there = pl.ds(pl.multiple_of((c * CHUNK + s) * heads, heads), heads)
+            part = slice(s * heads, (s + 1) * heads)
+            total_out[here, :] += page_out[there, :] * out_weight[part]
+            total_stat[here, :] = jnp.where(
+                keep_max, top[part], total_stat[here, :] + page_sum[there, :] * weight[part]
+            )
 
     lane = lax.broadcasted_iota(jnp.int32, (heads, LANES), 1)
     for b in range(blocks):
@@ -198,14 +242,13 @@
         out[b, : mine * heads, :] = total_out[first : first + mine * heads, :].astype(jnp.bfloat16)
         stat = jnp.zeros((heads, LANES), jnp.float32)
         for r in range(mine):
-            part = slice(first + r * heads, first + (r + 1) * heads)
-            both = jnp.where(lane % STAT < STAT // 2, total_max[part, :], total_sum[part, :])
-            hi = both.astype(jnp.bfloat16).astype(jnp.float32)
-            rest = both - hi
-            mid = rest.astype(jnp.bfloat16).astype(jnp.float32)
-            piece = jnp.where(lane < STAT, hi, jnp.where(lane < 2 * STAT, mid, rest - mid))
-            stat = jnp.where(lane % (STAT // 2) == r, piece, stat)
-        out[b, mine * heads :, :] = stat.astype(jnp.bfloat16)
+            both = total_stat[first + r * heads : first + (r + 1) * heads, :]
+            stat = jnp.where(lane % (STAT // 2) == r, both, stat)
+        hi = stat.astype(jnp.bfloat16).astype(jnp.float32)
+        rest = stat - hi
+        mid = rest.astype(jnp.bfloat16).astype(jnp.float32)
+        piece = jnp.where(lane < STAT, hi, jnp.where(lane < 2 * STAT, mid, rest - mid))
+        out[b, mine * heads :, :] = piece.astype(jnp.bfloat16)
 
 
 def finish_kernel(got, query, keyval, out):
@@ -288,18 +331,27 @@
     def on_lanes(x):
         return jnp.broadcast_to(x, (slots, heads_local)).reshape(slots // CHUNK, LANES)
 
-    key_factor = on_lanes(
-        jnp.repeat(key_scale * inverse_square_root, heads_local // kv_local, axis=1)
+    def per_head(x):
+        return on_lanes(jnp.repeat(x, heads_local // kv_local, axis=1))
+
+    tables = jnp.concatenate(
+        [
+            per_head(key_scale * inverse_square_root),
+            on_lanes(page_valid[:, None].astype(jnp.float32)),
+            per_head(value_scale),
+            on_lanes(owner[:, None].astype(jnp.float32)),
+        ],
+        axis=0,
     )
-    valid = on_lanes(page_valid[:, None])
-    owner_lanes = on_lanes(owner[:, None])
+    place_of = row_of * 65536 + owner
 
     part_query = jnp.dot(hidden_in, w_query, preferred_element_type=jnp.float32)
     part_keyval = jnp.dot(hidden_in, w_keyval, preferred_element_type=jnp.float32)
     part_all = jnp.concatenate([part_query, part_keyval], axis=1)
-    sums = scatter_sum(
-        part_all.reshape(seq_size, mine, part_all.shape[1]), "seq", seq_size
-    ).astype(jnp.bfloat16)
+    sums, (tables, place_of) = scatter_sum(
+        part_all.reshape(seq_size, mine, part_all.shape[1]), "seq", seq_size, (tables, place_of)
+    )
+    sums = sums.astype(jnp.bfloat16)
     my_query = sums[:, :wide].reshape(mine * heads_local, HD)
     my_keyval = sums[:, wide:].reshape(mine * 2 * kv_local, HD)
     query = gather_relative(my_query, "seq", seq_size)
@@ -313,40 +365,31 @@
     totals = pl.pallas_call(
         attention_kernel,
         out_shape=jax.ShapeDtypeStruct((seq_size, block_rows, HD), jnp.bfloat16),
-        in_specs=[smem, smem, smem, vmem, vmem, vmem, vmem, hbm, hbm],
+        in_specs=[smem, vmem, vmem, hbm, hbm],
         out_specs=vmem,
         scratch_shapes=[
             pltpu.VMEM((every_row, HD), jnp.bfloat16),
             pltpu.VMEM((every_row, HD), jnp.bfloat16),
             pltpu.VMEM(key_cache.shape, jnp.bfloat16),
             pltpu.VMEM(value_cache.shape, jnp.bfloat16),
-            pltpu.VMEM((chunks, PAGE, LANES), jnp.float32),
+            pltpu.VMEM((chunks, LANES, PAGE), jnp.bfloat16),
+            pltpu.VMEM((slots * heads_local, HD), jnp.float32),
+            pltpu.VMEM((slots * heads_local, HD), jnp.float32),
             pltpu.VMEM((chunks, LANES), jnp.float32),
             pltpu.VMEM((chunks, LANES), jnp.float32),
-            pltpu.VMEM((every_row, HD), jnp.float32),
             pltpu.VMEM((every_row, HD), jnp.float32),
             pltpu.VMEM((every_row, HD), jnp.float32),
             pltpu.SemaphoreType.DMA((chunks,)),
             pltpu.SemaphoreType.DMA((chunks,)),
         ],
-        compiler_params=pltpu.CompilerParams(vmem_limit_bytes=40 * 2**20),
+        compiler_params=pltpu.CompilerParams(vmem_limit_bytes=58 * 2**20),
         cost_estimate=pl.CostEstimate(
             flops=4 * slots * PAGE * wide,
             bytes_accessed=2 * (key_cache.size + value_cache.size),
             transcendentals=slots * PAGE * heads_local,
         ),
         name="paged_attention",
-    )(
-        row_of,
-        owner,
-        value_scale.reshape(slots * kv_local),
-        query,
-        key_factor,
-        valid,
-        owner_lanes,
-        key_cache,
-        value_cache,
-    )
+    )(place_of, query, tables, key_cache, value_cache)
 
     got = lax.all_to_all(totals, "seq", 0, 0)
     my_context = pl.pallas_call(
@@ -354,9 +397,10 @@
         out_shape=jax.ShapeDtypeStruct((mine * heads_local, HD), jnp.bfloat16),
         in_specs=[vmem, vmem, vmem],
         out_specs=vmem,
+        compiler_params=pltpu.CompilerParams(vmem_limit_bytes=6 * 2**20),
         name="finish",
     )(got, my_query, my_keyval).reshape(mine, wide)
-    context = gather_direct(my_context, "seq", seq_size)
+    context = gather_in_order(my_context, "seq", seq_size)
 
     total = jnp.dot(context, w_out, preferred_element_type=jnp.float32)
     step = 1

time: 93.3 us -> 85.6 us (0.917)
  blocking collectives: 11 us -> 0 us
  waiting for transfers between devices: 29.9 us -> 35 us
  local copies, waits for them, and re-layouts: 7.07 us -> 2.6 us
  starting transfers between devices: 20.1 us -> 24.5 us
  Pallas kernels: 16.7 us -> 14 us
  other arithmetic: 1.26 us -> 2.42 us
    all_to_all x1 -> x0, blocking collectives: 11 us -> none  [gather_direct(): lax.all_to_all(jnp.broadcast_to(x[None], (n, *x.shape)), axis, 0, 0)]
    ppermute x10 -> x14, waiting for transfers between devices: 22.1 us -> 26.5 us  [swap(): return lax.ppermute(x, axis, [(j, j ^ mask) for j in range(n)])]
    ppermute x10 -> x14, starting transfers between devices: 15.8 us -> 20.1 us  [swap(): return lax.ppermute(x, axis, [(j, j ^ mask) for j in range(n)])]
    unnamed x24 -> x21, local copies, waits for them, and re-layouts: 4.28 us -> 0.87 us
    pallas_call x1, Pallas kernels: 2.02 us -> 0.42 us  [body(): pl.pallas_call(finish_kernel, out_shape=jax.ShapeDtypeStruct((mine * head...]
    pallas_call x1, Pallas kernels: 14.7 us -> 13.5 us  [body(): pl.pallas_call(attention_kernel, out_shape=jax.ShapeDtypeStruct((seq_size...]
  transfers between devices with their start and end apart: 11 -> 15, of which waited for: 10 -> 14; matrix products, arithmetic and copies ran while one was open for 3% -> 4% of each run, Pallas kernels for 0% -> 0%
where the time goes in v4:
time: 85.6 us; the launch traced here: 85.3 us
  waiting for transfers between devices  35 us (41%)
  starting transfers between devices  24.5 us (29%)
  Pallas kernels  14 us (16%)
  matrix products  6.49 us (8%)
  local copies, waits for them, and re-layouts  2.6 us (3%)
  other arithmetic  2.42 us (3%)
    ppermute x14, waiting for transfers between devices, swap(): return lax.ppermute(x, axis, [(j, j ^ mask) for j in range(n)])  26.5 us
    ppermute x14, starting transfers between devices, swap(): return lax.ppermute(x, axis, [(j, j ^ mask) for j in range(n)])  20.1 us
    pallas_call x1, Pallas kernels, body(): pl.pallas_call(attention_kernel, out_shape=jax.ShapeDtypeStruct((seq_size...  13.5 us
    all_to_all x1, waiting for transfers between devices, body(): got = lax.all_to_all(totals, 'seq', 0, 0)  8.53 us
    all_to_all x1, starting transfers between devices, body(): got = lax.all_to_all(totals, 'seq', 0, 0)  4.44 us
    dot_general x1, matrix products, body(): part_query = jnp.dot(hidden_in, w_query, preferred_element_type=jnp.float32)  3.18 us
    dot_general x1, matrix products, body(): total = jnp.dot(context, w_out, preferred_element_type=jnp.float32)  3.03 us
  transfers between devices with their start and end apart: 15, of which 14 were waited for; matrix products, arithmetic and copies ran while one was open for 4% of the time, Pallas kernels for 0%

profile of v4, /device:TPU:0, one launch (start us, length us, event | category | flops | bytes accessed | tf_op | source)
XLA Modules:
  0.0 85.3 jit_solution(4100759729132418240)
XLA Ops:
  0.0 3.2 %fusion.4 = f32[64,2048]{1,0:T(8,128)S(1)} fusion(bf16[64,1024]{1,0:T(8,128)(2,1)} %param.11, bf16[1024,2048]{1,0:T(8,128)(2,1)} %param.12), kind=kOutput, calls=%fused_computation.43 | convolution fusion | flops 268435456 | bytes 4849664 | tf_op jit(solution)/shard_map/dot_general | solution.py:348
  3.7 3.0 %collective-permute-start = (f32[2,8,2560]{2,1,0:T(8,128)S(1)}, f32[2,8,2560]{2,1,0:T(8,128)S(1)}, u32[]{:S(2)}, u32[]{:S(2)}) collective-permute-start(f32[2,8,2560]{2,1,0:T(8,128)S(1)} %get-tuple-element.19), channel_id=1, source_target_pairs={{0,4},{4,0},{8,12},{12,8},{16,20},{20,16},{24,28},{28,24},{1,5},{5... | collective-permute-start | bytes 491528 | tf_op jit(solution)/shard_map/ppermute | solution.py:22
  6.7 1.6 %collective-permute-start.1 = (f32[2,8,2560]{2,1,0:T(8,128)S(1)}, f32[2,8,2560]{2,1,0:T(8,128)S(1)}, u32[]{:S(2)}, u32[]{:S(2)}) collective-permute-start(f32[2,8,2560]{2,1,0:T(8,128)S(1)} %get-tuple-element.18), channel_id=1, source_target_pairs={{0,8},{4,12},{8,0},{12,4},{16,24},{20,28},{24,16},{28,20},{1,9},{5... | collective-permute-start | bytes 491528 | tf_op jit(solution)/shard_map/ppermute | solution.py:22
  11.6 2.2 %collective-permute-done.1 = f32[2,8,2560]{2,1,0:T(8,128)S(1)} collective-permute-done((f32[2,8,2560]{2,1,0:T(8,128)S(1)}, f32[2,8,2560]{2,1,0:T(8,128)S(1)}, u32[]{:S(2)}, u32[]{:S(2)}) %collective-permute-start.1) | collective-permute-done | bytes 163872 | tf_op jit(solution)/shard_map/ppermute | solution.py:22
  13.8 1.8 %collective-permute-done.2 = f32[2,8,2560]{2,1,0:T(8,128)S(1)} collective-permute-done((f32[2,8,2560]{2,1,0:T(8,128)S(1)}, f32[2,8,2560]{2,1,0:T(8,128)S(1)}, u32[]{:S(2)}, u32[]{:S(2)}) %collective-permute-start.2) | collective-permute-done | bytes 163872 | tf_op jit(solution)/shard_map/ppermute | solution.py:22
  15.7 2.8 %collective-permute-start.3 = (f32[1,8,2560]{2,1,0:T(8,128)S(1)}, f32[1,8,2560]{2,1,0:T(8,128)S(1)}, u32[]{:S(2)}, u32[]{:S(2)}) collective-permute-start(f32[1,8,2560]{2,1,0:T(8,128)S(1)} %constant_dynamic-slice_fusion), channel_id=1, source_target_pairs={{0,16},{4,20},{8,24},{12,28},{16,0},{20,4},{24,8},{28,12},{1,17},{... | collective-permute-start | bytes 245768 | tf_op jit(solution)/shard_map/ppermute | solution.py:22
  18.5 2.6 %collective-permute-done.3 = f32[1,8,2560]{2,1,0:T(8,128)S(1)} collective-permute-done((f32[1,8,2560]{2,1,0:T(8,128)S(1)}, f32[1,8,2560]{2,1,0:T(8,128)S(1)}, u32[]{:S(2)}, u32[]{:S(2)}) %collective-permute-start.3) | collective-permute-done | bytes 81952 | tf_op jit(solution)/shard_map/ppermute | solution.py:22
  21.2 2.9 %collective-permute-start.4 = (bf16[128,128]{1,0:T(8,128)(2,1)S(1)}, bf16[128,128]{1,0:T(8,128)(2,1)S(1)}, u32[]{:S(2)}, u32[]{:S(2)}) collective-permute-start(bf16[128,128]{1,0:T(8,128)(2,1)S(1)} %reshape.60.query), channel_id=1, source_target_pairs={{0,16},{4,20},{8,24},{12,28},{16,0},{20,4},{24,8},{28,12},{1,17},{... | collective-permute-start | bytes 98312 | tf_op jit(solution)/shard_map/ppermute | solution.py:22
  24.1 2.0 %collective-permute-done.4 = bf16[128,128]{1,0:T(8,128)(2,1)S(1)} collective-permute-done((bf16[128,128]{1,0:T(8,128)(2,1)S(1)}, bf16[128,128]{1,0:T(8,128)(2,1)S(1)}, u32[]{:S(2)}, u32[]{:S(2)}) %collective-permute-start.4) | collective-permute-done | bytes 32800 | tf_op jit(solution)/shard_map/ppermute | solution.py:22
  26.1 1.7 %collective-permute-start.5 = (bf16[256,128]{1,0:T(8,128)(2,1)S(1)}, bf16[256,128]{1,0:T(8,128)(2,1)S(1)}, u32[]{:S(2)}, u32[]{:S(2)}) collective-permute-start(bf16[256,128]{1,0:T(8,128)(2,1)S(1)} %get-tuple-element.24), channel_id=1, source_target_pairs={{0,4},{4,0},{8,12},{12,8},{16,20},{20,16},{24,28},{28,24},{1,5},{5... | collective-permute-start | bytes 196616 | tf_op jit(solution)/shard_map/ppermute | solution.py:22
  27.8 2.0 %collective-permute-start.6 = (bf16[256,128]{1,0:T(8,128)(2,1)S(1)}, bf16[256,128]{1,0:T(8,128)(2,1)S(1)}, u32[]{:S(2)}, u32[]{:S(2)}) collective-permute-start(bf16[256,128]{1,0:T(8,128)(2,1)S(1)} %get-tuple-element.24), channel_id=1, source_target_pairs={{0,8},{4,12},{8,0},{12,4},{16,24},{20,28},{24,16},{28,20},{1,9},{5... | collective-permute-start | bytes 196616 | tf_op jit(solution)/shard_map/ppermute | solution.py:22
  30.8 1.3 %collective-permute-done.6 = bf16[256,128]{1,0:T(8,128)(2,1)S(1)} collective-permute-done((bf16[256,128]{1,0:T(8,128)(2,1)S(1)}, bf16[256,128]{1,0:T(8,128)(2,1)S(1)}, u32[]{:S(2)}, u32[]{:S(2)}) %collective-permute-start.6) | collective-permute-done | bytes 65568 | tf_op jit(solution)/shard_map/ppermute | solution.py:22
  32.1 2.9 %collective-permute-done.7 = bf16[256,128]{1,0:T(8,128)(2,1)S(1)} collective-permute-done((bf16[256,128]{1,0:T(8,128)(2,1)S(1)}, bf16[256,128]{1,0:T(8,128)(2,1)S(1)}, u32[]{:S(2)}, u32[]{:S(2)}) %collective-permute-start.7) | collective-permute-done | bytes 65568 | tf_op jit(solution)/shard_map/ppermute | solution.py:22
  35.7 13.5 %paged_attention.1 = bf16[8,144,128]{2,1,0:T(8,128)(2,1)} custom-call(s32[128]{0:T(128)} %get-tuple-element.10.place_of, bf16[1024,128]{1,0:T(8,128)(2,1)} %copy-done.2, f32[64,128]{1,0:T(8,128)} %pad_maximum_fusion.1.tables, bf16[128,128,256]{2,1,0:T(8,128)(2,1)} %key_cache.1, bf16[128,128,256]{2,1,0:T(8,128)(2,1)} %value_cache.1), custom_call_target="tpu_custom_call" | custom-call | flops 134217728 | bytes 16777216 | tf_op jit(solution)/shard_map/paged_attention/pallas_call | solution.py:365
  49.2 4.4 %all-to-all-start = ((bf16[8,144,128]{2,1,0:T(8,128)(2,1)}), bf16[8,144,128]{2,1,0:T(8,128)(2,1)S(1)}, u32[]{:S(2)}, u32[]{:S(2)}) async-start(bf16[8,144,128]{2,1,0:T(8,128)(2,1)} %paged_attention.1), calls=%async_computation | async-start | bytes 589824 | tf_op jit(solution)/shard_map/all_to_all | solution.py:394
  53.7 8.5 %all-to-all-done.got = bf16[8,144,128]{2,1,0:T(8,128)(2,1)S(1)} async-done(((bf16[8,144,128]{2,1,0:T(8,128)(2,1)}), bf16[8,144,128]{2,1,0:T(8,128)(2,1)S(1)}, u32[]{:S(2)}, u32[]{:S(2)}) %all-to-all-start) | async-done | bytes 294944 | tf_op jit(solution)/shard_map/all_to_all | solution.py:394
  63.6 3.9 %collective-permute-done.8 = bf16[8,2048]{1,0:T(8,128)(2,1)S(1)} collective-permute-done((bf16[8,2048]{1,0:T(8,128)(2,1)S(1)}, bf16[8,2048]{1,0:T(8,128)(2,1)S(1)}, u32[]{:S(2)}, u32[]{:S(2)}) %collective-permute-start.8) | collective-permute-done | bytes 32800 | tf_op jit(solution)/shard_map/ppermute | solution.py:22
  67.6 1.3 %collective-permute-start.9 = (bf16[16,2048]{1,0:T(8,128)(2,1)S(1)}, bf16[16,2048]{1,0:T(8,128)(2,1)S(1)}, u32[]{:S(2)}, u32[]{:S(2)}) collective-permute-start(bf16[16,2048]{1,0:T(8,128)(2,1)S(1)} %get-tuple-element.20), channel_id=1, source_target_pairs={{0,4},{4,0},{8,12},{12,8},{16,20},{20,16},{24,28},{28,24},{1,5},{5... | collective-permute-start | bytes 196616 | tf_op jit(solution)/shard_map/ppermute | solution.py:22
  69.1 2.0 %collective-permute-start.11 = (bf16[16,2048]{1,0:T(8,128)(2,1)S(1)}, bf16[16,2048]{1,0:T(8,128)(2,1)S(1)}, u32[]{:S(2)}, u32[]{:S(2)}) collective-permute-start(bf16[16,2048]{1,0:T(8,128)(2,1)S(1)} %get-tuple-element.20), channel_id=1, source_target_pairs={{0,12},{4,8},{8,4},{12,0},{16,28},{20,24},{24,20},{28,16},{1,13},{... | collective-permute-start | bytes 196616 | tf_op jit(solution)/shard_map/ppermute | solution.py:22
  71.9 1.3 %collective-permute-done.10 = bf16[16,2048]{1,0:T(8,128)(2,1)S(1)} collective-permute-done((bf16[16,2048]{1,0:T(8,128)(2,1)S(1)}, bf16[16,2048]{1,0:T(8,128)(2,1)S(1)}, u32[]{:S(2)}, u32[]{:S(2)}) %collective-permute-start.10) | collective-permute-done | bytes 65568 | tf_op jit(solution)/shard_map/ppermute | solution.py:22
  74.3 3.0 %fusion.6 = f32[64,1024]{1,0:T(8,128)S(1)} fusion(bf16[64,2048]{1,0:T(8,128)(2,1)S(1)} %slice_dynamic-update-slice_fusion, bf16[2048,1024]{1,0:T(8,128)(2,1)} %param.14), kind=kOutput, calls=%fused_computation.45 | convolution fusion | flops 268435456 | bytes 4718592 | tf_op jit(solution)/shard_map/dot_general | solution.py:405
  77.4 1.5 %collective-permute-done.12 = f32[64,1024]{1,0:T(8,128)S(1)} collective-permute-done((f32[64,1024]{1,0:T(8,128)S(1)}, f32[64,1024]{1,0:T(8,128)S(1)}, u32[]{:S(2)}, u32[]{:S(2)}) %collective-permute-start.12) | collective-permute-done | bytes 262176 | tf_op jit(solution)/shard_map/ppermute | solution.py:22
  79.0 1.6 %collective-permute-start.13 = (bf16[64,1024]{1,0:T(8,128)(2,1)S(1)}, bf16[64,1024]{1,0:T(8,128)(2,1)S(1)}, u32[]{:S(2)}, u32[]{:S(2)}) collective-permute-start(bf16[64,1024]{1,0:T(8,128)(2,1)S(1)} %fusion.2), channel_id=1, source_target_pairs={{0,2},{1,3},{2,0},{3,1},{4,6},{5,7},{6,4},{7,5},{8,10},{9,11},{10,... | collective-permute-start | bytes 393224 | tf_op jit(solution)/shard_map/ppermute | solution.py:22
  80.5 4.0 %collective-permute-done.13 = bf16[64,1024]{1,0:T(8,128)(2,1)S(1)} collective-permute-done((bf16[64,1024]{1,0:T(8,128)(2,1)S(1)}, bf16[64,1024]{1,0:T(8,128)(2,1)S(1)}, u32[]{:S(2)}, u32[]{:S(2)}) %collective-permute-start.13) | collective-permute-done | bytes 131104 | tf_op jit(solution)/shard_map/ppermute | solution.py:22
  (75 shorter events, 9.8 us)
Async XLA Ops:
  0.0 3.2 %copy-start = (bf16[1024,512]{1,0:T(8,128)(2,1)S(1)}, bf16[1024,512]{1,0:T(8,128)(2,1)}, u32[]{:S(2)}) copy-start(bf16[1024,512]{1,0:T(8,128)(2,1)} %param.13) | copy-start | bytes 3145732
  0.0 3.2 %copy-start.1 = (bf16[64,1024]{1,0:T(8,128)(2,1)S(1)}, bf16[64,1024]{1,0:T(8,128)(2,1)}, u32[]{:S(2)}) copy-start(bf16[64,1024]{1,0:T(8,128)(2,1)} %param.11) | copy-start | bytes 393220
  0.0 8.3 %copy-start.3 = (s32[64]{0:T(128)S(1)}, s32[64]{0:T(128)}, u32[]{:S(2)}) copy-start(s32[64]{0:T(128)} %param.19) | copy-start | bytes 772
  0.0 8.6 %copy-start.6 = (s32[64]{0:T(128)S(1)}, s32[64]{0:T(128)}, u32[]{:S(2)}) copy-start(s32[64]{0:T(128)} %param.21) | copy-start | bytes 772
  0.0 8.6 %copy-start.7 = (s32[128]{0:T(128)S(1)}, s32[128]{0:T(128)}, u32[]{:S(2)}) copy-start(s32[128]{0:T(128)} %param.20) | copy-start | bytes 1540
  0.0 8.7 %copy-start.5 = (f32[128,2]{0,1:T(2,128)S(1)}, f32[128,2]{0,1:T(2,128)}, u32[]{:S(2)}) copy-start(f32[128,2]{0,1:T(2,128)} %param.17) | copy-start | bytes 3076
  0.0 10.4 %copy-start.4 = (f32[128,2]{0,1:T(2,128)S(1)}, f32[128,2]{0,1:T(2,128)}, u32[]{:S(2)}) copy-start(f32[128,2]{0,1:T(2,128)} %param.18) | copy-start | bytes 3076
  3.7 7.9 %collective-permute-start = (f32[2,8,2560]{2,1,0:T(8,128)S(1)}, f32[2,8,2560]{2,1,0:T(8,128)S(1)}, u32[]{:S(2)}, u32[]{:S(2)}) collective-permute-start(f32[2,8,2560]{2,1,0:T(8,128)S(1)} %get-tuple-element.19), channel_id=1, source_target_pairs={{0,4},{4,0},{8,12},{12,8},{16,20},{20,16},{24,28},{28,24},{1,5},{5... | collective-permute-start | bytes 491528 | tf_op jit(solution)/shard_map/ppermute | solution.py:22
  6.7 7.1 %collective-permute-start.1 = (f32[2,8,2560]{2,1,0:T(8,128)S(1)}, f32[2,8,2560]{2,1,0:T(8,128)S(1)}, u32[]{:S(2)}, u32[]{:S(2)}) collective-permute-start(f32[2,8,2560]{2,1,0:T(8,128)S(1)} %get-tuple-element.18), channel_id=1, source_target_pairs={{0,8},{4,12},{8,0},{12,4},{16,24},{20,28},{24,16},{28,20},{1,9},{5... | collective-permute-start | bytes 491528 | tf_op jit(solution)/shard_map/ppermute | solution.py:22
  8.3 7.4 %collective-permute-start.2 = (f32[2,8,2560]{2,1,0:T(8,128)S(1)}, f32[2,8,2560]{2,1,0:T(8,128)S(1)}, u32[]{:S(2)}, u32[]{:S(2)}) collective-permute-start(f32[2,8,2560]{2,1,0:T(8,128)S(1)} %get-tuple-element.17), channel_id=1, source_target_pairs={{0,12},{4,8},{8,4},{12,0},{16,28},{20,24},{24,20},{28,16},{1,13},{... | collective-permute-start | bytes 491528 | tf_op jit(solution)/shard_map/ppermute | solution.py:22
  15.7 5.4 %collective-permute-start.3 = (f32[1,8,2560]{2,1,0:T(8,128)S(1)}, f32[1,8,2560]{2,1,0:T(8,128)S(1)}, u32[]{:S(2)}, u32[]{:S(2)}) collective-permute-start(f32[1,8,2560]{2,1,0:T(8,128)S(1)} %constant_dynamic-slice_fusion), channel_id=1, source_target_pairs={{0,16},{4,20},{8,24},{12,28},{16,0},{20,4},{24,8},{28,12},{1,17},{... | collective-permute-start | bytes 245768 | tf_op jit(solution)/shard_map/ppermute | solution.py:22
  21.2 4.9 %collective-permute-start.4 = (bf16[128,128]{1,0:T(8,128)(2,1)S(1)}, bf16[128,128]{1,0:T(8,128)(2,1)S(1)}, u32[]{:S(2)}, u32[]{:S(2)}) collective-permute-start(bf16[128,128]{1,0:T(8,128)(2,1)S(1)} %reshape.60.query), channel_id=1, source_target_pairs={{0,16},{4,20},{8,24},{12,28},{16,0},{20,4},{24,8},{28,12},{1,17},{... | collective-permute-start | bytes 98312 | tf_op jit(solution)/shard_map/ppermute | solution.py:22
  26.1 4.7 %collective-permute-start.5 = (bf16[256,128]{1,0:T(8,128)(2,1)S(1)}, bf16[256,128]{1,0:T(8,128)(2,1)S(1)}, u32[]{:S(2)}, u32[]{:S(2)}) collective-permute-start(bf16[256,128]{1,0:T(8,128)(2,1)S(1)} %get-tuple-element.24), channel_id=1, source_target_pairs={{0,4},{4,0},{8,12},{12,8},{16,20},{20,16},{24,28},{28,24},{1,5},{5... | collective-permute-start | bytes 196616 | tf_op jit(solution)/shard_map/ppermute | solution.py:22
  27.8 4.3 %collective-permute-start.6 = (bf16[256,128]{1,0:T(8,128)(2,1)S(1)}, bf16[256,128]{1,0:T(8,128)(2,1)S(1)}, u32[]{:S(2)}, u32[]{:S(2)}) collective-permute-start(bf16[256,128]{1,0:T(8,128)(2,1)S(1)} %get-tuple-element.24), channel_id=1, source_target_pairs={{0,8},{4,12},{8,0},{12,4},{16,24},{20,28},{24,16},{28,20},{1,9},{5... | collective-permute-start | bytes 196616 | tf_op jit(solution)/shard_map/ppermute | solution.py:22
  29.8 5.2 %collective-permute-start.7 = (bf16[256,128]{1,0:T(8,128)(2,1)S(1)}, bf16[256,128]{1,0:T(8,128)(2,1)S(1)}, u32[]{:S(2)}, u32[]{:S(2)}) collective-permute-start(bf16[256,128]{1,0:T(8,128)(2,1)S(1)} %get-tuple-element.24), channel_id=1, source_target_pairs={{0,12},{4,8},{8,4},{12,0},{16,28},{20,24},{24,20},{28,16},{1,13},{... | collective-permute-start | bytes 196616 | tf_op jit(solution)/shard_map/ppermute | solution.py:22
  35.0 0.7 copy-start.2
  49.2 13.0 %all-to-all-start = ((bf16[8,144,128]{2,1,0:T(8,128)(2,1)}), bf16[8,144,128]{2,1,0:T(8,128)(2,1)S(1)}, u32[]{:S(2)}, u32[]{:S(2)}) async-start(bf16[8,144,128]{2,1,0:T(8,128)(2,1)} %paged_attention.1), calls=%async_computation | async-start | bytes 589824 | tf_op jit(solution)/shard_map/all_to_all | solution.py:394
  62.7 4.9 %collective-permute-start.8 = (bf16[8,2048]{1,0:T(8,128)(2,1)S(1)}, bf16[8,2048]{1,0:T(8,128)(2,1)S(1)}, u32[]{:S(2)}, u32[]{:S(2)}) collective-permute-start(bf16[8,2048]{1,0:T(8,128)(2,1)S(1)} %reshape.62), channel_id=1, source_target_pairs={{0,16},{4,20},{8,24},{12,28},{16,0},{20,4},{24,8},{28,12},{1,17},{... | collective-permute-start | bytes 98312 | tf_op jit(solution)/shard_map/ppermute | solution.py:22
  67.6 4.3 %collective-permute-start.9 = (bf16[16,2048]{1,0:T(8,128)(2,1)S(1)}, bf16[16,2048]{1,0:T(8,128)(2,1)S(1)}, u32[]{:S(2)}, u32[]{:S(2)}) collective-permute-start(bf16[16,2048]{1,0:T(8,128)(2,1)S(1)} %get-tuple-element.20), channel_id=1, source_target_pairs={{0,4},{4,0},{8,12},{12,8},{16,20},{20,16},{24,28},{28,24},{1,5},{5... | collective-permute-start | bytes 196616 | tf_op jit(solution)/shard_map/ppermute | solution.py:22
  68.9 4.3 %collective-permute-start.10 = (bf16[16,2048]{1,0:T(8,128)(2,1)S(1)}, bf16[16,2048]{1,0:T(8,128)(2,1)S(1)}, u32[]{:S(2)}, u32[]{:S(2)}) collective-permute-start(bf16[16,2048]{1,0:T(8,128)(2,1)S(1)} %get-tuple-element.20), channel_id=1, source_target_pairs={{0,8},{4,12},{8,0},{12,4},{16,24},{20,28},{24,16},{28,20},{1,9},{5... | collective-permute-start | bytes 196616 | tf_op jit(solution)/shard_map/ppermute | solution.py:22
  69.1 5.2 %collective-permute-start.11 = (bf16[16,2048]{1,0:T(8,128)(2,1)S(1)}, bf16[16,2048]{1,0:T(8,128)(2,1)S(1)}, u32[]{:S(2)}, u32[]{:S(2)}) collective-permute-start(bf16[16,2048]{1,0:T(8,128)(2,1)S(1)} %get-tuple-element.20), channel_id=1, source_target_pairs={{0,12},{4,8},{8,4},{12,0},{16,28},{20,24},{24,20},{28,16},{1,13},{... | collective-permute-start | bytes 196616 | tf_op jit(solution)/shard_map/ppermute | solution.py:22
  77.3 1.6 %collective-permute-start.12 = (f32[64,1024]{1,0:T(8,128)S(1)}, f32[64,1024]{1,0:T(8,128)S(1)}, u32[]{:S(2)}, u32[]{:S(2)}) collective-permute-start(f32[64,1024]{1,0:T(8,128)S(1)} %fusion.6), channel_id=1, source_target_pairs={{0,1},{1,0},{2,3},{3,2},{4,5},{5,4},{6,7},{7,6},{8,9},{9,8},{10,11... | collective-permute-start | bytes 786440 | tf_op jit(solution)/shard_map/ppermute | solution.py:22
  79.0 5.6 %collective-permute-start.13 = (bf16[64,1024]{1,0:T(8,128)(2,1)S(1)}, bf16[64,1024]{1,0:T(8,128)(2,1)S(1)}, u32[]{:S(2)}, u32[]{:S(2)}) collective-permute-start(bf16[64,1024]{1,0:T(8,128)(2,1)S(1)} %fusion.2), channel_id=1, source_target_pairs={{0,2},{1,3},{2,0},{3,1},{4,6},{5,7},{6,4},{7,5},{8,10},{9,11},{10,... | collective-permute-start | bytes 393224 | tf_op jit(solution)/shard_map/ppermute | solution.py:22

commit v5 on v4

--- a/solution.py
+++ b/solution.py
@@ -31,53 +31,88 @@
     return groups
 
 
+def lower_groups(n):
+    return bit_groups(n)[:-1]
+
+
+def last_group(n):
+    return bit_groups(n)[-1]
+
+
+def pick_digit(x, axis, shift, size, offset):
+    digit = (lax.axis_index(axis) >> shift) % size
+    x = x.reshape(x.shape[0] // size, size, *x.shape[1:])
+    return lax.dynamic_index_in_dim(x, digit ^ offset, axis=1, keepdims=False)
+
+
 def scatter_sum(x, axis, n, beside):
-    me = lax.axis_index(axis)
-    for shift, size in bit_groups(n):
-        digit = (me >> shift) % size
-        x = x.reshape(x.shape[0] // size, size, *x.shape[1:])
-
-        def block(offset):
-            return lax.dynamic_index_in_dim(x, digit ^ offset, axis=1, keepdims=False)
-
-        parts = [swap(block(d), axis, n, d << shift) for d in range(1, size)]
+    for shift, size in lower_groups(n):
+        parts = [
+            swap(pick_digit(x, axis, shift, size, d), axis, n, d << shift) for d in range(1, size)
+        ]
         if shift == 0:
             parts, beside = lax.optimization_barrier((parts, beside))
-        x = sum(parts, block(0))
-    return x[0], beside
+        x = sum(parts, pick_digit(x, axis, shift, size, 0))
+    shift, size = last_group(n)
+    return sum([swap(x, axis, n, d << shift) for d in range(1, size)], x), beside
 
 
 def gather_relative(x, axis, n):
-    for shift, size in reversed(bit_groups(n)):
+    for shift, size in reversed(lower_groups(n)):
         parts = [x] + [swap(x, axis, n, d << shift) for d in range(1, size)]
         x = jnp.concatenate(parts, axis=0)
     return x
 
 
+def relative_place(block, axis, n):
+    last_shift, last_size = last_group(n)
+    offset = lax.axis_index(axis) ^ block
+    place, weight = block >> last_shift, n
+    for shift, size in lower_groups(n):
+        weight //= size
+        place = place + ((offset >> shift) & (size - 1)) * weight
+    return place
+
+
 def gather_in_order(x, axis, n):
-    rows = x.shape[0]
-    me = lax.axis_index(axis)
+    last_shift, last_size = last_group(n)
+    rows = x.shape[0] // last_size
+    me = lax.axis_index(axis) & ((1 << last_shift) - 1)
     held = [(0, x)]
     out = jnp.zeros((n * rows, x.shape[1]), x.dtype)
-    for shift, size in reversed(bit_groups(n)):
-        stacked = jnp.concatenate([block for _, block in held], axis=0)
+    for shift, size in reversed(lower_groups(n)):
+        stacked = jnp.concatenate([part for _, part in held], axis=0)
+        height = x.shape[0]
         held = [
-            (d << shift | offset, part[i * rows : (i + 1) * rows])
+            (d << shift | offset, part[i * height : (i + 1) * height])
             for d in range(size)
             for part in [swap(stacked, axis, n, d << shift) if d else stacked]
             for i, (offset, _) in enumerate(held)
         ]
-    for offset, block in held:
-        out = lax.dynamic_update_slice_in_dim(out, block, (me ^ offset) * rows, axis=0)
+    for offset, part in held:
+        for c in range(last_size):
+            out = lax.dynamic_update_slice_in_dim(
+                out,
+                part[c * rows : (c + 1) * rows],
+                ((c << last_shift) + (me ^ offset)) * rows,
+                axis=0,
+            )
     return out
 
 
-def relative_place(offset, n):
-    place, weight = 0, n
-    for shift, size in bit_groups(n):
-        weight //= size
-        place = place + ((offset >> shift) & (size - 1)) * weight
-    return place
+def split_stat(stat, lane):
+    hi = stat.astype(jnp.bfloat16).astype(jnp.float32)
+    rest = stat - hi
+    mid = rest.astype(jnp.bfloat16).astype(jnp.float32)
+    piece = jnp.where(lane < STAT, hi, jnp.where(lane < 2 * STAT, mid, rest - mid))
+    return piece.astype(jnp.bfloat16)
+
+
+def join_stat(pieces):
+    pieces = pieces.astype(jnp.float32)
+    return (pieces + pltpu.roll(pieces, LANES - STAT, 1)) + pltpu.roll(
+        pieces, LANES - 2 * STAT, 1
+    )
 
 
 def attention_kernel(
@@ -107,7 +142,6 @@
     chunks = slots // CHUNK
     blocks, block_rows, _ = out.shape
     mine = block_rows // heads - 1
-    chunk_rows = CHUNK * heads
 
     def key_copy(c):
         part = pl.ds(c * CHUNK, CHUNK)
@@ -158,16 +192,14 @@
         score = jnp.where(token < table(1, c), score * table(0, c), masked_low)
         top = jnp.max(score, axis=0, keepdims=True)
         page_max[pl.ds(c, 1), :] = top
-        probs[c] = jnp.exp(score - top).T.astype(jnp.bfloat16)
-
-    ones = jnp.ones((PAGE, LANES), jnp.bfloat16)
+        prob = jnp.exp(score - top).astype(jnp.bfloat16).astype(jnp.float32)
+        page_sum[pl.ds(c, 1), :] = jnp.sum(prob, axis=0, keepdims=True)
+        probs[c] = prob.T.astype(jnp.bfloat16)
+
     empty = jnp.zeros((heads, PAGE), jnp.bfloat16)
 
     def value_chunk(c):
         prob = probs[c]
-        page_sum[pl.ds(pl.multiple_of(c * chunk_rows, chunk_rows), chunk_rows), :] = jnp.dot(
-            prob, ones, preferred_element_type=jnp.float32
-        )
         for s in range(0, CHUNK, 2):
             pair = jnp.concatenate(
                 [
@@ -190,18 +222,24 @@
                 )
             )
 
-    key_copy(0).wait()
-    score_chunk(0)
-
-    @pl.loop(1, chunks)
-    def _(c):
+    for c in range(2):
         key_copy(c).wait()
-        value_copy(c - 1).wait()
-        value_chunk(c - 1)
+    for c in range(2):
         score_chunk(c)
 
-    value_copy(chunks - 1).wait()
-    value_chunk(chunks - 1)
+    @pl.loop(1, chunks // 2)
+    def _(step):
+        for c in range(2):
+            key_copy(2 * step + c).wait()
+            value_copy(2 * step + c - 2).wait()
+        for c in range(2):
+            value_chunk(2 * step + c - 2)
+            score_chunk(2 * step + c)
+
+    for c in range(chunks - 2, chunks):
+        value_copy(c).wait()
+    for c in range(chunks - 2, chunks):
+        value_chunk(c)
 
     biggest, who = page_max[...], tables[3 * chunks :, :]
     best = biggest
@@ -216,25 +254,25 @@
 
     keep_max = lax.broadcasted_iota(jnp.int32, (heads, LANES), 1) % STAT < STAT // 2
 
-    @pl.loop(0, chunks)
-    def _(c):
-        top = dev_max[pl.ds(c, 1), :]
-        weight = jnp.exp(page_max[pl.ds(c, 1), :] - top)
-
-        def on_rows(x):
-            return jnp.broadcast_to(x, (PAGE, LANES)).T
-
-        out_weight, weight, top = on_rows(weight * table(2, c)), on_rows(weight), on_rows(top)
-        for s in range(CHUNK):
-            here = pl.ds(
-                pl.multiple_of((place_of[c * CHUNK + s] & 0xFFFF) * heads, heads), heads
-            )
-            there = pl.ds(pl.multiple_of((c * CHUNK + s) * heads, heads), heads)
-            part = slice(s * heads, (s + 1) * heads)
-            total_out[here, :] += page_out[there, :] * out_weight[part]
-            total_stat[here, :] = jnp.where(
-                keep_max, top[part], total_stat[here, :] + page_sum[there, :] * weight[part]
-            )
+    keep_max_row = lax.broadcasted_iota(jnp.int32, (PAGE, LANES), 0) % STAT < STAT // 2
+
+    @pl.loop(0, chunks // 2)
+    def _(step):
+        for c in (2 * step, 2 * step + 1):
+            top = dev_max[pl.ds(c, 1), :]
+            weight = jnp.exp(page_max[pl.ds(c, 1), :] - top)
+            out_weight = jnp.broadcast_to(weight * table(2, c), (PAGE, LANES)).T
+            stat = jnp.where(keep_max_row, top, weight * page_sum[pl.ds(c, 1), :]).T
+            for s in range(CHUNK):
+                here = pl.ds(
+                    pl.multiple_of((place_of[c * CHUNK + s] & 0xFFFF) * heads, heads), heads
+                )
+                there = pl.ds(pl.multiple_of((c * CHUNK + s) * heads, heads), heads)
+                part = slice(s * heads, (s + 1) * heads)
+                total_out[here, :] += page_out[there, :] * out_weight[part]
+                total_stat[here, :] = jnp.where(
+                    keep_max, stat[part], total_stat[here, :] + stat[part]
+                )
 
     lane = lax.broadcasted_iota(jnp.int32, (heads, LANES), 1)
     for b in range(blocks):
@@ -244,15 +282,40 @@
         for r in range(mine):
             both = total_stat[first + r * heads : first + (r + 1) * heads, :]
             stat = jnp.where(lane % (STAT // 2) == r, both, stat)
-        hi = stat.astype(jnp.bfloat16).astype(jnp.float32)
-        rest = stat - hi
-        mid = rest.astype(jnp.bfloat16).astype(jnp.float32)
-        piece = jnp.where(lane < STAT, hi, jnp.where(lane < 2 * STAT, mid, rest - mid))
-        out[b, mine * heads :, :] = piece.astype(jnp.bfloat16)
-
-
-def finish_kernel(got, query, keyval, out):
-    sources, block_rows, _ = got.shape
+        out[b, mine * heads :, :] = split_stat(stat, lane)
+
+
+def combine_kernel(*refs):
+    *parts, out = refs
+    blocks, block_rows, _ = out.shape
+    heads = LANES // CHUNK
+    mine = block_rows // heads - 1
+    lane = lax.broadcasted_iota(jnp.int32, (heads, LANES), 1)
+    for b in range(blocks):
+        stats = [join_stat(part[b, mine * heads :, :]) for part in parts]
+        maxima = [jnp.where(lane < mine, stat, 0.0) for stat in stats]
+        top = functools.reduce(jnp.maximum, maxima)
+        factors = [jnp.exp(m - top) for m in maxima]
+        sums = sum(
+            pltpu.roll(f, STAT // 2, 1) * jnp.where(lane < STAT, stat, 0.0)
+            for f, stat in zip(factors, stats)
+        )
+        both = jnp.where(lane < STAT // 2, top, sums)
+        both = jnp.where(lane < STAT, both, 0.0)
+        both = (both + pltpu.roll(both, STAT, 1)) + pltpu.roll(both, 2 * STAT, 1)
+        out[b, mine * heads :, :] = split_stat(both, lane)
+        for r in range(mine):
+            rows = slice(r * heads, (r + 1) * heads)
+            numer = sum(
+                f[:, r : r + 1] * part[b, rows, :].astype(jnp.float32)
+                for f, part in zip(factors, parts)
+            )
+            out[b, rows, :] = numer.astype(jnp.bfloat16)
+
+
+def finish_kernel(*refs):
+    *parts, query, keyval, out = refs
+    blocks, block_rows, _ = parts[0].shape
     heads = LANES // CHUNK
     group = heads // 2
     mine = block_rows // heads - 1
@@ -265,29 +328,31 @@
         high = jnp.broadcast_to(new[4 * r + 2 + which : 4 * r + 3 + which], (heads, LANES))
         return jnp.where(low_head, low, high)
 
-    own = jnp.zeros((heads, LANES), jnp.float32)
-    for r in range(mine):
-        rows = query[r * heads : (r + 1) * heads, :].astype(jnp.float32)
-        dot = jnp.sum(rows * spread(r, 0), axis=1, keepdims=True) * (1.0 / math.sqrt(HD))
-        own = jnp.where(lane == r, dot, own)
-    maxima, sums = [], []
-    for j in range(sources):
-        stat = got[j, mine * heads :, :].astype(jnp.float32)
-        whole = (stat + pltpu.roll(stat, LANES - STAT, 1)) + pltpu.roll(stat, LANES - 2 * STAT, 1)
-        maxima.append(jnp.where(lane < mine, whole, 0.0))
-        sums.append(jnp.where(lane < mine, pltpu.roll(whole, LANES - STAT // 2, 1), 0.0))
-    top = functools.reduce(jnp.maximum, maxima, own)
-    fresh = jnp.exp(own - top)
-    factors = [jnp.exp(m - top) for m in maxima]
-    denom = sum((s * f for s, f in zip(sums, factors)), fresh)
-    fresh = fresh / denom
-    factors = [f / denom for f in factors]
-    for r in range(mine):
-        numer = fresh[:, r : r + 1] * spread(r, 1)
-        for j in range(sources):
-            part = got[j, r * heads : (r + 1) * heads, :].astype(jnp.float32)
-            numer = numer + factors[j][:, r : r + 1] * part
-        out[r * heads : (r + 1) * heads, :] = numer.astype(jnp.bfloat16)
+    for b in range(blocks):
+        own = jnp.zeros((heads, LANES), jnp.float32)
+        for r in range(mine):
+            request = b * mine + r
+            rows = query[request * heads : (request + 1) * heads, :].astype(jnp.float32)
+            dot = jnp.sum(rows * spread(request, 0), axis=1, keepdims=True)
+            own = jnp.where(lane == r, dot * (1.0 / math.sqrt(HD)), own)
+        maxima, sums = [], []
+        for part in parts:
+            whole = join_stat(part[b, mine * heads :, :])
+            maxima.append(jnp.where(lane < mine, whole, 0.0))
+            sums.append(jnp.where(lane < mine, pltpu.roll(whole, LANES - STAT // 2, 1), 0.0))
+        top = functools.reduce(jnp.maximum, maxima, own)
+        fresh = jnp.exp(own - top)
+        factors = [jnp.exp(m - top) for m in maxima]
+        denom = sum((s * f for s, f in zip(sums, factors)), fresh)
+        fresh = fresh / denom
+        factors = [f / denom for f in factors]
+        for r in range(mine):
+            numer = fresh[:, r : r + 1] * spread(b * mine + r, 1)
+            for part, f in zip(parts, factors):
+                rows = part[b, r * heads : (r + 1) * heads, :].astype(jnp.float32)
+                numer = numer + f[:, r : r + 1] * rows
+            request = b * mine + r
+            out[request * heads : (request + 1) * heads, :] = numer.astype(jnp.bfloat16)
 
 
 def body(
@@ -324,9 +389,7 @@
     lengths = PAGE * page_counts - trim
     page_valid = jnp.sum(select_int * lengths[None, :], axis=1) - index * PAGE
     block = owner // mine
-    row_of = (
-        relative_place(lax.axis_index("seq") ^ block, seq_size) * mine + owner - block * mine
-    )
+    row_of = relative_place(block, "seq", seq_size) * mine + owner - block * mine
 
     def on_lanes(x):
         return jnp.broadcast_to(x, (slots, heads_local)).reshape(slots // CHUNK, LANES)
@@ -352,8 +415,10 @@
         part_all.reshape(seq_size, mine, part_all.shape[1]), "seq", seq_size, (tables, place_of)
     )
     sums = sums.astype(jnp.bfloat16)
-    my_query = sums[:, :wide].reshape(mine * heads_local, HD)
-    my_keyval = sums[:, wide:].reshape(mine * 2 * kv_local, HD)
+    held = last_group(seq_size)[1] * mine
+    sums = sums.reshape(held, -1)
+    my_query = sums[:, :wide].reshape(held * heads_local, HD)
+    my_keyval = sums[:, wide:].reshape(held * 2 * kv_local, HD)
     query = gather_relative(my_query, "seq", seq_size)
 
     smem = pl.BlockSpec(memory_space=pltpu.SMEM)
@@ -374,7 +439,7 @@
             pltpu.VMEM(value_cache.shape, jnp.bfloat16),
             pltpu.VMEM((chunks, LANES, PAGE), jnp.bfloat16),
             pltpu.VMEM((slots * heads_local, HD), jnp.float32),
-            pltpu.VMEM((slots * heads_local, HD), jnp.float32),
+            pltpu.VMEM((chunks, LANES), jnp.float32),
             pltpu.VMEM((chunks, LANES), jnp.float32),
             pltpu.VMEM((chunks, LANES), jnp.float32),
             pltpu.VMEM((every_row, HD), jnp.float32),
@@ -391,15 +456,29 @@
         name="paged_attention",
     )(place_of, query, tables, key_cache, value_cache)
 
-    got = lax.all_to_all(totals, "seq", 0, 0)
+    for shift, size in lower_groups(seq_size):
+        parts = [pick_digit(totals, "seq", shift, size, 0)] + [
+            swap(pick_digit(totals, "seq", shift, size, d), "seq", seq_size, d << shift)
+            for d in range(1, size)
+        ]
+        totals = pl.pallas_call(
+            combine_kernel,
+            out_shape=jax.ShapeDtypeStruct(parts[0].shape, jnp.bfloat16),
+            in_specs=[vmem] * size,
+            out_specs=vmem,
+            compiler_params=pltpu.CompilerParams(vmem_limit_bytes=6 * 2**20),
+            name="combine",
+        )(*parts)
+    shift, size = last_group(seq_size)
+    parts = [totals] + [swap(totals, "seq", seq_size, d << shift) for d in range(1, size)]
     my_context = pl.pallas_call(
         finish_kernel,
-        out_shape=jax.ShapeDtypeStruct((mine * heads_local, HD), jnp.bfloat16),
-        in_specs=[vmem, vmem, vmem],
+        out_shape=jax.ShapeDtypeStruct((held * heads_local, HD), jnp.bfloat16),
+        in_specs=[vmem] * (size + 2),
         out_specs=vmem,
         compiler_params=pltpu.CompilerParams(vmem_limit_bytes=6 * 2**20),
         name="finish",
-    )(got, my_query, my_keyval).reshape(mine, wide)
+    )(*parts, my_query, my_keyval).reshape(held, wide)
     context = gather_in_order(my_context, "seq", seq_size)
 
     total = jnp.dot(context, w_out, preferred_element_type=jnp.float32)

time: 85.6 us -> 77.7 us (0.908)
  waiting for transfers between devices: 35 us -> 30.2 us
  Pallas kernels: 14 us -> 11.6 us
  starting transfers between devices: 24.5 us -> 22.8 us
    all_to_all x1 -> x0, waiting for transfers between devices: 8.53 us -> none  [body(): got = lax.all_to_all(totals, 'seq', 0, 0)]
    all_to_all x1 -> x0, starting transfers between devices: 4.44 us -> none  [body(): got = lax.all_to_all(totals, 'seq', 0, 0)]
    ppermute x14 -> x16, waiting for transfers between devices: 26.5 us -> 30.2 us  [swap(): return lax.ppermute(x, axis, [(j, j ^ mask) for j in range(n)])]
    pallas_call x1, Pallas kernels: 13.5 us -> 10.7 us  [body(): pl.pallas_call(attention_kernel, out_shape=jax.ShapeDtypeStruct((seq_size...]
    ppermute x14 -> x16, starting transfers between devices: 20.1 us -> 22.8 us  [swap(): return lax.ppermute(x, axis, [(j, j ^ mask) for j in range(n)])]
    squeeze x2, local copies, waits for them, and re-layouts: 0.06 us -> 1.08 us  [pick_digit(): return lax.dynamic_index_in_dim(x, digit ^ offset, axis=1, keepdims=False)]
  transfers between devices with their start and end apart: 15 -> 16, of which waited for: 14 -> 15; matrix products, arithmetic and copies ran while one was open for 4% -> 4% of each run, Pallas kernels for 0% -> 0%
where the time goes in v5:
time: 77.7 us; the launch traced here: 77.5 us
  waiting for transfers between devices  30.2 us (39%)
  starting transfers between devices  22.8 us (29%)
  Pallas kernels  11.6 us (15%)
  matrix products  6.49 us (8%)
  other arithmetic  3.09 us (4%)
  local copies, waits for them, and re-layouts  2.96 us (4%)
    ppermute x16, waiting for transfers between devices, swap(): return lax.ppermute(x, axis, [(j, j ^ mask) for j in range(n)])  30.2 us
    ppermute x16, starting transfers between devices, swap(): return lax.ppermute(x, axis, [(j, j ^ mask) for j in range(n)])  22.8 us
    pallas_call x1, Pallas kernels, body(): pl.pallas_call(attention_kernel, out_shape=jax.ShapeDtypeStruct((seq_size...  10.7 us
    dot_general x1, matrix products, body(): part_query = jnp.dot(hidden_in, w_query, preferred_element_type=jnp.float32)  3.18 us
    dot_general x1, matrix products, body(): total = jnp.dot(context, w_out, preferred_element_type=jnp.float32)  3.03 us
  transfers between devices with their start and end apart: 16, of which 15 were waited for; matrix products, arithmetic and copies ran while one was open for 4% of the time, Pallas kernels for 0%

profile of v5, /device:TPU:0, one launch (start us, length us, event | category | flops | bytes accessed | tf_op | source)
XLA Modules:
  0.0 77.5 jit_solution(6421291282225935443)
XLA Ops:
  0.0 3.2 %fusion.5 = f32[64,2048]{1,0:T(8,128)S(1)} fusion(bf16[64,1024]{1,0:T(8,128)(2,1)} %param.11, bf16[1024,2048]{1,0:T(8,128)(2,1)} %param.12), kind=kOutput, calls=%fused_computation.39 | convolution fusion | flops 268435456 | bytes 4849664 | tf_op jit(solution)/shard_map/dot_general | solution.py:411
  3.7 3.0 %collective-permute-start = (f32[2,8,2560]{2,1,0:T(8,128)S(1)}, f32[2,8,2560]{2,1,0:T(8,128)S(1)}, u32[]{:S(2)}, u32[]{:S(2)}) collective-permute-start(f32[2,8,2560]{2,1,0:T(8,128)S(1)} %get-tuple-element.19), channel_id=1, source_target_pairs={{0,4},{4,0},{8,12},{12,8},{16,20},{20,16},{24,28},{28,24},{1,5},{5... | collective-permute-start | bytes 491528 | tf_op jit(solution)/shard_map/ppermute | solution.py:22
  6.7 1.6 %collective-permute-start.1 = (f32[2,8,2560]{2,1,0:T(8,128)S(1)}, f32[2,8,2560]{2,1,0:T(8,128)S(1)}, u32[]{:S(2)}, u32[]{:S(2)}) collective-permute-start(f32[2,8,2560]{2,1,0:T(8,128)S(1)} %get-tuple-element.18), channel_id=1, source_target_pairs={{0,8},{4,12},{8,0},{12,4},{16,24},{20,28},{24,16},{28,20},{1,9},{5... | collective-permute-start | bytes 491528 | tf_op jit(solution)/shard_map/ppermute | solution.py:22
  11.5 2.3 %collective-permute-done.1 = f32[2,8,2560]{2,1,0:T(8,128)S(1)} collective-permute-done((f32[2,8,2560]{2,1,0:T(8,128)S(1)}, f32[2,8,2560]{2,1,0:T(8,128)S(1)}, u32[]{:S(2)}, u32[]{:S(2)}) %collective-permute-start.1) | collective-permute-done | bytes 163872 | tf_op jit(solution)/shard_map/ppermute | solution.py:22
  13.8 1.8 %collective-permute-done.2 = f32[2,8,2560]{2,1,0:T(8,128)S(1)} collective-permute-done((f32[2,8,2560]{2,1,0:T(8,128)S(1)}, f32[2,8,2560]{2,1,0:T(8,128)S(1)}, u32[]{:S(2)}, u32[]{:S(2)}) %collective-permute-start.2) | collective-permute-done | bytes 163872 | tf_op jit(solution)/shard_map/ppermute | solution.py:22
  15.7 2.8 %collective-permute-start.3 = (f32[2,8,2560]{2,1,0:T(8,128)S(1)}, f32[2,8,2560]{2,1,0:T(8,128)S(1)}, u32[]{:S(2)}, u32[]{:S(2)}) collective-permute-start(f32[2,8,2560]{2,1,0:T(8,128)S(1)} %fusion.1), channel_id=1, source_target_pairs={{0,16},{4,20},{8,24},{12,28},{16,0},{20,4},{24,8},{28,12},{1,17},{... | collective-permute-start | bytes 491528 | tf_op jit(solution)/shard_map/ppermute | solution.py:22
  18.5 6.8 %collective-permute-done.3 = f32[2,8,2560]{2,1,0:T(8,128)S(1)} collective-permute-done((f32[2,8,2560]{2,1,0:T(8,128)S(1)}, f32[2,8,2560]{2,1,0:T(8,128)S(1)}, u32[]{:S(2)}, u32[]{:S(2)}) %collective-permute-start.3) | collective-permute-done | bytes 163872 | tf_op jit(solution)/shard_map/ppermute | solution.py:22
  25.4 1.3 %collective-permute-start.4 = (bf16[256,128]{1,0:T(8,128)(2,1)S(1)}, bf16[256,128]{1,0:T(8,128)(2,1)S(1)}, u32[]{:S(2)}, u32[]{:S(2)}) collective-permute-start(bf16[256,128]{1,0:T(8,128)(2,1)S(1)} %reshape.66.refs_2_), channel_id=1, source_target_pairs={{0,4},{4,0},{8,12},{12,8},{16,20},{20,16},{24,28},{28,24},{1,5},{5... | collective-permute-start | bytes 196616 | tf_op jit(solution)/shard_map/ppermute | solution.py:22
  27.4 1.5 %collective-permute-start.6 = (bf16[256,128]{1,0:T(8,128)(2,1)S(1)}, bf16[256,128]{1,0:T(8,128)(2,1)S(1)}, u32[]{:S(2)}, u32[]{:S(2)}) collective-permute-start(bf16[256,128]{1,0:T(8,128)(2,1)S(1)} %reshape.66.refs_2_), channel_id=1, source_target_pairs={{0,12},{4,8},{8,4},{12,0},{16,28},{20,24},{24,20},{28,16},{1,13},{... | collective-permute-start | bytes 196616 | tf_op jit(solution)/shard_map/ppermute | solution.py:22
  29.7 1.3 %collective-permute-done.5 = bf16[256,128]{1,0:T(8,128)(2,1)S(1)} collective-permute-done((bf16[256,128]{1,0:T(8,128)(2,1)S(1)}, bf16[256,128]{1,0:T(8,128)(2,1)S(1)}, u32[]{:S(2)}, u32[]{:S(2)}) %collective-permute-start.5) | collective-permute-done | bytes 65568 | tf_op jit(solution)/shard_map/ppermute | solution.py:22
  31.0 1.6 %collective-permute-done.6 = bf16[256,128]{1,0:T(8,128)(2,1)S(1)} collective-permute-done((bf16[256,128]{1,0:T(8,128)(2,1)S(1)}, bf16[256,128]{1,0:T(8,128)(2,1)S(1)}, u32[]{:S(2)}, u32[]{:S(2)}) %collective-permute-start.6) | collective-permute-done | bytes 65568 | tf_op jit(solution)/shard_map/ppermute | solution.py:22
  33.3 10.7 %paged_attention.1 = bf16[8,144,128]{2,1,0:T(8,128)(2,1)} custom-call(s32[128]{0:T(128)} %get-tuple-element.10.place_of, bf16[1024,128]{1,0:T(8,128)(2,1)} %pad_maximum_fusion.1.query, f32[64,128]{1,0:T(8,128)} %pad_maximum_fusion.2.tables, bf16[128,128,256]{2,1,0:T(8,128)(2,1)} %key_cache.1, bf16[128,128,256]{2,1,0:T(8,128)(2,1)} %value_cache.1), custom_call_target="tpu_custom_call" | custom-call | flops 134217728 | bytes 16777216 | tf_op jit(solution)/shard_map/paged_attention/pallas_call | solution.py:430
  45.7 1.5 %collective-permute-start.8 = (bf16[2,144,128]{2,1,0:T(8,128)(2,1)S(1)}, bf16[2,144,128]{2,1,0:T(8,128)(2,1)S(1)}, u32[]{:S(2)}, u32[]{:S(2)}) collective-permute-start(bf16[2,144,128]{2,1,0:T(8,128)(2,1)S(1)} %get-tuple-element.21), channel_id=1, source_target_pairs={{0,8},{4,12},{8,0},{12,4},{16,24},{20,28},{24,16},{28,20},{1,9},{5... | collective-permute-start | bytes 221192 | tf_op jit(solution)/shard_map/ppermute | solution.py:22
  47.2 1.4 %collective-permute-start.9 = (bf16[2,144,128]{2,1,0:T(8,128)(2,1)S(1)}, bf16[2,144,128]{2,1,0:T(8,128)(2,1)S(1)}, u32[]{:S(2)}, u32[]{:S(2)}) collective-permute-start(bf16[2,144,128]{2,1,0:T(8,128)(2,1)S(1)} %get-tuple-element.20), channel_id=1, source_target_pairs={{0,12},{4,8},{8,4},{12,0},{16,28},{20,24},{24,20},{28,16},{1,13},{... | collective-permute-start | bytes 221192 | tf_op jit(solution)/shard_map/ppermute | solution.py:22
  50.0 2.4 %collective-permute-done.9.refs_3_ = bf16[2,144,128]{2,1,0:T(8,128)(2,1)S(1)} collective-permute-done((bf16[2,144,128]{2,1,0:T(8,128)(2,1)S(1)}, bf16[2,144,128]{2,1,0:T(8,128)(2,1)S(1)}, u32[]{:S(2)}, u32[]{:S(2)}) %collective-permute-start.9) | collective-permute-done | bytes 73760 | tf_op jit(solution)/shard_map/ppermute | solution.py:22
  52.9 3.1 %collective-permute-start.10 = (bf16[2,144,128]{2,1,0:T(8,128)(2,1)S(1)}, bf16[2,144,128]{2,1,0:T(8,128)(2,1)S(1)}, u32[]{:S(2)}, u32[]{:S(2)}) collective-permute-start(bf16[2,144,128]{2,1,0:T(8,128)(2,1)S(1)} %combine.1.refs_0_), channel_id=1, source_target_pairs={{0,16},{4,20},{8,24},{12,28},{16,0},{20,4},{24,8},{28,12},{1,17},{... | collective-permute-start | bytes 221192 | tf_op jit(solution)/shard_map/ppermute | solution.py:22
  56.1 3.1 %collective-permute-done.10.refs_1_ = bf16[2,144,128]{2,1,0:T(8,128)(2,1)S(1)} collective-permute-done((bf16[2,144,128]{2,1,0:T(8,128)(2,1)S(1)}, bf16[2,144,128]{2,1,0:T(8,128)(2,1)S(1)}, u32[]{:S(2)}, u32[]{:S(2)}) %collective-permute-start.10) | collective-permute-done | bytes 73760 | tf_op jit(solution)/shard_map/ppermute | solution.py:22
  59.7 1.2 %collective-permute-start.11 = (bf16[16,2048]{1,0:T(8,128)(2,1)S(1)}, bf16[16,2048]{1,0:T(8,128)(2,1)S(1)}, u32[]{:S(2)}, u32[]{:S(2)}) collective-permute-start(bf16[16,2048]{1,0:T(8,128)(2,1)S(1)} %reshape.69), channel_id=1, source_target_pairs={{0,4},{4,0},{8,12},{12,8},{16,20},{20,16},{24,28},{28,24},{1,5},{5... | collective-permute-start | bytes 196616 | tf_op jit(solution)/shard_map/ppermute | solution.py:22
  61.3 1.9 %collective-permute-start.13 = (bf16[16,2048]{1,0:T(8,128)(2,1)S(1)}, bf16[16,2048]{1,0:T(8,128)(2,1)S(1)}, u32[]{:S(2)}, u32[]{:S(2)}) collective-permute-start(bf16[16,2048]{1,0:T(8,128)(2,1)S(1)} %reshape.69), channel_id=1, source_target_pairs={{0,12},{4,8},{8,4},{12,0},{16,28},{20,24},{24,20},{28,16},{1,13},{... | collective-permute-start | bytes 196616 | tf_op jit(solution)/shard_map/ppermute | solution.py:22
  65.1 1.3 %collective-permute-done.13 = bf16[16,2048]{1,0:T(8,128)(2,1)S(1)} collective-permute-done((bf16[16,2048]{1,0:T(8,128)(2,1)S(1)}, bf16[16,2048]{1,0:T(8,128)(2,1)S(1)}, u32[]{:S(2)}, u32[]{:S(2)}) %collective-permute-start.13) | collective-permute-done | bytes 65568 | tf_op jit(solution)/shard_map/ppermute | solution.py:22
  66.5 3.0 %fusion.7 = f32[64,1024]{1,0:T(8,128)S(1)} fusion(bf16[64,2048]{1,0:T(8,128)(2,1)S(1)} %slice_dynamic-update-slice_fusion, bf16[2048,1024]{1,0:T(8,128)(2,1)} %param.14), kind=kOutput, calls=%fused_computation.41 | convolution fusion | flops 268435456 | bytes 4718592 | tf_op jit(solution)/shard_map/dot_general | solution.py:484
  69.6 1.5 %collective-permute-done.14 = f32[64,1024]{1,0:T(8,128)S(1)} collective-permute-done((f32[64,1024]{1,0:T(8,128)S(1)}, f32[64,1024]{1,0:T(8,128)S(1)}, u32[]{:S(2)}, u32[]{:S(2)}) %collective-permute-start.14) | collective-permute-done | bytes 262176 | tf_op jit(solution)/shard_map/ppermute | solution.py:22
  71.1 1.6 %collective-permute-start.15 = (bf16[64,1024]{1,0:T(8,128)(2,1)S(1)}, bf16[64,1024]{1,0:T(8,128)(2,1)S(1)}, u32[]{:S(2)}, u32[]{:S(2)}) collective-permute-start(bf16[64,1024]{1,0:T(8,128)(2,1)S(1)} %fusion.2), channel_id=1, source_target_pairs={{0,2},{1,3},{2,0},{3,1},{4,6},{5,7},{6,4},{7,5},{8,10},{9,11},{10,... | collective-permute-start | bytes 393224 | tf_op jit(solution)/shard_map/ppermute | solution.py:22
  72.7 4.0 %collective-permute-done.15 = bf16[64,1024]{1,0:T(8,128)(2,1)S(1)} collective-permute-done((bf16[64,1024]{1,0:T(8,128)(2,1)S(1)}, bf16[64,1024]{1,0:T(8,128)(2,1)S(1)}, u32[]{:S(2)}, u32[]{:S(2)}) %collective-permute-start.15) | collective-permute-done | bytes 131104 | tf_op jit(solution)/shard_map/ppermute | solution.py:22
  (75 shorter events, 13.1 us)
Async XLA Ops:
  0.0 3.2 %copy-start = (bf16[1024,512]{1,0:T(8,128)(2,1)S(1)}, bf16[1024,512]{1,0:T(8,128)(2,1)}, u32[]{:S(2)}) copy-start(bf16[1024,512]{1,0:T(8,128)(2,1)} %param.13) | copy-start | bytes 3145732
  0.0 3.2 %copy-start.1 = (bf16[64,1024]{1,0:T(8,128)(2,1)S(1)}, bf16[64,1024]{1,0:T(8,128)(2,1)}, u32[]{:S(2)}) copy-start(bf16[64,1024]{1,0:T(8,128)(2,1)} %param.11) | copy-start | bytes 393220
  0.0 8.3 %copy-start.2 = (s32[64]{0:T(128)S(1)}, s32[64]{0:T(128)}, u32[]{:S(2)}) copy-start(s32[64]{0:T(128)} %param.19) | copy-start | bytes 772
  0.0 8.6 %copy-start.5 = (s32[64]{0:T(128)S(1)}, s32[64]{0:T(128)}, u32[]{:S(2)}) copy-start(s32[64]{0:T(128)} %param.21) | copy-start | bytes 772
  0.0 8.6 %copy-start.6 = (s32[128]{0:T(128)S(1)}, s32[128]{0:T(128)}, u32[]{:S(2)}) copy-start(s32[128]{0:T(128)} %param.20) | copy-start | bytes 1540
  0.0 8.7 %copy-start.4 = (f32[128,2]{0,1:T(2,128)S(1)}, f32[128,2]{0,1:T(2,128)}, u32[]{:S(2)}) copy-start(f32[128,2]{0,1:T(2,128)} %param.17) | copy-start | bytes 3076
  0.0 10.4 %copy-start.3 = (f32[128,2]{0,1:T(2,128)S(1)}, f32[128,2]{0,1:T(2,128)}, u32[]{:S(2)}) copy-start(f32[128,2]{0,1:T(2,128)} %param.18) | copy-start | bytes 3076
  3.7 7.9 %collective-permute-start = (f32[2,8,2560]{2,1,0:T(8,128)S(1)}, f32[2,8,2560]{2,1,0:T(8,128)S(1)}, u32[]{:S(2)}, u32[]{:S(2)}) collective-permute-start(f32[2,8,2560]{2,1,0:T(8,128)S(1)} %get-tuple-element.19), channel_id=1, source_target_pairs={{0,4},{4,0},{8,12},{12,8},{16,20},{20,16},{24,28},{28,24},{1,5},{5... | collective-permute-start | bytes 491528 | tf_op jit(solution)/shard_map/ppermute | solution.py:22
  6.7 7.1 %collective-permute-start.1 = (f32[2,8,2560]{2,1,0:T(8,128)S(1)}, f32[2,8,2560]{2,1,0:T(8,128)S(1)}, u32[]{:S(2)}, u32[]{:S(2)}) collective-permute-start(f32[2,8,2560]{2,1,0:T(8,128)S(1)} %get-tuple-element.18), channel_id=1, source_target_pairs={{0,8},{4,12},{8,0},{12,4},{16,24},{20,28},{24,16},{28,20},{1,9},{5... | collective-permute-start | bytes 491528 | tf_op jit(solution)/shard_map/ppermute | solution.py:22
  8.3 7.4 %collective-permute-start.2 = (f32[2,8,2560]{2,1,0:T(8,128)S(1)}, f32[2,8,2560]{2,1,0:T(8,128)S(1)}, u32[]{:S(2)}, u32[]{:S(2)}) collective-permute-start(f32[2,8,2560]{2,1,0:T(8,128)S(1)} %get-tuple-element.17), channel_id=1, source_target_pairs={{0,12},{4,8},{8,4},{12,0},{16,28},{20,24},{24,20},{28,16},{1,13},{... | collective-permute-start | bytes 491528 | tf_op jit(solution)/shard_map/ppermute | solution.py:22
  15.7 9.6 %collective-permute-start.3 = (f32[2,8,2560]{2,1,0:T(8,128)S(1)}, f32[2,8,2560]{2,1,0:T(8,128)S(1)}, u32[]{:S(2)}, u32[]{:S(2)}) collective-permute-start(f32[2,8,2560]{2,1,0:T(8,128)S(1)} %fusion.1), channel_id=1, source_target_pairs={{0,16},{4,20},{8,24},{12,28},{16,0},{20,4},{24,8},{28,12},{1,17},{... | collective-permute-start | bytes 491528 | tf_op jit(solution)/shard_map/ppermute | solution.py:22
  25.4 4.3 %collective-permute-start.4 = (bf16[256,128]{1,0:T(8,128)(2,1)S(1)}, bf16[256,128]{1,0:T(8,128)(2,1)S(1)}, u32[]{:S(2)}, u32[]{:S(2)}) collective-permute-start(bf16[256,128]{1,0:T(8,128)(2,1)S(1)} %reshape.66.refs_2_), channel_id=1, source_target_pairs={{0,4},{4,0},{8,12},{12,8},{16,20},{20,16},{24,28},{28,24},{1,5},{5... | collective-permute-start | bytes 196616 | tf_op jit(solution)/shard_map/ppermute | solution.py:22
  26.7 4.3 %collective-permute-start.5 = (bf16[256,128]{1,0:T(8,128)(2,1)S(1)}, bf16[256,128]{1,0:T(8,128)(2,1)S(1)}, u32[]{:S(2)}, u32[]{:S(2)}) collective-permute-start(bf16[256,128]{1,0:T(8,128)(2,1)S(1)} %reshape.66.refs_2_), channel_id=1, source_target_pairs={{0,8},{4,12},{8,0},{12,4},{16,24},{20,28},{24,16},{28,20},{1,9},{5... | collective-permute-start | bytes 196616 | tf_op jit(solution)/shard_map/ppermute | solution.py:22
  27.4 5.2 %collective-permute-start.6 = (bf16[256,128]{1,0:T(8,128)(2,1)S(1)}, bf16[256,128]{1,0:T(8,128)(2,1)S(1)}, u32[]{:S(2)}, u32[]{:S(2)}) collective-permute-start(bf16[256,128]{1,0:T(8,128)(2,1)S(1)} %reshape.66.refs_2_), channel_id=1, source_target_pairs={{0,12},{4,8},{8,4},{12,0},{16,28},{20,24},{24,20},{28,16},{1,13},{... | collective-permute-start | bytes 196616 | tf_op jit(solution)/shard_map/ppermute | solution.py:22
  45.0 4.4 %collective-permute-start.7 = (bf16[2,144,128]{2,1,0:T(8,128)(2,1)S(1)}, bf16[2,144,128]{2,1,0:T(8,128)(2,1)S(1)}, u32[]{:S(2)}, u32[]{:S(2)}) collective-permute-start(bf16[2,144,128]{2,1,0:T(8,128)(2,1)S(1)} %get-tuple-element.22), channel_id=1, source_target_pairs={{0,4},{4,0},{8,12},{12,8},{16,20},{20,16},{24,28},{28,24},{1,5},{5... | collective-permute-start | bytes 221192 | tf_op jit(solution)/shard_map/ppermute | solution.py:22
  45.7 4.4 %collective-permute-start.8 = (bf16[2,144,128]{2,1,0:T(8,128)(2,1)S(1)}, bf16[2,144,128]{2,1,0:T(8,128)(2,1)S(1)}, u32[]{:S(2)}, u32[]{:S(2)}) collective-permute-start(bf16[2,144,128]{2,1,0:T(8,128)(2,1)S(1)} %get-tuple-element.21), channel_id=1, source_target_pairs={{0,8},{4,12},{8,0},{12,4},{16,24},{20,28},{24,16},{28,20},{1,9},{5... | collective-permute-start | bytes 221192 | tf_op jit(solution)/shard_map/ppermute | solution.py:22
  47.2 5.3 %collective-permute-start.9 = (bf16[2,144,128]{2,1,0:T(8,128)(2,1)S(1)}, bf16[2,144,128]{2,1,0:T(8,128)(2,1)S(1)}, u32[]{:S(2)}, u32[]{:S(2)}) collective-permute-start(bf16[2,144,128]{2,1,0:T(8,128)(2,1)S(1)} %get-tuple-element.20), channel_id=1, source_target_pairs={{0,12},{4,8},{8,4},{12,0},{16,28},{20,24},{24,20},{28,16},{1,13},{... | collective-permute-start | bytes 221192 | tf_op jit(solution)/shard_map/ppermute | solution.py:22
  52.9 6.3 %collective-permute-start.10 = (bf16[2,144,128]{2,1,0:T(8,128)(2,1)S(1)}, bf16[2,144,128]{2,1,0:T(8,128)(2,1)S(1)}, u32[]{:S(2)}, u32[]{:S(2)}) collective-permute-start(bf16[2,144,128]{2,1,0:T(8,128)(2,1)S(1)} %combine.1.refs_0_), channel_id=1, source_target_pairs={{0,16},{4,20},{8,24},{12,28},{16,0},{20,4},{24,8},{28,12},{1,17},{... | collective-permute-start | bytes 221192 | tf_op jit(solution)/shard_map/ppermute | solution.py:22
  59.7 4.3 %collective-permute-start.11 = (bf16[16,2048]{1,0:T(8,128)(2,1)S(1)}, bf16[16,2048]{1,0:T(8,128)(2,1)S(1)}, u32[]{:S(2)}, u32[]{:S(2)}) collective-permute-start(bf16[16,2048]{1,0:T(8,128)(2,1)S(1)} %reshape.69), channel_id=1, source_target_pairs={{0,4},{4,0},{8,12},{12,8},{16,20},{20,16},{24,28},{28,24},{1,5},{5... | collective-permute-start | bytes 196616 | tf_op jit(solution)/shard_map/ppermute | solution.py:22
  60.8 4.3 %collective-permute-start.12 = (bf16[16,2048]{1,0:T(8,128)(2,1)S(1)}, bf16[16,2048]{1,0:T(8,128)(2,1)S(1)}, u32[]{:S(2)}, u32[]{:S(2)}) collective-permute-start(bf16[16,2048]{1,0:T(8,128)(2,1)S(1)} %reshape.69), channel_id=1, source_target_pairs={{0,8},{4,12},{8,0},{12,4},{16,24},{20,28},{24,16},{28,20},{1,9},{5... | collective-permute-start | bytes 196616 | tf_op jit(solution)/shard_map/ppermute | solution.py:22
  61.3 5.2 %collective-permute-start.13 = (bf16[16,2048]{1,0:T(8,128)(2,1)S(1)}, bf16[16,2048]{1,0:T(8,128)(2,1)S(1)}, u32[]{:S(2)}, u32[]{:S(2)}) collective-permute-start(bf16[16,2048]{1,0:T(8,128)(2,1)S(1)} %reshape.69), channel_id=1, source_target_pairs={{0,12},{4,8},{8,4},{12,0},{16,28},{20,24},{24,20},{28,16},{1,13},{... | collective-permute-start | bytes 196616 | tf_op jit(solution)/shard_map/ppermute | solution.py:22
  69.5 1.6 %collective-permute-start.14 = (f32[64,1024]{1,0:T(8,128)S(1)}, f32[64,1024]{1,0:T(8,128)S(1)}, u32[]{:S(2)}, u32[]{:S(2)}) collective-permute-start(f32[64,1024]{1,0:T(8,128)S(1)} %fusion.7), channel_id=1, source_target_pairs={{0,1},{1,0},{2,3},{3,2},{4,5},{5,4},{6,7},{7,6},{8,9},{9,8},{10,11... | collective-permute-start | bytes 786440 | tf_op jit(solution)/shard_map/ppermute | solution.py:22
  71.1 5.6 %collective-permute-start.15 = (bf16[64,1024]{1,0:T(8,128)(2,1)S(1)}, bf16[64,1024]{1,0:T(8,128)(2,1)S(1)}, u32[]{:S(2)}, u32[]{:S(2)}) collective-permute-start(bf16[64,1024]{1,0:T(8,128)(2,1)S(1)} %fusion.2), channel_id=1, source_target_pairs={{0,2},{1,3},{2,0},{3,1},{4,6},{5,7},{6,4},{7,5},{8,10},{9,11},{10,... | collective-permute-start | bytes 393224 | tf_op jit(solution)/shard_map/ppermute | solution.py:22

commit v6 on v5

--- a/solution.py
+++ b/solution.py
@@ -45,23 +45,40 @@
     return lax.dynamic_index_in_dim(x, digit ^ offset, axis=1, keepdims=False)
 
 
-def scatter_sum(x, axis, n, beside):
+def after(parts, *earlier):
+    return lax.optimization_barrier((parts, *earlier))[0]
+
+
+def scatter_sums(halves, axis, n, beside):
     for shift, size in lower_groups(n):
-        parts = [
-            swap(pick_digit(x, axis, shift, size, d), axis, n, d << shift) for d in range(1, size)
+        sent = [
+            [swap(pick_digit(x, axis, shift, size, d), axis, n, d << shift) for d in range(1, size)]
+            for x in halves
         ]
         if shift == 0:
-            parts, beside = lax.optimization_barrier((parts, beside))
-        x = sum(parts, pick_digit(x, axis, shift, size, 0))
+            sent[0], beside = lax.optimization_barrier((sent[0], beside))
+        sums = []
+        for x, parts in zip(halves, sent):
+            if sums:
+                parts = after(parts, sums[-1])
+            sums.append(sum(parts, pick_digit(x, axis, shift, size, 0)))
+        halves = sums
     shift, size = last_group(n)
-    return sum([swap(x, axis, n, d << shift) for d in range(1, size)], x), beside
+    sent = [[swap(x, axis, n, d << shift) for d in range(1, size)] for x in halves]
+    sums = []
+    for x, parts in zip(halves, sent):
+        if sums:
+            parts = after(parts, sums[-1])
+        sums.append(sum(parts, x).astype(jnp.bfloat16))
+    return sums, beside
 
 
 def gather_relative(x, axis, n):
+    parts = [x]
     for shift, size in reversed(lower_groups(n)):
+        x = jnp.concatenate(parts, axis=0) if len(parts) > 1 else parts[0]
         parts = [x] + [swap(x, axis, n, d << shift) for d in range(1, size)]
-        x = jnp.concatenate(parts, axis=0)
-    return x
+    return parts
 
 
 def relative_place(block, axis, n):
@@ -115,33 +132,32 @@
     )
 
 
-def attention_kernel(
-    place_of,
-    query,
-    tables,
-    key_cache,
-    value_cache,
-    out,
-    query_low,
-    query_high,
-    keys,
-    values,
-    probs,
-    page_out,
-    page_sum,
-    page_max,
-    dev_max,
-    total_out,
-    total_stat,
-    key_sem,
-    value_sem,
-):
+def attention_kernel(ways, place_of, *refs):
+    queries, refs = refs[: 2 * ways], refs[2 * ways :]
+    (tables, key_cache, value_cache), refs = refs[:3], refs[3:]
+    outs, refs = refs[:ways], refs[ways:]
+    (
+        query_low,
+        query_high,
+        keys,
+        values,
+        probs,
+        page_out,
+        page_sum,
+        page_max,
+        dev_max,
+        total_out,
+        total_stat,
+        key_sem,
+        value_sem,
+    ) = refs
     slots = key_cache.shape[0]
     heads = LANES // CHUNK
     group = heads // 2
     chunks = slots // CHUNK
-    blocks, block_rows, _ = out.shape
+    blocks, block_rows, _ = outs[0].shape
     mine = block_rows // heads - 1
+    step_chunks = 4
 
     def key_copy(c):
         part = pl.ds(c * CHUNK, CHUNK)
@@ -151,15 +167,21 @@
         part = pl.ds(c * CHUNK, CHUNK)
         return pltpu.make_async_copy(value_cache.at[part], values.at[part], value_sem.at[c])
 
-    for c in range(chunks):
-        key_copy(c).start()
-        value_copy(c).start()
-
-    rows = query[...]
-    low_head = lax.broadcasted_iota(jnp.int32, rows.shape, 0) % heads < group
-    zero = jnp.zeros_like(rows)
-    query_low[...] = jnp.where(low_head, rows, zero)
-    query_high[...] = jnp.where(low_head, zero, rows)
+    for c in range(chunks + step_chunks):
+        if c >= step_chunks:
+            value_copy(c - step_chunks).start()
+        if c < chunks:
+            key_copy(c).start()
+
+    for ref, parts in ((query_low, queries[:ways]), (query_high, queries[ways:])):
+        for d, part in enumerate(parts):
+            count = part.shape[0]
+            rows = part[...].astype(jnp.float32).reshape(count // group, group, HD)
+            zero = jnp.zeros_like(rows)
+            both = [rows, zero] if ref is query_low else [zero, rows]
+            ref[2 * count * d : 2 * count * (d + 1), :] = (
+                jnp.concatenate(both, axis=1).reshape(2 * count, HD).astype(jnp.bfloat16)
+            )
     total_out[...] = jnp.zeros_like(total_out)
     stat_lane = lax.broadcasted_iota(jnp.int32, total_stat.shape, 1) % STAT
     total_stat[...] = jnp.where(stat_lane < STAT // 2, masked_low, 0.0)
@@ -172,7 +194,7 @@
 
     def score_chunk(c):
         places = [
-            pl.multiple_of((place_of[c * CHUNK + s] >> 16) * heads, heads)
+            pl.multiple_of(((place_of[c * CHUNK + s] >> 16) & 0xFF) * heads, heads)
             for s in range(CHUNK)
         ]
         chosen = jnp.concatenate(
@@ -222,23 +244,23 @@
                 )
             )
 
-    for c in range(2):
+    for c in range(step_chunks):
         key_copy(c).wait()
-    for c in range(2):
         score_chunk(c)
 
-    @pl.loop(1, chunks // 2)
+    @pl.loop(1, chunks // step_chunks)
     def _(step):
-        for c in range(2):
-            key_copy(2 * step + c).wait()
-            value_copy(2 * step + c - 2).wait()
-        for c in range(2):
-            value_chunk(2 * step + c - 2)
-            score_chunk(2 * step + c)
-
-    for c in range(chunks - 2, chunks):
+        first = step * step_chunks
+        for c in range(step_chunks):
+            key_copy(first + c).wait()
+            value_copy(first + c - step_chunks).wait()
+        for c in range(step_chunks):
+            value_chunk(first + c - step_chunks)
+            score_chunk(first + c)
+
+    for c in range(chunks - step_chunks, chunks):
         value_copy(c).wait()
-    for c in range(chunks - 2, chunks):
+    for c in range(chunks - step_chunks, chunks):
         value_chunk(c)
 
     biggest, who = page_max[...], tables[3 * chunks :, :]
@@ -256,9 +278,9 @@
 
     keep_max_row = lax.broadcasted_iota(jnp.int32, (PAGE, LANES), 0) % STAT < STAT // 2
 
-    @pl.loop(0, chunks // 2)
+    @pl.loop(0, chunks // step_chunks)
     def _(step):
-        for c in (2 * step, 2 * step + 1):
+        for c in [step * step_chunks + c for c in range(step_chunks)]:
             top = dev_max[pl.ds(c, 1), :]
             weight = jnp.exp(page_max[pl.ds(c, 1), :] - top)
             out_weight = jnp.broadcast_to(weight * table(2, c), (PAGE, LANES)).T
@@ -275,14 +297,19 @@
                 )
 
     lane = lax.broadcasted_iota(jnp.int32, (heads, LANES), 1)
-    for b in range(blocks):
-        first = b * mine * heads
-        out[b, : mine * heads, :] = total_out[first : first + mine * heads, :].astype(jnp.bfloat16)
-        stat = jnp.zeros((heads, LANES), jnp.float32)
-        for r in range(mine):
-            both = total_stat[first + r * heads : first + (r + 1) * heads, :]
-            stat = jnp.where(lane % (STAT // 2) == r, both, stat)
-        out[b, mine * heads :, :] = split_stat(stat, lane)
+    digit = place_of[0] >> 24
+    for d, out in enumerate(outs):
+        for b in range(blocks):
+            first = (b * ways + (digit ^ d)) * (mine * heads)
+            rows = pl.ds(pl.multiple_of(first, mine * heads), mine * heads)
+            out[b, : mine * heads, :] = total_out[rows, :].astype(jnp.bfloat16)
+            both = total_stat[rows, :]
+            stat = jnp.zeros((heads, LANES), jnp.float32)
+            for r in range(mine):
+                stat = jnp.where(
+                    lane % (STAT // 2) == r, both[r * heads : (r + 1) * heads], stat
+                )
+            out[b, mine * heads :, :] = split_stat(stat, lane)
 
 
 def combine_kernel(*refs):
@@ -314,25 +341,29 @@
 
 
 def finish_kernel(*refs):
-    *parts, query, keyval, out = refs
+    *parts, query_low, query_high, new_low, new_high, out = refs
     blocks, block_rows, _ = parts[0].shape
     heads = LANES // CHUNK
     group = heads // 2
     mine = block_rows // heads - 1
     lane = lax.broadcasted_iota(jnp.int32, (heads, LANES), 1)
     low_head = lax.broadcasted_iota(jnp.int32, (heads, LANES), 0) < group
-    new = keyval[...].astype(jnp.float32)
+    news = [ref[...].astype(jnp.float32) for ref in (new_low, new_high)]
+    queries = [ref[...].astype(jnp.float32) for ref in (query_low, query_high)]
 
     def spread(r, which):
-        low = jnp.broadcast_to(new[4 * r + which : 4 * r + which + 1], (heads, LANES))
-        high = jnp.broadcast_to(new[4 * r + 2 + which : 4 * r + 3 + which], (heads, LANES))
+        low, high = [
+            jnp.broadcast_to(new[2 * r + which : 2 * r + which + 1], (heads, LANES)) for new in news
+        ]
         return jnp.where(low_head, low, high)
 
     for b in range(blocks):
         own = jnp.zeros((heads, LANES), jnp.float32)
         for r in range(mine):
             request = b * mine + r
-            rows = query[request * heads : (request + 1) * heads, :].astype(jnp.float32)
+            rows = jnp.concatenate(
+                [query[request * group : (request + 1) * group] for query in queries], axis=0
+            )
             dot = jnp.sum(rows * spread(request, 0), axis=1, keepdims=True)
             own = jnp.where(lane == r, dot * (1.0 / math.sqrt(HD)), own)
         maxima, sums = [], []
@@ -375,6 +406,7 @@
     kv_local = w_keyval.shape[1] // (2 * HD)
     heads_local = w_query.shape[1] // HD
     wide = heads_local * HD
+    group = heads_local // kv_local
     assert kv_local == 2 and heads_local * CHUNK == LANES
     assert slots % CHUNK == 0
     mine = requests // seq_size
@@ -406,20 +438,28 @@
         ],
         axis=0,
     )
-    place_of = row_of * 65536 + owner
+    ways = lower_groups(seq_size)[0][1]
+    digit = lax.axis_index("seq") & (ways - 1)
+    place_of = (digit << 24) + row_of * 65536 + owner
 
     part_query = jnp.dot(hidden_in, w_query, preferred_element_type=jnp.float32)
     part_keyval = jnp.dot(hidden_in, w_keyval, preferred_element_type=jnp.float32)
-    part_all = jnp.concatenate([part_query, part_keyval], axis=1)
-    sums, (tables, place_of) = scatter_sum(
-        part_all.reshape(seq_size, mine, part_all.shape[1]), "seq", seq_size, (tables, place_of)
-    )
-    sums = sums.astype(jnp.bfloat16)
     held = last_group(seq_size)[1] * mine
-    sums = sums.reshape(held, -1)
-    my_query = sums[:, :wide].reshape(held * heads_local, HD)
-    my_keyval = sums[:, wide:].reshape(held * 2 * kv_local, HD)
-    query = gather_relative(my_query, "seq", seq_size)
+    halves = [
+        jnp.concatenate(
+            [
+                part_query[:, g * group * HD : (g + 1) * group * HD],
+                part_keyval[:, g * 2 * HD : (g + 1) * 2 * HD],
+            ],
+            axis=1,
+        ).reshape(seq_size, mine, -1)
+        for g in range(kv_local)
+    ]
+    sums, (tables, place_of) = scatter_sums(halves, "seq", seq_size, (tables, place_of))
+    sums = [half.reshape(held, -1) for half in sums]
+    my_query = [half[:, : group * HD].reshape(held * group, HD) for half in sums]
+    my_keyval = [half[:, group * HD :].reshape(held * 2, HD) for half in sums]
+    query = [part for half in my_query for part in gather_relative(half, "seq", seq_size)]
 
     smem = pl.BlockSpec(memory_space=pltpu.SMEM)
     vmem = pl.BlockSpec(memory_space=pltpu.VMEM)
@@ -428,10 +468,10 @@
     every_row = requests * heads_local
     block_rows = (mine + 1) * heads_local
     totals = pl.pallas_call(
-        attention_kernel,
-        out_shape=jax.ShapeDtypeStruct((seq_size, block_rows, HD), jnp.bfloat16),
-        in_specs=[smem, vmem, vmem, hbm, hbm],
-        out_specs=vmem,
+        functools.partial(attention_kernel, ways),
+        out_shape=[jax.ShapeDtypeStruct((seq_size // ways, block_rows, HD), jnp.bfloat16)] * ways,
+        in_specs=[smem] + [vmem] * (2 * ways + 1) + [hbm, hbm],
+        out_specs=[vmem] * ways,
         scratch_shapes=[
             pltpu.VMEM((every_row, HD), jnp.bfloat16),
             pltpu.VMEM((every_row, HD), jnp.bfloat16),
@@ -447,19 +487,20 @@
             pltpu.SemaphoreType.DMA((chunks,)),
             pltpu.SemaphoreType.DMA((chunks,)),
         ],
-        compiler_params=pltpu.CompilerParams(vmem_limit_bytes=58 * 2**20),
+        compiler_params=pltpu.CompilerParams(vmem_limit_bytes=48 * 2**20),
         cost_estimate=pl.CostEstimate(
             flops=4 * slots * PAGE * wide,
             bytes_accessed=2 * (key_cache.size + value_cache.size),
             transcendentals=slots * PAGE * heads_local,
         ),
         name="paged_attention",
-    )(place_of, query, tables, key_cache, value_cache)
+    )(place_of, *query, tables, key_cache, value_cache)
 
     for shift, size in lower_groups(seq_size):
-        parts = [pick_digit(totals, "seq", shift, size, 0)] + [
-            swap(pick_digit(totals, "seq", shift, size, d), "seq", seq_size, d << shift)
-            for d in range(1, size)
+        if shift:
+            totals = [pick_digit(totals, "seq", shift, size, d) for d in range(size)]
+        parts = [
+            swap(part, "seq", seq_size, d << shift) if d else part for d, part in enumerate(totals)
         ]
         totals = pl.pallas_call(
             combine_kernel,
@@ -474,11 +515,11 @@
     my_context = pl.pallas_call(
         finish_kernel,
         out_shape=jax.ShapeDtypeStruct((held * heads_local, HD), jnp.bfloat16),
-        in_specs=[vmem] * (size + 2),
+        in_specs=[vmem] * (size + 4),
         out_specs=vmem,
         compiler_params=pltpu.CompilerParams(vmem_limit_bytes=6 * 2**20),
         name="finish",
-    )(*parts, my_query, my_keyval).reshape(held, wide)
+    )(*parts, *my_query, *my_keyval).reshape(held, wide)
     context = gather_in_order(my_context, "seq", seq_size)
 
     total = jnp.dot(context, w_out, preferred_element_type=jnp.float32)

time: 77.7 us -> 78.6 us (1.012)
  starting transfers between devices: 22.8 us -> 32.4 us
  waiting for transfers between devices: 30.2 us -> 25.8 us
  other arithmetic: 3.09 us -> 1.29 us
  Pallas kernels: 11.6 us -> 10.1 us
  local copies, waits for them, and re-layouts: 2.96 us -> 1.99 us
    ppermute x16 -> x23, starting transfers between devices: 22.8 us -> 32.4 us  [swap(): return lax.ppermute(x, axis, [(j, j ^ mask) for j in range(n)])]
    ppermute x16 -> x23, waiting for transfers between devices: 30.2 us -> 25.8 us  [swap(): return lax.ppermute(x, axis, [(j, j ^ mask) for j in range(n)])]
    pallas_call x1, Pallas kernels: 10.7 us -> 9.24 us  [body(): pl.pallas_call(functools.partial(attention_kernel, ways), out_shape=[jax....]
    squeeze x2, local copies, waits for them, and re-layouts: 1.08 us -> 0.05 us  [pick_digit(): return lax.dynamic_index_in_dim(x, digit ^ offset, axis=1, keepdims=False)]
  transfers between devices with their start and end apart: 16 -> 23, of which waited for: 15 -> 14; matrix products, arithmetic and copies ran while one was open for 4% -> 3% of each run, Pallas kernels for 0% -> 0%
where the time goes in v6:
time: 78.6 us; the launch traced here: 78.4 us
  starting transfers between devices  32.4 us (41%)
  waiting for transfers between devices  25.8 us (33%)
  Pallas kernels  10.1 us (13%)
  matrix products  6.49 us (8%)
  local copies, waits for them, and re-layouts  1.99 us (3%)
  other arithmetic  1.29 us (2%)
    ppermute x23, starting transfers between devices, swap(): return lax.ppermute(x, axis, [(j, j ^ mask) for j in range(n)])  32.4 us
    ppermute x23, waiting for transfers between devices, swap(): return lax.ppermute(x, axis, [(j, j ^ mask) for j in range(n)])  25.8 us
    pallas_call x1, Pallas kernels, body(): pl.pallas_call(functools.partial(attention_kernel, ways), out_shape=[jax....  9.24 us
    dot_general x1, matrix products, body(): part_query = jnp.dot(hidden_in, w_query, preferred_element_type=jnp.float32)  3.18 us
    dot_general x1, matrix products, body(): total = jnp.dot(context, w_out, preferred_element_type=jnp.float32)  3.03 us
  transfers between devices with their start and end apart: 23, of which 14 were waited for; matrix products, arithmetic and copies ran while one was open for 3% of the time, Pallas kernels for 0%

profile of v6, /device:TPU:0, one launch (start us, length us, event | category | flops | bytes accessed | tf_op | source)
XLA Modules:
  0.0 78.4 jit_solution(15883779392644002012)
XLA Ops:
  0.0 3.2 %fusion.9 = f32[64,2048]{1,0:T(8,128)S(1)} fusion(bf16[64,1024]{1,0:T(8,128)(2,1)} %param.11, bf16[1024,2048]{1,0:T(8,128)(2,1)} %param.12), kind=kOutput, calls=%fused_computation.44 | convolution fusion | flops 268435456 | bytes 4849664 | tf_op jit(solution)/shard_map/dot_general | solution.py:445
  3.7 3.0 %collective-permute-start = (f32[2,8,1280]{2,1,0:T(8,128)S(1)}, f32[2,8,1280]{2,1,0:T(8,128)S(1)}, u32[]{:S(2)}, u32[]{:S(2)}) collective-permute-start(f32[2,8,1280]{2,1,0:T(8,128)S(1)} %get-tuple-element.40), channel_id=1, source_target_pairs={{0,4},{4,0},{8,12},{12,8},{16,20},{20,16},{24,28},{28,24},{1,5},{5... | collective-permute-start | bytes 245768 | tf_op jit(solution)/shard_map/ppermute | solution.py:22
  6.8 1.6 %collective-permute-start.1 = (f32[2,8,1280]{2,1,0:T(8,128)S(1)}, f32[2,8,1280]{2,1,0:T(8,128)S(1)}, u32[]{:S(2)}, u32[]{:S(2)}) collective-permute-start(f32[2,8,1280]{2,1,0:T(8,128)S(1)} %get-tuple-element.39), channel_id=1, source_target_pairs={{0,8},{4,12},{8,0},{12,4},{16,24},{20,28},{24,16},{28,20},{1,9},{5... | collective-permute-start | bytes 245768 | tf_op jit(solution)/shard_map/ppermute | solution.py:22
  8.4 2.0 %collective-permute-start.7 = (f32[2,8,1280]{2,1,0:T(8,128)S(1)}, f32[2,8,1280]{2,1,0:T(8,128)S(1)}, u32[]{:S(2)}, u32[]{:S(2)}) collective-permute-start(f32[2,8,1280]{2,1,0:T(8,128)S(1)} %get-tuple-element.37), channel_id=1, source_target_pairs={{0,4},{4,0},{8,12},{12,8},{16,20},{20,16},{24,28},{28,24},{1,5},{5... | collective-permute-start | bytes 245768 | tf_op jit(solution)/shard_map/ppermute | solution.py:22
  10.3 1.6 %collective-permute-start.8 = (f32[2,8,1280]{2,1,0:T(8,128)S(1)}, f32[2,8,1280]{2,1,0:T(8,128)S(1)}, u32[]{:S(2)}, u32[]{:S(2)}) collective-permute-start(f32[2,8,1280]{2,1,0:T(8,128)S(1)} %get-tuple-element.36), channel_id=1, source_target_pairs={{0,8},{4,12},{8,0},{12,4},{16,24},{20,28},{24,16},{28,20},{1,9},{5... | collective-permute-start | bytes 245768 | tf_op jit(solution)/shard_map/ppermute | solution.py:22
  14.2 3.0 %collective-permute-start.3 = (f32[2,8,1280]{2,1,0:T(8,128)S(1)}, f32[2,8,1280]{2,1,0:T(8,128)S(1)}, u32[]{:S(2)}, u32[]{:S(2)}) collective-permute-start(f32[2,8,1280]{2,1,0:T(8,128)S(1)} %fusion.4), channel_id=1, source_target_pairs={{0,16},{4,20},{8,24},{12,28},{16,0},{20,4},{24,8},{28,12},{1,17},{... | collective-permute-start | bytes 245768 | tf_op jit(solution)/shard_map/ppermute | solution.py:22
  17.2 2.3 %collective-permute-done.9 = f32[2,8,1280]{2,1,0:T(8,128)S(1)} collective-permute-done((f32[2,8,1280]{2,1,0:T(8,128)S(1)}, f32[2,8,1280]{2,1,0:T(8,128)S(1)}, u32[]{:S(2)}, u32[]{:S(2)}) %collective-permute-start.9) | collective-permute-done | bytes 81952 | tf_op jit(solution)/shard_map/ppermute | solution.py:22
  19.5 3.2 %collective-permute-start.10 = (f32[2,8,1280]{2,1,0:T(8,128)S(1)}, f32[2,8,1280]{2,1,0:T(8,128)S(1)}, u32[]{:S(2)}, u32[]{:S(2)}) collective-permute-start(f32[2,8,1280]{2,1,0:T(8,128)S(1)} %fusion.2), channel_id=1, source_target_pairs={{0,16},{4,20},{8,24},{12,28},{16,0},{20,4},{24,8},{28,12},{1,17},{... | collective-permute-start | bytes 245768 | tf_op jit(solution)/shard_map/ppermute | solution.py:22
  22.8 3.3 %collective-permute-done.10 = f32[2,8,1280]{2,1,0:T(8,128)S(1)} collective-permute-done((f32[2,8,1280]{2,1,0:T(8,128)S(1)}, f32[2,8,1280]{2,1,0:T(8,128)S(1)}, u32[]{:S(2)}, u32[]{:S(2)}) %collective-permute-start.10) | collective-permute-done | bytes 81952 | tf_op jit(solution)/shard_map/ppermute | solution.py:22
  26.5 3.1 %collective-permute-start.13 = (bf16[128,128]{1,0:T(8,128)(2,1)S(1)}, bf16[128,128]{1,0:T(8,128)(2,1)S(1)}, u32[]{:S(2)}, u32[]{:S(2)}) collective-permute-start(bf16[128,128]{1,0:T(8,128)(2,1)S(1)} %reshape.71.refs_4_.refs_3_), channel_id=1, source_target_pairs={{0,12},{4,8},{8,4},{12,0},{16,28},{20,24},{24,20},{28,16},{1,13},{... | collective-permute-start | bytes 98312 | tf_op jit(solution)/shard_map/ppermute | solution.py:22
  30.3 2.9 %collective-permute-start.6 = (bf16[128,128]{1,0:T(8,128)(2,1)S(1)}, bf16[128,128]{1,0:T(8,128)(2,1)S(1)}, u32[]{:S(2)}, u32[]{:S(2)}) collective-permute-start(bf16[128,128]{1,0:T(8,128)(2,1)S(1)} %reshape.69.refs_0_.refs_2_), channel_id=1, source_target_pairs={{0,12},{4,8},{8,4},{12,0},{16,28},{20,24},{24,20},{28,16},{1,13},{... | collective-permute-start | bytes 98312 | tf_op jit(solution)/shard_map/ppermute | solution.py:22
  34.0 1.5 %collective-permute-done.6.refs_3_ = bf16[128,128]{1,0:T(8,128)(2,1)S(1)} collective-permute-done((bf16[128,128]{1,0:T(8,128)(2,1)S(1)}, bf16[128,128]{1,0:T(8,128)(2,1)S(1)}, u32[]{:S(2)}, u32[]{:S(2)}) %collective-permute-start.6) | collective-permute-done | bytes 32800 | tf_op jit(solution)/shard_map/ppermute | solution.py:22
  35.5 9.2 %paged_attention.1 = (bf16[2,144,128]{2,1,0:T(8,128)(2,1)S(1)}, bf16[2,144,128]{2,1,0:T(8,128)(2,1)S(1)}, bf16[2,144,128]{2,1,0:T(8,128)(2,1)S(1)}, bf16[2,144,128]{2,1,0:T(8,128)(2,1)S(1)}) custom-call(s32[128]{0:T(128)S(1)} %get-tuple-element.18.place_of, bf16[128,128]{1,0:T(8,128)(2,1)S(1)} %reshape.69.refs_0_.refs_2_, ...), custom_call_target="tpu_custom_call" | custom-call | flops 134217728 | bytes 16777216 | tf_op jit(solution)/shard_map/paged_attention/pallas_call | solution.py:470
  46.0 1.9 %collective-permute-start.15 = (bf16[2,144,128]{2,1,0:T(8,128)(2,1)S(1)}, bf16[2,144,128]{2,1,0:T(8,128)(2,1)S(1)}, u32[]{:S(2)}, u32[]{:S(2)}) collective-permute-start(bf16[2,144,128]{2,1,0:T(8,128)(2,1)S(1)} %get-tuple-element.29), channel_id=1, source_target_pairs={{0,8},{4,12},{8,0},{12,4},{16,24},{20,28},{24,16},{28,20},{1,9},{5... | collective-permute-start | bytes 221192 | tf_op jit(solution)/shard_map/ppermute | solution.py:22
  49.1 1.7 %collective-permute-done.15.refs_2_ = bf16[2,144,128]{2,1,0:T(8,128)(2,1)S(1)} collective-permute-done((bf16[2,144,128]{2,1,0:T(8,128)(2,1)S(1)}, bf16[2,144,128]{2,1,0:T(8,128)(2,1)S(1)}, u32[]{:S(2)}, u32[]{:S(2)}) %collective-permute-start.15) | collective-permute-done | bytes 73760 | tf_op jit(solution)/shard_map/ppermute | solution.py:22
  50.8 2.3 %collective-permute-done.16.refs_3_ = bf16[2,144,128]{2,1,0:T(8,128)(2,1)S(1)} collective-permute-done((bf16[2,144,128]{2,1,0:T(8,128)(2,1)S(1)}, bf16[2,144,128]{2,1,0:T(8,128)(2,1)S(1)}, u32[]{:S(2)}, u32[]{:S(2)}) %collective-permute-start.16) | collective-permute-done | bytes 73760 | tf_op jit(solution)/shard_map/ppermute | solution.py:22
  53.6 2.1 %collective-permute-start.17 = (bf16[2,144,128]{2,1,0:T(8,128)(2,1)S(1)}, bf16[2,144,128]{2,1,0:T(8,128)(2,1)S(1)}, u32[]{:S(2)}, u32[]{:S(2)}) collective-permute-start(bf16[2,144,128]{2,1,0:T(8,128)(2,1)S(1)} %combine.1.refs_0_), channel_id=1, source_target_pairs={{0,16},{4,20},{8,24},{12,28},{16,0},{20,4},{24,8},{28,12},{1,17},{... | collective-permute-start | bytes 221192 | tf_op jit(solution)/shard_map/ppermute | solution.py:22
  55.8 3.8 %collective-permute-done.17.refs_1_ = bf16[2,144,128]{2,1,0:T(8,128)(2,1)S(1)} collective-permute-done((bf16[2,144,128]{2,1,0:T(8,128)(2,1)S(1)}, bf16[2,144,128]{2,1,0:T(8,128)(2,1)S(1)}, u32[]{:S(2)}, u32[]{:S(2)}) %collective-permute-start.17) | collective-permute-done | bytes 73760 | tf_op jit(solution)/shard_map/ppermute | solution.py:22
  60.2 2.1 %collective-permute-start.19 = (bf16[16,2048]{1,0:T(8,128)(2,1)S(1)}, bf16[16,2048]{1,0:T(8,128)(2,1)S(1)}, u32[]{:S(2)}, u32[]{:S(2)}) collective-permute-start(bf16[16,2048]{1,0:T(8,128)(2,1)S(1)} %reshape.74), channel_id=1, source_target_pairs={{0,8},{4,12},{8,0},{12,4},{16,24},{20,28},{24,16},{28,20},{1,9},{5... | collective-permute-start | bytes 196616 | tf_op jit(solution)/shard_map/ppermute | solution.py:22
  64.5 2.9 %collective-permute-done.20 = bf16[16,2048]{1,0:T(8,128)(2,1)S(1)} collective-permute-done((bf16[16,2048]{1,0:T(8,128)(2,1)S(1)}, bf16[16,2048]{1,0:T(8,128)(2,1)S(1)}, u32[]{:S(2)}, u32[]{:S(2)}) %collective-permute-start.20) | collective-permute-done | bytes 65568 | tf_op jit(solution)/shard_map/ppermute | solution.py:22
  67.4 3.0 %fusion.11 = f32[64,1024]{1,0:T(8,128)S(1)} fusion(bf16[64,2048]{1,0:T(8,128)(2,1)S(1)} %slice_dynamic-update-slice_fusion, bf16[2048,1024]{1,0:T(8,128)(2,1)} %param.14), kind=kOutput, calls=%fused_computation.46 | convolution fusion | flops 268435456 | bytes 4718592 | tf_op jit(solution)/shard_map/dot_general | solution.py:525
  70.5 1.5 %collective-permute-done.21 = f32[64,1024]{1,0:T(8,128)S(1)} collective-permute-done((f32[64,1024]{1,0:T(8,128)S(1)}, f32[64,1024]{1,0:T(8,128)S(1)}, u32[]{:S(2)}, u32[]{:S(2)}) %collective-permute-start.21) | collective-permute-done | bytes 262176 | tf_op jit(solution)/shard_map/ppermute | solution.py:22
  72.1 1.4 %collective-permute-start.22 = (bf16[64,1024]{1,0:T(8,128)(2,1)S(1)}, bf16[64,1024]{1,0:T(8,128)(2,1)S(1)}, u32[]{:S(2)}, u32[]{:S(2)}) collective-permute-start(bf16[64,1024]{1,0:T(8,128)(2,1)S(1)} %fusion), channel_id=1, source_target_pairs={{0,2},{1,3},{2,0},{3,1},{4,6},{5,7},{6,4},{7,5},{8,10},{9,11},{10,... | collective-permute-start | bytes 393224 | tf_op jit(solution)/shard_map/ppermute | solution.py:22
  73.5 4.2 %collective-permute-done.22 = bf16[64,1024]{1,0:T(8,128)(2,1)S(1)} collective-permute-done((bf16[64,1024]{1,0:T(8,128)(2,1)S(1)}, bf16[64,1024]{1,0:T(8,128)(2,1)S(1)}, u32[]{:S(2)}, u32[]{:S(2)}) %collective-permute-start.22) | collective-permute-done | bytes 131104 | tf_op jit(solution)/shard_map/ppermute | solution.py:22
  (96 shorter events, 11.2 us)
Async XLA Ops:
  0.0 13.5 %copy-start.3 = (f32[128,2]{0,1:T(2,128)S(1)}, f32[128,2]{0,1:T(2,128)}, u32[]{:S(2)}) copy-start(f32[128,2]{0,1:T(2,128)} %param.18) | copy-start | bytes 3076
  3.7 10.3 %collective-permute-start = (f32[2,8,1280]{2,1,0:T(8,128)S(1)}, f32[2,8,1280]{2,1,0:T(8,128)S(1)}, u32[]{:S(2)}, u32[]{:S(2)}) collective-permute-start(f32[2,8,1280]{2,1,0:T(8,128)S(1)} %get-tuple-element.40), channel_id=1, source_target_pairs={{0,4},{4,0},{8,12},{12,8},{16,20},{20,16},{24,28},{28,24},{1,5},{5... | collective-permute-start | bytes 245768 | tf_op jit(solution)/shard_map/ppermute | solution.py:22
  6.8 7.4 %collective-permute-start.1 = (f32[2,8,1280]{2,1,0:T(8,128)S(1)}, f32[2,8,1280]{2,1,0:T(8,128)S(1)}, u32[]{:S(2)}, u32[]{:S(2)}) collective-permute-start(f32[2,8,1280]{2,1,0:T(8,128)S(1)} %get-tuple-element.39), channel_id=1, source_target_pairs={{0,8},{4,12},{8,0},{12,4},{16,24},{20,28},{24,16},{28,20},{1,9},{5... | collective-permute-start | bytes 245768 | tf_op jit(solution)/shard_map/ppermute | solution.py:22
  8.3 5.8 %collective-permute-start.2 = (f32[2,8,1280]{2,1,0:T(8,128)S(1)}, f32[2,8,1280]{2,1,0:T(8,128)S(1)}, u32[]{:S(2)}, u32[]{:S(2)}) collective-permute-start(f32[2,8,1280]{2,1,0:T(8,128)S(1)} %get-tuple-element.38), channel_id=1, source_target_pairs={{0,12},{4,8},{8,4},{12,0},{16,28},{20,24},{24,20},{28,16},{1,13},{... | collective-permute-start | bytes 245768 | tf_op jit(solution)/shard_map/ppermute | solution.py:22
  8.4 8.9 %collective-permute-start.7 = (f32[2,8,1280]{2,1,0:T(8,128)S(1)}, f32[2,8,1280]{2,1,0:T(8,128)S(1)}, u32[]{:S(2)}, u32[]{:S(2)}) collective-permute-start(f32[2,8,1280]{2,1,0:T(8,128)S(1)} %get-tuple-element.37), channel_id=1, source_target_pairs={{0,4},{4,0},{8,12},{12,8},{16,20},{20,16},{24,28},{28,24},{1,5},{5... | collective-permute-start | bytes 245768 | tf_op jit(solution)/shard_map/ppermute | solution.py:22
  10.3 6.9 %collective-permute-start.8 = (f32[2,8,1280]{2,1,0:T(8,128)S(1)}, f32[2,8,1280]{2,1,0:T(8,128)S(1)}, u32[]{:S(2)}, u32[]{:S(2)}) collective-permute-start(f32[2,8,1280]{2,1,0:T(8,128)S(1)} %get-tuple-element.36), channel_id=1, source_target_pairs={{0,8},{4,12},{8,0},{12,4},{16,24},{20,28},{24,16},{28,20},{1,9},{5... | collective-permute-start | bytes 245768 | tf_op jit(solution)/shard_map/ppermute | solution.py:22
  14.1 5.4 %collective-permute-start.9 = (f32[2,8,1280]{2,1,0:T(8,128)S(1)}, f32[2,8,1280]{2,1,0:T(8,128)S(1)}, u32[]{:S(2)}, u32[]{:S(2)}) collective-permute-start(f32[2,8,1280]{2,1,0:T(8,128)S(1)} %get-tuple-element.35), channel_id=1, source_target_pairs={{0,12},{4,8},{8,4},{12,0},{16,28},{20,24},{24,20},{28,16},{1,13},{... | collective-permute-start | bytes 245768 | tf_op jit(solution)/shard_map/ppermute | solution.py:22
  14.2 8.5 %collective-permute-start.3 = (f32[2,8,1280]{2,1,0:T(8,128)S(1)}, f32[2,8,1280]{2,1,0:T(8,128)S(1)}, u32[]{:S(2)}, u32[]{:S(2)}) collective-permute-start(f32[2,8,1280]{2,1,0:T(8,128)S(1)} %fusion.4), channel_id=1, source_target_pairs={{0,16},{4,20},{8,24},{12,28},{16,0},{20,4},{24,8},{28,12},{1,17},{... | collective-permute-start | bytes 245768 | tf_op jit(solution)/shard_map/ppermute | solution.py:22
  19.5 6.5 %collective-permute-start.10 = (f32[2,8,1280]{2,1,0:T(8,128)S(1)}, f32[2,8,1280]{2,1,0:T(8,128)S(1)}, u32[]{:S(2)}, u32[]{:S(2)}) collective-permute-start(f32[2,8,1280]{2,1,0:T(8,128)S(1)} %fusion.2), channel_id=1, source_target_pairs={{0,16},{4,20},{8,24},{12,28},{16,0},{20,4},{24,8},{28,12},{1,17},{... | collective-permute-start | bytes 245768 | tf_op jit(solution)/shard_map/ppermute | solution.py:22
  26.1 4.2 %collective-permute-start.11 = (bf16[128,128]{1,0:T(8,128)(2,1)S(1)}, bf16[128,128]{1,0:T(8,128)(2,1)S(1)}, u32[]{:S(2)}, u32[]{:S(2)}) collective-permute-start(bf16[128,128]{1,0:T(8,128)(2,1)S(1)} %reshape.71.refs_4_.refs_3_), channel_id=1, source_target_pairs={{0,4},{4,0},{8,12},{12,8},{16,20},{20,16},{24,28},{28,24},{1,5},{5... | collective-permute-start | bytes 98312 | tf_op jit(solution)/shard_map/ppermute | solution.py:22
  26.5 6.8 %collective-permute-start.12 = (bf16[128,128]{1,0:T(8,128)(2,1)S(1)}, bf16[128,128]{1,0:T(8,128)(2,1)S(1)}, u32[]{:S(2)}, u32[]{:S(2)}) collective-permute-start(bf16[128,128]{1,0:T(8,128)(2,1)S(1)} %reshape.71.refs_4_.refs_3_), channel_id=1, source_target_pairs={{0,8},{4,12},{8,0},{12,4},{16,24},{20,28},{24,16},{28,20},{1,9},{5... | collective-permute-start | bytes 98312 | tf_op jit(solution)/shard_map/ppermute | solution.py:22
  26.5 6.7 %collective-permute-start.13 = (bf16[128,128]{1,0:T(8,128)(2,1)S(1)}, bf16[128,128]{1,0:T(8,128)(2,1)S(1)}, u32[]{:S(2)}, u32[]{:S(2)}) collective-permute-start(bf16[128,128]{1,0:T(8,128)(2,1)S(1)} %reshape.71.refs_4_.refs_3_), channel_id=1, source_target_pairs={{0,12},{4,8},{8,4},{12,0},{16,28},{20,24},{24,20},{28,16},{1,13},{... | collective-permute-start | bytes 98312 | tf_op jit(solution)/shard_map/ppermute | solution.py:22
  29.7 4.0 %collective-permute-start.4 = (bf16[128,128]{1,0:T(8,128)(2,1)S(1)}, bf16[128,128]{1,0:T(8,128)(2,1)S(1)}, u32[]{:S(2)}, u32[]{:S(2)}) collective-permute-start(bf16[128,128]{1,0:T(8,128)(2,1)S(1)} %reshape.69.refs_0_.refs_2_), channel_id=1, source_target_pairs={{0,4},{4,0},{8,12},{12,8},{16,20},{20,16},{24,28},{28,24},{1,5},{5... | collective-permute-start | bytes 98312 | tf_op jit(solution)/shard_map/ppermute | solution.py:22
  30.0 3.9 %collective-permute-start.5 = (bf16[128,128]{1,0:T(8,128)(2,1)S(1)}, bf16[128,128]{1,0:T(8,128)(2,1)S(1)}, u32[]{:S(2)}, u32[]{:S(2)}) collective-permute-start(bf16[128,128]{1,0:T(8,128)(2,1)S(1)} %reshape.69.refs_0_.refs_2_), channel_id=1, source_target_pairs={{0,8},{4,12},{8,0},{12,4},{16,24},{20,28},{24,16},{28,20},{1,9},{5... | collective-permute-start | bytes 98312 | tf_op jit(solution)/shard_map/ppermute | solution.py:22
  30.3 5.2 %collective-permute-start.6 = (bf16[128,128]{1,0:T(8,128)(2,1)S(1)}, bf16[128,128]{1,0:T(8,128)(2,1)S(1)}, u32[]{:S(2)}, u32[]{:S(2)}) collective-permute-start(bf16[128,128]{1,0:T(8,128)(2,1)S(1)} %reshape.69.refs_0_.refs_2_), channel_id=1, source_target_pairs={{0,12},{4,8},{8,4},{12,0},{16,28},{20,24},{24,20},{28,16},{1,13},{... | collective-permute-start | bytes 98312 | tf_op jit(solution)/shard_map/ppermute | solution.py:22
  44.7 4.4 %collective-permute-start.14 = (bf16[2,144,128]{2,1,0:T(8,128)(2,1)S(1)}, bf16[2,144,128]{2,1,0:T(8,128)(2,1)S(1)}, u32[]{:S(2)}, u32[]{:S(2)}) collective-permute-start(bf16[2,144,128]{2,1,0:T(8,128)(2,1)S(1)} %get-tuple-element.28), channel_id=1, source_target_pairs={{0,4},{4,0},{8,12},{12,8},{16,20},{20,16},{24,28},{28,24},{1,5},{5... | collective-permute-start | bytes 221192 | tf_op jit(solution)/shard_map/ppermute | solution.py:22
  46.0 4.8 %collective-permute-start.15 = (bf16[2,144,128]{2,1,0:T(8,128)(2,1)S(1)}, bf16[2,144,128]{2,1,0:T(8,128)(2,1)S(1)}, u32[]{:S(2)}, u32[]{:S(2)}) collective-permute-start(bf16[2,144,128]{2,1,0:T(8,128)(2,1)S(1)} %get-tuple-element.29), channel_id=1, source_target_pairs={{0,8},{4,12},{8,0},{12,4},{16,24},{20,28},{24,16},{28,20},{1,9},{5... | collective-permute-start | bytes 221192 | tf_op jit(solution)/shard_map/ppermute | solution.py:22
  47.9 5.3 %collective-permute-start.16 = (bf16[2,144,128]{2,1,0:T(8,128)(2,1)S(1)}, bf16[2,144,128]{2,1,0:T(8,128)(2,1)S(1)}, u32[]{:S(2)}, u32[]{:S(2)}) collective-permute-start(bf16[2,144,128]{2,1,0:T(8,128)(2,1)S(1)} %get-tuple-element.30), channel_id=1, source_target_pairs={{0,12},{4,8},{8,4},{12,0},{16,28},{20,24},{24,20},{28,16},{1,13},{... | collective-permute-start | bytes 221192 | tf_op jit(solution)/shard_map/ppermute | solution.py:22
  53.6 6.0 %collective-permute-start.17 = (bf16[2,144,128]{2,1,0:T(8,128)(2,1)S(1)}, bf16[2,144,128]{2,1,0:T(8,128)(2,1)S(1)}, u32[]{:S(2)}, u32[]{:S(2)}) collective-permute-start(bf16[2,144,128]{2,1,0:T(8,128)(2,1)S(1)} %combine.1.refs_0_), channel_id=1, source_target_pairs={{0,16},{4,20},{8,24},{12,28},{16,0},{20,4},{24,8},{28,12},{1,17},{... | collective-permute-start | bytes 221192 | tf_op jit(solution)/shard_map/ppermute | solution.py:22
  60.1 4.3 %collective-permute-start.18 = (bf16[16,2048]{1,0:T(8,128)(2,1)S(1)}, bf16[16,2048]{1,0:T(8,128)(2,1)S(1)}, u32[]{:S(2)}, u32[]{:S(2)}) collective-permute-start(bf16[16,2048]{1,0:T(8,128)(2,1)S(1)} %reshape.74), channel_id=1, source_target_pairs={{0,4},{4,0},{8,12},{12,8},{16,20},{20,16},{24,28},{28,24},{1,5},{5... | collective-permute-start | bytes 196616 | tf_op jit(solution)/shard_map/ppermute | solution.py:22
  60.2 4.3 %collective-permute-start.19 = (bf16[16,2048]{1,0:T(8,128)(2,1)S(1)}, bf16[16,2048]{1,0:T(8,128)(2,1)S(1)}, u32[]{:S(2)}, u32[]{:S(2)}) collective-permute-start(bf16[16,2048]{1,0:T(8,128)(2,1)S(1)} %reshape.74), channel_id=1, source_target_pairs={{0,8},{4,12},{8,0},{12,4},{16,24},{20,28},{24,16},{28,20},{1,9},{5... | collective-permute-start | bytes 196616 | tf_op jit(solution)/shard_map/ppermute | solution.py:22
  62.2 5.2 %collective-permute-start.20 = (bf16[16,2048]{1,0:T(8,128)(2,1)S(1)}, bf16[16,2048]{1,0:T(8,128)(2,1)S(1)}, u32[]{:S(2)}, u32[]{:S(2)}) collective-permute-start(bf16[16,2048]{1,0:T(8,128)(2,1)S(1)} %reshape.74), channel_id=1, source_target_pairs={{0,12},{4,8},{8,4},{12,0},{16,28},{20,24},{24,20},{28,16},{1,13},{... | collective-permute-start | bytes 196616 | tf_op jit(solution)/shard_map/ppermute | solution.py:22
  70.4 1.6 %collective-permute-start.21 = (f32[64,1024]{1,0:T(8,128)S(1)}, f32[64,1024]{1,0:T(8,128)S(1)}, u32[]{:S(2)}, u32[]{:S(2)}) collective-permute-start(f32[64,1024]{1,0:T(8,128)S(1)} %fusion.11), channel_id=1, source_target_pairs={{0,1},{1,0},{2,3},{3,2},{4,5},{5,4},{6,7},{7,6},{8,9},{9,8},{10,11... | collective-permute-start | bytes 786440 | tf_op jit(solution)/shard_map/ppermute | solution.py:22
  72.1 5.6 %collective-permute-start.22 = (bf16[64,1024]{1,0:T(8,128)(2,1)S(1)}, bf16[64,1024]{1,0:T(8,128)(2,1)S(1)}, u32[]{:S(2)}, u32[]{:S(2)}) collective-permute-start(bf16[64,1024]{1,0:T(8,128)(2,1)S(1)} %fusion), channel_id=1, source_target_pairs={{0,2},{1,3},{2,0},{3,1},{4,6},{5,7},{6,4},{7,5},{8,10},{9,11},{10,... | collective-permute-start | bytes 393224 | tf_op jit(solution)/shard_map/ppermute | solution.py:22
  (6 other events, 55.9 us)

commit v7 on v6

--- a/solution.py
+++ b/solution.py
@@ -45,32 +45,16 @@
     return lax.dynamic_index_in_dim(x, digit ^ offset, axis=1, keepdims=False)
 
 
-def after(parts, *earlier):
-    return lax.optimization_barrier((parts, *earlier))[0]
-
-
-def scatter_sums(halves, axis, n, beside):
+def scatter_sum(parts, axis, n, beside):
     for shift, size in lower_groups(n):
-        sent = [
-            [swap(pick_digit(x, axis, shift, size, d), axis, n, d << shift) for d in range(1, size)]
-            for x in halves
-        ]
+        if shift:
+            parts = [pick_digit(x, axis, shift, size, d) for d in range(size)]
+        sent = [swap(parts[d], axis, n, d << shift) for d in range(1, size)]
         if shift == 0:
-            sent[0], beside = lax.optimization_barrier((sent[0], beside))
-        sums = []
-        for x, parts in zip(halves, sent):
-            if sums:
-                parts = after(parts, sums[-1])
-            sums.append(sum(parts, pick_digit(x, axis, shift, size, 0)))
-        halves = sums
+            sent, beside = lax.optimization_barrier((sent, beside))
+        x = sum(sent, parts[0])
     shift, size = last_group(n)
-    sent = [[swap(x, axis, n, d << shift) for d in range(1, size)] for x in halves]
-    sums = []
-    for x, parts in zip(halves, sent):
-        if sums:
-            parts = after(parts, sums[-1])
-        sums.append(sum(parts, x).astype(jnp.bfloat16))
-    return sums, beside
+    return sum([swap(x, axis, n, d << shift) for d in range(1, size)], x), beside
 
 
 def gather_relative(x, axis, n):
@@ -91,30 +75,68 @@
     return place
 
 
-def gather_in_order(x, axis, n):
+def gathered_blocks(me, n):
     last_shift, last_size = last_group(n)
-    rows = x.shape[0] // last_size
-    me = lax.axis_index(axis) & ((1 << last_shift) - 1)
-    held = [(0, x)]
-    out = jnp.zeros((n * rows, x.shape[1]), x.dtype)
+    offsets = [0]
     for shift, size in reversed(lower_groups(n)):
-        stacked = jnp.concatenate([part for _, part in held], axis=0)
-        height = x.shape[0]
-        held = [
-            (d << shift | offset, part[i * height : (i + 1) * height])
-            for d in range(size)
-            for part in [swap(stacked, axis, n, d << shift) if d else stacked]
-            for i, (offset, _) in enumerate(held)
-        ]
-    for offset, part in held:
-        for c in range(last_size):
-            out = lax.dynamic_update_slice_in_dim(
-                out,
-                part[c * rows : (c + 1) * rows],
-                ((c << last_shift) + (me ^ offset)) * rows,
-                axis=0,
-            )
-    return out
+        offsets = [d << shift | e for d in range(size) for e in offsets]
+    low = me & ((1 << last_shift) - 1)
+    return [(c << last_shift) + (low ^ e) for e in offsets for c in range(last_size)]
+
+
+def project_kernel(ways, me, hidden, w_query, w_keyval, *refs):
+    outs, (query, keyval, result, sem) = refs[:ways], refs[ways:]
+    tile = min(512, w_keyval.shape[1])
+    jobs = [
+        (ref, held, col, base + col)
+        for ref, held, base in ((w_query, query, 0), (w_keyval, keyval, w_query.shape[1]))
+        for col in range(0, ref.shape[1], tile)
+    ]
+    copies = [
+        pltpu.make_async_copy(
+            ref.at[:, pl.ds(col, tile)], held.at[:, pl.ds(col, tile)], sem.at[i]
+        )
+        for i, (ref, held, col, _) in enumerate(jobs)
+    ]
+    for copy in copies:
+        copy.start()
+    rows = hidden[...]
+    for copy, (_, held, col, place) in zip(copies, jobs):
+        copy.wait()
+        result[:, place : place + tile] = jnp.dot(
+            rows, held[:, col : col + tile], preferred_element_type=jnp.float32
+        )
+    digit = me[0] & (ways - 1)
+    for d, out in enumerate(outs):
+        blocks, mine, _ = out.shape
+        for b in range(blocks):
+            if mine % 8 == 0:
+                first = (b * ways + (digit ^ d)) * mine
+                out[b] = result[pl.ds(pl.multiple_of(first, mine), mine), :]
+                continue
+            chosen = result[b * ways * mine : (b * ways + 1) * mine, :]
+            for j in range(1, ways):
+                first = (b * ways + j) * mine
+                chosen = jnp.where((digit ^ d) == j, result[first : first + mine, :], chosen)
+            out[b] = chosen
+
+
+def output_kernel(ways, seq_size, me, *refs):
+    parts, (w_out, out) = refs[:ways], refs[ways:]
+    rows = jnp.concatenate([part[...] for part in parts], axis=0)
+    total = jnp.dot(rows, w_out[...], preferred_element_type=jnp.float32)
+    blocks = gathered_blocks(me[0], seq_size)
+    mine = rows.shape[0] // len(blocks)
+    if mine % 8 == 0:
+        for i, block in enumerate(blocks):
+            here = pl.ds(pl.multiple_of(block * mine, mine), mine)
+            out[here, :] = total[i * mine : (i + 1) * mine]
+        return
+    for place in range(len(blocks)):
+        chosen = total[:mine]
+        for i, block in enumerate(blocks):
+            chosen = jnp.where(block == place, total[i * mine : (i + 1) * mine], chosen)
+        out[place * mine : (place + 1) * mine, :] = chosen
 
 
 def split_stat(stat, lane):
@@ -133,7 +155,7 @@
 
 
 def attention_kernel(ways, place_of, *refs):
-    queries, refs = refs[: 2 * ways], refs[2 * ways :]
+    queries, refs = refs[:ways], refs[ways:]
     (tables, key_cache, value_cache), refs = refs[:3], refs[3:]
     outs, refs = refs[:ways], refs[ways:]
     (
@@ -173,17 +195,15 @@
         if c < chunks:
             key_copy(c).start()
 
-    for ref, parts in ((query_low, queries[:ways]), (query_high, queries[ways:])):
-        for d, part in enumerate(parts):
-            count = part.shape[0]
-            rows = part[...].astype(jnp.float32).reshape(count // group, group, HD)
-            zero = jnp.zeros_like(rows)
-            both = [rows, zero] if ref is query_low else [zero, rows]
-            ref[2 * count * d : 2 * count * (d + 1), :] = (
-                jnp.concatenate(both, axis=1).reshape(2 * count, HD).astype(jnp.bfloat16)
-            )
+    for d, part in enumerate(queries):
+        rows = part[...]
+        low_head = lax.broadcasted_iota(jnp.int32, rows.shape, 0) % heads < group
+        zero = jnp.zeros_like(rows)
+        here = slice(rows.shape[0] * d, rows.shape[0] * (d + 1))
+        query_low[here, :] = jnp.where(low_head, rows, zero)
+        query_high[here, :] = jnp.where(low_head, zero, rows)
     total_out[...] = jnp.zeros_like(total_out)
-    stat_lane = lax.broadcasted_iota(jnp.int32, total_stat.shape, 1) % STAT
+    stat_lane = lax.broadcasted_iota(jnp.int32, total_stat.shape, 2) % STAT
     total_stat[...] = jnp.where(stat_lane < STAT // 2, masked_low, 0.0)
 
     def table(which, c):
@@ -291,9 +311,10 @@
                 )
                 there = pl.ds(pl.multiple_of((c * CHUNK + s) * heads, heads), heads)
                 part = slice(s * heads, (s + 1) * heads)
-                total_out[here, :] += page_out[there, :] * out_weight[part]
-                total_stat[here, :] = jnp.where(
-                    keep_max, stat[part], total_stat[here, :] + stat[part]
+                turn = s % 2
+                total_out[turn, here, :] += page_out[there, :] * out_weight[part]
+                total_stat[turn, here, :] = jnp.where(
+                    keep_max, stat[part], total_stat[turn, here, :] + stat[part]
                 )
 
     lane = lax.broadcasted_iota(jnp.int32, (heads, LANES), 1)
@@ -302,8 +323,12 @@
         for b in range(blocks):
             first = (b * ways + (digit ^ d)) * (mine * heads)
             rows = pl.ds(pl.multiple_of(first, mine * heads), mine * heads)
-            out[b, : mine * heads, :] = total_out[rows, :].astype(jnp.bfloat16)
-            both = total_stat[rows, :]
+            out[b, : mine * heads, :] = (total_out[0, rows, :] + total_out[1, rows, :]).astype(
+                jnp.bfloat16
+            )
+            even, odd = total_stat[0, rows, :], total_stat[1, rows, :]
+            is_max = lax.broadcasted_iota(jnp.int32, even.shape, 1) % STAT < STAT // 2
+            both = jnp.where(is_max, jnp.maximum(even, odd), even + odd)
             stat = jnp.zeros((heads, LANES), jnp.float32)
             for r in range(mine):
                 stat = jnp.where(
@@ -341,29 +366,25 @@
 
 
 def finish_kernel(*refs):
-    *parts, query_low, query_high, new_low, new_high, out = refs
+    *parts, query, keyval, out, numers = refs
     blocks, block_rows, _ = parts[0].shape
     heads = LANES // CHUNK
     group = heads // 2
     mine = block_rows // heads - 1
     lane = lax.broadcasted_iota(jnp.int32, (heads, LANES), 1)
     low_head = lax.broadcasted_iota(jnp.int32, (heads, LANES), 0) < group
-    news = [ref[...].astype(jnp.float32) for ref in (new_low, new_high)]
-    queries = [ref[...].astype(jnp.float32) for ref in (query_low, query_high)]
+    new = keyval[...].astype(jnp.float32)
 
     def spread(r, which):
-        low, high = [
-            jnp.broadcast_to(new[2 * r + which : 2 * r + which + 1], (heads, LANES)) for new in news
-        ]
+        low = jnp.broadcast_to(new[4 * r + which : 4 * r + which + 1], (heads, LANES))
+        high = jnp.broadcast_to(new[4 * r + 2 + which : 4 * r + 3 + which], (heads, LANES))
         return jnp.where(low_head, low, high)
 
     for b in range(blocks):
         own = jnp.zeros((heads, LANES), jnp.float32)
         for r in range(mine):
             request = b * mine + r
-            rows = jnp.concatenate(
-                [query[request * group : (request + 1) * group] for query in queries], axis=0
-            )
+            rows = query[request * heads : (request + 1) * heads, :].astype(jnp.float32)
             dot = jnp.sum(rows * spread(request, 0), axis=1, keepdims=True)
             own = jnp.where(lane == r, dot * (1.0 / math.sqrt(HD)), own)
         maxima, sums = [], []
@@ -383,7 +404,11 @@
                 rows = part[b, r * heads : (r + 1) * heads, :].astype(jnp.float32)
                 numer = numer + f[:, r : r + 1] * rows
             request = b * mine + r
-            out[request * heads : (request + 1) * heads, :] = numer.astype(jnp.bfloat16)
+            numers[request * heads : (request + 1) * heads, :] = numer
+    for h in range(heads):
+        out[:, h * HD : (h + 1) * HD] = numers[
+            pl.ds(h, blocks * mine, stride=heads), :
+        ].astype(jnp.bfloat16)
 
 
 def body(
@@ -442,35 +467,41 @@
     digit = lax.axis_index("seq") & (ways - 1)
     place_of = (digit << 24) + row_of * 65536 + owner
 
-    part_query = jnp.dot(hidden_in, w_query, preferred_element_type=jnp.float32)
-    part_keyval = jnp.dot(hidden_in, w_keyval, preferred_element_type=jnp.float32)
     held = last_group(seq_size)[1] * mine
-    halves = [
-        jnp.concatenate(
-            [
-                part_query[:, g * group * HD : (g + 1) * group * HD],
-                part_keyval[:, g * 2 * HD : (g + 1) * 2 * HD],
-            ],
-            axis=1,
-        ).reshape(seq_size, mine, -1)
-        for g in range(kv_local)
-    ]
-    sums, (tables, place_of) = scatter_sums(halves, "seq", seq_size, (tables, place_of))
-    sums = [half.reshape(held, -1) for half in sums]
-    my_query = [half[:, : group * HD].reshape(held * group, HD) for half in sums]
-    my_keyval = [half[:, group * HD :].reshape(held * 2, HD) for half in sums]
-    query = [part for half in my_query for part in gather_relative(half, "seq", seq_size)]
-
+    columns = w_query.shape[1] + w_keyval.shape[1]
     smem = pl.BlockSpec(memory_space=pltpu.SMEM)
     vmem = pl.BlockSpec(memory_space=pltpu.VMEM)
-    hbm = pl.BlockSpec(memory_space=pl.ANY)
+    hbm = pl.BlockSpec(memory_space=pltpu.HBM)
+    me = lax.axis_index("seq").reshape(1)
+    part_shape = jax.ShapeDtypeStruct((seq_size // ways, mine, columns), jnp.float32)
+    parts = pl.pallas_call(
+        functools.partial(project_kernel, ways),
+        out_shape=[part_shape] * ways,
+        in_specs=[smem, vmem, hbm, hbm],
+        out_specs=[vmem] * ways,
+        scratch_shapes=[
+            pltpu.VMEM(w_query.shape, jnp.bfloat16),
+            pltpu.VMEM(w_keyval.shape, jnp.bfloat16),
+            pltpu.VMEM((requests, columns), jnp.float32),
+            pltpu.SemaphoreType.DMA((columns // min(512, w_keyval.shape[1]),)),
+        ],
+        compiler_params=pltpu.CompilerParams(vmem_limit_bytes=53 * 2**20),
+        name="project",
+    )(me, hidden_in, w_query, w_keyval)
+    sums, (tables, place_of) = scatter_sum(parts, "seq", seq_size, (tables, place_of))
+    sums = sums.astype(jnp.bfloat16).reshape(held, columns)
+    my_query = sums[:, :wide].reshape(held * heads_local, HD)
+    my_keyval = sums[:, wide:].reshape(held * 2 * kv_local, HD)
+    query = gather_relative(my_query, "seq", seq_size)
+    query, my_keyval = lax.optimization_barrier((query, my_keyval))
+
     chunks = slots // CHUNK
     every_row = requests * heads_local
     block_rows = (mine + 1) * heads_local
     totals = pl.pallas_call(
         functools.partial(attention_kernel, ways),
         out_shape=[jax.ShapeDtypeStruct((seq_size // ways, block_rows, HD), jnp.bfloat16)] * ways,
-        in_specs=[smem] + [vmem] * (2 * ways + 1) + [hbm, hbm],
+        in_specs=[smem] + [vmem] * (ways + 1) + [hbm, hbm],
         out_specs=[vmem] * ways,
         scratch_shapes=[
             pltpu.VMEM((every_row, HD), jnp.bfloat16),
@@ -482,8 +513,8 @@
             pltpu.VMEM((chunks, LANES), jnp.float32),
             pltpu.VMEM((chunks, LANES), jnp.float32),
             pltpu.VMEM((chunks, LANES), jnp.float32),
-            pltpu.VMEM((every_row, HD), jnp.float32),
-            pltpu.VMEM((every_row, HD), jnp.float32),
+            pltpu.VMEM((2, every_row, HD), jnp.float32),
+            pltpu.VMEM((2, every_row, HD), jnp.float32),
             pltpu.SemaphoreType.DMA((chunks,)),
             pltpu.SemaphoreType.DMA((chunks,)),
         ],
@@ -514,15 +545,22 @@
     parts = [totals] + [swap(totals, "seq", seq_size, d << shift) for d in range(1, size)]
     my_context = pl.pallas_call(
         finish_kernel,
-        out_shape=jax.ShapeDtypeStruct((held * heads_local, HD), jnp.bfloat16),
-        in_specs=[vmem] * (size + 4),
+        out_shape=jax.ShapeDtypeStruct((held, wide), jnp.bfloat16),
+        in_specs=[vmem] * (size + 2),
         out_specs=vmem,
+        scratch_shapes=[pltpu.VMEM((held * heads_local, HD), jnp.float32)],
         compiler_params=pltpu.CompilerParams(vmem_limit_bytes=6 * 2**20),
         name="finish",
-    )(*parts, *my_query, *my_keyval).reshape(held, wide)
-    context = gather_in_order(my_context, "seq", seq_size)
-
-    total = jnp.dot(context, w_out, preferred_element_type=jnp.float32)
+    )(*parts, my_query, my_keyval)
+
+    total = pl.pallas_call(
+        functools.partial(output_kernel, ways, seq_size),
+        out_shape=jax.ShapeDtypeStruct((requests, w_out.shape[1]), jnp.float32),
+        in_specs=[smem] + [vmem] * (ways + 1),
+        out_specs=vmem,
+        compiler_params=pltpu.CompilerParams(vmem_limit_bytes=16 * 2**20),
+        name="project_out",
+    )(me, *gather_relative(my_context, "seq", seq_size), w_out)
     step = 1
     while step < head_size:
         if step > 1:

time: 78.6 us -> 72.6 us (0.924)
  starting transfers between devices: 32.4 us -> 23.6 us
  matrix products: 6.49 us -> 0 us
  Pallas kernels: 10.1 us -> 13.9 us
  other arithmetic: 1.29 us -> 3.9 us
  local copies, waits for them, and re-layouts: 1.99 us -> 3.95 us
  waiting for transfers between devices: 25.8 us -> 26.9 us
    ppermute x23 -> x16, starting transfers between devices: 32.4 us -> 23.6 us  [swap(): return lax.ppermute(x, axis, [(j, j ^ mask) for j in range(n)])]
    dot_general x3 -> x0, matrix products: 6.49 us -> none  [the longest x1 3.18 us: body(): part_query = jnp.dot(hidden_in, w_query, preferred_element_type=jnp.float32)]
    pallas_call x1 -> x3, Pallas kernels: 0.42 us -> 4.23 us  [the longest x1 2.9 us: body(): pl.pallas_call(functools.partial(project_kernel, ways), out_shape=[part_s...]
    unnamed x15 -> x5, local copies, waits for them, and re-layouts: 0.14 us -> 1.7 us
    ppermute x23 -> x16, waiting for transfers between devices: 25.8 us -> 26.9 us  [swap(): return lax.ppermute(x, axis, [(j, j ^ mask) for j in range(n)])]
  transfers between devices with their start and end apart: 23 -> 16, of which waited for: 14 -> 14; matrix products, arithmetic and copies ran while one was open for 3% -> 8% of each run, Pallas kernels for 0% -> 0%
where the time goes in v7:
time: 72.6 us; the launch traced here: 72.4 us
  waiting for transfers between devices  26.9 us (37%)
  starting transfers between devices  23.6 us (33%)
  Pallas kernels  13.9 us (19%)
  local copies, waits for them, and re-layouts  3.95 us (5%)
  other arithmetic  3.9 us (5%)
    ppermute x16, waiting for transfers between devices, swap(): return lax.ppermute(x, axis, [(j, j ^ mask) for j in range(n)])  26.9 us
    ppermute x16, starting transfers between devices, swap(): return lax.ppermute(x, axis, [(j, j ^ mask) for j in range(n)])  23.6 us
    pallas_call x1, Pallas kernels, body(): pl.pallas_call(functools.partial(attention_kernel, ways), out_shape=[jax....  9.26 us
    pallas_call x1, Pallas kernels, body(): pl.pallas_call(functools.partial(project_kernel, ways), out_shape=[part_s...  2.9 us
    unnamed x5, local copies, waits for them, and re-layouts  1.7 us
  transfers between devices with their start and end apart: 16, of which 14 were waited for; matrix products, arithmetic and copies ran while one was open for 8% of the time, Pallas kernels for 0%

profile of v7, /device:TPU:0, one launch (start us, length us, event | category | flops | bytes accessed | tf_op | source)
XLA Modules:
  0.0 72.4 jit_solution(18395074533679482458)
XLA Ops:
  0.0 0.9 %copy-done.1 = bf16[64,1024]{1,0:T(8,128)(2,1)S(1)} copy-done((bf16[64,1024]{1,0:T(8,128)(2,1)S(1)}, bf16[64,1024]{1,0:T(8,128)(2,1)}, u32[]{:S(2)}) %copy-start.1) | copy-done | bytes 131096
  0.9 2.9 %project.1 = (f32[2,8,2560]{2,1,0:T(8,128)S(1)}, f32[2,8,2560]{2,1,0:T(8,128)S(1)}, f32[2,8,2560]{2,1,0:T(8,128)S(1)}, f32[2,8,2560]{2,1,0:T(8,128)S(1)}) custom-call(s32[1]{0:T(128)} %bitcast.me, bf16[64,1024]{1,0:T(8,128)(2,1)S(1)} %copy-done.1, bf16[1024,2048]{1,0:T(8,128)(2,1)} %w_query.1, bf16[1024,512]{1,0:T(8,128)(2,1)} %w_keyval.1), custom_call_target="tpu_custom_call" | custom-call | tf_op jit(solution)/shard_map/project/pallas_call | solution.py:477
  3.8 3.0 %collective-permute-start = (f32[2,8,2560]{2,1,0:T(8,128)S(1)}, f32[2,8,2560]{2,1,0:T(8,128)S(1)}, u32[]{:S(2)}, u32[]{:S(2)}) collective-permute-start(f32[2,8,2560]{2,1,0:T(8,128)S(1)} %get-tuple-element.23), channel_id=1, source_target_pairs={{0,4},{4,0},{8,12},{12,8},{16,20},{20,16},{24,28},{28,24},{1,5},{5... | collective-permute-start | bytes 491528 | tf_op jit(solution)/shard_map/ppermute | solution.py:22
  6.8 1.6 %collective-permute-start.1 = (f32[2,8,2560]{2,1,0:T(8,128)S(1)}, f32[2,8,2560]{2,1,0:T(8,128)S(1)}, u32[]{:S(2)}, u32[]{:S(2)}) collective-permute-start(f32[2,8,2560]{2,1,0:T(8,128)S(1)} %get-tuple-element.24), channel_id=1, source_target_pairs={{0,8},{4,12},{8,0},{12,4},{16,24},{20,28},{24,16},{28,20},{1,9},{5... | collective-permute-start | bytes 491528 | tf_op jit(solution)/shard_map/ppermute | solution.py:22
  14.5 1.3 %collective-permute-done.2 = f32[2,8,2560]{2,1,0:T(8,128)S(1)} collective-permute-done((f32[2,8,2560]{2,1,0:T(8,128)S(1)}, f32[2,8,2560]{2,1,0:T(8,128)S(1)}, u32[]{:S(2)}, u32[]{:S(2)}) %collective-permute-start.2) | collective-permute-done | bytes 163872 | tf_op jit(solution)/shard_map/ppermute | solution.py:22
  15.9 2.8 %collective-permute-start.3 = (f32[2,8,2560]{2,1,0:T(8,128)S(1)}, f32[2,8,2560]{2,1,0:T(8,128)S(1)}, u32[]{:S(2)}, u32[]{:S(2)}) collective-permute-start(f32[2,8,2560]{2,1,0:T(8,128)S(1)} %add_add_fusion), channel_id=1, source_target_pairs={{0,16},{4,20},{8,24},{12,28},{16,0},{20,4},{24,8},{28,12},{1,17},{... | collective-permute-start | bytes 491528 | tf_op jit(solution)/shard_map/ppermute | solution.py:22
  18.7 6.8 %collective-permute-done.3 = f32[2,8,2560]{2,1,0:T(8,128)S(1)} collective-permute-done((f32[2,8,2560]{2,1,0:T(8,128)S(1)}, f32[2,8,2560]{2,1,0:T(8,128)S(1)}, u32[]{:S(2)}, u32[]{:S(2)}) %collective-permute-start.3) | collective-permute-done | bytes 163872 | tf_op jit(solution)/shard_map/ppermute | solution.py:22
  25.6 1.4 %collective-permute-start.6 = (bf16[256,128]{1,0:T(8,128)(2,1)S(1)}, bf16[256,128]{1,0:T(8,128)(2,1)S(1)}, u32[]{:S(2)}, u32[]{:S(2)}) collective-permute-start(bf16[256,128]{1,0:T(8,128)(2,1)S(1)} %reshape.59.refs_0_.refs_2_), channel_id=1, source_target_pairs={{0,12},{4,8},{8,4},{12,0},{16,28},{20,24},{24,20},{28,16},{1,13},{... | collective-permute-start | bytes 196616 | tf_op jit(solution)/shard_map/ppermute | solution.py:22
  27.0 1.4 %collective-permute-start.5 = (bf16[256,128]{1,0:T(8,128)(2,1)S(1)}, bf16[256,128]{1,0:T(8,128)(2,1)S(1)}, u32[]{:S(2)}, u32[]{:S(2)}) collective-permute-start(bf16[256,128]{1,0:T(8,128)(2,1)S(1)} %reshape.59.refs_0_.refs_2_), channel_id=1, source_target_pairs={{0,8},{4,12},{8,0},{12,4},{16,24},{20,28},{24,16},{28,20},{1,9},{5... | collective-permute-start | bytes 196616 | tf_op jit(solution)/shard_map/ppermute | solution.py:22
  29.2 1.6 %collective-permute-done.6.refs_3_ = bf16[256,128]{1,0:T(8,128)(2,1)S(1)} collective-permute-done((bf16[256,128]{1,0:T(8,128)(2,1)S(1)}, bf16[256,128]{1,0:T(8,128)(2,1)S(1)}, u32[]{:S(2)}, u32[]{:S(2)}) %collective-permute-start.6) | collective-permute-done | bytes 65568 | tf_op jit(solution)/shard_map/ppermute | solution.py:22
  31.3 1.3 %collective-permute-done.4.refs_1_ = bf16[256,128]{1,0:T(8,128)(2,1)S(1)} collective-permute-done((bf16[256,128]{1,0:T(8,128)(2,1)S(1)}, bf16[256,128]{1,0:T(8,128)(2,1)S(1)}, u32[]{:S(2)}, u32[]{:S(2)}) %collective-permute-start.4) | collective-permute-done | bytes 65568 | tf_op jit(solution)/shard_map/ppermute | solution.py:22
  32.6 9.3 %paged_attention.1 = (bf16[2,144,128]{2,1,0:T(8,128)(2,1)S(1)}, bf16[2,144,128]{2,1,0:T(8,128)(2,1)S(1)}, bf16[2,144,128]{2,1,0:T(8,128)(2,1)S(1)}, bf16[2,144,128]{2,1,0:T(8,128)(2,1)S(1)}) custom-call(s32[128]{0:T(128)S(1)} %get-tuple-element.26.place_of, bf16[256,128]{1,0:T(8,128)(2,1)S(1)} %reshape.59.refs_0_.refs_2_, ...), custom_call_target="tpu_custom_call" | custom-call | flops 134217728 | bytes 16777216 | tf_op jit(solution)/shard_map/paged_attention/pallas_call | solution.py:501
  43.3 2.2 %collective-permute-start.9 = (bf16[2,144,128]{2,1,0:T(8,128)(2,1)S(1)}, bf16[2,144,128]{2,1,0:T(8,128)(2,1)S(1)}, u32[]{:S(2)}, u32[]{:S(2)}) collective-permute-start(bf16[2,144,128]{2,1,0:T(8,128)(2,1)S(1)} %get-tuple-element.39), channel_id=1, source_target_pairs={{0,12},{4,8},{8,4},{12,0},{16,28},{20,24},{24,20},{28,16},{1,13},{... | collective-permute-start | bytes 221192 | tf_op jit(solution)/shard_map/ppermute | solution.py:22
  45.5 0.9 %collective-permute-done.7.refs_1_ = bf16[2,144,128]{2,1,0:T(8,128)(2,1)S(1)} collective-permute-done((bf16[2,144,128]{2,1,0:T(8,128)(2,1)S(1)}, bf16[2,144,128]{2,1,0:T(8,128)(2,1)S(1)}, u32[]{:S(2)}, u32[]{:S(2)}) %collective-permute-start.7) | collective-permute-done | bytes 73760 | tf_op jit(solution)/shard_map/ppermute | solution.py:22
  47.1 1.5 %collective-permute-done.9.refs_3_ = bf16[2,144,128]{2,1,0:T(8,128)(2,1)S(1)} collective-permute-done((bf16[2,144,128]{2,1,0:T(8,128)(2,1)S(1)}, bf16[2,144,128]{2,1,0:T(8,128)(2,1)S(1)}, u32[]{:S(2)}, u32[]{:S(2)}) %collective-permute-start.9) | collective-permute-done | bytes 73760 | tf_op jit(solution)/shard_map/ppermute | solution.py:22
  49.0 3.9 %collective-permute-start.10 = (bf16[2,144,128]{2,1,0:T(8,128)(2,1)S(1)}, bf16[2,144,128]{2,1,0:T(8,128)(2,1)S(1)}, u32[]{:S(2)}, u32[]{:S(2)}) collective-permute-start(bf16[2,144,128]{2,1,0:T(8,128)(2,1)S(1)} %combine.1.refs_0_), channel_id=1, source_target_pairs={{0,16},{4,20},{8,24},{12,28},{16,0},{20,4},{24,8},{28,12},{1,17},{... | collective-permute-start | bytes 221192 | tf_op jit(solution)/shard_map/ppermute | solution.py:22
  52.9 3.1 %collective-permute-done.10.refs_1_ = bf16[2,144,128]{2,1,0:T(8,128)(2,1)S(1)} collective-permute-done((bf16[2,144,128]{2,1,0:T(8,128)(2,1)S(1)}, bf16[2,144,128]{2,1,0:T(8,128)(2,1)S(1)}, u32[]{:S(2)}, u32[]{:S(2)}) %collective-permute-start.10) | collective-permute-done | bytes 73760 | tf_op jit(solution)/shard_map/ppermute | solution.py:22
  57.1 2.2 %collective-permute-start.12 = (bf16[16,2048]{1,0:T(8,128)(2,1)S(1)}, bf16[16,2048]{1,0:T(8,128)(2,1)S(1)}, u32[]{:S(2)}, u32[]{:S(2)}) collective-permute-start(bf16[16,2048]{1,0:T(8,128)(2,1)S(1)} %finish.1.refs_0_), channel_id=1, source_target_pairs={{0,8},{4,12},{8,0},{12,4},{16,24},{20,28},{24,16},{28,20},{1,9},{5... | collective-permute-start | bytes 196616 | tf_op jit(solution)/shard_map/ppermute | solution.py:22
  60.1 1.7 %collective-permute-done.13.refs_3_ = bf16[16,2048]{1,0:T(8,128)(2,1)S(1)} collective-permute-done((bf16[16,2048]{1,0:T(8,128)(2,1)S(1)}, bf16[16,2048]{1,0:T(8,128)(2,1)S(1)}, u32[]{:S(2)}, u32[]{:S(2)}) %collective-permute-start.13) | collective-permute-done | bytes 65568 | tf_op jit(solution)/shard_map/ppermute | solution.py:22
  62.3 1.3 %collective-permute-done.11.refs_1_ = bf16[16,2048]{1,0:T(8,128)(2,1)S(1)} collective-permute-done((bf16[16,2048]{1,0:T(8,128)(2,1)S(1)}, bf16[16,2048]{1,0:T(8,128)(2,1)S(1)}, u32[]{:S(2)}, u32[]{:S(2)}) %collective-permute-start.11) | collective-permute-done | bytes 65568 | tf_op jit(solution)/shard_map/ppermute | solution.py:22
  63.6 0.8 %project_out.1 = f32[64,1024]{1,0:T(8,128)S(1)} custom-call(s32[1]{0:T(128)} %bitcast.me, bf16[16,2048]{1,0:T(8,128)(2,1)S(1)} %finish.1.refs_0_, bf16[16,2048]{1,0:T(8,128)(2,1)S(1)} %collective-permute-done.11.refs_1_, bf16[16,2048]{1,0:T(8,128)(2,1)S(1)} %collective-permute-done.12.refs_2_, bf16[16,2048]{1,0:T(8,128)(2,1)S(1)} %collective-permute-done.13.refs_3_, ...), custom_call_target="tpu_custom_call" | custom-call | tf_op jit(solution)/shard_map/project_out/pallas_call | solution.py:556
  64.5 1.5 %collective-permute-done.14 = f32[64,1024]{1,0:T(8,128)S(1)} collective-permute-done((f32[64,1024]{1,0:T(8,128)S(1)}, f32[64,1024]{1,0:T(8,128)S(1)}, u32[]{:S(2)}, u32[]{:S(2)}) %collective-permute-start.14) | collective-permute-done | bytes 262176 | tf_op jit(solution)/shard_map/ppermute | solution.py:22
  66.1 1.6 %collective-permute-start.15 = (bf16[64,1024]{1,0:T(8,128)(2,1)S(1)}, bf16[64,1024]{1,0:T(8,128)(2,1)S(1)}, u32[]{:S(2)}, u32[]{:S(2)}) collective-permute-start(bf16[64,1024]{1,0:T(8,128)(2,1)S(1)} %fusion), channel_id=1, source_target_pairs={{0,2},{1,3},{2,0},{3,1},{4,6},{5,7},{6,4},{7,5},{8,10},{9,11},{10,... | collective-permute-start | bytes 393224 | tf_op jit(solution)/shard_map/ppermute | solution.py:22
  67.7 4.0 %collective-permute-done.15 = bf16[64,1024]{1,0:T(8,128)(2,1)S(1)} collective-permute-done((bf16[64,1024]{1,0:T(8,128)(2,1)S(1)}, bf16[64,1024]{1,0:T(8,128)(2,1)S(1)}, u32[]{:S(2)}, u32[]{:S(2)}) %collective-permute-start.15) | collective-permute-done | bytes 131104 | tf_op jit(solution)/shard_map/ppermute | solution.py:22
  (47 shorter events, 13.2 us)
Async XLA Ops:
  0.0 0.9 %copy-start.1 = (bf16[64,1024]{1,0:T(8,128)(2,1)S(1)}, bf16[64,1024]{1,0:T(8,128)(2,1)}, u32[]{:S(2)}) copy-start(bf16[64,1024]{1,0:T(8,128)(2,1)} %hidden.1) | copy-start | bytes 393220
  3.8 10.7 %collective-permute-start = (f32[2,8,2560]{2,1,0:T(8,128)S(1)}, f32[2,8,2560]{2,1,0:T(8,128)S(1)}, u32[]{:S(2)}, u32[]{:S(2)}) collective-permute-start(f32[2,8,2560]{2,1,0:T(8,128)S(1)} %get-tuple-element.23), channel_id=1, source_target_pairs={{0,4},{4,0},{8,12},{12,8},{16,20},{20,16},{24,28},{28,24},{1,5},{5... | collective-permute-start | bytes 491528 | tf_op jit(solution)/shard_map/ppermute | solution.py:22
  6.8 7.7 %collective-permute-start.1 = (f32[2,8,2560]{2,1,0:T(8,128)S(1)}, f32[2,8,2560]{2,1,0:T(8,128)S(1)}, u32[]{:S(2)}, u32[]{:S(2)}) collective-permute-start(f32[2,8,2560]{2,1,0:T(8,128)S(1)} %get-tuple-element.24), channel_id=1, source_target_pairs={{0,8},{4,12},{8,0},{12,4},{16,24},{20,28},{24,16},{28,20},{1,9},{5... | collective-permute-start | bytes 491528 | tf_op jit(solution)/shard_map/ppermute | solution.py:22
  8.4 7.4 %collective-permute-start.2 = (f32[2,8,2560]{2,1,0:T(8,128)S(1)}, f32[2,8,2560]{2,1,0:T(8,128)S(1)}, u32[]{:S(2)}, u32[]{:S(2)}) collective-permute-start(f32[2,8,2560]{2,1,0:T(8,128)S(1)} %get-tuple-element.25), channel_id=1, source_target_pairs={{0,12},{4,8},{8,4},{12,0},{16,28},{20,24},{24,20},{28,16},{1,13},{... | collective-permute-start | bytes 491528 | tf_op jit(solution)/shard_map/ppermute | solution.py:22
  15.9 9.6 %collective-permute-start.3 = (f32[2,8,2560]{2,1,0:T(8,128)S(1)}, f32[2,8,2560]{2,1,0:T(8,128)S(1)}, u32[]{:S(2)}, u32[]{:S(2)}) collective-permute-start(f32[2,8,2560]{2,1,0:T(8,128)S(1)} %add_add_fusion), channel_id=1, source_target_pairs={{0,16},{4,20},{8,24},{12,28},{16,0},{20,4},{24,8},{28,12},{1,17},{... | collective-permute-start | bytes 491528 | tf_op jit(solution)/shard_map/ppermute | solution.py:22
  25.6 5.2 %collective-permute-start.6 = (bf16[256,128]{1,0:T(8,128)(2,1)S(1)}, bf16[256,128]{1,0:T(8,128)(2,1)S(1)}, u32[]{:S(2)}, u32[]{:S(2)}) collective-permute-start(bf16[256,128]{1,0:T(8,128)(2,1)S(1)} %reshape.59.refs_0_.refs_2_), channel_id=1, source_target_pairs={{0,12},{4,8},{8,4},{12,0},{16,28},{20,24},{24,20},{28,16},{1,13},{... | collective-permute-start | bytes 196616 | tf_op jit(solution)/shard_map/ppermute | solution.py:22
  27.0 4.3 %collective-permute-start.5 = (bf16[256,128]{1,0:T(8,128)(2,1)S(1)}, bf16[256,128]{1,0:T(8,128)(2,1)S(1)}, u32[]{:S(2)}, u32[]{:S(2)}) collective-permute-start(bf16[256,128]{1,0:T(8,128)(2,1)S(1)} %reshape.59.refs_0_.refs_2_), channel_id=1, source_target_pairs={{0,8},{4,12},{8,0},{12,4},{16,24},{20,28},{24,16},{28,20},{1,9},{5... | collective-permute-start | bytes 196616 | tf_op jit(solution)/shard_map/ppermute | solution.py:22
  28.4 4.3 %collective-permute-start.4 = (bf16[256,128]{1,0:T(8,128)(2,1)S(1)}, bf16[256,128]{1,0:T(8,128)(2,1)S(1)}, u32[]{:S(2)}, u32[]{:S(2)}) collective-permute-start(bf16[256,128]{1,0:T(8,128)(2,1)S(1)} %reshape.59.refs_0_.refs_2_), channel_id=1, source_target_pairs={{0,4},{4,0},{8,12},{12,8},{16,20},{20,16},{24,28},{28,24},{1,5},{5... | collective-permute-start | bytes 196616 | tf_op jit(solution)/shard_map/ppermute | solution.py:22
  29.1 34.5 %copy-start = (bf16[2048,1024]{1,0:T(8,128)(2,1)S(1)}, bf16[2048,1024]{1,0:T(8,128)(2,1)}, u32[]{:S(2)}) copy-start(bf16[2048,1024]{1,0:T(8,128)(2,1)} %refs_4_.1) | copy-start | bytes 12582916
  41.9 4.4 %collective-permute-start.7 = (bf16[2,144,128]{2,1,0:T(8,128)(2,1)S(1)}, bf16[2,144,128]{2,1,0:T(8,128)(2,1)S(1)}, u32[]{:S(2)}, u32[]{:S(2)}) collective-permute-start(bf16[2,144,128]{2,1,0:T(8,128)(2,1)S(1)} %get-tuple-element.37), channel_id=1, source_target_pairs={{0,4},{4,0},{8,12},{12,8},{16,20},{20,16},{24,28},{28,24},{1,5},{5... | collective-permute-start | bytes 221192 | tf_op jit(solution)/shard_map/ppermute | solution.py:22
  42.7 4.4 %collective-permute-start.8 = (bf16[2,144,128]{2,1,0:T(8,128)(2,1)S(1)}, bf16[2,144,128]{2,1,0:T(8,128)(2,1)S(1)}, u32[]{:S(2)}, u32[]{:S(2)}) collective-permute-start(bf16[2,144,128]{2,1,0:T(8,128)(2,1)S(1)} %get-tuple-element.38), channel_id=1, source_target_pairs={{0,8},{4,12},{8,0},{12,4},{16,24},{20,28},{24,16},{28,20},{1,9},{5... | collective-permute-start | bytes 221192 | tf_op jit(solution)/shard_map/ppermute | solution.py:22
  43.3 5.3 %collective-permute-start.9 = (bf16[2,144,128]{2,1,0:T(8,128)(2,1)S(1)}, bf16[2,144,128]{2,1,0:T(8,128)(2,1)S(1)}, u32[]{:S(2)}, u32[]{:S(2)}) collective-permute-start(bf16[2,144,128]{2,1,0:T(8,128)(2,1)S(1)} %get-tuple-element.39), channel_id=1, source_target_pairs={{0,12},{4,8},{8,4},{12,0},{16,28},{20,24},{24,20},{28,16},{1,13},{... | collective-permute-start | bytes 221192 | tf_op jit(solution)/shard_map/ppermute | solution.py:22
  49.0 7.0 %collective-permute-start.10 = (bf16[2,144,128]{2,1,0:T(8,128)(2,1)S(1)}, bf16[2,144,128]{2,1,0:T(8,128)(2,1)S(1)}, u32[]{:S(2)}, u32[]{:S(2)}) collective-permute-start(bf16[2,144,128]{2,1,0:T(8,128)(2,1)S(1)} %combine.1.refs_0_), channel_id=1, source_target_pairs={{0,16},{4,20},{8,24},{12,28},{16,0},{20,4},{24,8},{28,12},{1,17},{... | collective-permute-start | bytes 221192 | tf_op jit(solution)/shard_map/ppermute | solution.py:22
  56.5 5.2 %collective-permute-start.13 = (bf16[16,2048]{1,0:T(8,128)(2,1)S(1)}, bf16[16,2048]{1,0:T(8,128)(2,1)S(1)}, u32[]{:S(2)}, u32[]{:S(2)}) collective-permute-start(bf16[16,2048]{1,0:T(8,128)(2,1)S(1)} %finish.1.refs_0_), channel_id=1, source_target_pairs={{0,12},{4,8},{8,4},{12,0},{16,28},{20,24},{24,20},{28,16},{1,13},{... | collective-permute-start | bytes 196616 | tf_op jit(solution)/shard_map/ppermute | solution.py:22
  57.1 5.2 %collective-permute-start.12 = (bf16[16,2048]{1,0:T(8,128)(2,1)S(1)}, bf16[16,2048]{1,0:T(8,128)(2,1)S(1)}, u32[]{:S(2)}, u32[]{:S(2)}) collective-permute-start(bf16[16,2048]{1,0:T(8,128)(2,1)S(1)} %finish.1.refs_0_), channel_id=1, source_target_pairs={{0,8},{4,12},{8,0},{12,4},{16,24},{20,28},{24,16},{28,20},{1,9},{5... | collective-permute-start | bytes 196616 | tf_op jit(solution)/shard_map/ppermute | solution.py:22
  59.3 4.3 %collective-permute-start.11 = (bf16[16,2048]{1,0:T(8,128)(2,1)S(1)}, bf16[16,2048]{1,0:T(8,128)(2,1)S(1)}, u32[]{:S(2)}, u32[]{:S(2)}) collective-permute-start(bf16[16,2048]{1,0:T(8,128)(2,1)S(1)} %finish.1.refs_0_), channel_id=1, source_target_pairs={{0,4},{4,0},{8,12},{12,8},{16,20},{20,16},{24,28},{28,24},{1,5},{5... | collective-permute-start | bytes 196616 | tf_op jit(solution)/shard_map/ppermute | solution.py:22
  64.5 1.6 %collective-permute-start.14 = (f32[64,1024]{1,0:T(8,128)S(1)}, f32[64,1024]{1,0:T(8,128)S(1)}, u32[]{:S(2)}, u32[]{:S(2)}) collective-permute-start(f32[64,1024]{1,0:T(8,128)S(1)} %project_out.1), channel_id=1, source_target_pairs={{0,1},{1,0},{2,3},{3,2},{4,5},{5,4},{6,7},{7,6},{8,9},{9,8},{10,11... | collective-permute-start | bytes 786440 | tf_op jit(solution)/shard_map/ppermute | solution.py:22
  66.1 5.6 %collective-permute-start.15 = (bf16[64,1024]{1,0:T(8,128)(2,1)S(1)}, bf16[64,1024]{1,0:T(8,128)(2,1)S(1)}, u32[]{:S(2)}, u32[]{:S(2)}) collective-permute-start(bf16[64,1024]{1,0:T(8,128)(2,1)S(1)} %fusion), channel_id=1, source_target_pairs={{0,2},{1,3},{2,0},{3,1},{4,6},{5,7},{6,4},{7,5},{8,10},{9,11},{10,... | collective-permute-start | bytes 393224 | tf_op jit(solution)/shard_map/ppermute | solution.py:22

commit v8 on v7

--- a/solution.py
+++ b/solution.py
@@ -45,7 +45,7 @@
     return lax.dynamic_index_in_dim(x, digit ^ offset, axis=1, keepdims=False)
 
 
-def scatter_sum(parts, axis, n, beside):
+def scatter_terms(parts, axis, n, beside):
     for shift, size in lower_groups(n):
         if shift:
             parts = [pick_digit(x, axis, shift, size, d) for d in range(size)]
@@ -54,7 +54,7 @@
             sent, beside = lax.optimization_barrier((sent, beside))
         x = sum(sent, parts[0])
     shift, size = last_group(n)
-    return sum([swap(x, axis, n, d << shift) for d in range(1, size)], x), beside
+    return [x] + [swap(x, axis, n, d << shift) for d in range(1, size)], beside
 
 
 def gather_relative(x, axis, n):
@@ -86,26 +86,28 @@
 
 def project_kernel(ways, me, hidden, w_query, w_keyval, *refs):
     outs, (query, keyval, result, sem) = refs[:ways], refs[ways:]
-    tile = min(512, w_keyval.shape[1])
-    jobs = [
-        (ref, held, col, base + col)
-        for ref, held, base in ((w_query, query, 0), (w_keyval, keyval, w_query.shape[1]))
-        for col in range(0, ref.shape[1], tile)
+    depth = w_query.shape[0]
+    tile = min(256, depth)
+    wide = w_query.shape[1]
+    copies = [
+        [
+            pltpu.make_async_copy(
+                ref.at[pl.ds(row, tile)], held.at[pl.ds(row, tile)], sem.at[which, row // tile]
+            )
+            for which, (ref, held) in enumerate(((w_query, query), (w_keyval, keyval)))
+        ]
+        for row in range(0, depth, tile)
     ]
-    copies = [
-        pltpu.make_async_copy(
-            ref.at[:, pl.ds(col, tile)], held.at[:, pl.ds(col, tile)], sem.at[i]
-        )
-        for i, (ref, held, col, _) in enumerate(jobs)
-    ]
-    for copy in copies:
-        copy.start()
-    rows = hidden[...]
-    for copy, (_, held, col, place) in zip(copies, jobs):
-        copy.wait()
-        result[:, place : place + tile] = jnp.dot(
-            rows, held[:, col : col + tile], preferred_element_type=jnp.float32
-        )
+    for pair in copies:
+        for copy in pair:
+            copy.start()
+    for row, pair in zip(range(0, depth, tile), copies):
+        here = slice(row, row + tile)
+        rows = hidden[:, here]
+        for copy, held, place in zip(pair, (query, keyval), (slice(0, wide), slice(wide, None))):
+            copy.wait()
+            part = jnp.dot(rows, held[here, :], preferred_element_type=jnp.float32)
+            result[:, place] = result[:, place] + part if row else part
     digit = me[0] & (ways - 1)
     for d, out in enumerate(outs):
         blocks, mine, _ = out.shape
@@ -139,6 +141,22 @@
         out[place * mine : (place + 1) * mine, :] = chosen
 
 
+def join_kernel(*refs):
+    *parts, query, keyval, query_rows, keyval_rows = refs
+    blocks, mine, columns = parts[0].shape
+    held = blocks * mine
+    whole = functools.reduce(jnp.add, [part[...] for part in parts]).reshape(held, columns)
+    heads = query.shape[0] // held
+    others = keyval.shape[0] // held
+    for h in range(heads):
+        query_rows[pl.ds(h, held, stride=heads), :] = whole[:, h * HD : (h + 1) * HD]
+    for h in range(others):
+        place = (heads + h) * HD
+        keyval_rows[pl.ds(h, held, stride=others), :] = whole[:, place : place + HD]
+    query[...] = query_rows[...].astype(jnp.bfloat16)
+    keyval[...] = keyval_rows[...].astype(jnp.bfloat16)
+
+
 def split_stat(stat, lane):
     hi = stat.astype(jnp.bfloat16).astype(jnp.float32)
     rest = stat - hi
@@ -156,13 +174,11 @@
 
 def attention_kernel(ways, place_of, *refs):
     queries, refs = refs[:ways], refs[ways:]
-    (tables, key_cache, value_cache), refs = refs[:3], refs[3:]
+    (tables, keys, values), refs = refs[:3], refs[3:]
     outs, refs = refs[:ways], refs[ways:]
     (
         query_low,
         query_high,
-        keys,
-        values,
         probs,
         page_out,
         page_sum,
@@ -170,30 +186,14 @@
         dev_max,
         total_out,
         total_stat,
-        key_sem,
-        value_sem,
     ) = refs
-    slots = key_cache.shape[0]
+    slots = keys.shape[0]
     heads = LANES // CHUNK
     group = heads // 2
     chunks = slots // CHUNK
     blocks, block_rows, _ = outs[0].shape
     mine = block_rows // heads - 1
     step_chunks = 4
-
-    def key_copy(c):
-        part = pl.ds(c * CHUNK, CHUNK)
-        return pltpu.make_async_copy(key_cache.at[part], keys.at[part], key_sem.at[c])
-
-    def value_copy(c):
-        part = pl.ds(c * CHUNK, CHUNK)
-        return pltpu.make_async_copy(value_cache.at[part], values.at[part], value_sem.at[c])
-
-    for c in range(chunks + step_chunks):
-        if c >= step_chunks:
-            value_copy(c - step_chunks).start()
-        if c < chunks:
-            key_copy(c).start()
 
     for d, part in enumerate(queries):
         rows = part[...]
@@ -265,21 +265,15 @@
             )
 
     for c in range(step_chunks):
-        key_copy(c).wait()
         score_chunk(c)
 
     @pl.loop(1, chunks // step_chunks)
     def _(step):
         first = step * step_chunks
         for c in range(step_chunks):
-            key_copy(first + c).wait()
-            value_copy(first + c - step_chunks).wait()
-        for c in range(step_chunks):
             value_chunk(first + c - step_chunks)
             score_chunk(first + c)
 
-    for c in range(chunks - step_chunks, chunks):
-        value_copy(c).wait()
     for c in range(chunks - step_chunks, chunks):
         value_chunk(c)
 
@@ -483,17 +477,28 @@
             pltpu.VMEM(w_query.shape, jnp.bfloat16),
             pltpu.VMEM(w_keyval.shape, jnp.bfloat16),
             pltpu.VMEM((requests, columns), jnp.float32),
-            pltpu.SemaphoreType.DMA((columns // min(512, w_keyval.shape[1]),)),
+            pltpu.SemaphoreType.DMA((2, pl.cdiv(w_query.shape[0], 256))),
         ],
         compiler_params=pltpu.CompilerParams(vmem_limit_bytes=53 * 2**20),
         name="project",
     )(me, hidden_in, w_query, w_keyval)
-    sums, (tables, place_of) = scatter_sum(parts, "seq", seq_size, (tables, place_of))
-    sums = sums.astype(jnp.bfloat16).reshape(held, columns)
-    my_query = sums[:, :wide].reshape(held * heads_local, HD)
-    my_keyval = sums[:, wide:].reshape(held * 2 * kv_local, HD)
+    terms, (tables, place_of) = scatter_terms(parts, "seq", seq_size, (tables, place_of))
+    row_shapes = [(held * heads_local, HD), (held * 2 * kv_local, HD)]
+    my_query, my_keyval = pl.pallas_call(
+        join_kernel,
+        out_shape=[jax.ShapeDtypeStruct(shape, jnp.bfloat16) for shape in row_shapes],
+        in_specs=[vmem] * len(terms),
+        out_specs=[vmem] * 2,
+        scratch_shapes=[pltpu.VMEM(shape, jnp.float32) for shape in row_shapes],
+        compiler_params=pltpu.CompilerParams(vmem_limit_bytes=6 * 2**20),
+        cost_estimate=pl.CostEstimate(
+            flops=10**10,
+            bytes_accessed=10**7,
+            transcendentals=0,
+        ),
+        name="join",
+    )(*terms)
     query = gather_relative(my_query, "seq", seq_size)
-    query, my_keyval = lax.optimization_barrier((query, my_keyval))
 
     chunks = slots // CHUNK
     every_row = requests * heads_local
@@ -501,13 +506,11 @@
     totals = pl.pallas_call(
         functools.partial(attention_kernel, ways),
         out_shape=[jax.ShapeDtypeStruct((seq_size // ways, block_rows, HD), jnp.bfloat16)] * ways,
-        in_specs=[smem] + [vmem] * (ways + 1) + [hbm, hbm],
+        in_specs=[smem] + [vmem] * (ways + 3),
         out_specs=[vmem] * ways,
         scratch_shapes=[
             pltpu.VMEM((every_row, HD), jnp.bfloat16),
             pltpu.VMEM((every_row, HD), jnp.bfloat16),
-            pltpu.VMEM(key_cache.shape, jnp.bfloat16),
-            pltpu.VMEM(value_cache.shape, jnp.bfloat16),
             pltpu.VMEM((chunks, LANES, PAGE), jnp.bfloat16),
             pltpu.VMEM((slots * heads_local, HD), jnp.float32),
             pltpu.VMEM((chunks, LANES), jnp.float32),
@@ -515,10 +518,8 @@
             pltpu.VMEM((chunks, LANES), jnp.float32),
             pltpu.VMEM((2, every_row, HD), jnp.float32),
             pltpu.VMEM((2, every_row, HD), jnp.float32),
-            pltpu.SemaphoreType.DMA((chunks,)),
-            pltpu.SemaphoreType.DMA((chunks,)),
         ],
-        compiler_params=pltpu.CompilerParams(vmem_limit_bytes=48 * 2**20),
+        compiler_params=pltpu.CompilerParams(vmem_limit_bytes=24 * 2**20),
         cost_estimate=pl.CostEstimate(
             flops=4 * slots * PAGE * wide,
             bytes_accessed=2 * (key_cache.size + value_cache.size),

time: 72.6 us -> 70.2 us (0.967)
  Pallas kernels: 13.9 us -> 11.6 us
    pallas_call x1, Pallas kernels: 9.26 us -> 6.77 us  [body(): pl.pallas_call(functools.partial(attention_kernel, ways), out_shape=[jax....]
    unnamed x5 -> x13, local copies, waits for them, and re-layouts: 1.7 us -> 1.72 us
  transfers between devices with their start and end apart: 16 -> 16, of which waited for: 14 -> 14; matrix products, arithmetic and copies ran while one was open for 8% -> 9% of each run, Pallas kernels for 0% -> 0%
where the time goes in v8:
time: 70.2 us; the launch traced here: 70 us
  waiting for transfers between devices  26.9 us (38%)
  starting transfers between devices  23.6 us (34%)
  Pallas kernels  11.6 us (17%)
  local copies, waits for them, and re-layouts  3.9 us (6%)
  other arithmetic  3.88 us (6%)
    ppermute x16, waiting for transfers between devices, swap(): return lax.ppermute(x, axis, [(j, j ^ mask) for j in range(n)])  26.9 us
    ppermute x16, starting transfers between devices, swap(): return lax.ppermute(x, axis, [(j, j ^ mask) for j in range(n)])  23.6 us
    pallas_call x1, Pallas kernels, body(): pl.pallas_call(functools.partial(attention_kernel, ways), out_shape=[jax....  6.77 us
    pallas_call x1, Pallas kernels, body(): pl.pallas_call(functools.partial(project_kernel, ways), out_shape=[part_s...  2.98 us
    unnamed x13, local copies, waits for them, and re-layouts  1.72 us
  transfers between devices with their start and end apart: 16, of which 14 were waited for; matrix products, arithmetic and copies ran while one was open for 9% of the time, Pallas kernels for 0%

profile of v8, /device:TPU:0, one launch (start us, length us, event | category | flops | bytes accessed | tf_op | source)
XLA Modules:
  0.0 70.0 jit_solution(2997692932772055194)
XLA Ops:
  0.0 0.9 %copy-done.1 = bf16[64,1024]{1,0:T(8,128)(2,1)S(1)} copy-done((bf16[64,1024]{1,0:T(8,128)(2,1)S(1)}, bf16[64,1024]{1,0:T(8,128)(2,1)}, u32[]{:S(2)}) %copy-start.1) | copy-done | bytes 131096
  0.9 3.0 %project.1 = (f32[2,8,2560]{2,1,0:T(8,128)S(1)}, f32[2,8,2560]{2,1,0:T(8,128)S(1)}, f32[2,8,2560]{2,1,0:T(8,128)S(1)}, f32[2,8,2560]{2,1,0:T(8,128)S(1)}) custom-call(s32[1]{0:T(128)} %bitcast.me, bf16[64,1024]{1,0:T(8,128)(2,1)S(1)} %copy-done.1, bf16[1024,2048]{1,0:T(8,128)(2,1)} %w_query.1, bf16[1024,512]{1,0:T(8,128)(2,1)} %w_keyval.1), custom_call_target="tpu_custom_call" | custom-call | tf_op jit(solution)/shard_map/project/pallas_call | solution.py:471
  3.9 3.0 %collective-permute-start = (f32[2,8,2560]{2,1,0:T(8,128)S(1)}, f32[2,8,2560]{2,1,0:T(8,128)S(1)}, u32[]{:S(2)}, u32[]{:S(2)}) collective-permute-start(f32[2,8,2560]{2,1,0:T(8,128)S(1)} %get-tuple-element.20), channel_id=1, source_target_pairs={{0,4},{4,0},{8,12},{12,8},{16,20},{20,16},{24,28},{28,24},{1,5},{5... | collective-permute-start | bytes 491528 | tf_op jit(solution)/shard_map/ppermute | solution.py:22
  6.9 1.6 %collective-permute-start.1 = (f32[2,8,2560]{2,1,0:T(8,128)S(1)}, f32[2,8,2560]{2,1,0:T(8,128)S(1)}, u32[]{:S(2)}, u32[]{:S(2)}) collective-permute-start(f32[2,8,2560]{2,1,0:T(8,128)S(1)} %get-tuple-element.21), channel_id=1, source_target_pairs={{0,8},{4,12},{8,0},{12,4},{16,24},{20,28},{24,16},{28,20},{1,9},{5... | collective-permute-start | bytes 491528 | tf_op jit(solution)/shard_map/ppermute | solution.py:22
  14.6 1.3 %collective-permute-done.2 = f32[2,8,2560]{2,1,0:T(8,128)S(1)} collective-permute-done((f32[2,8,2560]{2,1,0:T(8,128)S(1)}, f32[2,8,2560]{2,1,0:T(8,128)S(1)}, u32[]{:S(2)}, u32[]{:S(2)}) %collective-permute-start.2) | collective-permute-done | bytes 163872 | tf_op jit(solution)/shard_map/ppermute | solution.py:22
  16.0 2.8 %collective-permute-start.3 = (f32[2,8,2560]{2,1,0:T(8,128)S(1)}, f32[2,8,2560]{2,1,0:T(8,128)S(1)}, u32[]{:S(2)}, u32[]{:S(2)}) collective-permute-start(f32[2,8,2560]{2,1,0:T(8,128)S(1)} %add_add_fusion.refs_0_), channel_id=1, source_target_pairs={{0,16},{4,20},{8,24},{12,28},{16,0},{20,4},{24,8},{28,12},{1,17},{... | collective-permute-start | bytes 491528 | tf_op jit(solution)/shard_map/ppermute | solution.py:22
  18.8 6.8 %collective-permute-done.3.refs_1_ = f32[2,8,2560]{2,1,0:T(8,128)S(1)} collective-permute-done((f32[2,8,2560]{2,1,0:T(8,128)S(1)}, f32[2,8,2560]{2,1,0:T(8,128)S(1)}, u32[]{:S(2)}, u32[]{:S(2)}) %collective-permute-start.3) | collective-permute-done | bytes 163872 | tf_op jit(solution)/shard_map/ppermute | solution.py:22
  25.7 1.4 %collective-permute-start.6 = (bf16[256,128]{1,0:T(8,128)(2,1)S(1)}, bf16[256,128]{1,0:T(8,128)(2,1)S(1)}, u32[]{:S(2)}, u32[]{:S(2)}) collective-permute-start(bf16[256,128]{1,0:T(8,128)(2,1)S(1)} %get-tuple-element.28.refs_0_.refs_2_), channel_id=1, source_target_pairs={{0,12},{4,8},{8,4},{12,0},{16,28},{20,24},{24,20},{28,16},{1,13},{... | collective-permute-start | bytes 196616 | tf_op jit(solution)/shard_map/ppermute | solution.py:22
  27.1 1.3 %collective-permute-start.5 = (bf16[256,128]{1,0:T(8,128)(2,1)S(1)}, bf16[256,128]{1,0:T(8,128)(2,1)S(1)}, u32[]{:S(2)}, u32[]{:S(2)}) collective-permute-start(bf16[256,128]{1,0:T(8,128)(2,1)S(1)} %get-tuple-element.28.refs_0_.refs_2_), channel_id=1, source_target_pairs={{0,8},{4,12},{8,0},{12,4},{16,24},{20,28},{24,16},{28,20},{1,9},{5... | collective-permute-start | bytes 196616 | tf_op jit(solution)/shard_map/ppermute | solution.py:22
  29.2 1.7 %collective-permute-done.6.refs_3_ = bf16[256,128]{1,0:T(8,128)(2,1)S(1)} collective-permute-done((bf16[256,128]{1,0:T(8,128)(2,1)S(1)}, bf16[256,128]{1,0:T(8,128)(2,1)S(1)}, u32[]{:S(2)}, u32[]{:S(2)}) %collective-permute-start.6) | collective-permute-done | bytes 65568 | tf_op jit(solution)/shard_map/ppermute | solution.py:22
  31.4 1.3 %collective-permute-done.4.refs_1_ = bf16[256,128]{1,0:T(8,128)(2,1)S(1)} collective-permute-done((bf16[256,128]{1,0:T(8,128)(2,1)S(1)}, bf16[256,128]{1,0:T(8,128)(2,1)S(1)}, u32[]{:S(2)}, u32[]{:S(2)}) %collective-permute-start.4) | collective-permute-done | bytes 65568 | tf_op jit(solution)/shard_map/ppermute | solution.py:22
  32.8 6.8 %paged_attention.1 = (bf16[2,144,128]{2,1,0:T(8,128)(2,1)S(1)}, bf16[2,144,128]{2,1,0:T(8,128)(2,1)S(1)}, bf16[2,144,128]{2,1,0:T(8,128)(2,1)S(1)}, bf16[2,144,128]{2,1,0:T(8,128)(2,1)S(1)}) custom-call(s32[128]{0:T(128)S(1)} %get-tuple-element.23.place_of, bf16[256,128]{1,0:T(8,128)(2,1)S(1)} %get-tuple-element.28.refs_0_.refs_2_, ...), custom_call_target="tpu_custom_call" | custom-call | flops 134217728 | bytes 16777216 | tf_op jit(solution)/shard_map/paged_attention/pallas_call | solution.py:506
  40.9 2.2 %collective-permute-start.9 = (bf16[2,144,128]{2,1,0:T(8,128)(2,1)S(1)}, bf16[2,144,128]{2,1,0:T(8,128)(2,1)S(1)}, u32[]{:S(2)}, u32[]{:S(2)}) collective-permute-start(bf16[2,144,128]{2,1,0:T(8,128)(2,1)S(1)} %get-tuple-element.33), channel_id=1, source_target_pairs={{0,12},{4,8},{8,4},{12,0},{16,28},{20,24},{24,20},{28,16},{1,13},{... | collective-permute-start | bytes 221192 | tf_op jit(solution)/shard_map/ppermute | solution.py:22
  43.1 0.9 %collective-permute-done.7.refs_1_ = bf16[2,144,128]{2,1,0:T(8,128)(2,1)S(1)} collective-permute-done((bf16[2,144,128]{2,1,0:T(8,128)(2,1)S(1)}, bf16[2,144,128]{2,1,0:T(8,128)(2,1)S(1)}, u32[]{:S(2)}, u32[]{:S(2)}) %collective-permute-start.7) | collective-permute-done | bytes 73760 | tf_op jit(solution)/shard_map/ppermute | solution.py:22
  44.7 1.5 %collective-permute-done.9.refs_3_ = bf16[2,144,128]{2,1,0:T(8,128)(2,1)S(1)} collective-permute-done((bf16[2,144,128]{2,1,0:T(8,128)(2,1)S(1)}, bf16[2,144,128]{2,1,0:T(8,128)(2,1)S(1)}, u32[]{:S(2)}, u32[]{:S(2)}) %collective-permute-start.9) | collective-permute-done | bytes 73760 | tf_op jit(solution)/shard_map/ppermute | solution.py:22
  46.7 3.9 %collective-permute-start.10 = (bf16[2,144,128]{2,1,0:T(8,128)(2,1)S(1)}, bf16[2,144,128]{2,1,0:T(8,128)(2,1)S(1)}, u32[]{:S(2)}, u32[]{:S(2)}) collective-permute-start(bf16[2,144,128]{2,1,0:T(8,128)(2,1)S(1)} %combine.1.refs_0_), channel_id=1, source_target_pairs={{0,16},{4,20},{8,24},{12,28},{16,0},{20,4},{24,8},{28,12},{1,17},{... | collective-permute-start | bytes 221192 | tf_op jit(solution)/shard_map/ppermute | solution.py:22
  50.5 3.1 %collective-permute-done.10.refs_1_ = bf16[2,144,128]{2,1,0:T(8,128)(2,1)S(1)} collective-permute-done((bf16[2,144,128]{2,1,0:T(8,128)(2,1)S(1)}, bf16[2,144,128]{2,1,0:T(8,128)(2,1)S(1)}, u32[]{:S(2)}, u32[]{:S(2)}) %collective-permute-start.10) | collective-permute-done | bytes 73760 | tf_op jit(solution)/shard_map/ppermute | solution.py:22
  54.7 2.2 %collective-permute-start.12 = (bf16[16,2048]{1,0:T(8,128)(2,1)S(1)}, bf16[16,2048]{1,0:T(8,128)(2,1)S(1)}, u32[]{:S(2)}, u32[]{:S(2)}) collective-permute-start(bf16[16,2048]{1,0:T(8,128)(2,1)S(1)} %finish.1.refs_0_), channel_id=1, source_target_pairs={{0,8},{4,12},{8,0},{12,4},{16,24},{20,28},{24,16},{28,20},{1,9},{5... | collective-permute-start | bytes 196616 | tf_op jit(solution)/shard_map/ppermute | solution.py:22
  57.7 1.7 %collective-permute-done.13.refs_3_ = bf16[16,2048]{1,0:T(8,128)(2,1)S(1)} collective-permute-done((bf16[16,2048]{1,0:T(8,128)(2,1)S(1)}, bf16[16,2048]{1,0:T(8,128)(2,1)S(1)}, u32[]{:S(2)}, u32[]{:S(2)}) %collective-permute-start.13) | collective-permute-done | bytes 65568 | tf_op jit(solution)/shard_map/ppermute | solution.py:22
  59.9 1.3 %collective-permute-done.11.refs_1_ = bf16[16,2048]{1,0:T(8,128)(2,1)S(1)} collective-permute-done((bf16[16,2048]{1,0:T(8,128)(2,1)S(1)}, bf16[16,2048]{1,0:T(8,128)(2,1)S(1)}, u32[]{:S(2)}, u32[]{:S(2)}) %collective-permute-start.11) | collective-permute-done | bytes 65568 | tf_op jit(solution)/shard_map/ppermute | solution.py:22
  61.2 0.8 %project_out.1 = f32[64,1024]{1,0:T(8,128)S(1)} custom-call(s32[1]{0:T(128)} %bitcast.me, bf16[16,2048]{1,0:T(8,128)(2,1)S(1)} %finish.1.refs_0_, bf16[16,2048]{1,0:T(8,128)(2,1)S(1)} %collective-permute-done.11.refs_1_, bf16[16,2048]{1,0:T(8,128)(2,1)S(1)} %collective-permute-done.12.refs_2_, bf16[16,2048]{1,0:T(8,128)(2,1)S(1)} %collective-permute-done.13.refs_3_, ...), custom_call_target="tpu_custom_call" | custom-call | tf_op jit(solution)/shard_map/project_out/pallas_call | solution.py:557
  62.2 1.5 %collective-permute-done.14 = f32[64,1024]{1,0:T(8,128)S(1)} collective-permute-done((f32[64,1024]{1,0:T(8,128)S(1)}, f32[64,1024]{1,0:T(8,128)S(1)}, u32[]{:S(2)}, u32[]{:S(2)}) %collective-permute-start.14) | collective-permute-done | bytes 262176 | tf_op jit(solution)/shard_map/ppermute | solution.py:22
  63.7 1.6 %collective-permute-start.15 = (bf16[64,1024]{1,0:T(8,128)(2,1)S(1)}, bf16[64,1024]{1,0:T(8,128)(2,1)S(1)}, u32[]{:S(2)}, u32[]{:S(2)}) collective-permute-start(bf16[64,1024]{1,0:T(8,128)(2,1)S(1)} %fusion), channel_id=1, source_target_pairs={{0,2},{1,3},{2,0},{3,1},{4,6},{5,7},{6,4},{7,5},{8,10},{9,11},{10,... | collective-permute-start | bytes 393224 | tf_op jit(solution)/shard_map/ppermute | solution.py:22
  65.3 4.0 %collective-permute-done.15 = bf16[64,1024]{1,0:T(8,128)(2,1)S(1)} collective-permute-done((bf16[64,1024]{1,0:T(8,128)(2,1)S(1)}, bf16[64,1024]{1,0:T(8,128)(2,1)S(1)}, u32[]{:S(2)}, u32[]{:S(2)}) %collective-permute-start.15) | collective-permute-done | bytes 131104 | tf_op jit(solution)/shard_map/ppermute | solution.py:22
  (53 shorter events, 13.2 us)
Async XLA Ops:
  0.0 0.9 %copy-start.1 = (bf16[64,1024]{1,0:T(8,128)(2,1)S(1)}, bf16[64,1024]{1,0:T(8,128)(2,1)}, u32[]{:S(2)}) copy-start(bf16[64,1024]{1,0:T(8,128)(2,1)} %hidden.1) | copy-start | bytes 393220
  3.9 10.7 %collective-permute-start = (f32[2,8,2560]{2,1,0:T(8,128)S(1)}, f32[2,8,2560]{2,1,0:T(8,128)S(1)}, u32[]{:S(2)}, u32[]{:S(2)}) collective-permute-start(f32[2,8,2560]{2,1,0:T(8,128)S(1)} %get-tuple-element.20), channel_id=1, source_target_pairs={{0,4},{4,0},{8,12},{12,8},{16,20},{20,16},{24,28},{28,24},{1,5},{5... | collective-permute-start | bytes 491528 | tf_op jit(solution)/shard_map/ppermute | solution.py:22
  6.9 7.7 %collective-permute-start.1 = (f32[2,8,2560]{2,1,0:T(8,128)S(1)}, f32[2,8,2560]{2,1,0:T(8,128)S(1)}, u32[]{:S(2)}, u32[]{:S(2)}) collective-permute-start(f32[2,8,2560]{2,1,0:T(8,128)S(1)} %get-tuple-element.21), channel_id=1, source_target_pairs={{0,8},{4,12},{8,0},{12,4},{16,24},{20,28},{24,16},{28,20},{1,9},{5... | collective-permute-start | bytes 491528 | tf_op jit(solution)/shard_map/ppermute | solution.py:22
  8.5 7.4 %collective-permute-start.2 = (f32[2,8,2560]{2,1,0:T(8,128)S(1)}, f32[2,8,2560]{2,1,0:T(8,128)S(1)}, u32[]{:S(2)}, u32[]{:S(2)}) collective-permute-start(f32[2,8,2560]{2,1,0:T(8,128)S(1)} %get-tuple-element.22), channel_id=1, source_target_pairs={{0,12},{4,8},{8,4},{12,0},{16,28},{20,24},{24,20},{28,16},{1,13},{... | collective-permute-start | bytes 491528 | tf_op jit(solution)/shard_map/ppermute | solution.py:22
  15.9 16.8 %slice-start = ((s8[8388608]{0:T(1024)(128)(4,1)}), s8[4194304]{0:T(1024)(128)(4,1)S(1)}, s32[]{:S(2)}) async-start(s8[8388608]{0:T(1024)(128)(4,1)} %bitcast.2), calls=%async_computation | async-start | bytes 8388608
  15.9 16.8 %slice-start.2 = ((s8[8388608]{0:T(1024)(128)(4,1)}), s8[4194304]{0:T(1024)(128)(4,1)S(1)}, s32[]{:S(2)}) async-start(s8[8388608]{0:T(1024)(128)(4,1)} %bitcast.4), calls=%async_computation.2 | async-start | bytes 8388608
  15.9 16.8 %slice-start.1 = ((s8[8388608]{0:T(1024)(128)(4,1)}), s8[4194304]{0:T(1024)(128)(4,1)S(1)}, s32[]{:S(2)}) async-start(s8[8388608]{0:T(1024)(128)(4,1)} %bitcast.2), calls=%async_computation.1 | async-start | bytes 8388608
  16.0 16.8 %slice-start.3 = ((s8[8388608]{0:T(1024)(128)(4,1)}), s8[4194304]{0:T(1024)(128)(4,1)S(1)}, s32[]{:S(2)}) async-start(s8[8388608]{0:T(1024)(128)(4,1)} %bitcast.4), calls=%async_computation.3 | async-start | bytes 8388608
  16.0 9.6 %collective-permute-start.3 = (f32[2,8,2560]{2,1,0:T(8,128)S(1)}, f32[2,8,2560]{2,1,0:T(8,128)S(1)}, u32[]{:S(2)}, u32[]{:S(2)}) collective-permute-start(f32[2,8,2560]{2,1,0:T(8,128)S(1)} %add_add_fusion.refs_0_), channel_id=1, source_target_pairs={{0,16},{4,20},{8,24},{12,28},{16,0},{20,4},{24,8},{28,12},{1,17},{... | collective-permute-start | bytes 491528 | tf_op jit(solution)/shard_map/ppermute | solution.py:22
  25.6 35.6 %copy-start = (bf16[2048,1024]{1,0:T(8,128)(2,1)S(1)}, bf16[2048,1024]{1,0:T(8,128)(2,1)}, u32[]{:S(2)}) copy-start(bf16[2048,1024]{1,0:T(8,128)(2,1)} %refs_4_.1) | copy-start | bytes 12582916
  25.7 5.2 %collective-permute-start.6 = (bf16[256,128]{1,0:T(8,128)(2,1)S(1)}, bf16[256,128]{1,0:T(8,128)(2,1)S(1)}, u32[]{:S(2)}, u32[]{:S(2)}) collective-permute-start(bf16[256,128]{1,0:T(8,128)(2,1)S(1)} %get-tuple-element.28.refs_0_.refs_2_), channel_id=1, source_target_pairs={{0,12},{4,8},{8,4},{12,0},{16,28},{20,24},{24,20},{28,16},{1,13},{... | collective-permute-start | bytes 196616 | tf_op jit(solution)/shard_map/ppermute | solution.py:22
  27.1 4.3 %collective-permute-start.5 = (bf16[256,128]{1,0:T(8,128)(2,1)S(1)}, bf16[256,128]{1,0:T(8,128)(2,1)S(1)}, u32[]{:S(2)}, u32[]{:S(2)}) collective-permute-start(bf16[256,128]{1,0:T(8,128)(2,1)S(1)} %get-tuple-element.28.refs_0_.refs_2_), channel_id=1, source_target_pairs={{0,8},{4,12},{8,0},{12,4},{16,24},{20,28},{24,16},{28,20},{1,9},{5... | collective-permute-start | bytes 196616 | tf_op jit(solution)/shard_map/ppermute | solution.py:22
  28.5 4.3 %collective-permute-start.4 = (bf16[256,128]{1,0:T(8,128)(2,1)S(1)}, bf16[256,128]{1,0:T(8,128)(2,1)S(1)}, u32[]{:S(2)}, u32[]{:S(2)}) collective-permute-start(bf16[256,128]{1,0:T(8,128)(2,1)S(1)} %get-tuple-element.28.refs_0_.refs_2_), channel_id=1, source_target_pairs={{0,4},{4,0},{8,12},{12,8},{16,20},{20,16},{24,28},{28,24},{1,5},{5... | collective-permute-start | bytes 196616 | tf_op jit(solution)/shard_map/ppermute | solution.py:22
  39.5 4.4 %collective-permute-start.7 = (bf16[2,144,128]{2,1,0:T(8,128)(2,1)S(1)}, bf16[2,144,128]{2,1,0:T(8,128)(2,1)S(1)}, u32[]{:S(2)}, u32[]{:S(2)}) collective-permute-start(bf16[2,144,128]{2,1,0:T(8,128)(2,1)S(1)} %get-tuple-element.31), channel_id=1, source_target_pairs={{0,4},{4,0},{8,12},{12,8},{16,20},{20,16},{24,28},{28,24},{1,5},{5... | collective-permute-start | bytes 221192 | tf_op jit(solution)/shard_map/ppermute | solution.py:22
  40.4 4.4 %collective-permute-start.8 = (bf16[2,144,128]{2,1,0:T(8,128)(2,1)S(1)}, bf16[2,144,128]{2,1,0:T(8,128)(2,1)S(1)}, u32[]{:S(2)}, u32[]{:S(2)}) collective-permute-start(bf16[2,144,128]{2,1,0:T(8,128)(2,1)S(1)} %get-tuple-element.32), channel_id=1, source_target_pairs={{0,8},{4,12},{8,0},{12,4},{16,24},{20,28},{24,16},{28,20},{1,9},{5... | collective-permute-start | bytes 221192 | tf_op jit(solution)/shard_map/ppermute | solution.py:22
  40.9 5.3 %collective-permute-start.9 = (bf16[2,144,128]{2,1,0:T(8,128)(2,1)S(1)}, bf16[2,144,128]{2,1,0:T(8,128)(2,1)S(1)}, u32[]{:S(2)}, u32[]{:S(2)}) collective-permute-start(bf16[2,144,128]{2,1,0:T(8,128)(2,1)S(1)} %get-tuple-element.33), channel_id=1, source_target_pairs={{0,12},{4,8},{8,4},{12,0},{16,28},{20,24},{24,20},{28,16},{1,13},{... | collective-permute-start | bytes 221192 | tf_op jit(solution)/shard_map/ppermute | solution.py:22
  46.7 7.0 %collective-permute-start.10 = (bf16[2,144,128]{2,1,0:T(8,128)(2,1)S(1)}, bf16[2,144,128]{2,1,0:T(8,128)(2,1)S(1)}, u32[]{:S(2)}, u32[]{:S(2)}) collective-permute-start(bf16[2,144,128]{2,1,0:T(8,128)(2,1)S(1)} %combine.1.refs_0_), channel_id=1, source_target_pairs={{0,16},{4,20},{8,24},{12,28},{16,0},{20,4},{24,8},{28,12},{1,17},{... | collective-permute-start | bytes 221192 | tf_op jit(solution)/shard_map/ppermute | solution.py:22
  54.1 5.2 %collective-permute-start.13 = (bf16[16,2048]{1,0:T(8,128)(2,1)S(1)}, bf16[16,2048]{1,0:T(8,128)(2,1)S(1)}, u32[]{:S(2)}, u32[]{:S(2)}) collective-permute-start(bf16[16,2048]{1,0:T(8,128)(2,1)S(1)} %finish.1.refs_0_), channel_id=1, source_target_pairs={{0,12},{4,8},{8,4},{12,0},{16,28},{20,24},{24,20},{28,16},{1,13},{... | collective-permute-start | bytes 196616 | tf_op jit(solution)/shard_map/ppermute | solution.py:22
  54.7 5.2 %collective-permute-start.12 = (bf16[16,2048]{1,0:T(8,128)(2,1)S(1)}, bf16[16,2048]{1,0:T(8,128)(2,1)S(1)}, u32[]{:S(2)}, u32[]{:S(2)}) collective-permute-start(bf16[16,2048]{1,0:T(8,128)(2,1)S(1)} %finish.1.refs_0_), channel_id=1, source_target_pairs={{0,8},{4,12},{8,0},{12,4},{16,24},{20,28},{24,16},{28,20},{1,9},{5... | collective-permute-start | bytes 196616 | tf_op jit(solution)/shard_map/ppermute | solution.py:22
  57.0 4.3 %collective-permute-start.11 = (bf16[16,2048]{1,0:T(8,128)(2,1)S(1)}, bf16[16,2048]{1,0:T(8,128)(2,1)S(1)}, u32[]{:S(2)}, u32[]{:S(2)}) collective-permute-start(bf16[16,2048]{1,0:T(8,128)(2,1)S(1)} %finish.1.refs_0_), channel_id=1, source_target_pairs={{0,4},{4,0},{8,12},{12,8},{16,20},{20,16},{24,28},{28,24},{1,5},{5... | collective-permute-start | bytes 196616 | tf_op jit(solution)/shard_map/ppermute | solution.py:22
  62.1 1.6 %collective-permute-start.14 = (f32[64,1024]{1,0:T(8,128)S(1)}, f32[64,1024]{1,0:T(8,128)S(1)}, u32[]{:S(2)}, u32[]{:S(2)}) collective-permute-start(f32[64,1024]{1,0:T(8,128)S(1)} %project_out.1), channel_id=1, source_target_pairs={{0,1},{1,0},{2,3},{3,2},{4,5},{5,4},{6,7},{7,6},{8,9},{9,8},{10,11... | collective-permute-start | bytes 786440 | tf_op jit(solution)/shard_map/ppermute | solution.py:22
  63.7 5.6 %collective-permute-start.15 = (bf16[64,1024]{1,0:T(8,128)(2,1)S(1)}, bf16[64,1024]{1,0:T(8,128)(2,1)S(1)}, u32[]{:S(2)}, u32[]{:S(2)}) collective-permute-start(bf16[64,1024]{1,0:T(8,128)(2,1)S(1)} %fusion), channel_id=1, source_target_pairs={{0,2},{1,3},{2,0},{3,1},{4,6},{5,7},{6,4},{7,5},{8,10},{9,11},{10,... | collective-permute-start | bytes 393224 | tf_op jit(solution)/shard_map/ppermute | solution.py:22

commit v9 on v8

--- a/solution.py
+++ b/solution.py
@@ -65,9 +65,9 @@
     return parts
 
 
-def relative_place(block, axis, n):
-    last_shift, last_size = last_group(n)
-    offset = lax.axis_index(axis) ^ block
+def relative_place(block, me, n):
+    last_shift, _ = last_group(n)
+    offset = me ^ block
     place, weight = block >> last_shift, n
     for shift, size in lower_groups(n):
         weight //= size
@@ -84,11 +84,61 @@
     return [(c << last_shift) + (low ^ e) for e in offsets for c in range(last_size)]
 
 
+def table_kernel(seq_size, ways, me, counts, trim, pages, key_scale, value_scale, tables, place_of):
+    requests = counts.shape[0]
+    chunks = tables.shape[0] // 4
+    heads = LANES // CHUNK
+    mine = requests // seq_size
+    page = pages[...]
+    owner, first, length = [jnp.zeros_like(page)] * 3
+    start = 0
+    for r in range(requests):
+        end = start + counts[r]
+        inside = (page >= start) & (page < end)
+        owner = owner + jnp.where(page >= end, 1, 0)
+        first = jnp.where(inside, start, first)
+        length = jnp.where(inside, PAGE * counts[r] - trim[r], length)
+        start = end
+    valid = length - (page - first) * PAGE
+    block = owner >> (mine.bit_length() - 1)
+    row = relative_place(block, me[0], seq_size) * mine + (owner & (mine - 1))
+    place_of[...] = ((me[0] & (ways - 1)) << 24) + (row << 16) + owner
+
+    chunk_slot = lax.broadcasted_iota(jnp.int32, (chunks, LANES), 1) // CHUNK
+    in_chunk = chunk_slot == lax.broadcasted_iota(jnp.int32, (chunks, LANES), 0)
+    slot = lax.broadcasted_iota(jnp.int32, (LANES, LANES), 0) % CHUNK
+    lane = lax.broadcasted_iota(jnp.int32, (LANES, LANES), 1)
+    same_slot = slot == lane // heads
+    low_head = lane % heads < heads // 2
+
+    def spread(row, to):
+        rest = jnp.where(in_chunk, jnp.broadcast_to(row, (chunks, LANES)), 0.0)
+        total = jnp.zeros((chunks, LANES), jnp.float32)
+        for _ in range(3):
+            piece = rest.astype(jnp.bfloat16)
+            rest = rest - piece.astype(jnp.float32)
+            total = total + jnp.dot(
+                piece,
+                jnp.where(to, 1.0, 0.0).astype(jnp.bfloat16),
+                preferred_element_type=jnp.float32,
+            )
+        return total
+
+    def by_head(scale):
+        return spread(scale[0:1, :], same_slot & low_head) + spread(
+            scale[1:2, :], same_slot & jnp.logical_not(low_head)
+        )
+
+    tables[:chunks, :] = by_head(key_scale) * (1.0 / math.sqrt(HD))
+    tables[chunks : 2 * chunks, :] = spread(valid.astype(jnp.float32), same_slot)
+    tables[2 * chunks : 3 * chunks, :] = by_head(value_scale)
+    tables[3 * chunks :, :] = spread(owner.astype(jnp.float32), same_slot)
+
+
 def project_kernel(ways, me, hidden, w_query, w_keyval, *refs):
-    outs, (query, keyval, result, sem) = refs[:ways], refs[ways:]
+    outs, (keyval_out, query, keyval, result, sem) = refs[:ways], refs[ways:]
     depth = w_query.shape[0]
     tile = min(256, depth)
-    wide = w_query.shape[1]
     copies = [
         [
             pltpu.make_async_copy(
@@ -104,10 +154,10 @@
     for row, pair in zip(range(0, depth, tile), copies):
         here = slice(row, row + tile)
         rows = hidden[:, here]
-        for copy, held, place in zip(pair, (query, keyval), (slice(0, wide), slice(wide, None))):
+        for copy, held, to in zip(pair, (query, keyval), (result, keyval_out)):
             copy.wait()
             part = jnp.dot(rows, held[here, :], preferred_element_type=jnp.float32)
-            result[:, place] = result[:, place] + part if row else part
+            to[...] = to[...] + part if row else part
     digit = me[0] & (ways - 1)
     for d, out in enumerate(outs):
         blocks, mine, _ = out.shape
@@ -124,7 +174,7 @@
 
 
 def output_kernel(ways, seq_size, me, *refs):
-    parts, (w_out, out) = refs[:ways], refs[ways:]
+    parts, (w_out, rounded, out) = refs[:ways], refs[ways:]
     rows = jnp.concatenate([part[...] for part in parts], axis=0)
     total = jnp.dot(rows, w_out[...], preferred_element_type=jnp.float32)
     blocks = gathered_blocks(me[0], seq_size)
@@ -133,28 +183,29 @@
         for i, block in enumerate(blocks):
             here = pl.ds(pl.multiple_of(block * mine, mine), mine)
             out[here, :] = total[i * mine : (i + 1) * mine]
+        rounded[...] = out[...].astype(jnp.bfloat16)
         return
     for place in range(len(blocks)):
         chosen = total[:mine]
         for i, block in enumerate(blocks):
             chosen = jnp.where(block == place, total[i * mine : (i + 1) * mine], chosen)
         out[place * mine : (place + 1) * mine, :] = chosen
+    rounded[...] = out[...].astype(jnp.bfloat16)
 
 
 def join_kernel(*refs):
-    *parts, query, keyval, query_rows, keyval_rows = refs
+    *parts, out, rows = refs
     blocks, mine, columns = parts[0].shape
     held = blocks * mine
     whole = functools.reduce(jnp.add, [part[...] for part in parts]).reshape(held, columns)
-    heads = query.shape[0] // held
-    others = keyval.shape[0] // held
+    heads = columns // HD
     for h in range(heads):
-        query_rows[pl.ds(h, held, stride=heads), :] = whole[:, h * HD : (h + 1) * HD]
-    for h in range(others):
-        place = (heads + h) * HD
-        keyval_rows[pl.ds(h, held, stride=others), :] = whole[:, place : place + HD]
-    query[...] = query_rows[...].astype(jnp.bfloat16)
-    keyval[...] = keyval_rows[...].astype(jnp.bfloat16)
+        rows[pl.ds(h, held, stride=heads), :] = whole[:, h * HD : (h + 1) * HD]
+    out[...] = rows[...].astype(jnp.bfloat16)
+
+
+def new_rows(mine):
+    return -(-4 * mine // 16) * 16
 
 
 def split_stat(stat, lane):
@@ -172,9 +223,9 @@
     )
 
 
-def attention_kernel(ways, place_of, *refs):
+def attention_kernel(ways, mine, place_of, *refs):
     queries, refs = refs[:ways], refs[ways:]
-    (tables, keys, values), refs = refs[:3], refs[3:]
+    (keyval, tables, keys, values), refs = refs[:4], refs[4:]
     outs, refs = refs[:ways], refs[ways:]
     (
         query_low,
@@ -186,13 +237,13 @@
         dev_max,
         total_out,
         total_stat,
+        keyval_rows,
     ) = refs
     slots = keys.shape[0]
     heads = LANES // CHUNK
     group = heads // 2
     chunks = slots // CHUNK
-    blocks, block_rows, _ = outs[0].shape
-    mine = block_rows // heads - 1
+    blocks = outs[0].shape[0]
     step_chunks = 4
 
     for d, part in enumerate(queries):
@@ -313,10 +364,12 @@
 
     lane = lax.broadcasted_iota(jnp.int32, (heads, LANES), 1)
     digit = place_of[0] >> 24
+    for j in range(4):
+        keyval_rows[pl.ds(j, keyval.shape[0], stride=4), :] = keyval[:, j * HD : (j + 1) * HD]
     for d, out in enumerate(outs):
         for b in range(blocks):
-            first = (b * ways + (digit ^ d)) * (mine * heads)
-            rows = pl.ds(pl.multiple_of(first, mine * heads), mine * heads)
+            block = b * ways + (digit ^ d)
+            rows = pl.ds(pl.multiple_of(block * (mine * heads), mine * heads), mine * heads)
             out[b, : mine * heads, :] = (total_out[0, rows, :] + total_out[1, rows, :]).astype(
                 jnp.bfloat16
             )
@@ -328,17 +381,21 @@
                 stat = jnp.where(
                     lane % (STAT // 2) == r, both[r * heads : (r + 1) * heads], stat
                 )
-            out[b, mine * heads :, :] = split_stat(stat, lane)
-
-
-def combine_kernel(*refs):
+            out[b, mine * heads : (mine + 1) * heads, :] = split_stat(stat, lane)
+            new = keyval_rows[pl.ds(pl.multiple_of(block * (4 * mine), 4 * mine), 4 * mine), :]
+            if new.shape[0] < new_rows(mine):
+                empty_rows = jnp.zeros((new_rows(mine) - new.shape[0], LANES), jnp.float32)
+                new = jnp.concatenate([new, empty_rows], axis=0)
+            out[b, (mine + 1) * heads :, :] = new.astype(jnp.bfloat16)
+
+
+def combine_kernel(mine, *refs):
     *parts, out = refs
-    blocks, block_rows, _ = out.shape
+    blocks = out.shape[0]
     heads = LANES // CHUNK
-    mine = block_rows // heads - 1
     lane = lax.broadcasted_iota(jnp.int32, (heads, LANES), 1)
     for b in range(blocks):
-        stats = [join_stat(part[b, mine * heads :, :]) for part in parts]
+        stats = [join_stat(part[b, mine * heads : (mine + 1) * heads, :]) for part in parts]
         maxima = [jnp.where(lane < mine, stat, 0.0) for stat in stats]
         top = functools.reduce(jnp.maximum, maxima)
         factors = [jnp.exp(m - top) for m in maxima]
@@ -349,7 +406,9 @@
         both = jnp.where(lane < STAT // 2, top, sums)
         both = jnp.where(lane < STAT, both, 0.0)
         both = (both + pltpu.roll(both, STAT, 1)) + pltpu.roll(both, 2 * STAT, 1)
-        out[b, mine * heads :, :] = split_stat(both, lane)
+        out[b, mine * heads : (mine + 1) * heads, :] = split_stat(both, lane)
+        new = sum(part[b, (mine + 1) * heads :, :].astype(jnp.float32) for part in parts)
+        out[b, (mine + 1) * heads :, :] = new.astype(jnp.bfloat16)
         for r in range(mine):
             rows = slice(r * heads, (r + 1) * heads)
             numer = sum(
@@ -359,31 +418,30 @@
             out[b, rows, :] = numer.astype(jnp.bfloat16)
 
 
-def finish_kernel(*refs):
-    *parts, query, keyval, out, numers = refs
-    blocks, block_rows, _ = parts[0].shape
+def finish_kernel(mine, *refs):
+    *parts, query, out, numers = refs
+    blocks = parts[0].shape[0]
     heads = LANES // CHUNK
     group = heads // 2
-    mine = block_rows // heads - 1
     lane = lax.broadcasted_iota(jnp.int32, (heads, LANES), 1)
     low_head = lax.broadcasted_iota(jnp.int32, (heads, LANES), 0) < group
-    new = keyval[...].astype(jnp.float32)
-
-    def spread(r, which):
+    def spread(new, r, which):
         low = jnp.broadcast_to(new[4 * r + which : 4 * r + which + 1], (heads, LANES))
         high = jnp.broadcast_to(new[4 * r + 2 + which : 4 * r + 3 + which], (heads, LANES))
         return jnp.where(low_head, low, high)
 
     for b in range(blocks):
+        new = sum(part[b, (mine + 1) * heads :, :].astype(jnp.float32) for part in parts)
+        new = new.astype(jnp.bfloat16).astype(jnp.float32)
         own = jnp.zeros((heads, LANES), jnp.float32)
         for r in range(mine):
             request = b * mine + r
             rows = query[request * heads : (request + 1) * heads, :].astype(jnp.float32)
-            dot = jnp.sum(rows * spread(request, 0), axis=1, keepdims=True)
+            dot = jnp.sum(rows * spread(new, r, 0), axis=1, keepdims=True)
             own = jnp.where(lane == r, dot * (1.0 / math.sqrt(HD)), own)
         maxima, sums = [], []
         for part in parts:
-            whole = join_stat(part[b, mine * heads :, :])
+            whole = join_stat(part[b, mine * heads : (mine + 1) * heads, :])
             maxima.append(jnp.where(lane < mine, whole, 0.0))
             sums.append(jnp.where(lane < mine, pltpu.roll(whole, LANES - STAT // 2, 1), 0.0))
         top = functools.reduce(jnp.maximum, maxima, own)
@@ -393,7 +451,7 @@
         fresh = fresh / denom
         factors = [f / denom for f in factors]
         for r in range(mine):
-            numer = fresh[:, r : r + 1] * spread(b * mine + r, 1)
+            numer = fresh[:, r : r + 1] * spread(new, r, 1)
             for part, f in zip(parts, factors):
                 rows = part[b, r * heads : (r + 1) * heads, :].astype(jnp.float32)
                 numer = numer + f[:, r : r + 1] * rows
@@ -431,82 +489,64 @@
     mine = requests // seq_size
     inverse_square_root = 1.0 / math.sqrt(HD)
 
-    start = jnp.cumsum(page_counts) - page_counts
-    ends = start + page_counts
-    owner = jnp.sum((ends[None, :] <= slot_pages[:, None]).astype(jnp.int32), axis=1)
-    selector = owner[:, None] == jnp.arange(requests, dtype=jnp.int32)[None, :]
-    select_int = selector.astype(jnp.int32)
-    index = slot_pages - jnp.sum(select_int * start[None, :], axis=1)
-    lengths = PAGE * page_counts - trim
-    page_valid = jnp.sum(select_int * lengths[None, :], axis=1) - index * PAGE
-    block = owner // mine
-    row_of = relative_place(block, "seq", seq_size) * mine + owner - block * mine
-
-    def on_lanes(x):
-        return jnp.broadcast_to(x, (slots, heads_local)).reshape(slots // CHUNK, LANES)
-
-    def per_head(x):
-        return on_lanes(jnp.repeat(x, heads_local // kv_local, axis=1))
-
-    tables = jnp.concatenate(
-        [
-            per_head(key_scale * inverse_square_root),
-            on_lanes(page_valid[:, None].astype(jnp.float32)),
-            per_head(value_scale),
-            on_lanes(owner[:, None].astype(jnp.float32)),
-        ],
-        axis=0,
-    )
+    assert slots == LANES and mine & (mine - 1) == 0
     ways = lower_groups(seq_size)[0][1]
-    digit = lax.axis_index("seq") & (ways - 1)
-    place_of = (digit << 24) + row_of * 65536 + owner
-
-    held = last_group(seq_size)[1] * mine
-    columns = w_query.shape[1] + w_keyval.shape[1]
+    chunks = slots // CHUNK
     smem = pl.BlockSpec(memory_space=pltpu.SMEM)
     vmem = pl.BlockSpec(memory_space=pltpu.VMEM)
-    hbm = pl.BlockSpec(memory_space=pltpu.HBM)
+    hbm = pl.BlockSpec(memory_space=pl.ANY)
+    small = pltpu.CompilerParams(vmem_limit_bytes=6 * 2**20)
     me = lax.axis_index("seq").reshape(1)
-    part_shape = jax.ShapeDtypeStruct((seq_size // ways, mine, columns), jnp.float32)
-    parts = pl.pallas_call(
+
+    tables, place_of = pl.pallas_call(
+        functools.partial(table_kernel, seq_size, ways),
+        out_shape=[
+            jax.ShapeDtypeStruct((4 * chunks, LANES), jnp.float32),
+            jax.ShapeDtypeStruct((1, slots), jnp.int32),
+        ],
+        in_specs=[smem, smem, smem, vmem, vmem, vmem],
+        out_specs=[vmem, vmem],
+        compiler_params=small,
+        name="page_table",
+    )(me, page_counts, trim, slot_pages.reshape(1, slots), key_scale.T, value_scale.T)
+    place_of = place_of.reshape(slots)
+
+    held = last_group(seq_size)[1] * mine
+    part_shape = jax.ShapeDtypeStruct((seq_size // ways, mine, wide), jnp.float32)
+    keyval_shape = jax.ShapeDtypeStruct((requests, w_keyval.shape[1]), jnp.float32)
+    *parts, keyval = pl.pallas_call(
         functools.partial(project_kernel, ways),
-        out_shape=[part_shape] * ways,
+        out_shape=[part_shape] * ways + [keyval_shape],
         in_specs=[smem, vmem, hbm, hbm],
-        out_specs=[vmem] * ways,
+        out_specs=[vmem] * (ways + 1),
         scratch_shapes=[
             pltpu.VMEM(w_query.shape, jnp.bfloat16),
             pltpu.VMEM(w_keyval.shape, jnp.bfloat16),
-            pltpu.VMEM((requests, columns), jnp.float32),
+            pltpu.VMEM((requests, wide), jnp.float32),
             pltpu.SemaphoreType.DMA((2, pl.cdiv(w_query.shape[0], 256))),
         ],
         compiler_params=pltpu.CompilerParams(vmem_limit_bytes=53 * 2**20),
         name="project",
     )(me, hidden_in, w_query, w_keyval)
     terms, (tables, place_of) = scatter_terms(parts, "seq", seq_size, (tables, place_of))
-    row_shapes = [(held * heads_local, HD), (held * 2 * kv_local, HD)]
-    my_query, my_keyval = pl.pallas_call(
+    my_query = pl.pallas_call(
         join_kernel,
-        out_shape=[jax.ShapeDtypeStruct(shape, jnp.bfloat16) for shape in row_shapes],
+        out_shape=jax.ShapeDtypeStruct((held * heads_local, HD), jnp.bfloat16),
         in_specs=[vmem] * len(terms),
-        out_specs=[vmem] * 2,
-        scratch_shapes=[pltpu.VMEM(shape, jnp.float32) for shape in row_shapes],
-        compiler_params=pltpu.CompilerParams(vmem_limit_bytes=6 * 2**20),
-        cost_estimate=pl.CostEstimate(
-            flops=10**10,
-            bytes_accessed=10**7,
-            transcendentals=0,
-        ),
+        out_specs=vmem,
+        scratch_shapes=[pltpu.VMEM((held * heads_local, HD), jnp.float32)],
+        compiler_params=small,
+        cost_estimate=pl.CostEstimate(flops=10**10, bytes_accessed=10**7, transcendentals=0),
         name="join",
     )(*terms)
     query = gather_relative(my_query, "seq", seq_size)
 
-    chunks = slots // CHUNK
     every_row = requests * heads_local
-    block_rows = (mine + 1) * heads_local
+    block_rows = (mine + 1) * heads_local + new_rows(mine)
     totals = pl.pallas_call(
-        functools.partial(attention_kernel, ways),
+        functools.partial(attention_kernel, ways, mine),
         out_shape=[jax.ShapeDtypeStruct((seq_size // ways, block_rows, HD), jnp.bfloat16)] * ways,
-        in_specs=[smem] + [vmem] * (ways + 3),
+        in_specs=[smem] + [vmem] * (ways + 4),
         out_specs=[vmem] * ways,
         scratch_shapes=[
             pltpu.VMEM((every_row, HD), jnp.bfloat16),
@@ -518,6 +558,7 @@
             pltpu.VMEM((chunks, LANES), jnp.float32),
             pltpu.VMEM((2, every_row, HD), jnp.float32),
             pltpu.VMEM((2, every_row, HD), jnp.float32),
+            pltpu.VMEM((requests * 2 * kv_local, HD), jnp.float32),
         ],
         compiler_params=pltpu.CompilerParams(vmem_limit_bytes=24 * 2**20),
         cost_estimate=pl.CostEstimate(
@@ -526,7 +567,7 @@
             transcendentals=slots * PAGE * heads_local,
         ),
         name="paged_attention",
-    )(place_of, *query, tables, key_cache, value_cache)
+    )(place_of, *query, keyval, tables, key_cache, value_cache)
 
     for shift, size in lower_groups(seq_size):
         if shift:
@@ -535,7 +576,7 @@
             swap(part, "seq", seq_size, d << shift) if d else part for d, part in enumerate(totals)
         ]
         totals = pl.pallas_call(
-            combine_kernel,
+            functools.partial(combine_kernel, mine),
             out_shape=jax.ShapeDtypeStruct(parts[0].shape, jnp.bfloat16),
             in_specs=[vmem] * size,
             out_specs=vmem,
@@ -545,32 +586,34 @@
     shift, size = last_group(seq_size)
     parts = [totals] + [swap(totals, "seq", seq_size, d << shift) for d in range(1, size)]
     my_context = pl.pallas_call(
-        finish_kernel,
+        functools.partial(finish_kernel, mine),
         out_shape=jax.ShapeDtypeStruct((held, wide), jnp.bfloat16),
-        in_specs=[vmem] * (size + 2),
+        in_specs=[vmem] * (size + 1),
         out_specs=vmem,
         scratch_shapes=[pltpu.VMEM((held * heads_local, HD), jnp.float32)],
         compiler_params=pltpu.CompilerParams(vmem_limit_bytes=6 * 2**20),
         name="finish",
-    )(*parts, my_query, my_keyval)
+    )(*parts, my_query)
 
     total = pl.pallas_call(
         functools.partial(output_kernel, ways, seq_size),
-        out_shape=jax.ShapeDtypeStruct((requests, w_out.shape[1]), jnp.float32),
+        out_shape=jax.ShapeDtypeStruct((requests, w_out.shape[1]), jnp.bfloat16),
         in_specs=[smem] + [vmem] * (ways + 1),
         out_specs=vmem,
+        scratch_shapes=[pltpu.VMEM((requests, w_out.shape[1]), jnp.float32)],
         compiler_params=pltpu.CompilerParams(vmem_limit_bytes=16 * 2**20),
         name="project_out",
     )(me, *gather_relative(my_context, "seq", seq_size), w_out)
-    step = 1
-    while step < head_size:
-        if step > 1:
-            total = lax.reduce_precision(total, 8, 7)
-            other = swap(total.astype(jnp.bfloat16), "head", head_size, step)
+    mask = head_size // 2
+    while mask:
+        if mask > 1:
+            if total.dtype != jnp.bfloat16:
+                total = lax.reduce_precision(total, 8, 7).astype(jnp.bfloat16)
+            other = swap(total, "head", head_size, mask)
+            total = total.astype(jnp.float32) + other.astype(jnp.float32)
         else:
-            other = swap(total, "head", head_size, step)
-        total = total + other.astype(jnp.float32)
-        step *= 2
+            total = total + swap(total, "head", head_size, mask)
+        mask //= 2
     return total.astype(jnp.bfloat16)
 
 

time: 70.2 us -> 68.2 us (0.972)
  other arithmetic: 3.88 us -> 0.76 us
  Pallas kernels: 11.6 us -> 12.5 us
  starting transfers between devices: 23.6 us -> 22.8 us
    unnamed x13 -> x22, local copies, waits for them, and re-layouts: 1.72 us -> 4.25 us
    another operation x3 -> x0, local copies, waits for them, and re-layouts: 1.16 us -> none
    pallas_call x4 -> x5, Pallas kernels: 7.77 us -> 8.65 us  [the longest x1 6.79 us: body(): pl.pallas_call(functools.partial(attention_kernel, ways, mine), out_shape...]
    reduce_sum x2 -> x0, other arithmetic: 0.85 us -> none  [the longest x1 0.75 us: body(): jnp.sum((ends[None, :] <= slot_pages[:, None]).astype(jnp.int32), axis=1)]
    broadcast_in_dim x7 -> x0, local copies, waits for them, and re-layouts: 0.83 us -> none  [the longest x5 0.43 us: on_lanes(): jnp.broadcast_to(x, (slots, heads_local)).reshape(slots // CHUNK, LANES)]
    ppermute x16, starting transfers between devices: 23.6 us -> 22.8 us  [swap(): return lax.ppermute(x, axis, [(j, j ^ mask) for j in range(n)])]
  transfers between devices with their start and end apart: 16 -> 16, of which waited for: 14 -> 14; matrix products, arithmetic and copies ran while one was open for 9% -> 0% of each run, Pallas kernels for 0% -> 1%
where the time goes in v9:
time: 68.2 us; the launch traced here: 68 us
  waiting for transfers between devices  27.5 us (40%)
  starting transfers between devices  22.8 us (33%)
  Pallas kernels  12.5 us (18%)
  local copies, waits for them, and re-layouts  4.25 us (6%)
  other arithmetic  0.76 us (1%)
    ppermute x16, waiting for transfers between devices, swap(): return lax.ppermute(x, axis, [(j, j ^ mask) for j in range(n)])  27.5 us
    ppermute x16, starting transfers between devices, swap(): return lax.ppermute(x, axis, [(j, j ^ mask) for j in range(n)])  22.8 us
    pallas_call x1, Pallas kernels, body(): pl.pallas_call(functools.partial(attention_kernel, ways, mine), out_shape...  6.79 us
    unnamed x22, local copies, waits for them, and re-layouts  4.25 us
    pallas_call x1, Pallas kernels, body(): pl.pallas_call(functools.partial(project_kernel, ways), out_shape=[part_s...  2.98 us
  transfers between devices with their start and end apart: 16, of which 14 were waited for; matrix products, arithmetic and copies ran while one was open for 0% of the time, Pallas kernels for 1%

profile of v9, /device:TPU:0, one launch (start us, length us, event | category | flops | bytes accessed | tf_op | source)
XLA Modules:
  0.0 68.0 jit_solution(2776081476381536083)
XLA Ops:
  0.0 0.9 %copy-done.1 = bf16[64,1024]{1,0:T(8,128)(2,1)S(1)} copy-done((bf16[64,1024]{1,0:T(8,128)(2,1)S(1)}, bf16[64,1024]{1,0:T(8,128)(2,1)}, u32[]{:S(2)}) %copy-start.1) | copy-done | bytes 131096
  0.9 3.0 %project.1 = (f32[2,8,2048]{2,1,0:T(8,128)S(1)}, f32[2,8,2048]{2,1,0:T(8,128)S(1)}, f32[2,8,2048]{2,1,0:T(8,128)S(1)}, f32[2,8,2048]{2,1,0:T(8,128)S(1)}, f32[64,512]{1,0:T(8,128)S(1)}) custom-call(s32[1]{0:T(128)} %bitcast.me, bf16[64,1024]{1,0:T(8,128)(2,1)S(1)} %copy-done.1, bf16[1024,2048]{1,0:T(8,128)(2,1)} %w_query.1, bf16[1024,512]{1,0:T(8,128)(2,1)} %w_keyval.1), custom_call_target="tpu_custom_call" | custom-call | tf_op jit(solution)/shard_map/project/pallas_call | solution.py:517
  3.9 3.0 %collective-permute-start = (f32[2,8,2048]{2,1,0:T(8,128)S(1)}, f32[2,8,2048]{2,1,0:T(8,128)S(1)}, u32[]{:S(2)}, u32[]{:S(2)}) collective-permute-start(f32[2,8,2048]{2,1,0:T(8,128)S(1)} %get-tuple-element.21), channel_id=1, source_target_pairs={{0,4},{4,0},{8,12},{12,8},{16,20},{20,16},{24,28},{28,24},{1,5},{5... | collective-permute-start | bytes 393224 | tf_op jit(solution)/shard_map/ppermute | solution.py:22
  6.9 1.6 %collective-permute-start.1 = (f32[2,8,2048]{2,1,0:T(8,128)S(1)}, f32[2,8,2048]{2,1,0:T(8,128)S(1)}, u32[]{:S(2)}, u32[]{:S(2)}) collective-permute-start(f32[2,8,2048]{2,1,0:T(8,128)S(1)} %get-tuple-element.22), channel_id=1, source_target_pairs={{0,8},{4,12},{8,0},{12,4},{16,24},{20,28},{24,16},{28,20},{1,9},{5... | collective-permute-start | bytes 393224 | tf_op jit(solution)/shard_map/ppermute | solution.py:22
  13.3 1.2 %collective-permute-done.2 = f32[2,8,2048]{2,1,0:T(8,128)S(1)} collective-permute-done((f32[2,8,2048]{2,1,0:T(8,128)S(1)}, f32[2,8,2048]{2,1,0:T(8,128)S(1)}, u32[]{:S(2)}, u32[]{:S(2)}) %collective-permute-start.2) | collective-permute-done | bytes 131104 | tf_op jit(solution)/shard_map/ppermute | solution.py:22
  14.5 2.8 %collective-permute-start.3 = (f32[2,8,2048]{2,1,0:T(8,128)S(1)}, f32[2,8,2048]{2,1,0:T(8,128)S(1)}, u32[]{:S(2)}, u32[]{:S(2)}) collective-permute-start(f32[2,8,2048]{2,1,0:T(8,128)S(1)} %add_add_fusion.refs_0_), channel_id=1, source_target_pairs={{0,16},{4,20},{8,24},{12,28},{16,0},{20,4},{24,8},{28,12},{1,17},{... | collective-permute-start | bytes 393224 | tf_op jit(solution)/shard_map/ppermute | solution.py:22
  17.4 5.4 %collective-permute-done.3.refs_1_ = f32[2,8,2048]{2,1,0:T(8,128)S(1)} collective-permute-done((f32[2,8,2048]{2,1,0:T(8,128)S(1)}, f32[2,8,2048]{2,1,0:T(8,128)S(1)}, u32[]{:S(2)}, u32[]{:S(2)}) %collective-permute-start.3) | collective-permute-done | bytes 131104 | tf_op jit(solution)/shard_map/ppermute | solution.py:22
  22.8 1.0 %collective-permute-start.4 = (bf16[256,128]{1,0:T(8,128)(2,1)S(1)}, bf16[256,128]{1,0:T(8,128)(2,1)S(1)}, u32[]{:S(2)}, u32[]{:S(2)}) collective-permute-start(bf16[256,128]{1,0:T(8,128)(2,1)S(1)} %join.1.refs_0_.refs_2_), channel_id=1, source_target_pairs={{0,4},{4,0},{8,12},{12,8},{16,20},{20,16},{24,28},{28,24},{1,5},{5... | collective-permute-start | bytes 196616 | tf_op jit(solution)/shard_map/ppermute | solution.py:22
  24.5 1.8 %collective-permute-start.6 = (bf16[256,128]{1,0:T(8,128)(2,1)S(1)}, bf16[256,128]{1,0:T(8,128)(2,1)S(1)}, u32[]{:S(2)}, u32[]{:S(2)}) collective-permute-start(bf16[256,128]{1,0:T(8,128)(2,1)S(1)} %join.1.refs_0_.refs_2_), channel_id=1, source_target_pairs={{0,12},{4,8},{8,4},{12,0},{16,28},{20,24},{24,20},{28,16},{1,13},{... | collective-permute-start | bytes 196616 | tf_op jit(solution)/shard_map/ppermute | solution.py:22
  26.4 1.5 %collective-permute-done.4.refs_1_ = bf16[256,128]{1,0:T(8,128)(2,1)S(1)} collective-permute-done((bf16[256,128]{1,0:T(8,128)(2,1)S(1)}, bf16[256,128]{1,0:T(8,128)(2,1)S(1)}, u32[]{:S(2)}, u32[]{:S(2)}) %collective-permute-start.4) | collective-permute-done | bytes 65568 | tf_op jit(solution)/shard_map/ppermute | solution.py:22
  28.1 1.6 %collective-permute-done.6.refs_3_ = bf16[256,128]{1,0:T(8,128)(2,1)S(1)} collective-permute-done((bf16[256,128]{1,0:T(8,128)(2,1)S(1)}, bf16[256,128]{1,0:T(8,128)(2,1)S(1)}, u32[]{:S(2)}, u32[]{:S(2)}) %collective-permute-start.6) | collective-permute-done | bytes 65568 | tf_op jit(solution)/shard_map/ppermute | solution.py:22
  29.7 6.8 %paged_attention.1 = (bf16[2,176,128]{2,1,0:T(8,128)(2,1)S(1)}, bf16[2,176,128]{2,1,0:T(8,128)(2,1)S(1)}, bf16[2,176,128]{2,1,0:T(8,128)(2,1)S(1)}, bf16[2,176,128]{2,1,0:T(8,128)(2,1)S(1)}) custom-call(s32[128]{0:T(128)S(1)} %bitcast.11, bf16[256,128]{1,0:T(8,128)(2,1)S(1)} %join.1.refs_0_.refs_2_, bf16[256,128]{1,0:T(8,128)(2,1)S(1)} %collective-permute-done.4.refs_1_, ...), custom_call_target="tpu_custom_call" | custom-call | flops 134217728 | bytes 16777216 | tf_op jit(solution)/shard_map/paged_attention/pallas_call | solution.py:546
  37.2 1.8 %collective-permute-start.8 = (bf16[2,176,128]{2,1,0:T(8,128)(2,1)S(1)}, bf16[2,176,128]{2,1,0:T(8,128)(2,1)S(1)}, u32[]{:S(2)}, u32[]{:S(2)}) collective-permute-start(bf16[2,176,128]{2,1,0:T(8,128)(2,1)S(1)} %get-tuple-element.35), channel_id=1, source_target_pairs={{0,8},{4,12},{8,0},{12,4},{16,24},{20,28},{24,16},{28,20},{1,9},{5... | collective-permute-start | bytes 270344 | tf_op jit(solution)/shard_map/ppermute | solution.py:22
  39.0 1.1 %collective-permute-start.9 = (bf16[2,176,128]{2,1,0:T(8,128)(2,1)S(1)}, bf16[2,176,128]{2,1,0:T(8,128)(2,1)S(1)}, u32[]{:S(2)}, u32[]{:S(2)}) collective-permute-start(bf16[2,176,128]{2,1,0:T(8,128)(2,1)S(1)} %get-tuple-element.36), channel_id=1, source_target_pairs={{0,12},{4,8},{8,4},{12,0},{16,28},{20,24},{24,20},{28,16},{1,13},{... | collective-permute-start | bytes 270344 | tf_op jit(solution)/shard_map/ppermute | solution.py:22
  40.1 2.0 %collective-permute-done.7.refs_1_ = bf16[2,176,128]{2,1,0:T(8,128)(2,1)S(1)} collective-permute-done((bf16[2,176,128]{2,1,0:T(8,128)(2,1)S(1)}, bf16[2,176,128]{2,1,0:T(8,128)(2,1)S(1)}, u32[]{:S(2)}, u32[]{:S(2)}) %collective-permute-start.7) | collective-permute-done | bytes 90144 | tf_op jit(solution)/shard_map/ppermute | solution.py:22
  42.1 2.3 %collective-permute-done.9.refs_3_ = bf16[2,176,128]{2,1,0:T(8,128)(2,1)S(1)} collective-permute-done((bf16[2,176,128]{2,1,0:T(8,128)(2,1)S(1)}, bf16[2,176,128]{2,1,0:T(8,128)(2,1)S(1)}, u32[]{:S(2)}, u32[]{:S(2)}) %collective-permute-start.9) | collective-permute-done | bytes 90144 | tf_op jit(solution)/shard_map/ppermute | solution.py:22
  44.9 3.2 %collective-permute-start.10 = (bf16[2,176,128]{2,1,0:T(8,128)(2,1)S(1)}, bf16[2,176,128]{2,1,0:T(8,128)(2,1)S(1)}, u32[]{:S(2)}, u32[]{:S(2)}) collective-permute-start(bf16[2,176,128]{2,1,0:T(8,128)(2,1)S(1)} %combine.1.refs_0_), channel_id=1, source_target_pairs={{0,16},{4,20},{8,24},{12,28},{16,0},{20,4},{24,8},{28,12},{1,17},{... | collective-permute-start | bytes 270344 | tf_op jit(solution)/shard_map/ppermute | solution.py:22
  48.1 3.5 %collective-permute-done.10.refs_1_ = bf16[2,176,128]{2,1,0:T(8,128)(2,1)S(1)} collective-permute-done((bf16[2,176,128]{2,1,0:T(8,128)(2,1)S(1)}, bf16[2,176,128]{2,1,0:T(8,128)(2,1)S(1)}, u32[]{:S(2)}, u32[]{:S(2)}) %collective-permute-start.10) | collective-permute-done | bytes 90144 | tf_op jit(solution)/shard_map/ppermute | solution.py:22
  52.2 2.4 %collective-permute-start.12 = (bf16[16,2048]{1,0:T(8,128)(2,1)S(1)}, bf16[16,2048]{1,0:T(8,128)(2,1)S(1)}, u32[]{:S(2)}, u32[]{:S(2)}) collective-permute-start(bf16[16,2048]{1,0:T(8,128)(2,1)S(1)} %finish.1.refs_0_), channel_id=1, source_target_pairs={{0,8},{4,12},{8,0},{12,4},{16,24},{20,28},{24,16},{28,20},{1,9},{5... | collective-permute-start | bytes 196616 | tf_op jit(solution)/shard_map/ppermute | solution.py:22
  54.6 1.0 %collective-permute-start.13 = (bf16[16,2048]{1,0:T(8,128)(2,1)S(1)}, bf16[16,2048]{1,0:T(8,128)(2,1)S(1)}, u32[]{:S(2)}, u32[]{:S(2)}) collective-permute-start(bf16[16,2048]{1,0:T(8,128)(2,1)S(1)} %finish.1.refs_0_), channel_id=1, source_target_pairs={{0,12},{4,8},{8,4},{12,0},{16,28},{20,24},{24,20},{28,16},{1,13},{... | collective-permute-start | bytes 196616 | tf_op jit(solution)/shard_map/ppermute | solution.py:22
  56.8 2.9 %collective-permute-done.13.refs_3_ = bf16[16,2048]{1,0:T(8,128)(2,1)S(1)} collective-permute-done((bf16[16,2048]{1,0:T(8,128)(2,1)S(1)}, bf16[16,2048]{1,0:T(8,128)(2,1)S(1)}, u32[]{:S(2)}, u32[]{:S(2)}) %collective-permute-start.13) | collective-permute-done | bytes 65568 | tf_op jit(solution)/shard_map/ppermute | solution.py:22
  60.6 1.5 %collective-permute-start.14 = (bf16[64,1024]{1,0:T(8,128)(2,1)S(1)}, bf16[64,1024]{1,0:T(8,128)(2,1)S(1)}, u32[]{:S(2)}, u32[]{:S(2)}) collective-permute-start(bf16[64,1024]{1,0:T(8,128)(2,1)S(1)} %project_out.1), channel_id=1, source_target_pairs={{0,2},{1,3},{2,0},{3,1},{4,6},{5,7},{6,4},{7,5},{8,10},{9,11},{10,... | collective-permute-start | bytes 393224 | tf_op jit(solution)/shard_map/ppermute | solution.py:22
  62.1 3.5 %collective-permute-done.14 = bf16[64,1024]{1,0:T(8,128)(2,1)S(1)} collective-permute-done((bf16[64,1024]{1,0:T(8,128)(2,1)S(1)}, bf16[64,1024]{1,0:T(8,128)(2,1)S(1)}, u32[]{:S(2)}, u32[]{:S(2)}) %collective-permute-start.14) | collective-permute-done | bytes 131104 | tf_op jit(solution)/shard_map/ppermute | solution.py:22
  65.7 1.5 %collective-permute-done.15 = f32[64,1024]{1,0:T(8,128)S(1)} collective-permute-done((f32[64,1024]{1,0:T(8,128)S(1)}, f32[64,1024]{1,0:T(8,128)S(1)}, u32[]{:S(2)}, u32[]{:S(2)}) %collective-permute-start.15) | collective-permute-done | bytes 262176 | tf_op jit(solution)/shard_map/ppermute | solution.py:22
  (42 shorter events, 10.5 us)
Async XLA Ops:
  0.0 0.9 %copy-start.1 = (bf16[64,1024]{1,0:T(8,128)(2,1)S(1)}, bf16[64,1024]{1,0:T(8,128)(2,1)}, u32[]{:S(2)}) copy-start(bf16[64,1024]{1,0:T(8,128)(2,1)} %hidden.1) | copy-start | bytes 393220
  3.9 8.8 %collective-permute-start = (f32[2,8,2048]{2,1,0:T(8,128)S(1)}, f32[2,8,2048]{2,1,0:T(8,128)S(1)}, u32[]{:S(2)}, u32[]{:S(2)}) collective-permute-start(f32[2,8,2048]{2,1,0:T(8,128)S(1)} %get-tuple-element.21), channel_id=1, source_target_pairs={{0,4},{4,0},{8,12},{12,8},{16,20},{20,16},{24,28},{28,24},{1,5},{5... | collective-permute-start | bytes 393224 | tf_op jit(solution)/shard_map/ppermute | solution.py:22
  6.9 6.4 %collective-permute-start.1 = (f32[2,8,2048]{2,1,0:T(8,128)S(1)}, f32[2,8,2048]{2,1,0:T(8,128)S(1)}, u32[]{:S(2)}, u32[]{:S(2)}) collective-permute-start(f32[2,8,2048]{2,1,0:T(8,128)S(1)} %get-tuple-element.22), channel_id=1, source_target_pairs={{0,8},{4,12},{8,0},{12,4},{16,24},{20,28},{24,16},{28,20},{1,9},{5... | collective-permute-start | bytes 393224 | tf_op jit(solution)/shard_map/ppermute | solution.py:22
  8.5 6.0 %collective-permute-start.2 = (f32[2,8,2048]{2,1,0:T(8,128)S(1)}, f32[2,8,2048]{2,1,0:T(8,128)S(1)}, u32[]{:S(2)}, u32[]{:S(2)}) collective-permute-start(f32[2,8,2048]{2,1,0:T(8,128)S(1)} %get-tuple-element.23), channel_id=1, source_target_pairs={{0,12},{4,8},{8,4},{12,0},{16,28},{20,24},{24,20},{28,16},{1,13},{... | collective-permute-start | bytes 393224 | tf_op jit(solution)/shard_map/ppermute | solution.py:22
  8.5 0.7 copy-start.2
  9.2 0.7 copy-start.3
  14.5 15.2 %slice-start = ((s8[8388608]{0:T(1024)(128)(4,1)}), s8[4194304]{0:T(1024)(128)(4,1)S(1)}, s32[]{:S(2)}) async-start(s8[8388608]{0:T(1024)(128)(4,1)} %bitcast.5), calls=%async_computation | async-start | bytes 8388608
  14.5 15.2 %slice-start.2 = ((s8[8388608]{0:T(1024)(128)(4,1)}), s8[4194304]{0:T(1024)(128)(4,1)S(1)}, s32[]{:S(2)}) async-start(s8[8388608]{0:T(1024)(128)(4,1)} %bitcast.7), calls=%async_computation.2 | async-start | bytes 8388608
  14.5 15.2 %slice-start.1 = ((s8[8388608]{0:T(1024)(128)(4,1)}), s8[4194304]{0:T(1024)(128)(4,1)S(1)}, s32[]{:S(2)}) async-start(s8[8388608]{0:T(1024)(128)(4,1)} %bitcast.5), calls=%async_computation.1 | async-start | bytes 8388608
  14.5 15.2 %slice-start.3 = ((s8[8388608]{0:T(1024)(128)(4,1)}), s8[4194304]{0:T(1024)(128)(4,1)S(1)}, s32[]{:S(2)}) async-start(s8[8388608]{0:T(1024)(128)(4,1)} %bitcast.7), calls=%async_computation.3 | async-start | bytes 8388608
  14.5 8.2 %collective-permute-start.3 = (f32[2,8,2048]{2,1,0:T(8,128)S(1)}, f32[2,8,2048]{2,1,0:T(8,128)S(1)}, u32[]{:S(2)}, u32[]{:S(2)}) collective-permute-start(f32[2,8,2048]{2,1,0:T(8,128)S(1)} %add_add_fusion.refs_0_), channel_id=1, source_target_pairs={{0,16},{4,20},{8,24},{12,28},{16,0},{20,4},{24,8},{28,12},{1,17},{... | collective-permute-start | bytes 393224 | tf_op jit(solution)/shard_map/ppermute | solution.py:22
  22.8 5.0 %collective-permute-start.4 = (bf16[256,128]{1,0:T(8,128)(2,1)S(1)}, bf16[256,128]{1,0:T(8,128)(2,1)S(1)}, u32[]{:S(2)}, u32[]{:S(2)}) collective-permute-start(bf16[256,128]{1,0:T(8,128)(2,1)S(1)} %join.1.refs_0_.refs_2_), channel_id=1, source_target_pairs={{0,4},{4,0},{8,12},{12,8},{16,20},{20,16},{24,28},{28,24},{1,5},{5... | collective-permute-start | bytes 196616 | tf_op jit(solution)/shard_map/ppermute | solution.py:22
  23.8 4.3 %collective-permute-start.5 = (bf16[256,128]{1,0:T(8,128)(2,1)S(1)}, bf16[256,128]{1,0:T(8,128)(2,1)S(1)}, u32[]{:S(2)}, u32[]{:S(2)}) collective-permute-start(bf16[256,128]{1,0:T(8,128)(2,1)S(1)} %join.1.refs_0_.refs_2_), channel_id=1, source_target_pairs={{0,8},{4,12},{8,0},{12,4},{16,24},{20,28},{24,16},{28,20},{1,9},{5... | collective-permute-start | bytes 196616 | tf_op jit(solution)/shard_map/ppermute | solution.py:22
  24.5 5.2 %collective-permute-start.6 = (bf16[256,128]{1,0:T(8,128)(2,1)S(1)}, bf16[256,128]{1,0:T(8,128)(2,1)S(1)}, u32[]{:S(2)}, u32[]{:S(2)}) collective-permute-start(bf16[256,128]{1,0:T(8,128)(2,1)S(1)} %join.1.refs_0_.refs_2_), channel_id=1, source_target_pairs={{0,12},{4,8},{8,4},{12,0},{16,28},{20,24},{24,20},{28,16},{1,13},{... | collective-permute-start | bytes 196616 | tf_op jit(solution)/shard_map/ppermute | solution.py:22
  29.7 30.0 %copy-start = (bf16[2048,1024]{1,0:T(8,128)(2,1)S(1)}, bf16[2048,1024]{1,0:T(8,128)(2,1)}, u32[]{:S(2)}) copy-start(bf16[2048,1024]{1,0:T(8,128)(2,1)} %refs_4_.1) | copy-start | bytes 12582916
  36.5 5.5 %collective-permute-start.7 = (bf16[2,176,128]{2,1,0:T(8,128)(2,1)S(1)}, bf16[2,176,128]{2,1,0:T(8,128)(2,1)S(1)}, u32[]{:S(2)}, u32[]{:S(2)}) collective-permute-start(bf16[2,176,128]{2,1,0:T(8,128)(2,1)S(1)} %get-tuple-element.34), channel_id=1, source_target_pairs={{0,4},{4,0},{8,12},{12,8},{16,20},{20,16},{24,28},{28,24},{1,5},{5... | collective-permute-start | bytes 270344 | tf_op jit(solution)/shard_map/ppermute | solution.py:22
  37.2 4.9 %collective-permute-start.8 = (bf16[2,176,128]{2,1,0:T(8,128)(2,1)S(1)}, bf16[2,176,128]{2,1,0:T(8,128)(2,1)S(1)}, u32[]{:S(2)}, u32[]{:S(2)}) collective-permute-start(bf16[2,176,128]{2,1,0:T(8,128)(2,1)S(1)} %get-tuple-element.35), channel_id=1, source_target_pairs={{0,8},{4,12},{8,0},{12,4},{16,24},{20,28},{24,16},{28,20},{1,9},{5... | collective-permute-start | bytes 270344 | tf_op jit(solution)/shard_map/ppermute | solution.py:22
  39.0 5.4 %collective-permute-start.9 = (bf16[2,176,128]{2,1,0:T(8,128)(2,1)S(1)}, bf16[2,176,128]{2,1,0:T(8,128)(2,1)S(1)}, u32[]{:S(2)}, u32[]{:S(2)}) collective-permute-start(bf16[2,176,128]{2,1,0:T(8,128)(2,1)S(1)} %get-tuple-element.36), channel_id=1, source_target_pairs={{0,12},{4,8},{8,4},{12,0},{16,28},{20,24},{24,20},{28,16},{1,13},{... | collective-permute-start | bytes 270344 | tf_op jit(solution)/shard_map/ppermute | solution.py:22
  44.9 6.7 %collective-permute-start.10 = (bf16[2,176,128]{2,1,0:T(8,128)(2,1)S(1)}, bf16[2,176,128]{2,1,0:T(8,128)(2,1)S(1)}, u32[]{:S(2)}, u32[]{:S(2)}) collective-permute-start(bf16[2,176,128]{2,1,0:T(8,128)(2,1)S(1)} %combine.1.refs_0_), channel_id=1, source_target_pairs={{0,16},{4,20},{8,24},{12,28},{16,0},{20,4},{24,8},{28,12},{1,17},{... | collective-permute-start | bytes 270344 | tf_op jit(solution)/shard_map/ppermute | solution.py:22
  52.0 4.3 %collective-permute-start.11 = (bf16[16,2048]{1,0:T(8,128)(2,1)S(1)}, bf16[16,2048]{1,0:T(8,128)(2,1)S(1)}, u32[]{:S(2)}, u32[]{:S(2)}) collective-permute-start(bf16[16,2048]{1,0:T(8,128)(2,1)S(1)} %finish.1.refs_0_), channel_id=1, source_target_pairs={{0,4},{4,0},{8,12},{12,8},{16,20},{20,16},{24,28},{28,24},{1,5},{5... | collective-permute-start | bytes 196616 | tf_op jit(solution)/shard_map/ppermute | solution.py:22
  52.2 4.6 %collective-permute-start.12 = (bf16[16,2048]{1,0:T(8,128)(2,1)S(1)}, bf16[16,2048]{1,0:T(8,128)(2,1)S(1)}, u32[]{:S(2)}, u32[]{:S(2)}) collective-permute-start(bf16[16,2048]{1,0:T(8,128)(2,1)S(1)} %finish.1.refs_0_), channel_id=1, source_target_pairs={{0,8},{4,12},{8,0},{12,4},{16,24},{20,28},{24,16},{28,20},{1,9},{5... | collective-permute-start | bytes 196616 | tf_op jit(solution)/shard_map/ppermute | solution.py:22
  54.6 5.2 %collective-permute-start.13 = (bf16[16,2048]{1,0:T(8,128)(2,1)S(1)}, bf16[16,2048]{1,0:T(8,128)(2,1)S(1)}, u32[]{:S(2)}, u32[]{:S(2)}) collective-permute-start(bf16[16,2048]{1,0:T(8,128)(2,1)S(1)} %finish.1.refs_0_), channel_id=1, source_target_pairs={{0,12},{4,8},{8,4},{12,0},{16,28},{20,24},{24,20},{28,16},{1,13},{... | collective-permute-start | bytes 196616 | tf_op jit(solution)/shard_map/ppermute | solution.py:22
  60.6 5.0 %collective-permute-start.14 = (bf16[64,1024]{1,0:T(8,128)(2,1)S(1)}, bf16[64,1024]{1,0:T(8,128)(2,1)S(1)}, u32[]{:S(2)}, u32[]{:S(2)}) collective-permute-start(bf16[64,1024]{1,0:T(8,128)(2,1)S(1)} %project_out.1), channel_id=1, source_target_pairs={{0,2},{1,3},{2,0},{3,1},{4,6},{5,7},{6,4},{7,5},{8,10},{9,11},{10,... | collective-permute-start | bytes 393224 | tf_op jit(solution)/shard_map/ppermute | solution.py:22
  65.7 1.6 %collective-permute-start.15 = (f32[64,1024]{1,0:T(8,128)S(1)}, f32[64,1024]{1,0:T(8,128)S(1)}, u32[]{:S(2)}, u32[]{:S(2)}) collective-permute-start(f32[64,1024]{1,0:T(8,128)S(1)} %convert_add_fusion), channel_id=1, source_target_pairs={{0,1},{1,0},{2,3},{3,2},{4,5},{5,4},{6,7},{7,6},{8,9},{9,8},{10,11... | collective-permute-start | bytes 786440 | tf_op jit(solution)/shard_map/ppermute | solution.py:22
  (3 other events, 2.0 us)

commit v10 on v9

--- a/solution.py
+++ b/solution.py
@@ -20,6 +20,20 @@
 
 def swap(x, axis, n, mask):
     return lax.ppermute(x, axis, [(j, j ^ mask) for j in range(n)])
+
+
+def way_order(size):
+    return [0, size - 1, *range(1, size - 1)]
+
+
+def swap_all(parts, axis, n, shift):
+    return [
+        swap(parts[d], axis, n, d << shift) if d else parts[0] for d in way_order(len(parts))
+    ]
+
+
+def in_order(parts):
+    return [parts[i] for i in sorted(range(len(parts)), key=way_order(len(parts)).__getitem__)]
 
 
 def bit_groups(n):
@@ -49,10 +63,10 @@
     for shift, size in lower_groups(n):
         if shift:
             parts = [pick_digit(x, axis, shift, size, d) for d in range(size)]
-        sent = [swap(parts[d], axis, n, d << shift) for d in range(1, size)]
+        got = swap_all(parts, axis, n, shift)
         if shift == 0:
-            sent, beside = lax.optimization_barrier((sent, beside))
-        x = sum(sent, parts[0])
+            got, beside = lax.optimization_barrier((got, beside))
+        x = sum(got[1:], got[0])
     shift, size = last_group(n)
     return [x] + [swap(x, axis, n, d << shift) for d in range(1, size)], beside
 
@@ -60,8 +74,8 @@
 def gather_relative(x, axis, n):
     parts = [x]
     for shift, size in reversed(lower_groups(n)):
-        x = jnp.concatenate(parts, axis=0) if len(parts) > 1 else parts[0]
-        parts = [x] + [swap(x, axis, n, d << shift) for d in range(1, size)]
+        x = jnp.concatenate(in_order(parts), axis=0) if len(parts) > 1 else parts[0]
+        parts = swap_all([x] * size, axis, n, shift)
     return parts
 
 
@@ -175,7 +189,7 @@
 
 def output_kernel(ways, seq_size, me, *refs):
     parts, (w_out, rounded, out) = refs[:ways], refs[ways:]
-    rows = jnp.concatenate([part[...] for part in parts], axis=0)
+    rows = jnp.concatenate([part[...] for part in in_order(parts)], axis=0)
     total = jnp.dot(rows, w_out[...], preferred_element_type=jnp.float32)
     blocks = gathered_blocks(me[0], seq_size)
     mine = rows.shape[0] // len(blocks)
@@ -246,7 +260,7 @@
     blocks = outs[0].shape[0]
     step_chunks = 4
 
-    for d, part in enumerate(queries):
+    for d, part in enumerate(in_order(queries)):
         rows = part[...]
         low_head = lax.broadcasted_iota(jnp.int32, rows.shape, 0) % heads < group
         zero = jnp.zeros_like(rows)
@@ -572,9 +586,7 @@
     for shift, size in lower_groups(seq_size):
         if shift:
             totals = [pick_digit(totals, "seq", shift, size, d) for d in range(size)]
-        parts = [
-            swap(part, "seq", seq_size, d << shift) if d else part for d, part in enumerate(totals)
-        ]
+        parts = swap_all(totals, "seq", seq_size, shift)
         totals = pl.pallas_call(
             functools.partial(combine_kernel, mine),
             out_shape=jax.ShapeDtypeStruct(parts[0].shape, jnp.bfloat16),

time: 68.2 us -> 66.4 us (0.974)
  starting transfers between devices: 22.8 us -> 21.9 us
  waiting for transfers between devices: 27.5 us -> 26.7 us
    ppermute x16, starting transfers between devices: 22.8 us -> 21.9 us  [swap(): return lax.ppermute(x, axis, [(j, j ^ mask) for j in range(n)])]
    ppermute x16, waiting for transfers between devices: 27.5 us -> 26.7 us  [swap(): return lax.ppermute(x, axis, [(j, j ^ mask) for j in range(n)])]
where the time goes in v10:
time: 66.4 us; the launch traced here: 66.2 us
  waiting for transfers between devices  26.7 us (40%)
  starting transfers between devices  21.9 us (33%)
  Pallas kernels  12.5 us (19%)
  local copies, waits for them, and re-layouts  4.25 us (6%)
  other arithmetic  0.76 us (1%)
    ppermute x16, waiting for transfers between devices, swap(): return lax.ppermute(x, axis, [(j, j ^ mask) for j in range(n)])  26.7 us
    ppermute x16, starting transfers between devices, swap(): return lax.ppermute(x, axis, [(j, j ^ mask) for j in range(n)])  21.9 us
    pallas_call x1, Pallas kernels, body(): pl.pallas_call(functools.partial(attention_kernel, ways, mine), out_shape...  6.79 us
    unnamed x22, local copies, waits for them, and re-layouts  4.25 us
    pallas_call x1, Pallas kernels, body(): pl.pallas_call(functools.partial(project_kernel, ways), out_shape=[part_s...  2.98 us
  transfers between devices with their start and end apart: 16, of which 14 were waited for; matrix products, arithmetic and copies ran while one was open for 0% of the time, Pallas kernels for 1%

profile of v10, /device:TPU:0, one launch (start us, length us, event | category | flops | bytes accessed | tf_op | source)
XLA Modules:
  0.0 66.2 jit_solution(11466390519626626860)
XLA Ops:
  0.0 0.9 %copy-done.1 = bf16[64,1024]{1,0:T(8,128)(2,1)S(1)} copy-done((bf16[64,1024]{1,0:T(8,128)(2,1)S(1)}, bf16[64,1024]{1,0:T(8,128)(2,1)}, u32[]{:S(2)}) %copy-start.1) | copy-done | bytes 131096
  0.9 3.0 %project.1 = (f32[2,8,2048]{2,1,0:T(8,128)S(1)}, f32[2,8,2048]{2,1,0:T(8,128)S(1)}, f32[2,8,2048]{2,1,0:T(8,128)S(1)}, f32[2,8,2048]{2,1,0:T(8,128)S(1)}, f32[64,512]{1,0:T(8,128)S(1)}) custom-call(s32[1]{0:T(128)} %bitcast.me, bf16[64,1024]{1,0:T(8,128)(2,1)S(1)} %copy-done.1, bf16[1024,2048]{1,0:T(8,128)(2,1)} %w_query.1, bf16[1024,512]{1,0:T(8,128)(2,1)} %w_keyval.1), custom_call_target="tpu_custom_call" | custom-call | tf_op jit(solution)/shard_map/project/pallas_call | solution.py:531
  3.9 4.0 %collective-permute-start = (f32[2,8,2048]{2,1,0:T(8,128)S(1)}, f32[2,8,2048]{2,1,0:T(8,128)S(1)}, u32[]{:S(2)}, u32[]{:S(2)}) collective-permute-start(f32[2,8,2048]{2,1,0:T(8,128)S(1)} %get-tuple-element.23), channel_id=1, source_target_pairs={{0,12},{4,8},{8,4},{12,0},{16,28},{20,24},{24,20},{28,16},{1,13},{... | collective-permute-start | bytes 393224 | tf_op jit(solution)/shard_map/ppermute | solution.py:22
  11.9 0.9 %page_table.1 = (f32[64,128]{1,0:T(8,128)S(1)}, s32[1,128]{1,0:T(1,128)S(1)}) custom-call(s32[1]{0:T(128)} %bitcast.me, s32[64]{0:T(128)S(1)} %copy-done.4, s32[64]{0:T(128)S(1)} %copy-done.5, s32[1,128]{1,0:T(1,128)S(1)} %bitcast.12, f32[2,128]{1,0:T(2,128)S(1)} %bitcast.9, f32[2,128]{1,0:T(2,128)S(1)} %bitcast.10), custom_call_target="tpu_custom_call" | custom-call | tf_op jit(solution)/shard_map/page_table/pallas_call | solution.py:515
  12.8 1.5 %collective-permute-done.1 = f32[2,8,2048]{2,1,0:T(8,128)S(1)} collective-permute-done((f32[2,8,2048]{2,1,0:T(8,128)S(1)}, f32[2,8,2048]{2,1,0:T(8,128)S(1)}, u32[]{:S(2)}, u32[]{:S(2)}) %collective-permute-start.1) | collective-permute-done | bytes 131104 | tf_op jit(solution)/shard_map/ppermute | solution.py:22
  14.5 2.7 %collective-permute-start.3 = (f32[2,8,2048]{2,1,0:T(8,128)S(1)}, f32[2,8,2048]{2,1,0:T(8,128)S(1)}, u32[]{:S(2)}, u32[]{:S(2)}) collective-permute-start(f32[2,8,2048]{2,1,0:T(8,128)S(1)} %add_add_fusion.refs_0_), channel_id=1, source_target_pairs={{0,16},{4,20},{8,24},{12,28},{16,0},{20,4},{24,8},{28,12},{1,17},{... | collective-permute-start | bytes 393224 | tf_op jit(solution)/shard_map/ppermute | solution.py:22
  17.1 6.4 %collective-permute-done.3.refs_1_ = f32[2,8,2048]{2,1,0:T(8,128)S(1)} collective-permute-done((f32[2,8,2048]{2,1,0:T(8,128)S(1)}, f32[2,8,2048]{2,1,0:T(8,128)S(1)}, u32[]{:S(2)}, u32[]{:S(2)}) %collective-permute-start.3) | collective-permute-done | bytes 131104 | tf_op jit(solution)/shard_map/ppermute | solution.py:22
  23.9 2.0 %collective-permute-start.5 = (bf16[256,128]{1,0:T(8,128)(2,1)S(1)}, bf16[256,128]{1,0:T(8,128)(2,1)S(1)}, u32[]{:S(2)}, u32[]{:S(2)}) collective-permute-start(bf16[256,128]{1,0:T(8,128)(2,1)S(1)} %join.1.refs_0_.refs_2_), channel_id=1, source_target_pairs={{0,4},{4,0},{8,12},{12,8},{16,20},{20,16},{24,28},{28,24},{1,5},{5... | collective-permute-start | bytes 196616 | tf_op jit(solution)/shard_map/ppermute | solution.py:22
  25.9 1.3 %collective-permute-start.6 = (bf16[256,128]{1,0:T(8,128)(2,1)S(1)}, bf16[256,128]{1,0:T(8,128)(2,1)S(1)}, u32[]{:S(2)}, u32[]{:S(2)}) collective-permute-start(bf16[256,128]{1,0:T(8,128)(2,1)S(1)} %join.1.refs_0_.refs_2_), channel_id=1, source_target_pairs={{0,8},{4,12},{8,0},{12,4},{16,24},{20,28},{24,16},{28,20},{1,9},{5... | collective-permute-start | bytes 196616 | tf_op jit(solution)/shard_map/ppermute | solution.py:22
  27.2 1.9 %collective-permute-done.4.refs_1_ = bf16[256,128]{1,0:T(8,128)(2,1)S(1)} collective-permute-done((bf16[256,128]{1,0:T(8,128)(2,1)S(1)}, bf16[256,128]{1,0:T(8,128)(2,1)S(1)}, u32[]{:S(2)}, u32[]{:S(2)}) %collective-permute-start.4) | collective-permute-done | bytes 65568 | tf_op jit(solution)/shard_map/ppermute | solution.py:22
  29.1 1.1 %collective-permute-done.6.refs_3_ = bf16[256,128]{1,0:T(8,128)(2,1)S(1)} collective-permute-done((bf16[256,128]{1,0:T(8,128)(2,1)S(1)}, bf16[256,128]{1,0:T(8,128)(2,1)S(1)}, u32[]{:S(2)}, u32[]{:S(2)}) %collective-permute-start.6) | collective-permute-done | bytes 65568 | tf_op jit(solution)/shard_map/ppermute | solution.py:22
  30.2 6.8 %paged_attention.1 = (bf16[2,176,128]{2,1,0:T(8,128)(2,1)S(1)}, bf16[2,176,128]{2,1,0:T(8,128)(2,1)S(1)}, bf16[2,176,128]{2,1,0:T(8,128)(2,1)S(1)}, bf16[2,176,128]{2,1,0:T(8,128)(2,1)S(1)}) custom-call(s32[128]{0:T(128)S(1)} %bitcast.11, bf16[256,128]{1,0:T(8,128)(2,1)S(1)} %join.1.refs_0_.refs_2_, bf16[256,128]{1,0:T(8,128)(2,1)S(1)} %collective-permute-done.4.refs_1_, ...), custom_call_target="tpu_custom_call" | custom-call | flops 134217728 | bytes 16777216 | tf_op jit(solution)/shard_map/paged_attention/pallas_call | solution.py:560
  37.0 1.6 %collective-permute-start.7 = (bf16[2,176,128]{2,1,0:T(8,128)(2,1)S(1)}, bf16[2,176,128]{2,1,0:T(8,128)(2,1)S(1)}, u32[]{:S(2)}, u32[]{:S(2)}) collective-permute-start(bf16[2,176,128]{2,1,0:T(8,128)(2,1)S(1)} %get-tuple-element.36), channel_id=1, source_target_pairs={{0,12},{4,8},{8,4},{12,0},{16,28},{20,24},{24,20},{28,16},{1,13},{... | collective-permute-start | bytes 270344 | tf_op jit(solution)/shard_map/ppermute | solution.py:22
  38.6 1.2 %collective-permute-start.8 = (bf16[2,176,128]{2,1,0:T(8,128)(2,1)S(1)}, bf16[2,176,128]{2,1,0:T(8,128)(2,1)S(1)}, u32[]{:S(2)}, u32[]{:S(2)}) collective-permute-start(bf16[2,176,128]{2,1,0:T(8,128)(2,1)S(1)} %get-tuple-element.37), channel_id=1, source_target_pairs={{0,4},{4,0},{8,12},{12,8},{16,20},{20,16},{24,28},{28,24},{1,5},{5... | collective-permute-start | bytes 270344 | tf_op jit(solution)/shard_map/ppermute | solution.py:22
  40.6 2.3 %collective-permute-done.7.refs_1_ = bf16[2,176,128]{2,1,0:T(8,128)(2,1)S(1)} collective-permute-done((bf16[2,176,128]{2,1,0:T(8,128)(2,1)S(1)}, bf16[2,176,128]{2,1,0:T(8,128)(2,1)S(1)}, u32[]{:S(2)}, u32[]{:S(2)}) %collective-permute-start.7) | collective-permute-done | bytes 90144 | tf_op jit(solution)/shard_map/ppermute | solution.py:22
  42.8 0.9 %collective-permute-done.8.refs_2_ = bf16[2,176,128]{2,1,0:T(8,128)(2,1)S(1)} collective-permute-done((bf16[2,176,128]{2,1,0:T(8,128)(2,1)S(1)}, bf16[2,176,128]{2,1,0:T(8,128)(2,1)S(1)}, u32[]{:S(2)}, u32[]{:S(2)}) %collective-permute-start.8) | collective-permute-done | bytes 90144 | tf_op jit(solution)/shard_map/ppermute | solution.py:22
  44.8 2.3 %collective-permute-start.10 = (bf16[2,176,128]{2,1,0:T(8,128)(2,1)S(1)}, bf16[2,176,128]{2,1,0:T(8,128)(2,1)S(1)}, u32[]{:S(2)}, u32[]{:S(2)}) collective-permute-start(bf16[2,176,128]{2,1,0:T(8,128)(2,1)S(1)} %combine.1.refs_0_), channel_id=1, source_target_pairs={{0,16},{4,20},{8,24},{12,28},{16,0},{20,4},{24,8},{28,12},{1,17},{... | collective-permute-start | bytes 270344 | tf_op jit(solution)/shard_map/ppermute | solution.py:22
  47.1 4.2 %collective-permute-done.10.refs_1_ = bf16[2,176,128]{2,1,0:T(8,128)(2,1)S(1)} collective-permute-done((bf16[2,176,128]{2,1,0:T(8,128)(2,1)S(1)}, bf16[2,176,128]{2,1,0:T(8,128)(2,1)S(1)}, u32[]{:S(2)}, u32[]{:S(2)}) %collective-permute-start.10) | collective-permute-done | bytes 90144 | tf_op jit(solution)/shard_map/ppermute | solution.py:22
  52.2 1.5 %collective-permute-start.12 = (bf16[16,2048]{1,0:T(8,128)(2,1)S(1)}, bf16[16,2048]{1,0:T(8,128)(2,1)S(1)}, u32[]{:S(2)}, u32[]{:S(2)}) collective-permute-start(bf16[16,2048]{1,0:T(8,128)(2,1)S(1)} %finish.1.refs_0_), channel_id=1, source_target_pairs={{0,4},{4,0},{8,12},{12,8},{16,20},{20,16},{24,28},{28,24},{1,5},{5... | collective-permute-start | bytes 196616 | tf_op jit(solution)/shard_map/ppermute | solution.py:22
  53.7 1.6 %collective-permute-start.13 = (bf16[16,2048]{1,0:T(8,128)(2,1)S(1)}, bf16[16,2048]{1,0:T(8,128)(2,1)S(1)}, u32[]{:S(2)}, u32[]{:S(2)}) collective-permute-start(bf16[16,2048]{1,0:T(8,128)(2,1)S(1)} %finish.1.refs_0_), channel_id=1, source_target_pairs={{0,8},{4,12},{8,0},{12,4},{16,24},{20,28},{24,16},{28,20},{1,9},{5... | collective-permute-start | bytes 196616 | tf_op jit(solution)/shard_map/ppermute | solution.py:22
  55.3 1.8 %collective-permute-done.11.refs_1_ = bf16[16,2048]{1,0:T(8,128)(2,1)S(1)} collective-permute-done((bf16[16,2048]{1,0:T(8,128)(2,1)S(1)}, bf16[16,2048]{1,0:T(8,128)(2,1)S(1)}, u32[]{:S(2)}, u32[]{:S(2)}) %collective-permute-start.11) | collective-permute-done | bytes 65568 | tf_op jit(solution)/shard_map/ppermute | solution.py:22
  58.8 1.6 %collective-permute-start.14 = (bf16[64,1024]{1,0:T(8,128)(2,1)S(1)}, bf16[64,1024]{1,0:T(8,128)(2,1)S(1)}, u32[]{:S(2)}, u32[]{:S(2)}) collective-permute-start(bf16[64,1024]{1,0:T(8,128)(2,1)S(1)} %project_out.1), channel_id=1, source_target_pairs={{0,2},{1,3},{2,0},{3,1},{4,6},{5,7},{6,4},{7,5},{8,10},{9,11},{10,... | collective-permute-start | bytes 393224 | tf_op jit(solution)/shard_map/ppermute | solution.py:22
  60.4 3.5 %collective-permute-done.14 = bf16[64,1024]{1,0:T(8,128)(2,1)S(1)} collective-permute-done((bf16[64,1024]{1,0:T(8,128)(2,1)S(1)}, bf16[64,1024]{1,0:T(8,128)(2,1)S(1)}, u32[]{:S(2)}, u32[]{:S(2)}) %collective-permute-start.14) | collective-permute-done | bytes 131104 | tf_op jit(solution)/shard_map/ppermute | solution.py:22
  64.0 1.5 %collective-permute-done.15 = f32[64,1024]{1,0:T(8,128)S(1)} collective-permute-done((f32[64,1024]{1,0:T(8,128)S(1)}, f32[64,1024]{1,0:T(8,128)S(1)}, u32[]{:S(2)}, u32[]{:S(2)}) %collective-permute-start.15) | collective-permute-done | bytes 262176 | tf_op jit(solution)/shard_map/ppermute | solution.py:22
  (42 shorter events, 9.9 us)
Async XLA Ops:
  0.0 0.9 %copy-start.1 = (bf16[64,1024]{1,0:T(8,128)(2,1)S(1)}, bf16[64,1024]{1,0:T(8,128)(2,1)}, u32[]{:S(2)}) copy-start(bf16[64,1024]{1,0:T(8,128)(2,1)} %hidden.1) | copy-start | bytes 393220
  3.9 8.9 %collective-permute-start = (f32[2,8,2048]{2,1,0:T(8,128)S(1)}, f32[2,8,2048]{2,1,0:T(8,128)S(1)}, u32[]{:S(2)}, u32[]{:S(2)}) collective-permute-start(f32[2,8,2048]{2,1,0:T(8,128)S(1)} %get-tuple-element.23), channel_id=1, source_target_pairs={{0,12},{4,8},{8,4},{12,0},{16,28},{20,24},{24,20},{28,16},{1,13},{... | collective-permute-start | bytes 393224 | tf_op jit(solution)/shard_map/ppermute | solution.py:22
  7.9 6.3 %collective-permute-start.1 = (f32[2,8,2048]{2,1,0:T(8,128)S(1)}, f32[2,8,2048]{2,1,0:T(8,128)S(1)}, u32[]{:S(2)}, u32[]{:S(2)}) collective-permute-start(f32[2,8,2048]{2,1,0:T(8,128)S(1)} %get-tuple-element.24), channel_id=1, source_target_pairs={{0,4},{4,0},{8,12},{12,8},{16,20},{20,16},{24,28},{28,24},{1,5},{5... | collective-permute-start | bytes 393224 | tf_op jit(solution)/shard_map/ppermute | solution.py:22
  8.4 6.0 %collective-permute-start.2 = (f32[2,8,2048]{2,1,0:T(8,128)S(1)}, f32[2,8,2048]{2,1,0:T(8,128)S(1)}, u32[]{:S(2)}, u32[]{:S(2)}) collective-permute-start(f32[2,8,2048]{2,1,0:T(8,128)S(1)} %get-tuple-element.25), channel_id=1, source_target_pairs={{0,8},{4,12},{8,0},{12,4},{16,24},{20,28},{24,16},{28,20},{1,9},{5... | collective-permute-start | bytes 393224 | tf_op jit(solution)/shard_map/ppermute | solution.py:22
  8.6 0.7 %copy-start.2 = (f32[128,2]{0,1:T(2,128)S(1)}, f32[128,2]{0,1:T(2,128)}, u32[]{:S(2)}) copy-start(f32[128,2]{0,1:T(2,128)} %param.17) | copy-start | bytes 3076
  9.3 0.7 %copy-start.3 = (f32[128,2]{0,1:T(2,128)S(1)}, f32[128,2]{0,1:T(2,128)}, u32[]{:S(2)}) copy-start(f32[128,2]{0,1:T(2,128)} %param.18) | copy-start | bytes 3076
  14.4 15.8 %slice-start = ((s8[8388608]{0:T(1024)(128)(4,1)}), s8[4194304]{0:T(1024)(128)(4,1)S(1)}, s32[]{:S(2)}) async-start(s8[8388608]{0:T(1024)(128)(4,1)} %bitcast.5), calls=%async_computation | async-start | bytes 8388608
  14.4 15.8 %slice-start.2 = ((s8[8388608]{0:T(1024)(128)(4,1)}), s8[4194304]{0:T(1024)(128)(4,1)S(1)}, s32[]{:S(2)}) async-start(s8[8388608]{0:T(1024)(128)(4,1)} %bitcast.7), calls=%async_computation.2 | async-start | bytes 8388608
  14.4 15.7 %slice-start.1 = ((s8[8388608]{0:T(1024)(128)(4,1)}), s8[4194304]{0:T(1024)(128)(4,1)S(1)}, s32[]{:S(2)}) async-start(s8[8388608]{0:T(1024)(128)(4,1)} %bitcast.5), calls=%async_computation.1 | async-start | bytes 8388608
  14.5 15.7 %slice-start.3 = ((s8[8388608]{0:T(1024)(128)(4,1)}), s8[4194304]{0:T(1024)(128)(4,1)S(1)}, s32[]{:S(2)}) async-start(s8[8388608]{0:T(1024)(128)(4,1)} %bitcast.7), calls=%async_computation.3 | async-start | bytes 8388608
  14.5 9.1 %collective-permute-start.3 = (f32[2,8,2048]{2,1,0:T(8,128)S(1)}, f32[2,8,2048]{2,1,0:T(8,128)S(1)}, u32[]{:S(2)}, u32[]{:S(2)}) collective-permute-start(f32[2,8,2048]{2,1,0:T(8,128)S(1)} %add_add_fusion.refs_0_), channel_id=1, source_target_pairs={{0,16},{4,20},{8,24},{12,28},{16,0},{20,4},{24,8},{28,12},{1,17},{... | collective-permute-start | bytes 393224 | tf_op jit(solution)/shard_map/ppermute | solution.py:22
  23.6 5.5 %collective-permute-start.4 = (bf16[256,128]{1,0:T(8,128)(2,1)S(1)}, bf16[256,128]{1,0:T(8,128)(2,1)S(1)}, u32[]{:S(2)}, u32[]{:S(2)}) collective-permute-start(bf16[256,128]{1,0:T(8,128)(2,1)S(1)} %join.1.refs_0_.refs_2_), channel_id=1, source_target_pairs={{0,12},{4,8},{8,4},{12,0},{16,28},{20,24},{24,20},{28,16},{1,13},{... | collective-permute-start | bytes 196616 | tf_op jit(solution)/shard_map/ppermute | solution.py:22
  23.9 5.2 %collective-permute-start.5 = (bf16[256,128]{1,0:T(8,128)(2,1)S(1)}, bf16[256,128]{1,0:T(8,128)(2,1)S(1)}, u32[]{:S(2)}, u32[]{:S(2)}) collective-permute-start(bf16[256,128]{1,0:T(8,128)(2,1)S(1)} %join.1.refs_0_.refs_2_), channel_id=1, source_target_pairs={{0,4},{4,0},{8,12},{12,8},{16,20},{20,16},{24,28},{28,24},{1,5},{5... | collective-permute-start | bytes 196616 | tf_op jit(solution)/shard_map/ppermute | solution.py:22
  25.9 4.3 %collective-permute-start.6 = (bf16[256,128]{1,0:T(8,128)(2,1)S(1)}, bf16[256,128]{1,0:T(8,128)(2,1)S(1)}, u32[]{:S(2)}, u32[]{:S(2)}) collective-permute-start(bf16[256,128]{1,0:T(8,128)(2,1)S(1)} %join.1.refs_0_.refs_2_), channel_id=1, source_target_pairs={{0,8},{4,12},{8,0},{12,4},{16,24},{20,28},{24,16},{28,20},{1,9},{5... | collective-permute-start | bytes 196616 | tf_op jit(solution)/shard_map/ppermute | solution.py:22
  30.2 27.7 %copy-start = (bf16[2048,1024]{1,0:T(8,128)(2,1)S(1)}, bf16[2048,1024]{1,0:T(8,128)(2,1)}, u32[]{:S(2)}) copy-start(bf16[2048,1024]{1,0:T(8,128)(2,1)} %refs_4_.1) | copy-start | bytes 12582916
  37.0 5.8 %collective-permute-start.7 = (bf16[2,176,128]{2,1,0:T(8,128)(2,1)S(1)}, bf16[2,176,128]{2,1,0:T(8,128)(2,1)S(1)}, u32[]{:S(2)}, u32[]{:S(2)}) collective-permute-start(bf16[2,176,128]{2,1,0:T(8,128)(2,1)S(1)} %get-tuple-element.36), channel_id=1, source_target_pairs={{0,12},{4,8},{8,4},{12,0},{16,28},{20,24},{24,20},{28,16},{1,13},{... | collective-permute-start | bytes 270344 | tf_op jit(solution)/shard_map/ppermute | solution.py:22
  38.6 5.1 %collective-permute-start.8 = (bf16[2,176,128]{2,1,0:T(8,128)(2,1)S(1)}, bf16[2,176,128]{2,1,0:T(8,128)(2,1)S(1)}, u32[]{:S(2)}, u32[]{:S(2)}) collective-permute-start(bf16[2,176,128]{2,1,0:T(8,128)(2,1)S(1)} %get-tuple-element.37), channel_id=1, source_target_pairs={{0,4},{4,0},{8,12},{12,8},{16,20},{20,16},{24,28},{28,24},{1,5},{5... | collective-permute-start | bytes 270344 | tf_op jit(solution)/shard_map/ppermute | solution.py:22
  39.8 4.5 %collective-permute-start.9 = (bf16[2,176,128]{2,1,0:T(8,128)(2,1)S(1)}, bf16[2,176,128]{2,1,0:T(8,128)(2,1)S(1)}, u32[]{:S(2)}, u32[]{:S(2)}) collective-permute-start(bf16[2,176,128]{2,1,0:T(8,128)(2,1)S(1)} %get-tuple-element.38), channel_id=1, source_target_pairs={{0,8},{4,12},{8,0},{12,4},{16,24},{20,28},{24,16},{28,20},{1,9},{5... | collective-permute-start | bytes 270344 | tf_op jit(solution)/shard_map/ppermute | solution.py:22
  44.8 6.5 %collective-permute-start.10 = (bf16[2,176,128]{2,1,0:T(8,128)(2,1)S(1)}, bf16[2,176,128]{2,1,0:T(8,128)(2,1)S(1)}, u32[]{:S(2)}, u32[]{:S(2)}) collective-permute-start(bf16[2,176,128]{2,1,0:T(8,128)(2,1)S(1)} %combine.1.refs_0_), channel_id=1, source_target_pairs={{0,16},{4,20},{8,24},{12,28},{16,0},{20,4},{24,8},{28,12},{1,17},{... | collective-permute-start | bytes 270344 | tf_op jit(solution)/shard_map/ppermute | solution.py:22
  51.7 5.3 %collective-permute-start.11 = (bf16[16,2048]{1,0:T(8,128)(2,1)S(1)}, bf16[16,2048]{1,0:T(8,128)(2,1)S(1)}, u32[]{:S(2)}, u32[]{:S(2)}) collective-permute-start(bf16[16,2048]{1,0:T(8,128)(2,1)S(1)} %finish.1.refs_0_), channel_id=1, source_target_pairs={{0,12},{4,8},{8,4},{12,0},{16,28},{20,24},{24,20},{28,16},{1,13},{... | collective-permute-start | bytes 196616 | tf_op jit(solution)/shard_map/ppermute | solution.py:22
  52.2 5.0 %collective-permute-start.12 = (bf16[16,2048]{1,0:T(8,128)(2,1)S(1)}, bf16[16,2048]{1,0:T(8,128)(2,1)S(1)}, u32[]{:S(2)}, u32[]{:S(2)}) collective-permute-start(bf16[16,2048]{1,0:T(8,128)(2,1)S(1)} %finish.1.refs_0_), channel_id=1, source_target_pairs={{0,4},{4,0},{8,12},{12,8},{16,20},{20,16},{24,28},{28,24},{1,5},{5... | collective-permute-start | bytes 196616 | tf_op jit(solution)/shard_map/ppermute | solution.py:22
  53.7 4.3 %collective-permute-start.13 = (bf16[16,2048]{1,0:T(8,128)(2,1)S(1)}, bf16[16,2048]{1,0:T(8,128)(2,1)S(1)}, u32[]{:S(2)}, u32[]{:S(2)}) collective-permute-start(bf16[16,2048]{1,0:T(8,128)(2,1)S(1)} %finish.1.refs_0_), channel_id=1, source_target_pairs={{0,8},{4,12},{8,0},{12,4},{16,24},{20,28},{24,16},{28,20},{1,9},{5... | collective-permute-start | bytes 196616 | tf_op jit(solution)/shard_map/ppermute | solution.py:22
  58.8 5.0 %collective-permute-start.14 = (bf16[64,1024]{1,0:T(8,128)(2,1)S(1)}, bf16[64,1024]{1,0:T(8,128)(2,1)S(1)}, u32[]{:S(2)}, u32[]{:S(2)}) collective-permute-start(bf16[64,1024]{1,0:T(8,128)(2,1)S(1)} %project_out.1), channel_id=1, source_target_pairs={{0,2},{1,3},{2,0},{3,1},{4,6},{5,7},{6,4},{7,5},{8,10},{9,11},{10,... | collective-permute-start | bytes 393224 | tf_op jit(solution)/shard_map/ppermute | solution.py:22
  63.9 1.6 %collective-permute-start.15 = (f32[64,1024]{1,0:T(8,128)S(1)}, f32[64,1024]{1,0:T(8,128)S(1)}, u32[]{:S(2)}, u32[]{:S(2)}) collective-permute-start(f32[64,1024]{1,0:T(8,128)S(1)} %convert_add_fusion), channel_id=1, source_target_pairs={{0,1},{1,0},{2,3},{3,2},{4,5},{5,4},{6,7},{7,6},{8,9},{9,8},{10,11... | collective-permute-start | bytes 786440 | tf_op jit(solution)/shard_map/ppermute | solution.py:22
  (3 other events, 2.0 us)

commit v11 on v10

--- a/solution.py
+++ b/solution.py
@@ -150,7 +150,7 @@
 
 
 def project_kernel(ways, me, hidden, w_query, w_keyval, *refs):
-    outs, (keyval_out, query, keyval, result, sem) = refs[:ways], refs[ways:]
+    outs, (keyval_out, rows_held, query, keyval, result, sem, rows_sem) = refs[:ways], refs[ways:]
     depth = w_query.shape[0]
     tile = min(256, depth)
     copies = [
@@ -162,12 +162,15 @@
         ]
         for row in range(0, depth, tile)
     ]
+    rows_copy = pltpu.make_async_copy(hidden, rows_held, rows_sem)
+    rows_copy.start()
     for pair in copies:
         for copy in pair:
             copy.start()
+    rows_copy.wait()
     for row, pair in zip(range(0, depth, tile), copies):
         here = slice(row, row + tile)
-        rows = hidden[:, here]
+        rows = rows_held[:, here]
         for copy, held, to in zip(pair, (query, keyval), (result, keyval_out)):
             copy.wait()
             part = jnp.dot(rows, held[here, :], preferred_element_type=jnp.float32)
@@ -512,6 +515,9 @@
     small = pltpu.CompilerParams(vmem_limit_bytes=6 * 2**20)
     me = lax.axis_index("seq").reshape(1)
 
+    def in_hbm(x):
+        return pltpu.with_memory_space_constraint(x, pltpu.HBM)
+
     tables, place_of = pl.pallas_call(
         functools.partial(table_kernel, seq_size, ways),
         out_shape=[
@@ -531,17 +537,19 @@
     *parts, keyval = pl.pallas_call(
         functools.partial(project_kernel, ways),
         out_shape=[part_shape] * ways + [keyval_shape],
-        in_specs=[smem, vmem, hbm, hbm],
+        in_specs=[smem, hbm, hbm, hbm],
         out_specs=[vmem] * (ways + 1),
         scratch_shapes=[
+            pltpu.VMEM(hidden_in.shape, jnp.bfloat16),
             pltpu.VMEM(w_query.shape, jnp.bfloat16),
             pltpu.VMEM(w_keyval.shape, jnp.bfloat16),
             pltpu.VMEM((requests, wide), jnp.float32),
             pltpu.SemaphoreType.DMA((2, pl.cdiv(w_query.shape[0], 256))),
+            pltpu.SemaphoreType.DMA,
         ],
         compiler_params=pltpu.CompilerParams(vmem_limit_bytes=53 * 2**20),
         name="project",
-    )(me, hidden_in, w_query, w_keyval)
+    )(me, in_hbm(hidden_in), in_hbm(w_query), in_hbm(w_keyval))
     terms, (tables, place_of) = scatter_terms(parts, "seq", seq_size, (tables, place_of))
     my_query = pl.pallas_call(
         join_kernel,

time: 66.4 us -> 66.3 us (level)
  local copies, waits for them, and re-layouts: 4.25 us -> 3.35 us
  Pallas kernels: 12.5 us -> 13.3 us
    unnamed x22 -> x20, local copies, waits for them, and re-layouts: 4.25 us -> 3.35 us
    pallas_call x1, Pallas kernels: 2.98 us -> 3.76 us  [body(): pl.pallas_call(functools.partial(project_kernel, ways), out_shape=[part_s...]
where the time goes in v11:
time: 66.3 us; the launch traced here: 66.1 us
  waiting for transfers between devices  26.7 us (40%)
  starting transfers between devices  21.9 us (33%)
  Pallas kernels  13.3 us (20%)
  local copies, waits for them, and re-layouts  3.35 us (5%)
  other arithmetic  0.76 us (1%)
    ppermute x16, waiting for transfers between devices, swap(): return lax.ppermute(x, axis, [(j, j ^ mask) for j in range(n)])  26.7 us
    ppermute x16, starting transfers between devices, swap(): return lax.ppermute(x, axis, [(j, j ^ mask) for j in range(n)])  21.9 us
    pallas_call x1, Pallas kernels, body(): pl.pallas_call(functools.partial(attention_kernel, ways, mine), out_shape...  6.78 us
    pallas_call x1, Pallas kernels, body(): pl.pallas_call(functools.partial(project_kernel, ways), out_shape=[part_s...  3.76 us
    unnamed x20, local copies, waits for them, and re-layouts  3.35 us
  transfers between devices with their start and end apart: 16, of which 14 were waited for; matrix products, arithmetic and copies ran while one was open for 0% of the time, Pallas kernels for 1%

profile of v11, /device:TPU:0, one launch (start us, length us, event | category | flops | bytes accessed | tf_op | source)
XLA Modules:
  0.0 66.1 jit_solution(10549894789452769870)
XLA Ops:
  0.0 3.8 %project.1 = (f32[2,8,2048]{2,1,0:T(8,128)S(1)}, f32[2,8,2048]{2,1,0:T(8,128)S(1)}, f32[2,8,2048]{2,1,0:T(8,128)S(1)}, f32[2,8,2048]{2,1,0:T(8,128)S(1)}, f32[64,512]{1,0:T(8,128)S(1)}) custom-call(s32[1]{0:T(128)} %bitcast.me, bf16[64,1024]{1,0:T(8,128)(2,1)} %hidden.1, bf16[1024,2048]{1,0:T(8,128)(2,1)} %w_query.1, bf16[1024,512]{1,0:T(8,128)(2,1)} %w_keyval.1), custom_call_target="tpu_custom_call" | custom-call | tf_op jit(solution)/shard_map/project/pallas_call | solution.py:537
  3.8 4.0 %collective-permute-start = (f32[2,8,2048]{2,1,0:T(8,128)S(1)}, f32[2,8,2048]{2,1,0:T(8,128)S(1)}, u32[]{:S(2)}, u32[]{:S(2)}) collective-permute-start(f32[2,8,2048]{2,1,0:T(8,128)S(1)} %get-tuple-element.23), channel_id=1, source_target_pairs={{0,12},{4,8},{8,4},{12,0},{16,28},{20,24},{24,20},{28,16},{1,13},{... | collective-permute-start | bytes 393224 | tf_op jit(solution)/shard_map/ppermute | solution.py:22
  11.8 0.9 %page_table.1 = (f32[64,128]{1,0:T(8,128)S(1)}, s32[1,128]{1,0:T(1,128)S(1)}) custom-call(s32[1]{0:T(128)} %bitcast.me, s32[64]{0:T(128)S(1)} %copy-done.3, s32[64]{0:T(128)S(1)} %copy-done.4, s32[1,128]{1,0:T(1,128)S(1)} %bitcast.12, f32[2,128]{1,0:T(2,128)S(1)} %bitcast.9, f32[2,128]{1,0:T(2,128)S(1)} %bitcast.10), custom_call_target="tpu_custom_call" | custom-call | tf_op jit(solution)/shard_map/page_table/pallas_call | solution.py:521
  12.7 1.5 %collective-permute-done.1 = f32[2,8,2048]{2,1,0:T(8,128)S(1)} collective-permute-done((f32[2,8,2048]{2,1,0:T(8,128)S(1)}, f32[2,8,2048]{2,1,0:T(8,128)S(1)}, u32[]{:S(2)}, u32[]{:S(2)}) %collective-permute-start.1) | collective-permute-done | bytes 131104 | tf_op jit(solution)/shard_map/ppermute | solution.py:22
  14.3 2.6 %collective-permute-start.3 = (f32[2,8,2048]{2,1,0:T(8,128)S(1)}, f32[2,8,2048]{2,1,0:T(8,128)S(1)}, u32[]{:S(2)}, u32[]{:S(2)}) collective-permute-start(f32[2,8,2048]{2,1,0:T(8,128)S(1)} %add_add_fusion.refs_0_), channel_id=1, source_target_pairs={{0,16},{4,20},{8,24},{12,28},{16,0},{20,4},{24,8},{28,12},{1,17},{... | collective-permute-start | bytes 393224 | tf_op jit(solution)/shard_map/ppermute | solution.py:22
  17.0 6.4 %collective-permute-done.3.refs_1_ = f32[2,8,2048]{2,1,0:T(8,128)S(1)} collective-permute-done((f32[2,8,2048]{2,1,0:T(8,128)S(1)}, f32[2,8,2048]{2,1,0:T(8,128)S(1)}, u32[]{:S(2)}, u32[]{:S(2)}) %collective-permute-start.3) | collective-permute-done | bytes 131104 | tf_op jit(solution)/shard_map/ppermute | solution.py:22
  23.8 2.0 %collective-permute-start.5 = (bf16[256,128]{1,0:T(8,128)(2,1)S(1)}, bf16[256,128]{1,0:T(8,128)(2,1)S(1)}, u32[]{:S(2)}, u32[]{:S(2)}) collective-permute-start(bf16[256,128]{1,0:T(8,128)(2,1)S(1)} %join.1.refs_0_.refs_2_), channel_id=1, source_target_pairs={{0,4},{4,0},{8,12},{12,8},{16,20},{20,16},{24,28},{28,24},{1,5},{5... | collective-permute-start | bytes 196616 | tf_op jit(solution)/shard_map/ppermute | solution.py:22
  25.8 1.3 %collective-permute-start.6 = (bf16[256,128]{1,0:T(8,128)(2,1)S(1)}, bf16[256,128]{1,0:T(8,128)(2,1)S(1)}, u32[]{:S(2)}, u32[]{:S(2)}) collective-permute-start(bf16[256,128]{1,0:T(8,128)(2,1)S(1)} %join.1.refs_0_.refs_2_), channel_id=1, source_target_pairs={{0,8},{4,12},{8,0},{12,4},{16,24},{20,28},{24,16},{28,20},{1,9},{5... | collective-permute-start | bytes 196616 | tf_op jit(solution)/shard_map/ppermute | solution.py:22
  27.0 1.9 %collective-permute-done.4.refs_1_ = bf16[256,128]{1,0:T(8,128)(2,1)S(1)} collective-permute-done((bf16[256,128]{1,0:T(8,128)(2,1)S(1)}, bf16[256,128]{1,0:T(8,128)(2,1)S(1)}, u32[]{:S(2)}, u32[]{:S(2)}) %collective-permute-start.4) | collective-permute-done | bytes 65568 | tf_op jit(solution)/shard_map/ppermute | solution.py:22
  29.0 1.1 %collective-permute-done.6.refs_3_ = bf16[256,128]{1,0:T(8,128)(2,1)S(1)} collective-permute-done((bf16[256,128]{1,0:T(8,128)(2,1)S(1)}, bf16[256,128]{1,0:T(8,128)(2,1)S(1)}, u32[]{:S(2)}, u32[]{:S(2)}) %collective-permute-start.6) | collective-permute-done | bytes 65568 | tf_op jit(solution)/shard_map/ppermute | solution.py:22
  30.1 6.8 %paged_attention.1 = (bf16[2,176,128]{2,1,0:T(8,128)(2,1)S(1)}, bf16[2,176,128]{2,1,0:T(8,128)(2,1)S(1)}, bf16[2,176,128]{2,1,0:T(8,128)(2,1)S(1)}, bf16[2,176,128]{2,1,0:T(8,128)(2,1)S(1)}) custom-call(s32[128]{0:T(128)S(1)} %bitcast.11, bf16[256,128]{1,0:T(8,128)(2,1)S(1)} %join.1.refs_0_.refs_2_, bf16[256,128]{1,0:T(8,128)(2,1)S(1)} %collective-permute-done.4.refs_1_, ...), custom_call_target="tpu_custom_call" | custom-call | flops 134217728 | bytes 16777216 | tf_op jit(solution)/shard_map/paged_attention/pallas_call | solution.py:568
  36.9 1.6 %collective-permute-start.7 = (bf16[2,176,128]{2,1,0:T(8,128)(2,1)S(1)}, bf16[2,176,128]{2,1,0:T(8,128)(2,1)S(1)}, u32[]{:S(2)}, u32[]{:S(2)}) collective-permute-start(bf16[2,176,128]{2,1,0:T(8,128)(2,1)S(1)} %get-tuple-element.36), channel_id=1, source_target_pairs={{0,12},{4,8},{8,4},{12,0},{16,28},{20,24},{24,20},{28,16},{1,13},{... | collective-permute-start | bytes 270344 | tf_op jit(solution)/shard_map/ppermute | solution.py:22
  38.5 1.2 %collective-permute-start.8 = (bf16[2,176,128]{2,1,0:T(8,128)(2,1)S(1)}, bf16[2,176,128]{2,1,0:T(8,128)(2,1)S(1)}, u32[]{:S(2)}, u32[]{:S(2)}) collective-permute-start(bf16[2,176,128]{2,1,0:T(8,128)(2,1)S(1)} %get-tuple-element.37), channel_id=1, source_target_pairs={{0,4},{4,0},{8,12},{12,8},{16,20},{20,16},{24,28},{28,24},{1,5},{5... | collective-permute-start | bytes 270344 | tf_op jit(solution)/shard_map/ppermute | solution.py:22
  40.4 2.3 %collective-permute-done.7.refs_1_ = bf16[2,176,128]{2,1,0:T(8,128)(2,1)S(1)} collective-permute-done((bf16[2,176,128]{2,1,0:T(8,128)(2,1)S(1)}, bf16[2,176,128]{2,1,0:T(8,128)(2,1)S(1)}, u32[]{:S(2)}, u32[]{:S(2)}) %collective-permute-start.7) | collective-permute-done | bytes 90144 | tf_op jit(solution)/shard_map/ppermute | solution.py:22
  42.7 0.9 %collective-permute-done.8.refs_2_ = bf16[2,176,128]{2,1,0:T(8,128)(2,1)S(1)} collective-permute-done((bf16[2,176,128]{2,1,0:T(8,128)(2,1)S(1)}, bf16[2,176,128]{2,1,0:T(8,128)(2,1)S(1)}, u32[]{:S(2)}, u32[]{:S(2)}) %collective-permute-start.8) | collective-permute-done | bytes 90144 | tf_op jit(solution)/shard_map/ppermute | solution.py:22
  44.7 2.3 %collective-permute-start.10 = (bf16[2,176,128]{2,1,0:T(8,128)(2,1)S(1)}, bf16[2,176,128]{2,1,0:T(8,128)(2,1)S(1)}, u32[]{:S(2)}, u32[]{:S(2)}) collective-permute-start(bf16[2,176,128]{2,1,0:T(8,128)(2,1)S(1)} %combine.1.refs_0_), channel_id=1, source_target_pairs={{0,16},{4,20},{8,24},{12,28},{16,0},{20,4},{24,8},{28,12},{1,17},{... | collective-permute-start | bytes 270344 | tf_op jit(solution)/shard_map/ppermute | solution.py:22
  46.9 4.2 %collective-permute-done.10.refs_1_ = bf16[2,176,128]{2,1,0:T(8,128)(2,1)S(1)} collective-permute-done((bf16[2,176,128]{2,1,0:T(8,128)(2,1)S(1)}, bf16[2,176,128]{2,1,0:T(8,128)(2,1)S(1)}, u32[]{:S(2)}, u32[]{:S(2)}) %collective-permute-start.10) | collective-permute-done | bytes 90144 | tf_op jit(solution)/shard_map/ppermute | solution.py:22
  52.1 1.5 %collective-permute-start.12 = (bf16[16,2048]{1,0:T(8,128)(2,1)S(1)}, bf16[16,2048]{1,0:T(8,128)(2,1)S(1)}, u32[]{:S(2)}, u32[]{:S(2)}) collective-permute-start(bf16[16,2048]{1,0:T(8,128)(2,1)S(1)} %finish.1.refs_0_), channel_id=1, source_target_pairs={{0,4},{4,0},{8,12},{12,8},{16,20},{20,16},{24,28},{28,24},{1,5},{5... | collective-permute-start | bytes 196616 | tf_op jit(solution)/shard_map/ppermute | solution.py:22
  53.6 1.6 %collective-permute-start.13 = (bf16[16,2048]{1,0:T(8,128)(2,1)S(1)}, bf16[16,2048]{1,0:T(8,128)(2,1)S(1)}, u32[]{:S(2)}, u32[]{:S(2)}) collective-permute-start(bf16[16,2048]{1,0:T(8,128)(2,1)S(1)} %finish.1.refs_0_), channel_id=1, source_target_pairs={{0,8},{4,12},{8,0},{12,4},{16,24},{20,28},{24,16},{28,20},{1,9},{5... | collective-permute-start | bytes 196616 | tf_op jit(solution)/shard_map/ppermute | solution.py:22
  55.2 1.8 %collective-permute-done.11.refs_1_ = bf16[16,2048]{1,0:T(8,128)(2,1)S(1)} collective-permute-done((bf16[16,2048]{1,0:T(8,128)(2,1)S(1)}, bf16[16,2048]{1,0:T(8,128)(2,1)S(1)}, u32[]{:S(2)}, u32[]{:S(2)}) %collective-permute-start.11) | collective-permute-done | bytes 65568 | tf_op jit(solution)/shard_map/ppermute | solution.py:22
  57.8 0.9 %project_out.1 = bf16[64,1024]{1,0:T(8,128)(2,1)S(1)} custom-call(s32[1]{0:T(128)} %bitcast.me, bf16[16,2048]{1,0:T(8,128)(2,1)S(1)} %finish.1.refs_0_, bf16[16,2048]{1,0:T(8,128)(2,1)S(1)} %collective-permute-done.11.refs_1_, bf16[16,2048]{1,0:T(8,128)(2,1)S(1)} %collective-permute-done.12.refs_2_, bf16[16,2048]{1,0:T(8,128)(2,1)S(1)} %collective-permute-done.13.refs_3_, ...), custom_call_target="tpu_custom_call" | custom-call | tf_op jit(solution)/shard_map/project_out/pallas_call | solution.py:618
  58.7 1.6 %collective-permute-start.14 = (bf16[64,1024]{1,0:T(8,128)(2,1)S(1)}, bf16[64,1024]{1,0:T(8,128)(2,1)S(1)}, u32[]{:S(2)}, u32[]{:S(2)}) collective-permute-start(bf16[64,1024]{1,0:T(8,128)(2,1)S(1)} %project_out.1), channel_id=1, source_target_pairs={{0,2},{1,3},{2,0},{3,1},{4,6},{5,7},{6,4},{7,5},{8,10},{9,11},{10,... | collective-permute-start | bytes 393224 | tf_op jit(solution)/shard_map/ppermute | solution.py:22
  60.3 3.5 %collective-permute-done.14 = bf16[64,1024]{1,0:T(8,128)(2,1)S(1)} collective-permute-done((bf16[64,1024]{1,0:T(8,128)(2,1)S(1)}, bf16[64,1024]{1,0:T(8,128)(2,1)S(1)}, u32[]{:S(2)}, u32[]{:S(2)}) %collective-permute-start.14) | collective-permute-done | bytes 131104 | tf_op jit(solution)/shard_map/ppermute | solution.py:22
  63.8 1.5 %collective-permute-done.15 = f32[64,1024]{1,0:T(8,128)S(1)} collective-permute-done((f32[64,1024]{1,0:T(8,128)S(1)}, f32[64,1024]{1,0:T(8,128)S(1)}, u32[]{:S(2)}, u32[]{:S(2)}) %collective-permute-start.15) | collective-permute-done | bytes 262176 | tf_op jit(solution)/shard_map/ppermute | solution.py:22
  (40 shorter events, 9.1 us)
Async XLA Ops:
  3.8 8.9 %collective-permute-start = (f32[2,8,2048]{2,1,0:T(8,128)S(1)}, f32[2,8,2048]{2,1,0:T(8,128)S(1)}, u32[]{:S(2)}, u32[]{:S(2)}) collective-permute-start(f32[2,8,2048]{2,1,0:T(8,128)S(1)} %get-tuple-element.23), channel_id=1, source_target_pairs={{0,12},{4,8},{8,4},{12,0},{16,28},{20,24},{24,20},{28,16},{1,13},{... | collective-permute-start | bytes 393224 | tf_op jit(solution)/shard_map/ppermute | solution.py:22
  7.8 6.3 %collective-permute-start.1 = (f32[2,8,2048]{2,1,0:T(8,128)S(1)}, f32[2,8,2048]{2,1,0:T(8,128)S(1)}, u32[]{:S(2)}, u32[]{:S(2)}) collective-permute-start(f32[2,8,2048]{2,1,0:T(8,128)S(1)} %get-tuple-element.24), channel_id=1, source_target_pairs={{0,4},{4,0},{8,12},{12,8},{16,20},{20,16},{24,28},{28,24},{1,5},{5... | collective-permute-start | bytes 393224 | tf_op jit(solution)/shard_map/ppermute | solution.py:22
  8.3 6.0 %collective-permute-start.2 = (f32[2,8,2048]{2,1,0:T(8,128)S(1)}, f32[2,8,2048]{2,1,0:T(8,128)S(1)}, u32[]{:S(2)}, u32[]{:S(2)}) collective-permute-start(f32[2,8,2048]{2,1,0:T(8,128)S(1)} %get-tuple-element.25), channel_id=1, source_target_pairs={{0,8},{4,12},{8,0},{12,4},{16,24},{20,28},{24,16},{28,20},{1,9},{5... | collective-permute-start | bytes 393224 | tf_op jit(solution)/shard_map/ppermute | solution.py:22
  8.5 0.7 %copy-start.1 = (f32[128,2]{0,1:T(2,128)S(1)}, f32[128,2]{0,1:T(2,128)}, u32[]{:S(2)}) copy-start(f32[128,2]{0,1:T(2,128)} %param.17) | copy-start | bytes 3076
  9.1 0.7 %copy-start.2 = (f32[128,2]{0,1:T(2,128)S(1)}, f32[128,2]{0,1:T(2,128)}, u32[]{:S(2)}) copy-start(f32[128,2]{0,1:T(2,128)} %param.18) | copy-start | bytes 3076
  9.8 0.7 copy-start.3
  14.3 15.8 %slice-start = ((s8[8388608]{0:T(1024)(128)(4,1)}), s8[4194304]{0:T(1024)(128)(4,1)S(1)}, s32[]{:S(2)}) async-start(s8[8388608]{0:T(1024)(128)(4,1)} %bitcast.5), calls=%async_computation | async-start | bytes 8388608
  14.3 15.8 %slice-start.2 = ((s8[8388608]{0:T(1024)(128)(4,1)}), s8[4194304]{0:T(1024)(128)(4,1)S(1)}, s32[]{:S(2)}) async-start(s8[8388608]{0:T(1024)(128)(4,1)} %bitcast.7), calls=%async_computation.2 | async-start | bytes 8388608
  14.3 15.7 %slice-start.1 = ((s8[8388608]{0:T(1024)(128)(4,1)}), s8[4194304]{0:T(1024)(128)(4,1)S(1)}, s32[]{:S(2)}) async-start(s8[8388608]{0:T(1024)(128)(4,1)} %bitcast.5), calls=%async_computation.1 | async-start | bytes 8388608
  14.3 15.7 %slice-start.3 = ((s8[8388608]{0:T(1024)(128)(4,1)}), s8[4194304]{0:T(1024)(128)(4,1)S(1)}, s32[]{:S(2)}) async-start(s8[8388608]{0:T(1024)(128)(4,1)} %bitcast.7), calls=%async_computation.3 | async-start | bytes 8388608
  14.3 9.1 %collective-permute-start.3 = (f32[2,8,2048]{2,1,0:T(8,128)S(1)}, f32[2,8,2048]{2,1,0:T(8,128)S(1)}, u32[]{:S(2)}, u32[]{:S(2)}) collective-permute-start(f32[2,8,2048]{2,1,0:T(8,128)S(1)} %add_add_fusion.refs_0_), channel_id=1, source_target_pairs={{0,16},{4,20},{8,24},{12,28},{16,0},{20,4},{24,8},{28,12},{1,17},{... | collective-permute-start | bytes 393224 | tf_op jit(solution)/shard_map/ppermute | solution.py:22
  23.5 5.5 %collective-permute-start.4 = (bf16[256,128]{1,0:T(8,128)(2,1)S(1)}, bf16[256,128]{1,0:T(8,128)(2,1)S(1)}, u32[]{:S(2)}, u32[]{:S(2)}) collective-permute-start(bf16[256,128]{1,0:T(8,128)(2,1)S(1)} %join.1.refs_0_.refs_2_), channel_id=1, source_target_pairs={{0,12},{4,8},{8,4},{12,0},{16,28},{20,24},{24,20},{28,16},{1,13},{... | collective-permute-start | bytes 196616 | tf_op jit(solution)/shard_map/ppermute | solution.py:22
  23.8 5.2 %collective-permute-start.5 = (bf16[256,128]{1,0:T(8,128)(2,1)S(1)}, bf16[256,128]{1,0:T(8,128)(2,1)S(1)}, u32[]{:S(2)}, u32[]{:S(2)}) collective-permute-start(bf16[256,128]{1,0:T(8,128)(2,1)S(1)} %join.1.refs_0_.refs_2_), channel_id=1, source_target_pairs={{0,4},{4,0},{8,12},{12,8},{16,20},{20,16},{24,28},{28,24},{1,5},{5... | collective-permute-start | bytes 196616 | tf_op jit(solution)/shard_map/ppermute | solution.py:22
  25.8 4.3 %collective-permute-start.6 = (bf16[256,128]{1,0:T(8,128)(2,1)S(1)}, bf16[256,128]{1,0:T(8,128)(2,1)S(1)}, u32[]{:S(2)}, u32[]{:S(2)}) collective-permute-start(bf16[256,128]{1,0:T(8,128)(2,1)S(1)} %join.1.refs_0_.refs_2_), channel_id=1, source_target_pairs={{0,8},{4,12},{8,0},{12,4},{16,24},{20,28},{24,16},{28,20},{1,9},{5... | collective-permute-start | bytes 196616 | tf_op jit(solution)/shard_map/ppermute | solution.py:22
  30.1 27.8 %copy-start = (bf16[2048,1024]{1,0:T(8,128)(2,1)S(1)}, bf16[2048,1024]{1,0:T(8,128)(2,1)}, u32[]{:S(2)}) copy-start(bf16[2048,1024]{1,0:T(8,128)(2,1)} %refs_4_.1) | copy-start | bytes 12582916
  36.9 5.8 %collective-permute-start.7 = (bf16[2,176,128]{2,1,0:T(8,128)(2,1)S(1)}, bf16[2,176,128]{2,1,0:T(8,128)(2,1)S(1)}, u32[]{:S(2)}, u32[]{:S(2)}) collective-permute-start(bf16[2,176,128]{2,1,0:T(8,128)(2,1)S(1)} %get-tuple-element.36), channel_id=1, source_target_pairs={{0,12},{4,8},{8,4},{12,0},{16,28},{20,24},{24,20},{28,16},{1,13},{... | collective-permute-start | bytes 270344 | tf_op jit(solution)/shard_map/ppermute | solution.py:22
  38.5 5.1 %collective-permute-start.8 = (bf16[2,176,128]{2,1,0:T(8,128)(2,1)S(1)}, bf16[2,176,128]{2,1,0:T(8,128)(2,1)S(1)}, u32[]{:S(2)}, u32[]{:S(2)}) collective-permute-start(bf16[2,176,128]{2,1,0:T(8,128)(2,1)S(1)} %get-tuple-element.37), channel_id=1, source_target_pairs={{0,4},{4,0},{8,12},{12,8},{16,20},{20,16},{24,28},{28,24},{1,5},{5... | collective-permute-start | bytes 270344 | tf_op jit(solution)/shard_map/ppermute | solution.py:22
  39.7 4.5 %collective-permute-start.9 = (bf16[2,176,128]{2,1,0:T(8,128)(2,1)S(1)}, bf16[2,176,128]{2,1,0:T(8,128)(2,1)S(1)}, u32[]{:S(2)}, u32[]{:S(2)}) collective-permute-start(bf16[2,176,128]{2,1,0:T(8,128)(2,1)S(1)} %get-tuple-element.38), channel_id=1, source_target_pairs={{0,8},{4,12},{8,0},{12,4},{16,24},{20,28},{24,16},{28,20},{1,9},{5... | collective-permute-start | bytes 270344 | tf_op jit(solution)/shard_map/ppermute | solution.py:22
  44.7 6.5 %collective-permute-start.10 = (bf16[2,176,128]{2,1,0:T(8,128)(2,1)S(1)}, bf16[2,176,128]{2,1,0:T(8,128)(2,1)S(1)}, u32[]{:S(2)}, u32[]{:S(2)}) collective-permute-start(bf16[2,176,128]{2,1,0:T(8,128)(2,1)S(1)} %combine.1.refs_0_), channel_id=1, source_target_pairs={{0,16},{4,20},{8,24},{12,28},{16,0},{20,4},{24,8},{28,12},{1,17},{... | collective-permute-start | bytes 270344 | tf_op jit(solution)/shard_map/ppermute | solution.py:22
  51.6 5.3 %collective-permute-start.11 = (bf16[16,2048]{1,0:T(8,128)(2,1)S(1)}, bf16[16,2048]{1,0:T(8,128)(2,1)S(1)}, u32[]{:S(2)}, u32[]{:S(2)}) collective-permute-start(bf16[16,2048]{1,0:T(8,128)(2,1)S(1)} %finish.1.refs_0_), channel_id=1, source_target_pairs={{0,12},{4,8},{8,4},{12,0},{16,28},{20,24},{24,20},{28,16},{1,13},{... | collective-permute-start | bytes 196616 | tf_op jit(solution)/shard_map/ppermute | solution.py:22
  52.1 5.0 %collective-permute-start.12 = (bf16[16,2048]{1,0:T(8,128)(2,1)S(1)}, bf16[16,2048]{1,0:T(8,128)(2,1)S(1)}, u32[]{:S(2)}, u32[]{:S(2)}) collective-permute-start(bf16[16,2048]{1,0:T(8,128)(2,1)S(1)} %finish.1.refs_0_), channel_id=1, source_target_pairs={{0,4},{4,0},{8,12},{12,8},{16,20},{20,16},{24,28},{28,24},{1,5},{5... | collective-permute-start | bytes 196616 | tf_op jit(solution)/shard_map/ppermute | solution.py:22
  53.6 4.3 %collective-permute-start.13 = (bf16[16,2048]{1,0:T(8,128)(2,1)S(1)}, bf16[16,2048]{1,0:T(8,128)(2,1)S(1)}, u32[]{:S(2)}, u32[]{:S(2)}) collective-permute-start(bf16[16,2048]{1,0:T(8,128)(2,1)S(1)} %finish.1.refs_0_), channel_id=1, source_target_pairs={{0,8},{4,12},{8,0},{12,4},{16,24},{20,28},{24,16},{28,20},{1,9},{5... | collective-permute-start | bytes 196616 | tf_op jit(solution)/shard_map/ppermute | solution.py:22
  58.7 5.0 %collective-permute-start.14 = (bf16[64,1024]{1,0:T(8,128)(2,1)S(1)}, bf16[64,1024]{1,0:T(8,128)(2,1)S(1)}, u32[]{:S(2)}, u32[]{:S(2)}) collective-permute-start(bf16[64,1024]{1,0:T(8,128)(2,1)S(1)} %project_out.1), channel_id=1, source_target_pairs={{0,2},{1,3},{2,0},{3,1},{4,6},{5,7},{6,4},{7,5},{8,10},{9,11},{10,... | collective-permute-start | bytes 393224 | tf_op jit(solution)/shard_map/ppermute | solution.py:22
  63.8 1.6 %collective-permute-start.15 = (f32[64,1024]{1,0:T(8,128)S(1)}, f32[64,1024]{1,0:T(8,128)S(1)}, u32[]{:S(2)}, u32[]{:S(2)}) collective-permute-start(f32[64,1024]{1,0:T(8,128)S(1)} %convert_add_fusion), channel_id=1, source_target_pairs={{0,1},{1,0},{2,3},{3,2},{4,5},{5,4},{6,7},{7,6},{8,9},{9,8},{10,11... | collective-permute-start | bytes 786440 | tf_op jit(solution)/shard_map/ppermute | solution.py:22
  (2 other events, 1.3 us)

commit v12 on v11

--- a/solution.py
+++ b/solution.py
@@ -261,7 +261,7 @@
     group = heads // 2
     chunks = slots // CHUNK
     blocks = outs[0].shape[0]
-    step_chunks = 4
+    step_chunks = 8
 
     for d, part in enumerate(in_order(queries)):
         rows = part[...]

time: 66.3 us -> 64.9 us (0.979)
  Pallas kernels: 13.3 us -> 11.9 us
    pallas_call x1, Pallas kernels: 6.78 us -> 5.43 us  [body(): pl.pallas_call(functools.partial(attention_kernel, ways, mine), out_shape...]
where the time goes in v12:
time: 64.9 us; the launch traced here: 64.7 us
  waiting for transfers between devices  26.6 us (41%)
  starting transfers between devices  21.9 us (34%)
  Pallas kernels  11.9 us (18%)
  local copies, waits for them, and re-layouts  3.35 us (5%)
  other arithmetic  0.76 us (1%)
    ppermute x16, waiting for transfers between devices, swap(): return lax.ppermute(x, axis, [(j, j ^ mask) for j in range(n)])  26.6 us
    ppermute x16, starting transfers between devices, swap(): return lax.ppermute(x, axis, [(j, j ^ mask) for j in range(n)])  21.9 us
    pallas_call x1, Pallas kernels, body(): pl.pallas_call(functools.partial(attention_kernel, ways, mine), out_shape...  5.43 us
    pallas_call x1, Pallas kernels, body(): pl.pallas_call(functools.partial(project_kernel, ways), out_shape=[part_s...  3.76 us
    unnamed x20, local copies, waits for them, and re-layouts  3.35 us
  transfers between devices with their start and end apart: 16, of which 14 were waited for; matrix products, arithmetic and copies ran while one was open for 0% of the time, Pallas kernels for 1%

profile of v12, /device:TPU:0, one launch (start us, length us, event | category | flops | bytes accessed | tf_op | source)
XLA Modules:
  0.0 64.7 jit_solution(8092141172726300604)
XLA Ops:
  0.0 3.8 %project.1 = (f32[2,8,2048]{2,1,0:T(8,128)S(1)}, f32[2,8,2048]{2,1,0:T(8,128)S(1)}, f32[2,8,2048]{2,1,0:T(8,128)S(1)}, f32[2,8,2048]{2,1,0:T(8,128)S(1)}, f32[64,512]{1,0:T(8,128)S(1)}) custom-call(s32[1]{0:T(128)} %bitcast.me, bf16[64,1024]{1,0:T(8,128)(2,1)} %hidden.1, bf16[1024,2048]{1,0:T(8,128)(2,1)} %w_query.1, bf16[1024,512]{1,0:T(8,128)(2,1)} %w_keyval.1), custom_call_target="tpu_custom_call" | custom-call | tf_op jit(solution)/shard_map/project/pallas_call | solution.py:537
  3.8 4.0 %collective-permute-start = (f32[2,8,2048]{2,1,0:T(8,128)S(1)}, f32[2,8,2048]{2,1,0:T(8,128)S(1)}, u32[]{:S(2)}, u32[]{:S(2)}) collective-permute-start(f32[2,8,2048]{2,1,0:T(8,128)S(1)} %get-tuple-element.23), channel_id=1, source_target_pairs={{0,12},{4,8},{8,4},{12,0},{16,28},{20,24},{24,20},{28,16},{1,13},{... | collective-permute-start | bytes 393224 | tf_op jit(solution)/shard_map/ppermute | solution.py:22
  11.8 0.9 %page_table.1 = (f32[64,128]{1,0:T(8,128)S(1)}, s32[1,128]{1,0:T(1,128)S(1)}) custom-call(s32[1]{0:T(128)} %bitcast.me, s32[64]{0:T(128)S(1)} %copy-done.3, s32[64]{0:T(128)S(1)} %copy-done.4, s32[1,128]{1,0:T(1,128)S(1)} %bitcast.12, f32[2,128]{1,0:T(2,128)S(1)} %bitcast.9, f32[2,128]{1,0:T(2,128)S(1)} %bitcast.10), custom_call_target="tpu_custom_call" | custom-call | tf_op jit(solution)/shard_map/page_table/pallas_call | solution.py:521
  12.7 1.5 %collective-permute-done.1 = f32[2,8,2048]{2,1,0:T(8,128)S(1)} collective-permute-done((f32[2,8,2048]{2,1,0:T(8,128)S(1)}, f32[2,8,2048]{2,1,0:T(8,128)S(1)}, u32[]{:S(2)}, u32[]{:S(2)}) %collective-permute-start.1) | collective-permute-done | bytes 131104 | tf_op jit(solution)/shard_map/ppermute | solution.py:22
  14.3 2.6 %collective-permute-start.3 = (f32[2,8,2048]{2,1,0:T(8,128)S(1)}, f32[2,8,2048]{2,1,0:T(8,128)S(1)}, u32[]{:S(2)}, u32[]{:S(2)}) collective-permute-start(f32[2,8,2048]{2,1,0:T(8,128)S(1)} %add_add_fusion.refs_0_), channel_id=1, source_target_pairs={{0,16},{4,20},{8,24},{12,28},{16,0},{20,4},{24,8},{28,12},{1,17},{... | collective-permute-start | bytes 393224 | tf_op jit(solution)/shard_map/ppermute | solution.py:22
  17.0 6.4 %collective-permute-done.3.refs_1_ = f32[2,8,2048]{2,1,0:T(8,128)S(1)} collective-permute-done((f32[2,8,2048]{2,1,0:T(8,128)S(1)}, f32[2,8,2048]{2,1,0:T(8,128)S(1)}, u32[]{:S(2)}, u32[]{:S(2)}) %collective-permute-start.3) | collective-permute-done | bytes 131104 | tf_op jit(solution)/shard_map/ppermute | solution.py:22
  23.8 2.0 %collective-permute-start.5 = (bf16[256,128]{1,0:T(8,128)(2,1)S(1)}, bf16[256,128]{1,0:T(8,128)(2,1)S(1)}, u32[]{:S(2)}, u32[]{:S(2)}) collective-permute-start(bf16[256,128]{1,0:T(8,128)(2,1)S(1)} %join.1.refs_0_.refs_2_), channel_id=1, source_target_pairs={{0,4},{4,0},{8,12},{12,8},{16,20},{20,16},{24,28},{28,24},{1,5},{5... | collective-permute-start | bytes 196616 | tf_op jit(solution)/shard_map/ppermute | solution.py:22
  25.8 1.3 %collective-permute-start.6 = (bf16[256,128]{1,0:T(8,128)(2,1)S(1)}, bf16[256,128]{1,0:T(8,128)(2,1)S(1)}, u32[]{:S(2)}, u32[]{:S(2)}) collective-permute-start(bf16[256,128]{1,0:T(8,128)(2,1)S(1)} %join.1.refs_0_.refs_2_), channel_id=1, source_target_pairs={{0,8},{4,12},{8,0},{12,4},{16,24},{20,28},{24,16},{28,20},{1,9},{5... | collective-permute-start | bytes 196616 | tf_op jit(solution)/shard_map/ppermute | solution.py:22
  27.0 1.9 %collective-permute-done.4.refs_1_ = bf16[256,128]{1,0:T(8,128)(2,1)S(1)} collective-permute-done((bf16[256,128]{1,0:T(8,128)(2,1)S(1)}, bf16[256,128]{1,0:T(8,128)(2,1)S(1)}, u32[]{:S(2)}, u32[]{:S(2)}) %collective-permute-start.4) | collective-permute-done | bytes 65568 | tf_op jit(solution)/shard_map/ppermute | solution.py:22
  29.0 1.1 %collective-permute-done.6.refs_3_ = bf16[256,128]{1,0:T(8,128)(2,1)S(1)} collective-permute-done((bf16[256,128]{1,0:T(8,128)(2,1)S(1)}, bf16[256,128]{1,0:T(8,128)(2,1)S(1)}, u32[]{:S(2)}, u32[]{:S(2)}) %collective-permute-start.6) | collective-permute-done | bytes 65568 | tf_op jit(solution)/shard_map/ppermute | solution.py:22
  30.1 5.4 %paged_attention.1 = (bf16[2,176,128]{2,1,0:T(8,128)(2,1)S(1)}, bf16[2,176,128]{2,1,0:T(8,128)(2,1)S(1)}, bf16[2,176,128]{2,1,0:T(8,128)(2,1)S(1)}, bf16[2,176,128]{2,1,0:T(8,128)(2,1)S(1)}) custom-call(s32[128]{0:T(128)S(1)} %bitcast.11, bf16[256,128]{1,0:T(8,128)(2,1)S(1)} %join.1.refs_0_.refs_2_, bf16[256,128]{1,0:T(8,128)(2,1)S(1)} %collective-permute-done.4.refs_1_, ...), custom_call_target="tpu_custom_call" | custom-call | flops 134217728 | bytes 16777216 | tf_op jit(solution)/shard_map/paged_attention/pallas_call | solution.py:568
  35.5 1.6 %collective-permute-start.7 = (bf16[2,176,128]{2,1,0:T(8,128)(2,1)S(1)}, bf16[2,176,128]{2,1,0:T(8,128)(2,1)S(1)}, u32[]{:S(2)}, u32[]{:S(2)}) collective-permute-start(bf16[2,176,128]{2,1,0:T(8,128)(2,1)S(1)} %get-tuple-element.36), channel_id=1, source_target_pairs={{0,12},{4,8},{8,4},{12,0},{16,28},{20,24},{24,20},{28,16},{1,13},{... | collective-permute-start | bytes 270344 | tf_op jit(solution)/shard_map/ppermute | solution.py:22
  37.1 1.2 %collective-permute-start.8 = (bf16[2,176,128]{2,1,0:T(8,128)(2,1)S(1)}, bf16[2,176,128]{2,1,0:T(8,128)(2,1)S(1)}, u32[]{:S(2)}, u32[]{:S(2)}) collective-permute-start(bf16[2,176,128]{2,1,0:T(8,128)(2,1)S(1)} %get-tuple-element.37), channel_id=1, source_target_pairs={{0,4},{4,0},{8,12},{12,8},{16,20},{20,16},{24,28},{28,24},{1,5},{5... | collective-permute-start | bytes 270344 | tf_op jit(solution)/shard_map/ppermute | solution.py:22
  39.1 2.2 %collective-permute-done.7.refs_1_ = bf16[2,176,128]{2,1,0:T(8,128)(2,1)S(1)} collective-permute-done((bf16[2,176,128]{2,1,0:T(8,128)(2,1)S(1)}, bf16[2,176,128]{2,1,0:T(8,128)(2,1)S(1)}, u32[]{:S(2)}, u32[]{:S(2)}) %collective-permute-start.7) | collective-permute-done | bytes 90144 | tf_op jit(solution)/shard_map/ppermute | solution.py:22
  41.3 0.9 %collective-permute-done.8.refs_2_ = bf16[2,176,128]{2,1,0:T(8,128)(2,1)S(1)} collective-permute-done((bf16[2,176,128]{2,1,0:T(8,128)(2,1)S(1)}, bf16[2,176,128]{2,1,0:T(8,128)(2,1)S(1)}, u32[]{:S(2)}, u32[]{:S(2)}) %collective-permute-start.8) | collective-permute-done | bytes 90144 | tf_op jit(solution)/shard_map/ppermute | solution.py:22
  43.3 2.3 %collective-permute-start.10 = (bf16[2,176,128]{2,1,0:T(8,128)(2,1)S(1)}, bf16[2,176,128]{2,1,0:T(8,128)(2,1)S(1)}, u32[]{:S(2)}, u32[]{:S(2)}) collective-permute-start(bf16[2,176,128]{2,1,0:T(8,128)(2,1)S(1)} %combine.1.refs_0_), channel_id=1, source_target_pairs={{0,16},{4,20},{8,24},{12,28},{16,0},{20,4},{24,8},{28,12},{1,17},{... | collective-permute-start | bytes 270344 | tf_op jit(solution)/shard_map/ppermute | solution.py:22
  45.6 4.2 %collective-permute-done.10.refs_1_ = bf16[2,176,128]{2,1,0:T(8,128)(2,1)S(1)} collective-permute-done((bf16[2,176,128]{2,1,0:T(8,128)(2,1)S(1)}, bf16[2,176,128]{2,1,0:T(8,128)(2,1)S(1)}, u32[]{:S(2)}, u32[]{:S(2)}) %collective-permute-start.10) | collective-permute-done | bytes 90144 | tf_op jit(solution)/shard_map/ppermute | solution.py:22
  50.7 1.5 %collective-permute-start.12 = (bf16[16,2048]{1,0:T(8,128)(2,1)S(1)}, bf16[16,2048]{1,0:T(8,128)(2,1)S(1)}, u32[]{:S(2)}, u32[]{:S(2)}) collective-permute-start(bf16[16,2048]{1,0:T(8,128)(2,1)S(1)} %finish.1.refs_0_), channel_id=1, source_target_pairs={{0,4},{4,0},{8,12},{12,8},{16,20},{20,16},{24,28},{28,24},{1,5},{5... | collective-permute-start | bytes 196616 | tf_op jit(solution)/shard_map/ppermute | solution.py:22
  52.2 1.6 %collective-permute-start.13 = (bf16[16,2048]{1,0:T(8,128)(2,1)S(1)}, bf16[16,2048]{1,0:T(8,128)(2,1)S(1)}, u32[]{:S(2)}, u32[]{:S(2)}) collective-permute-start(bf16[16,2048]{1,0:T(8,128)(2,1)S(1)} %finish.1.refs_0_), channel_id=1, source_target_pairs={{0,8},{4,12},{8,0},{12,4},{16,24},{20,28},{24,16},{28,20},{1,9},{5... | collective-permute-start | bytes 196616 | tf_op jit(solution)/shard_map/ppermute | solution.py:22
  53.8 1.8 %collective-permute-done.11.refs_1_ = bf16[16,2048]{1,0:T(8,128)(2,1)S(1)} collective-permute-done((bf16[16,2048]{1,0:T(8,128)(2,1)S(1)}, bf16[16,2048]{1,0:T(8,128)(2,1)S(1)}, u32[]{:S(2)}, u32[]{:S(2)}) %collective-permute-start.11) | collective-permute-done | bytes 65568 | tf_op jit(solution)/shard_map/ppermute | solution.py:22
  56.5 0.9 %project_out.1 = bf16[64,1024]{1,0:T(8,128)(2,1)S(1)} custom-call(s32[1]{0:T(128)} %bitcast.me, bf16[16,2048]{1,0:T(8,128)(2,1)S(1)} %finish.1.refs_0_, bf16[16,2048]{1,0:T(8,128)(2,1)S(1)} %collective-permute-done.11.refs_1_, bf16[16,2048]{1,0:T(8,128)(2,1)S(1)} %collective-permute-done.12.refs_2_, bf16[16,2048]{1,0:T(8,128)(2,1)S(1)} %collective-permute-done.13.refs_3_, ...), custom_call_target="tpu_custom_call" | custom-call | tf_op jit(solution)/shard_map/project_out/pallas_call | solution.py:618
  57.3 1.6 %collective-permute-start.14 = (bf16[64,1024]{1,0:T(8,128)(2,1)S(1)}, bf16[64,1024]{1,0:T(8,128)(2,1)S(1)}, u32[]{:S(2)}, u32[]{:S(2)}) collective-permute-start(bf16[64,1024]{1,0:T(8,128)(2,1)S(1)} %project_out.1), channel_id=1, source_target_pairs={{0,2},{1,3},{2,0},{3,1},{4,6},{5,7},{6,4},{7,5},{8,10},{9,11},{10,... | collective-permute-start | bytes 393224 | tf_op jit(solution)/shard_map/ppermute | solution.py:22
  58.9 3.5 %collective-permute-done.14 = bf16[64,1024]{1,0:T(8,128)(2,1)S(1)} collective-permute-done((bf16[64,1024]{1,0:T(8,128)(2,1)S(1)}, bf16[64,1024]{1,0:T(8,128)(2,1)S(1)}, u32[]{:S(2)}, u32[]{:S(2)}) %collective-permute-start.14) | collective-permute-done | bytes 131104 | tf_op jit(solution)/shard_map/ppermute | solution.py:22
  62.5 1.5 %collective-permute-done.15 = f32[64,1024]{1,0:T(8,128)S(1)} collective-permute-done((f32[64,1024]{1,0:T(8,128)S(1)}, f32[64,1024]{1,0:T(8,128)S(1)}, u32[]{:S(2)}, u32[]{:S(2)}) %collective-permute-start.15) | collective-permute-done | bytes 262176 | tf_op jit(solution)/shard_map/ppermute | solution.py:22
  (40 shorter events, 9.1 us)
Async XLA Ops:
  3.8 8.9 %collective-permute-start = (f32[2,8,2048]{2,1,0:T(8,128)S(1)}, f32[2,8,2048]{2,1,0:T(8,128)S(1)}, u32[]{:S(2)}, u32[]{:S(2)}) collective-permute-start(f32[2,8,2048]{2,1,0:T(8,128)S(1)} %get-tuple-element.23), channel_id=1, source_target_pairs={{0,12},{4,8},{8,4},{12,0},{16,28},{20,24},{24,20},{28,16},{1,13},{... | collective-permute-start | bytes 393224 | tf_op jit(solution)/shard_map/ppermute | solution.py:22
  7.8 6.3 %collective-permute-start.1 = (f32[2,8,2048]{2,1,0:T(8,128)S(1)}, f32[2,8,2048]{2,1,0:T(8,128)S(1)}, u32[]{:S(2)}, u32[]{:S(2)}) collective-permute-start(f32[2,8,2048]{2,1,0:T(8,128)S(1)} %get-tuple-element.24), channel_id=1, source_target_pairs={{0,4},{4,0},{8,12},{12,8},{16,20},{20,16},{24,28},{28,24},{1,5},{5... | collective-permute-start | bytes 393224 | tf_op jit(solution)/shard_map/ppermute | solution.py:22
  8.3 6.0 %collective-permute-start.2 = (f32[2,8,2048]{2,1,0:T(8,128)S(1)}, f32[2,8,2048]{2,1,0:T(8,128)S(1)}, u32[]{:S(2)}, u32[]{:S(2)}) collective-permute-start(f32[2,8,2048]{2,1,0:T(8,128)S(1)} %get-tuple-element.25), channel_id=1, source_target_pairs={{0,8},{4,12},{8,0},{12,4},{16,24},{20,28},{24,16},{28,20},{1,9},{5... | collective-permute-start | bytes 393224 | tf_op jit(solution)/shard_map/ppermute | solution.py:22
  8.5 0.7 %copy-start.1 = (f32[128,2]{0,1:T(2,128)S(1)}, f32[128,2]{0,1:T(2,128)}, u32[]{:S(2)}) copy-start(f32[128,2]{0,1:T(2,128)} %param.17) | copy-start | bytes 3076
  9.1 0.7 %copy-start.2 = (f32[128,2]{0,1:T(2,128)S(1)}, f32[128,2]{0,1:T(2,128)}, u32[]{:S(2)}) copy-start(f32[128,2]{0,1:T(2,128)} %param.18) | copy-start | bytes 3076
  9.8 0.7 %copy-start.3 = (s32[64]{0:T(128)S(1)}, s32[64]{0:T(128)}, u32[]{:S(2)}) copy-start(s32[64]{0:T(128)} %counts.1) | copy-start | bytes 772
  14.3 15.8 %slice-start = ((s8[8388608]{0:T(1024)(128)(4,1)}), s8[4194304]{0:T(1024)(128)(4,1)S(1)}, s32[]{:S(2)}) async-start(s8[8388608]{0:T(1024)(128)(4,1)} %bitcast.5), calls=%async_computation | async-start | bytes 8388608
  14.3 15.8 %slice-start.2 = ((s8[8388608]{0:T(1024)(128)(4,1)}), s8[4194304]{0:T(1024)(128)(4,1)S(1)}, s32[]{:S(2)}) async-start(s8[8388608]{0:T(1024)(128)(4,1)} %bitcast.7), calls=%async_computation.2 | async-start | bytes 8388608
  14.3 15.7 %slice-start.1 = ((s8[8388608]{0:T(1024)(128)(4,1)}), s8[4194304]{0:T(1024)(128)(4,1)S(1)}, s32[]{:S(2)}) async-start(s8[8388608]{0:T(1024)(128)(4,1)} %bitcast.5), calls=%async_computation.1 | async-start | bytes 8388608
  14.3 15.7 %slice-start.3 = ((s8[8388608]{0:T(1024)(128)(4,1)}), s8[4194304]{0:T(1024)(128)(4,1)S(1)}, s32[]{:S(2)}) async-start(s8[8388608]{0:T(1024)(128)(4,1)} %bitcast.7), calls=%async_computation.3 | async-start | bytes 8388608
  14.3 9.1 %collective-permute-start.3 = (f32[2,8,2048]{2,1,0:T(8,128)S(1)}, f32[2,8,2048]{2,1,0:T(8,128)S(1)}, u32[]{:S(2)}, u32[]{:S(2)}) collective-permute-start(f32[2,8,2048]{2,1,0:T(8,128)S(1)} %add_add_fusion.refs_0_), channel_id=1, source_target_pairs={{0,16},{4,20},{8,24},{12,28},{16,0},{20,4},{24,8},{28,12},{1,17},{... | collective-permute-start | bytes 393224 | tf_op jit(solution)/shard_map/ppermute | solution.py:22
  23.5 5.5 %collective-permute-start.4 = (bf16[256,128]{1,0:T(8,128)(2,1)S(1)}, bf16[256,128]{1,0:T(8,128)(2,1)S(1)}, u32[]{:S(2)}, u32[]{:S(2)}) collective-permute-start(bf16[256,128]{1,0:T(8,128)(2,1)S(1)} %join.1.refs_0_.refs_2_), channel_id=1, source_target_pairs={{0,12},{4,8},{8,4},{12,0},{16,28},{20,24},{24,20},{28,16},{1,13},{... | collective-permute-start | bytes 196616 | tf_op jit(solution)/shard_map/ppermute | solution.py:22
  23.8 5.2 %collective-permute-start.5 = (bf16[256,128]{1,0:T(8,128)(2,1)S(1)}, bf16[256,128]{1,0:T(8,128)(2,1)S(1)}, u32[]{:S(2)}, u32[]{:S(2)}) collective-permute-start(bf16[256,128]{1,0:T(8,128)(2,1)S(1)} %join.1.refs_0_.refs_2_), channel_id=1, source_target_pairs={{0,4},{4,0},{8,12},{12,8},{16,20},{20,16},{24,28},{28,24},{1,5},{5... | collective-permute-start | bytes 196616 | tf_op jit(solution)/shard_map/ppermute | solution.py:22
  25.8 4.3 %collective-permute-start.6 = (bf16[256,128]{1,0:T(8,128)(2,1)S(1)}, bf16[256,128]{1,0:T(8,128)(2,1)S(1)}, u32[]{:S(2)}, u32[]{:S(2)}) collective-permute-start(bf16[256,128]{1,0:T(8,128)(2,1)S(1)} %join.1.refs_0_.refs_2_), channel_id=1, source_target_pairs={{0,8},{4,12},{8,0},{12,4},{16,24},{20,28},{24,16},{28,20},{1,9},{5... | collective-permute-start | bytes 196616 | tf_op jit(solution)/shard_map/ppermute | solution.py:22
  30.1 26.4 %copy-start = (bf16[2048,1024]{1,0:T(8,128)(2,1)S(1)}, bf16[2048,1024]{1,0:T(8,128)(2,1)}, u32[]{:S(2)}) copy-start(bf16[2048,1024]{1,0:T(8,128)(2,1)} %refs_4_.1) | copy-start | bytes 12582916
  35.5 5.8 %collective-permute-start.7 = (bf16[2,176,128]{2,1,0:T(8,128)(2,1)S(1)}, bf16[2,176,128]{2,1,0:T(8,128)(2,1)S(1)}, u32[]{:S(2)}, u32[]{:S(2)}) collective-permute-start(bf16[2,176,128]{2,1,0:T(8,128)(2,1)S(1)} %get-tuple-element.36), channel_id=1, source_target_pairs={{0,12},{4,8},{8,4},{12,0},{16,28},{20,24},{24,20},{28,16},{1,13},{... | collective-permute-start | bytes 270344 | tf_op jit(solution)/shard_map/ppermute | solution.py:22
  37.1 5.1 %collective-permute-start.8 = (bf16[2,176,128]{2,1,0:T(8,128)(2,1)S(1)}, bf16[2,176,128]{2,1,0:T(8,128)(2,1)S(1)}, u32[]{:S(2)}, u32[]{:S(2)}) collective-permute-start(bf16[2,176,128]{2,1,0:T(8,128)(2,1)S(1)} %get-tuple-element.37), channel_id=1, source_target_pairs={{0,4},{4,0},{8,12},{12,8},{16,20},{20,16},{24,28},{28,24},{1,5},{5... | collective-permute-start | bytes 270344 | tf_op jit(solution)/shard_map/ppermute | solution.py:22
  38.3 4.5 %collective-permute-start.9 = (bf16[2,176,128]{2,1,0:T(8,128)(2,1)S(1)}, bf16[2,176,128]{2,1,0:T(8,128)(2,1)S(1)}, u32[]{:S(2)}, u32[]{:S(2)}) collective-permute-start(bf16[2,176,128]{2,1,0:T(8,128)(2,1)S(1)} %get-tuple-element.38), channel_id=1, source_target_pairs={{0,8},{4,12},{8,0},{12,4},{16,24},{20,28},{24,16},{28,20},{1,9},{5... | collective-permute-start | bytes 270344 | tf_op jit(solution)/shard_map/ppermute | solution.py:22
  43.3 6.5 %collective-permute-start.10 = (bf16[2,176,128]{2,1,0:T(8,128)(2,1)S(1)}, bf16[2,176,128]{2,1,0:T(8,128)(2,1)S(1)}, u32[]{:S(2)}, u32[]{:S(2)}) collective-permute-start(bf16[2,176,128]{2,1,0:T(8,128)(2,1)S(1)} %combine.1.refs_0_), channel_id=1, source_target_pairs={{0,16},{4,20},{8,24},{12,28},{16,0},{20,4},{24,8},{28,12},{1,17},{... | collective-permute-start | bytes 270344 | tf_op jit(solution)/shard_map/ppermute | solution.py:22
  50.2 5.3 %collective-permute-start.11 = (bf16[16,2048]{1,0:T(8,128)(2,1)S(1)}, bf16[16,2048]{1,0:T(8,128)(2,1)S(1)}, u32[]{:S(2)}, u32[]{:S(2)}) collective-permute-start(bf16[16,2048]{1,0:T(8,128)(2,1)S(1)} %finish.1.refs_0_), channel_id=1, source_target_pairs={{0,12},{4,8},{8,4},{12,0},{16,28},{20,24},{24,20},{28,16},{1,13},{... | collective-permute-start | bytes 196616 | tf_op jit(solution)/shard_map/ppermute | solution.py:22
  50.7 5.0 %collective-permute-start.12 = (bf16[16,2048]{1,0:T(8,128)(2,1)S(1)}, bf16[16,2048]{1,0:T(8,128)(2,1)S(1)}, u32[]{:S(2)}, u32[]{:S(2)}) collective-permute-start(bf16[16,2048]{1,0:T(8,128)(2,1)S(1)} %finish.1.refs_0_), channel_id=1, source_target_pairs={{0,4},{4,0},{8,12},{12,8},{16,20},{20,16},{24,28},{28,24},{1,5},{5... | collective-permute-start | bytes 196616 | tf_op jit(solution)/shard_map/ppermute | solution.py:22
  52.2 4.3 %collective-permute-start.13 = (bf16[16,2048]{1,0:T(8,128)(2,1)S(1)}, bf16[16,2048]{1,0:T(8,128)(2,1)S(1)}, u32[]{:S(2)}, u32[]{:S(2)}) collective-permute-start(bf16[16,2048]{1,0:T(8,128)(2,1)S(1)} %finish.1.refs_0_), channel_id=1, source_target_pairs={{0,8},{4,12},{8,0},{12,4},{16,24},{20,28},{24,16},{28,20},{1,9},{5... | collective-permute-start | bytes 196616 | tf_op jit(solution)/shard_map/ppermute | solution.py:22
  57.3 5.0 %collective-permute-start.14 = (bf16[64,1024]{1,0:T(8,128)(2,1)S(1)}, bf16[64,1024]{1,0:T(8,128)(2,1)S(1)}, u32[]{:S(2)}, u32[]{:S(2)}) collective-permute-start(bf16[64,1024]{1,0:T(8,128)(2,1)S(1)} %project_out.1), channel_id=1, source_target_pairs={{0,2},{1,3},{2,0},{3,1},{4,6},{5,7},{6,4},{7,5},{8,10},{9,11},{10,... | collective-permute-start | bytes 393224 | tf_op jit(solution)/shard_map/ppermute | solution.py:22
  62.4 1.6 %collective-permute-start.15 = (f32[64,1024]{1,0:T(8,128)S(1)}, f32[64,1024]{1,0:T(8,128)S(1)}, u32[]{:S(2)}, u32[]{:S(2)}) collective-permute-start(f32[64,1024]{1,0:T(8,128)S(1)} %convert_add_fusion), channel_id=1, source_target_pairs={{0,1},{1,0},{2,3},{3,2},{4,5},{5,4},{6,7},{7,6},{8,9},{9,8},{10,11... | collective-permute-start | bytes 786440 | tf_op jit(solution)/shard_map/ppermute | solution.py:22
  (2 other events, 1.3 us)

commit v13 on v12

--- a/solution.py
+++ b/solution.py
@@ -261,7 +261,7 @@
     group = heads // 2
     chunks = slots // CHUNK
     blocks = outs[0].shape[0]
-    step_chunks = 8
+    lag = 4
 
     for d, part in enumerate(in_order(queries)):
         rows = part[...]
@@ -332,18 +332,11 @@
                 )
             )
 
-    for c in range(step_chunks):
-        score_chunk(c)
-
-    @pl.loop(1, chunks // step_chunks)
-    def _(step):
-        first = step * step_chunks
-        for c in range(step_chunks):
-            value_chunk(first + c - step_chunks)
-            score_chunk(first + c)
-
-    for c in range(chunks - step_chunks, chunks):
-        value_chunk(c)
+    for c in range(chunks + lag):
+        if c >= lag:
+            value_chunk(c - lag)
+        if c < chunks:
+            score_chunk(c)
 
     biggest, who = page_max[...], tables[3 * chunks :, :]
     best = biggest
@@ -360,24 +353,22 @@
 
     keep_max_row = lax.broadcasted_iota(jnp.int32, (PAGE, LANES), 0) % STAT < STAT // 2
 
-    @pl.loop(0, chunks // step_chunks)
-    def _(step):
-        for c in [step * step_chunks + c for c in range(step_chunks)]:
-            top = dev_max[pl.ds(c, 1), :]
-            weight = jnp.exp(page_max[pl.ds(c, 1), :] - top)
-            out_weight = jnp.broadcast_to(weight * table(2, c), (PAGE, LANES)).T
-            stat = jnp.where(keep_max_row, top, weight * page_sum[pl.ds(c, 1), :]).T
-            for s in range(CHUNK):
-                here = pl.ds(
-                    pl.multiple_of((place_of[c * CHUNK + s] & 0xFFFF) * heads, heads), heads
-                )
-                there = pl.ds(pl.multiple_of((c * CHUNK + s) * heads, heads), heads)
-                part = slice(s * heads, (s + 1) * heads)
-                turn = s % 2
-                total_out[turn, here, :] += page_out[there, :] * out_weight[part]
-                total_stat[turn, here, :] = jnp.where(
-                    keep_max, stat[part], total_stat[turn, here, :] + stat[part]
-                )
+    for c in range(chunks):
+        top = dev_max[pl.ds(c, 1), :]
+        weight = jnp.exp(page_max[pl.ds(c, 1), :] - top)
+        out_weight = jnp.broadcast_to(weight * table(2, c), (PAGE, LANES)).T
+        stat = jnp.where(keep_max_row, top, weight * page_sum[pl.ds(c, 1), :]).T
+        for s in range(CHUNK):
+            here = pl.ds(
+                pl.multiple_of((place_of[c * CHUNK + s] & 0xFFFF) * heads, heads), heads
+            )
+            there = pl.ds(pl.multiple_of((c * CHUNK + s) * heads, heads), heads)
+            part = slice(s * heads, (s + 1) * heads)
+            turn = s % 2
+            total_out[turn, here, :] += page_out[there, :] * out_weight[part]
+            total_stat[turn, here, :] = jnp.where(
+                keep_max, stat[part], total_stat[turn, here, :] + stat[part]
+            )
 
     lane = lax.broadcasted_iota(jnp.int32, (heads, LANES), 1)
     digit = place_of[0] >> 24

time: 64.9 us -> 64.8 us (level)
  no operation moved by 1% of the time
where the time goes in v13:
time: 64.8 us; the launch traced here: 64.6 us
  waiting for transfers between devices  26.7 us (41%)
  starting transfers between devices  21.9 us (34%)
  Pallas kernels  11.8 us (18%)
  local copies, waits for them, and re-layouts  3.35 us (5%)
  other arithmetic  0.76 us (1%)
    ppermute x16, waiting for transfers between devices, swap(): return lax.ppermute(x, axis, [(j, j ^ mask) for j in range(n)])  26.7 us
    ppermute x16, starting transfers between devices, swap(): return lax.ppermute(x, axis, [(j, j ^ mask) for j in range(n)])  21.9 us
    pallas_call x1, Pallas kernels, body(): pl.pallas_call(functools.partial(attention_kernel, ways, mine), out_shape...  5.29 us
    pallas_call x1, Pallas kernels, body(): pl.pallas_call(functools.partial(project_kernel, ways), out_shape=[part_s...  3.76 us
    unnamed x20, local copies, waits for them, and re-layouts  3.35 us
  transfers between devices with their start and end apart: 16, of which 14 were waited for; matrix products, arithmetic and copies ran while one was open for 0% of the time, Pallas kernels for 1%

profile of v13, /device:TPU:0, one launch (start us, length us, event | category | flops | bytes accessed | tf_op | source)
XLA Modules:
  0.0 64.6 jit_solution(12432454649660090094)
XLA Ops:
  0.0 3.8 %project.1 = (f32[2,8,2048]{2,1,0:T(8,128)S(1)}, f32[2,8,2048]{2,1,0:T(8,128)S(1)}, f32[2,8,2048]{2,1,0:T(8,128)S(1)}, f32[2,8,2048]{2,1,0:T(8,128)S(1)}, f32[64,512]{1,0:T(8,128)S(1)}) custom-call(s32[1]{0:T(128)} %bitcast.me, bf16[64,1024]{1,0:T(8,128)(2,1)} %hidden.1, bf16[1024,2048]{1,0:T(8,128)(2,1)} %w_query.1, bf16[1024,512]{1,0:T(8,128)(2,1)} %w_keyval.1), custom_call_target="tpu_custom_call" | custom-call | tf_op jit(solution)/shard_map/project/pallas_call | solution.py:528
  3.8 4.0 %collective-permute-start = (f32[2,8,2048]{2,1,0:T(8,128)S(1)}, f32[2,8,2048]{2,1,0:T(8,128)S(1)}, u32[]{:S(2)}, u32[]{:S(2)}) collective-permute-start(f32[2,8,2048]{2,1,0:T(8,128)S(1)} %get-tuple-element.23), channel_id=1, source_target_pairs={{0,12},{4,8},{8,4},{12,0},{16,28},{20,24},{24,20},{28,16},{1,13},{... | collective-permute-start | bytes 393224 | tf_op jit(solution)/shard_map/ppermute | solution.py:22
  11.8 0.9 %page_table.1 = (f32[64,128]{1,0:T(8,128)S(1)}, s32[1,128]{1,0:T(1,128)S(1)}) custom-call(s32[1]{0:T(128)} %bitcast.me, s32[64]{0:T(128)S(1)} %copy-done.3, s32[64]{0:T(128)S(1)} %copy-done.4, s32[1,128]{1,0:T(1,128)S(1)} %bitcast.12, f32[2,128]{1,0:T(2,128)S(1)} %bitcast.9, f32[2,128]{1,0:T(2,128)S(1)} %bitcast.10), custom_call_target="tpu_custom_call" | custom-call | tf_op jit(solution)/shard_map/page_table/pallas_call | solution.py:512
  12.7 1.5 %collective-permute-done.1 = f32[2,8,2048]{2,1,0:T(8,128)S(1)} collective-permute-done((f32[2,8,2048]{2,1,0:T(8,128)S(1)}, f32[2,8,2048]{2,1,0:T(8,128)S(1)}, u32[]{:S(2)}, u32[]{:S(2)}) %collective-permute-start.1) | collective-permute-done | bytes 131104 | tf_op jit(solution)/shard_map/ppermute | solution.py:22
  14.3 2.6 %collective-permute-start.3 = (f32[2,8,2048]{2,1,0:T(8,128)S(1)}, f32[2,8,2048]{2,1,0:T(8,128)S(1)}, u32[]{:S(2)}, u32[]{:S(2)}) collective-permute-start(f32[2,8,2048]{2,1,0:T(8,128)S(1)} %add_add_fusion.refs_0_), channel_id=1, source_target_pairs={{0,16},{4,20},{8,24},{12,28},{16,0},{20,4},{24,8},{28,12},{1,17},{... | collective-permute-start | bytes 393224 | tf_op jit(solution)/shard_map/ppermute | solution.py:22
  17.0 6.4 %collective-permute-done.3.refs_1_ = f32[2,8,2048]{2,1,0:T(8,128)S(1)} collective-permute-done((f32[2,8,2048]{2,1,0:T(8,128)S(1)}, f32[2,8,2048]{2,1,0:T(8,128)S(1)}, u32[]{:S(2)}, u32[]{:S(2)}) %collective-permute-start.3) | collective-permute-done | bytes 131104 | tf_op jit(solution)/shard_map/ppermute | solution.py:22
  23.8 2.0 %collective-permute-start.5 = (bf16[256,128]{1,0:T(8,128)(2,1)S(1)}, bf16[256,128]{1,0:T(8,128)(2,1)S(1)}, u32[]{:S(2)}, u32[]{:S(2)}) collective-permute-start(bf16[256,128]{1,0:T(8,128)(2,1)S(1)} %join.1.refs_0_.refs_2_), channel_id=1, source_target_pairs={{0,4},{4,0},{8,12},{12,8},{16,20},{20,16},{24,28},{28,24},{1,5},{5... | collective-permute-start | bytes 196616 | tf_op jit(solution)/shard_map/ppermute | solution.py:22
  25.8 1.3 %collective-permute-start.6 = (bf16[256,128]{1,0:T(8,128)(2,1)S(1)}, bf16[256,128]{1,0:T(8,128)(2,1)S(1)}, u32[]{:S(2)}, u32[]{:S(2)}) collective-permute-start(bf16[256,128]{1,0:T(8,128)(2,1)S(1)} %join.1.refs_0_.refs_2_), channel_id=1, source_target_pairs={{0,8},{4,12},{8,0},{12,4},{16,24},{20,28},{24,16},{28,20},{1,9},{5... | collective-permute-start | bytes 196616 | tf_op jit(solution)/shard_map/ppermute | solution.py:22
  27.0 1.9 %collective-permute-done.4.refs_1_ = bf16[256,128]{1,0:T(8,128)(2,1)S(1)} collective-permute-done((bf16[256,128]{1,0:T(8,128)(2,1)S(1)}, bf16[256,128]{1,0:T(8,128)(2,1)S(1)}, u32[]{:S(2)}, u32[]{:S(2)}) %collective-permute-start.4) | collective-permute-done | bytes 65568 | tf_op jit(solution)/shard_map/ppermute | solution.py:22
  29.0 1.1 %collective-permute-done.6.refs_3_ = bf16[256,128]{1,0:T(8,128)(2,1)S(1)} collective-permute-done((bf16[256,128]{1,0:T(8,128)(2,1)S(1)}, bf16[256,128]{1,0:T(8,128)(2,1)S(1)}, u32[]{:S(2)}, u32[]{:S(2)}) %collective-permute-start.6) | collective-permute-done | bytes 65568 | tf_op jit(solution)/shard_map/ppermute | solution.py:22
  30.1 5.3 %paged_attention.1 = (bf16[2,176,128]{2,1,0:T(8,128)(2,1)S(1)}, bf16[2,176,128]{2,1,0:T(8,128)(2,1)S(1)}, bf16[2,176,128]{2,1,0:T(8,128)(2,1)S(1)}, bf16[2,176,128]{2,1,0:T(8,128)(2,1)S(1)}) custom-call(s32[128]{0:T(128)S(1)} %bitcast.11, bf16[256,128]{1,0:T(8,128)(2,1)S(1)} %join.1.refs_0_.refs_2_, bf16[256,128]{1,0:T(8,128)(2,1)S(1)} %collective-permute-done.4.refs_1_, ...), custom_call_target="tpu_custom_call" | custom-call | flops 134217728 | bytes 16777216 | tf_op jit(solution)/shard_map/paged_attention/pallas_call | solution.py:559
  35.4 1.6 %collective-permute-start.7 = (bf16[2,176,128]{2,1,0:T(8,128)(2,1)S(1)}, bf16[2,176,128]{2,1,0:T(8,128)(2,1)S(1)}, u32[]{:S(2)}, u32[]{:S(2)}) collective-permute-start(bf16[2,176,128]{2,1,0:T(8,128)(2,1)S(1)} %get-tuple-element.36), channel_id=1, source_target_pairs={{0,12},{4,8},{8,4},{12,0},{16,28},{20,24},{24,20},{28,16},{1,13},{... | collective-permute-start | bytes 270344 | tf_op jit(solution)/shard_map/ppermute | solution.py:22
  37.0 1.2 %collective-permute-start.8 = (bf16[2,176,128]{2,1,0:T(8,128)(2,1)S(1)}, bf16[2,176,128]{2,1,0:T(8,128)(2,1)S(1)}, u32[]{:S(2)}, u32[]{:S(2)}) collective-permute-start(bf16[2,176,128]{2,1,0:T(8,128)(2,1)S(1)} %get-tuple-element.37), channel_id=1, source_target_pairs={{0,4},{4,0},{8,12},{12,8},{16,20},{20,16},{24,28},{28,24},{1,5},{5... | collective-permute-start | bytes 270344 | tf_op jit(solution)/shard_map/ppermute | solution.py:22
  38.9 2.3 %collective-permute-done.7.refs_1_ = bf16[2,176,128]{2,1,0:T(8,128)(2,1)S(1)} collective-permute-done((bf16[2,176,128]{2,1,0:T(8,128)(2,1)S(1)}, bf16[2,176,128]{2,1,0:T(8,128)(2,1)S(1)}, u32[]{:S(2)}, u32[]{:S(2)}) %collective-permute-start.7) | collective-permute-done | bytes 90144 | tf_op jit(solution)/shard_map/ppermute | solution.py:22
  41.2 0.9 %collective-permute-done.8.refs_2_ = bf16[2,176,128]{2,1,0:T(8,128)(2,1)S(1)} collective-permute-done((bf16[2,176,128]{2,1,0:T(8,128)(2,1)S(1)}, bf16[2,176,128]{2,1,0:T(8,128)(2,1)S(1)}, u32[]{:S(2)}, u32[]{:S(2)}) %collective-permute-start.8) | collective-permute-done | bytes 90144 | tf_op jit(solution)/shard_map/ppermute | solution.py:22
  43.2 2.3 %collective-permute-start.10 = (bf16[2,176,128]{2,1,0:T(8,128)(2,1)S(1)}, bf16[2,176,128]{2,1,0:T(8,128)(2,1)S(1)}, u32[]{:S(2)}, u32[]{:S(2)}) collective-permute-start(bf16[2,176,128]{2,1,0:T(8,128)(2,1)S(1)} %combine.1.refs_0_), channel_id=1, source_target_pairs={{0,16},{4,20},{8,24},{12,28},{16,0},{20,4},{24,8},{28,12},{1,17},{... | collective-permute-start | bytes 270344 | tf_op jit(solution)/shard_map/ppermute | solution.py:22
  45.4 4.2 %collective-permute-done.10.refs_1_ = bf16[2,176,128]{2,1,0:T(8,128)(2,1)S(1)} collective-permute-done((bf16[2,176,128]{2,1,0:T(8,128)(2,1)S(1)}, bf16[2,176,128]{2,1,0:T(8,128)(2,1)S(1)}, u32[]{:S(2)}, u32[]{:S(2)}) %collective-permute-start.10) | collective-permute-done | bytes 90144 | tf_op jit(solution)/shard_map/ppermute | solution.py:22
  50.6 1.5 %collective-permute-start.12 = (bf16[16,2048]{1,0:T(8,128)(2,1)S(1)}, bf16[16,2048]{1,0:T(8,128)(2,1)S(1)}, u32[]{:S(2)}, u32[]{:S(2)}) collective-permute-start(bf16[16,2048]{1,0:T(8,128)(2,1)S(1)} %finish.1.refs_0_), channel_id=1, source_target_pairs={{0,4},{4,0},{8,12},{12,8},{16,20},{20,16},{24,28},{28,24},{1,5},{5... | collective-permute-start | bytes 196616 | tf_op jit(solution)/shard_map/ppermute | solution.py:22
  52.1 1.6 %collective-permute-start.13 = (bf16[16,2048]{1,0:T(8,128)(2,1)S(1)}, bf16[16,2048]{1,0:T(8,128)(2,1)S(1)}, u32[]{:S(2)}, u32[]{:S(2)}) collective-permute-start(bf16[16,2048]{1,0:T(8,128)(2,1)S(1)} %finish.1.refs_0_), channel_id=1, source_target_pairs={{0,8},{4,12},{8,0},{12,4},{16,24},{20,28},{24,16},{28,20},{1,9},{5... | collective-permute-start | bytes 196616 | tf_op jit(solution)/shard_map/ppermute | solution.py:22
  53.7 1.8 %collective-permute-done.11.refs_1_ = bf16[16,2048]{1,0:T(8,128)(2,1)S(1)} collective-permute-done((bf16[16,2048]{1,0:T(8,128)(2,1)S(1)}, bf16[16,2048]{1,0:T(8,128)(2,1)S(1)}, u32[]{:S(2)}, u32[]{:S(2)}) %collective-permute-start.11) | collective-permute-done | bytes 65568 | tf_op jit(solution)/shard_map/ppermute | solution.py:22
  56.3 0.9 %project_out.1 = bf16[64,1024]{1,0:T(8,128)(2,1)S(1)} custom-call(s32[1]{0:T(128)} %bitcast.me, bf16[16,2048]{1,0:T(8,128)(2,1)S(1)} %finish.1.refs_0_, bf16[16,2048]{1,0:T(8,128)(2,1)S(1)} %collective-permute-done.11.refs_1_, bf16[16,2048]{1,0:T(8,128)(2,1)S(1)} %collective-permute-done.12.refs_2_, bf16[16,2048]{1,0:T(8,128)(2,1)S(1)} %collective-permute-done.13.refs_3_, ...), custom_call_target="tpu_custom_call" | custom-call | tf_op jit(solution)/shard_map/project_out/pallas_call | solution.py:609
  57.2 1.5 %collective-permute-start.14 = (bf16[64,1024]{1,0:T(8,128)(2,1)S(1)}, bf16[64,1024]{1,0:T(8,128)(2,1)S(1)}, u32[]{:S(2)}, u32[]{:S(2)}) collective-permute-start(bf16[64,1024]{1,0:T(8,128)(2,1)S(1)} %project_out.1), channel_id=1, source_target_pairs={{0,2},{1,3},{2,0},{3,1},{4,6},{5,7},{6,4},{7,5},{8,10},{9,11},{10,... | collective-permute-start | bytes 393224 | tf_op jit(solution)/shard_map/ppermute | solution.py:22
  58.7 3.5 %collective-permute-done.14 = bf16[64,1024]{1,0:T(8,128)(2,1)S(1)} collective-permute-done((bf16[64,1024]{1,0:T(8,128)(2,1)S(1)}, bf16[64,1024]{1,0:T(8,128)(2,1)S(1)}, u32[]{:S(2)}, u32[]{:S(2)}) %collective-permute-start.14) | collective-permute-done | bytes 131104 | tf_op jit(solution)/shard_map/ppermute | solution.py:22
  62.3 1.5 %collective-permute-done.15 = f32[64,1024]{1,0:T(8,128)S(1)} collective-permute-done((f32[64,1024]{1,0:T(8,128)S(1)}, f32[64,1024]{1,0:T(8,128)S(1)}, u32[]{:S(2)}, u32[]{:S(2)}) %collective-permute-start.15) | collective-permute-done | bytes 262176 | tf_op jit(solution)/shard_map/ppermute | solution.py:22
  (40 shorter events, 9.0 us)
Async XLA Ops:
  3.8 8.9 %collective-permute-start = (f32[2,8,2048]{2,1,0:T(8,128)S(1)}, f32[2,8,2048]{2,1,0:T(8,128)S(1)}, u32[]{:S(2)}, u32[]{:S(2)}) collective-permute-start(f32[2,8,2048]{2,1,0:T(8,128)S(1)} %get-tuple-element.23), channel_id=1, source_target_pairs={{0,12},{4,8},{8,4},{12,0},{16,28},{20,24},{24,20},{28,16},{1,13},{... | collective-permute-start | bytes 393224 | tf_op jit(solution)/shard_map/ppermute | solution.py:22
  7.8 6.3 %collective-permute-start.1 = (f32[2,8,2048]{2,1,0:T(8,128)S(1)}, f32[2,8,2048]{2,1,0:T(8,128)S(1)}, u32[]{:S(2)}, u32[]{:S(2)}) collective-permute-start(f32[2,8,2048]{2,1,0:T(8,128)S(1)} %get-tuple-element.24), channel_id=1, source_target_pairs={{0,4},{4,0},{8,12},{12,8},{16,20},{20,16},{24,28},{28,24},{1,5},{5... | collective-permute-start | bytes 393224 | tf_op jit(solution)/shard_map/ppermute | solution.py:22
  8.3 6.0 %collective-permute-start.2 = (f32[2,8,2048]{2,1,0:T(8,128)S(1)}, f32[2,8,2048]{2,1,0:T(8,128)S(1)}, u32[]{:S(2)}, u32[]{:S(2)}) collective-permute-start(f32[2,8,2048]{2,1,0:T(8,128)S(1)} %get-tuple-element.25), channel_id=1, source_target_pairs={{0,8},{4,12},{8,0},{12,4},{16,24},{20,28},{24,16},{28,20},{1,9},{5... | collective-permute-start | bytes 393224 | tf_op jit(solution)/shard_map/ppermute | solution.py:22
  8.5 0.7 %copy-start.1 = (f32[128,2]{0,1:T(2,128)S(1)}, f32[128,2]{0,1:T(2,128)}, u32[]{:S(2)}) copy-start(f32[128,2]{0,1:T(2,128)} %param.17) | copy-start | bytes 3076
  9.1 0.7 %copy-start.2 = (f32[128,2]{0,1:T(2,128)S(1)}, f32[128,2]{0,1:T(2,128)}, u32[]{:S(2)}) copy-start(f32[128,2]{0,1:T(2,128)} %param.18) | copy-start | bytes 3076
  9.8 0.7 %copy-start.3 = (s32[64]{0:T(128)S(1)}, s32[64]{0:T(128)}, u32[]{:S(2)}) copy-start(s32[64]{0:T(128)} %counts.1) | copy-start | bytes 772
  14.3 15.8 %slice-start = ((s8[8388608]{0:T(1024)(128)(4,1)}), s8[4194304]{0:T(1024)(128)(4,1)S(1)}, s32[]{:S(2)}) async-start(s8[8388608]{0:T(1024)(128)(4,1)} %bitcast.5), calls=%async_computation | async-start | bytes 8388608
  14.3 15.8 %slice-start.2 = ((s8[8388608]{0:T(1024)(128)(4,1)}), s8[4194304]{0:T(1024)(128)(4,1)S(1)}, s32[]{:S(2)}) async-start(s8[8388608]{0:T(1024)(128)(4,1)} %bitcast.7), calls=%async_computation.2 | async-start | bytes 8388608
  14.3 15.7 %slice-start.1 = ((s8[8388608]{0:T(1024)(128)(4,1)}), s8[4194304]{0:T(1024)(128)(4,1)S(1)}, s32[]{:S(2)}) async-start(s8[8388608]{0:T(1024)(128)(4,1)} %bitcast.5), calls=%async_computation.1 | async-start | bytes 8388608
  14.3 15.7 %slice-start.3 = ((s8[8388608]{0:T(1024)(128)(4,1)}), s8[4194304]{0:T(1024)(128)(4,1)S(1)}, s32[]{:S(2)}) async-start(s8[8388608]{0:T(1024)(128)(4,1)} %bitcast.7), calls=%async_computation.3 | async-start | bytes 8388608
  14.3 9.1 %collective-permute-start.3 = (f32[2,8,2048]{2,1,0:T(8,128)S(1)}, f32[2,8,2048]{2,1,0:T(8,128)S(1)}, u32[]{:S(2)}, u32[]{:S(2)}) collective-permute-start(f32[2,8,2048]{2,1,0:T(8,128)S(1)} %add_add_fusion.refs_0_), channel_id=1, source_target_pairs={{0,16},{4,20},{8,24},{12,28},{16,0},{20,4},{24,8},{28,12},{1,17},{... | collective-permute-start | bytes 393224 | tf_op jit(solution)/shard_map/ppermute | solution.py:22
  23.5 5.5 %collective-permute-start.4 = (bf16[256,128]{1,0:T(8,128)(2,1)S(1)}, bf16[256,128]{1,0:T(8,128)(2,1)S(1)}, u32[]{:S(2)}, u32[]{:S(2)}) collective-permute-start(bf16[256,128]{1,0:T(8,128)(2,1)S(1)} %join.1.refs_0_.refs_2_), channel_id=1, source_target_pairs={{0,12},{4,8},{8,4},{12,0},{16,28},{20,24},{24,20},{28,16},{1,13},{... | collective-permute-start | bytes 196616 | tf_op jit(solution)/shard_map/ppermute | solution.py:22
  23.8 5.2 %collective-permute-start.5 = (bf16[256,128]{1,0:T(8,128)(2,1)S(1)}, bf16[256,128]{1,0:T(8,128)(2,1)S(1)}, u32[]{:S(2)}, u32[]{:S(2)}) collective-permute-start(bf16[256,128]{1,0:T(8,128)(2,1)S(1)} %join.1.refs_0_.refs_2_), channel_id=1, source_target_pairs={{0,4},{4,0},{8,12},{12,8},{16,20},{20,16},{24,28},{28,24},{1,5},{5... | collective-permute-start | bytes 196616 | tf_op jit(solution)/shard_map/ppermute | solution.py:22
  25.8 4.3 %collective-permute-start.6 = (bf16[256,128]{1,0:T(8,128)(2,1)S(1)}, bf16[256,128]{1,0:T(8,128)(2,1)S(1)}, u32[]{:S(2)}, u32[]{:S(2)}) collective-permute-start(bf16[256,128]{1,0:T(8,128)(2,1)S(1)} %join.1.refs_0_.refs_2_), channel_id=1, source_target_pairs={{0,8},{4,12},{8,0},{12,4},{16,24},{20,28},{24,16},{28,20},{1,9},{5... | collective-permute-start | bytes 196616 | tf_op jit(solution)/shard_map/ppermute | solution.py:22
  30.1 26.2 %copy-start = (bf16[2048,1024]{1,0:T(8,128)(2,1)S(1)}, bf16[2048,1024]{1,0:T(8,128)(2,1)}, u32[]{:S(2)}) copy-start(bf16[2048,1024]{1,0:T(8,128)(2,1)} %refs_4_.1) | copy-start | bytes 12582916
  35.4 5.8 %collective-permute-start.7 = (bf16[2,176,128]{2,1,0:T(8,128)(2,1)S(1)}, bf16[2,176,128]{2,1,0:T(8,128)(2,1)S(1)}, u32[]{:S(2)}, u32[]{:S(2)}) collective-permute-start(bf16[2,176,128]{2,1,0:T(8,128)(2,1)S(1)} %get-tuple-element.36), channel_id=1, source_target_pairs={{0,12},{4,8},{8,4},{12,0},{16,28},{20,24},{24,20},{28,16},{1,13},{... | collective-permute-start | bytes 270344 | tf_op jit(solution)/shard_map/ppermute | solution.py:22
  37.0 5.1 %collective-permute-start.8 = (bf16[2,176,128]{2,1,0:T(8,128)(2,1)S(1)}, bf16[2,176,128]{2,1,0:T(8,128)(2,1)S(1)}, u32[]{:S(2)}, u32[]{:S(2)}) collective-permute-start(bf16[2,176,128]{2,1,0:T(8,128)(2,1)S(1)} %get-tuple-element.37), channel_id=1, source_target_pairs={{0,4},{4,0},{8,12},{12,8},{16,20},{20,16},{24,28},{28,24},{1,5},{5... | collective-permute-start | bytes 270344 | tf_op jit(solution)/shard_map/ppermute | solution.py:22
  38.2 4.5 %collective-permute-start.9 = (bf16[2,176,128]{2,1,0:T(8,128)(2,1)S(1)}, bf16[2,176,128]{2,1,0:T(8,128)(2,1)S(1)}, u32[]{:S(2)}, u32[]{:S(2)}) collective-permute-start(bf16[2,176,128]{2,1,0:T(8,128)(2,1)S(1)} %get-tuple-element.38), channel_id=1, source_target_pairs={{0,8},{4,12},{8,0},{12,4},{16,24},{20,28},{24,16},{28,20},{1,9},{5... | collective-permute-start | bytes 270344 | tf_op jit(solution)/shard_map/ppermute | solution.py:22
  43.2 6.5 %collective-permute-start.10 = (bf16[2,176,128]{2,1,0:T(8,128)(2,1)S(1)}, bf16[2,176,128]{2,1,0:T(8,128)(2,1)S(1)}, u32[]{:S(2)}, u32[]{:S(2)}) collective-permute-start(bf16[2,176,128]{2,1,0:T(8,128)(2,1)S(1)} %combine.1.refs_0_), channel_id=1, source_target_pairs={{0,16},{4,20},{8,24},{12,28},{16,0},{20,4},{24,8},{28,12},{1,17},{... | collective-permute-start | bytes 270344 | tf_op jit(solution)/shard_map/ppermute | solution.py:22
  50.1 5.3 %collective-permute-start.11 = (bf16[16,2048]{1,0:T(8,128)(2,1)S(1)}, bf16[16,2048]{1,0:T(8,128)(2,1)S(1)}, u32[]{:S(2)}, u32[]{:S(2)}) collective-permute-start(bf16[16,2048]{1,0:T(8,128)(2,1)S(1)} %finish.1.refs_0_), channel_id=1, source_target_pairs={{0,12},{4,8},{8,4},{12,0},{16,28},{20,24},{24,20},{28,16},{1,13},{... | collective-permute-start | bytes 196616 | tf_op jit(solution)/shard_map/ppermute | solution.py:22
  50.6 5.0 %collective-permute-start.12 = (bf16[16,2048]{1,0:T(8,128)(2,1)S(1)}, bf16[16,2048]{1,0:T(8,128)(2,1)S(1)}, u32[]{:S(2)}, u32[]{:S(2)}) collective-permute-start(bf16[16,2048]{1,0:T(8,128)(2,1)S(1)} %finish.1.refs_0_), channel_id=1, source_target_pairs={{0,4},{4,0},{8,12},{12,8},{16,20},{20,16},{24,28},{28,24},{1,5},{5... | collective-permute-start | bytes 196616 | tf_op jit(solution)/shard_map/ppermute | solution.py:22
  52.1 4.3 %collective-permute-start.13 = (bf16[16,2048]{1,0:T(8,128)(2,1)S(1)}, bf16[16,2048]{1,0:T(8,128)(2,1)S(1)}, u32[]{:S(2)}, u32[]{:S(2)}) collective-permute-start(bf16[16,2048]{1,0:T(8,128)(2,1)S(1)} %finish.1.refs_0_), channel_id=1, source_target_pairs={{0,8},{4,12},{8,0},{12,4},{16,24},{20,28},{24,16},{28,20},{1,9},{5... | collective-permute-start | bytes 196616 | tf_op jit(solution)/shard_map/ppermute | solution.py:22
  57.2 5.0 %collective-permute-start.14 = (bf16[64,1024]{1,0:T(8,128)(2,1)S(1)}, bf16[64,1024]{1,0:T(8,128)(2,1)S(1)}, u32[]{:S(2)}, u32[]{:S(2)}) collective-permute-start(bf16[64,1024]{1,0:T(8,128)(2,1)S(1)} %project_out.1), channel_id=1, source_target_pairs={{0,2},{1,3},{2,0},{3,1},{4,6},{5,7},{6,4},{7,5},{8,10},{9,11},{10,... | collective-permute-start | bytes 393224 | tf_op jit(solution)/shard_map/ppermute | solution.py:22
  62.3 1.6 %collective-permute-start.15 = (f32[64,1024]{1,0:T(8,128)S(1)}, f32[64,1024]{1,0:T(8,128)S(1)}, u32[]{:S(2)}, u32[]{:S(2)}) collective-permute-start(f32[64,1024]{1,0:T(8,128)S(1)} %convert_add_fusion), channel_id=1, source_target_pairs={{0,1},{1,0},{2,3},{3,2},{4,5},{5,4},{6,7},{7,6},{8,9},{9,8},{10,11... | collective-permute-start | bytes 786440 | tf_op jit(solution)/shard_map/ppermute | solution.py:22
  (2 other events, 1.3 us)

commit v14 on v13

--- a/solution.py
+++ b/solution.py
@@ -98,7 +98,7 @@
     return [(c << last_shift) + (low ^ e) for e in offsets for c in range(last_size)]
 
 
-def table_kernel(seq_size, ways, me, counts, trim, pages, key_scale, value_scale, tables, place_of):
+def table_kernel(seq_size, ways, counts, trim, pages, key_scale, value_scale, tables, place_of):
     requests = counts.shape[0]
     chunks = tables.shape[0] // 4
     heads = LANES // CHUNK
@@ -115,8 +115,9 @@
         start = end
     valid = length - (page - first) * PAGE
     block = owner >> (mine.bit_length() - 1)
-    row = relative_place(block, me[0], seq_size) * mine + (owner & (mine - 1))
-    place_of[...] = ((me[0] & (ways - 1)) << 24) + (row << 16) + owner
+    me = lax.axis_index("seq")
+    row = relative_place(block, me, seq_size) * mine + (owner & (mine - 1))
+    place_of[...] = ((me & (ways - 1)) << 24) + (row << 16) + owner
 
     chunk_slot = lax.broadcasted_iota(jnp.int32, (chunks, LANES), 1) // CHUNK
     in_chunk = chunk_slot == lax.broadcasted_iota(jnp.int32, (chunks, LANES), 0)
@@ -149,7 +150,7 @@
     tables[3 * chunks :, :] = spread(owner.astype(jnp.float32), same_slot)
 
 
-def project_kernel(ways, me, hidden, w_query, w_keyval, *refs):
+def project_kernel(ways, hidden, w_query, w_keyval, *refs):
     outs, (keyval_out, rows_held, query, keyval, result, sem, rows_sem) = refs[:ways], refs[ways:]
     depth = w_query.shape[0]
     tile = min(256, depth)
@@ -171,11 +172,12 @@
     for row, pair in zip(range(0, depth, tile), copies):
         here = slice(row, row + tile)
         rows = rows_held[:, here]
-        for copy, held, to in zip(pair, (query, keyval), (result, keyval_out)):
+        for copy in pair:
             copy.wait()
+        for held, to in ((query, result), (keyval, keyval_out)):
             part = jnp.dot(rows, held[here, :], preferred_element_type=jnp.float32)
             to[...] = to[...] + part if row else part
-    digit = me[0] & (ways - 1)
+    digit = lax.axis_index("seq") & (ways - 1)
     for d, out in enumerate(outs):
         blocks, mine, _ = out.shape
         for b in range(blocks):
@@ -190,11 +192,11 @@
             out[b] = chosen
 
 
-def output_kernel(ways, seq_size, me, *refs):
+def output_kernel(ways, seq_size, *refs):
     parts, (w_out, rounded, out) = refs[:ways], refs[ways:]
     rows = jnp.concatenate([part[...] for part in in_order(parts)], axis=0)
     total = jnp.dot(rows, w_out[...], preferred_element_type=jnp.float32)
-    blocks = gathered_blocks(me[0], seq_size)
+    blocks = gathered_blocks(lax.axis_index("seq"), seq_size)
     mine = rows.shape[0] // len(blocks)
     if mine % 8 == 0:
         for i, block in enumerate(blocks):
@@ -504,7 +506,6 @@
     vmem = pl.BlockSpec(memory_space=pltpu.VMEM)
     hbm = pl.BlockSpec(memory_space=pl.ANY)
     small = pltpu.CompilerParams(vmem_limit_bytes=6 * 2**20)
-    me = lax.axis_index("seq").reshape(1)
 
     def in_hbm(x):
         return pltpu.with_memory_space_constraint(x, pltpu.HBM)
@@ -515,11 +516,11 @@
             jax.ShapeDtypeStruct((4 * chunks, LANES), jnp.float32),
             jax.ShapeDtypeStruct((1, slots), jnp.int32),
         ],
-        in_specs=[smem, smem, smem, vmem, vmem, vmem],
+        in_specs=[smem, smem, vmem, vmem, vmem],
         out_specs=[vmem, vmem],
         compiler_params=small,
         name="page_table",
-    )(me, page_counts, trim, slot_pages.reshape(1, slots), key_scale.T, value_scale.T)
+    )(page_counts, trim, slot_pages.reshape(1, slots), key_scale.T, value_scale.T)
     place_of = place_of.reshape(slots)
 
     held = last_group(seq_size)[1] * mine
@@ -528,7 +529,7 @@
     *parts, keyval = pl.pallas_call(
         functools.partial(project_kernel, ways),
         out_shape=[part_shape] * ways + [keyval_shape],
-        in_specs=[smem, hbm, hbm, hbm],
+        in_specs=[hbm, hbm, hbm],
         out_specs=[vmem] * (ways + 1),
         scratch_shapes=[
             pltpu.VMEM(hidden_in.shape, jnp.bfloat16),
@@ -540,7 +541,7 @@
         ],
         compiler_params=pltpu.CompilerParams(vmem_limit_bytes=53 * 2**20),
         name="project",
-    )(me, in_hbm(hidden_in), in_hbm(w_query), in_hbm(w_keyval))
+    )(in_hbm(hidden_in), in_hbm(w_query), in_hbm(w_keyval))
     terms, (tables, place_of) = scatter_terms(parts, "seq", seq_size, (tables, place_of))
     my_query = pl.pallas_call(
         join_kernel,
@@ -609,12 +610,12 @@
     total = pl.pallas_call(
         functools.partial(output_kernel, ways, seq_size),
         out_shape=jax.ShapeDtypeStruct((requests, w_out.shape[1]), jnp.bfloat16),
-        in_specs=[smem] + [vmem] * (ways + 1),
+        in_specs=[vmem] * (ways + 1),
         out_specs=vmem,
         scratch_shapes=[pltpu.VMEM((requests, w_out.shape[1]), jnp.float32)],
         compiler_params=pltpu.CompilerParams(vmem_limit_bytes=16 * 2**20),
         name="project_out",
-    )(me, *gather_relative(my_context, "seq", seq_size), w_out)
+    )(*gather_relative(my_context, "seq", seq_size), w_out)
     mask = head_size // 2
     while mask:
         if mask > 1:

time: 64.8 us -> 64.6 us (level)
  no operation moved by 1% of the time
where the time goes in v14:
time: 64.6 us; the launch traced here: 64.4 us
  waiting for transfers between devices  26.7 us (41%)
  starting transfers between devices  21.9 us (34%)
  Pallas kernels  11.6 us (18%)
  local copies, waits for them, and re-layouts  3.35 us (5%)
  other arithmetic  0.78 us (1%)
    ppermute x16, waiting for transfers between devices, swap(): return lax.ppermute(x, axis, [(j, j ^ mask) for j in range(n)])  26.7 us
    ppermute x16, starting transfers between devices, swap(): return lax.ppermute(x, axis, [(j, j ^ mask) for j in range(n)])  21.9 us
    pallas_call x1, Pallas kernels, body(): pl.pallas_call(functools.partial(attention_kernel, ways, mine), out_shape...  5.28 us
    pallas_call x1, Pallas kernels, body(): pl.pallas_call(functools.partial(project_kernel, ways), out_shape=[part_s...  3.59 us
    unnamed x20, local copies, waits for them, and re-layouts  3.35 us
  transfers between devices with their start and end apart: 16, of which 14 were waited for; matrix products, arithmetic and copies ran while one was open for 0% of the time, Pallas kernels for 1%

profile of v14, /device:TPU:0, one launch (start us, length us, event | category | flops | bytes accessed | tf_op | source)
XLA Modules:
  0.0 64.4 jit_solution(3346381994065291611)
XLA Ops:
  0.0 3.6 %project.1 = (f32[2,8,2048]{2,1,0:T(8,128)S(1)}, f32[2,8,2048]{2,1,0:T(8,128)S(1)}, f32[2,8,2048]{2,1,0:T(8,128)S(1)}, f32[2,8,2048]{2,1,0:T(8,128)S(1)}, f32[64,512]{1,0:T(8,128)S(1)}) custom-call(bf16[64,1024]{1,0:T(8,128)(2,1)} %hidden.1, bf16[1024,2048]{1,0:T(8,128)(2,1)} %w_query.1, bf16[1024,512]{1,0:T(8,128)(2,1)} %w_keyval.1), custom_call_target="tpu_custom_call" | custom-call | tf_op jit(solution)/shard_map/project/pallas_call | solution.py:529
  3.6 4.0 %collective-permute-start = (f32[2,8,2048]{2,1,0:T(8,128)S(1)}, f32[2,8,2048]{2,1,0:T(8,128)S(1)}, u32[]{:S(2)}, u32[]{:S(2)}) collective-permute-start(f32[2,8,2048]{2,1,0:T(8,128)S(1)} %get-tuple-element.23), channel_id=1, source_target_pairs={{0,12},{4,8},{8,4},{12,0},{16,28},{20,24},{24,20},{28,16},{1,13},{... | collective-permute-start | bytes 393224 | tf_op jit(solution)/shard_map/ppermute | solution.py:22
  11.6 0.9 %page_table.1 = (f32[64,128]{1,0:T(8,128)S(1)}, s32[1,128]{1,0:T(1,128)S(1)}) custom-call(s32[64]{0:T(128)S(1)} %copy-done.3, s32[64]{0:T(128)S(1)} %copy-done.4, s32[1,128]{1,0:T(1,128)S(1)} %bitcast.11, f32[2,128]{1,0:T(2,128)S(1)} %bitcast.8, f32[2,128]{1,0:T(2,128)S(1)} %bitcast.9), custom_call_target="tpu_custom_call" | custom-call | tf_op jit(solution)/shard_map/page_table/pallas_call | solution.py:513
  12.5 1.5 %collective-permute-done.1 = f32[2,8,2048]{2,1,0:T(8,128)S(1)} collective-permute-done((f32[2,8,2048]{2,1,0:T(8,128)S(1)}, f32[2,8,2048]{2,1,0:T(8,128)S(1)}, u32[]{:S(2)}, u32[]{:S(2)}) %collective-permute-start.1) | collective-permute-done | bytes 131104 | tf_op jit(solution)/shard_map/ppermute | solution.py:22
  14.2 2.7 %collective-permute-start.3 = (f32[2,8,2048]{2,1,0:T(8,128)S(1)}, f32[2,8,2048]{2,1,0:T(8,128)S(1)}, u32[]{:S(2)}, u32[]{:S(2)}) collective-permute-start(f32[2,8,2048]{2,1,0:T(8,128)S(1)} %add_add_fusion.refs_0_), channel_id=1, source_target_pairs={{0,16},{4,20},{8,24},{12,28},{16,0},{20,4},{24,8},{28,12},{1,17},{... | collective-permute-start | bytes 393224 | tf_op jit(solution)/shard_map/ppermute | solution.py:22
  16.8 6.4 %collective-permute-done.3.refs_1_ = f32[2,8,2048]{2,1,0:T(8,128)S(1)} collective-permute-done((f32[2,8,2048]{2,1,0:T(8,128)S(1)}, f32[2,8,2048]{2,1,0:T(8,128)S(1)}, u32[]{:S(2)}, u32[]{:S(2)}) %collective-permute-start.3) | collective-permute-done | bytes 131104 | tf_op jit(solution)/shard_map/ppermute | solution.py:22
  23.7 1.9 %collective-permute-start.5 = (bf16[256,128]{1,0:T(8,128)(2,1)S(1)}, bf16[256,128]{1,0:T(8,128)(2,1)S(1)}, u32[]{:S(2)}, u32[]{:S(2)}) collective-permute-start(bf16[256,128]{1,0:T(8,128)(2,1)S(1)} %join.1.refs_0_.refs_2_), channel_id=1, source_target_pairs={{0,4},{4,0},{8,12},{12,8},{16,20},{20,16},{24,28},{28,24},{1,5},{5... | collective-permute-start | bytes 196616 | tf_op jit(solution)/shard_map/ppermute | solution.py:22
  25.6 1.3 %collective-permute-start.6 = (bf16[256,128]{1,0:T(8,128)(2,1)S(1)}, bf16[256,128]{1,0:T(8,128)(2,1)S(1)}, u32[]{:S(2)}, u32[]{:S(2)}) collective-permute-start(bf16[256,128]{1,0:T(8,128)(2,1)S(1)} %join.1.refs_0_.refs_2_), channel_id=1, source_target_pairs={{0,8},{4,12},{8,0},{12,4},{16,24},{20,28},{24,16},{28,20},{1,9},{5... | collective-permute-start | bytes 196616 | tf_op jit(solution)/shard_map/ppermute | solution.py:22
  26.9 1.9 %collective-permute-done.4.refs_1_ = bf16[256,128]{1,0:T(8,128)(2,1)S(1)} collective-permute-done((bf16[256,128]{1,0:T(8,128)(2,1)S(1)}, bf16[256,128]{1,0:T(8,128)(2,1)S(1)}, u32[]{:S(2)}, u32[]{:S(2)}) %collective-permute-start.4) | collective-permute-done | bytes 65568 | tf_op jit(solution)/shard_map/ppermute | solution.py:22
  28.8 1.1 %collective-permute-done.6.refs_3_ = bf16[256,128]{1,0:T(8,128)(2,1)S(1)} collective-permute-done((bf16[256,128]{1,0:T(8,128)(2,1)S(1)}, bf16[256,128]{1,0:T(8,128)(2,1)S(1)}, u32[]{:S(2)}, u32[]{:S(2)}) %collective-permute-start.6) | collective-permute-done | bytes 65568 | tf_op jit(solution)/shard_map/ppermute | solution.py:22
  29.9 5.3 %paged_attention.1 = (bf16[2,176,128]{2,1,0:T(8,128)(2,1)S(1)}, bf16[2,176,128]{2,1,0:T(8,128)(2,1)S(1)}, bf16[2,176,128]{2,1,0:T(8,128)(2,1)S(1)}, bf16[2,176,128]{2,1,0:T(8,128)(2,1)S(1)}) custom-call(s32[128]{0:T(128)S(1)} %bitcast.10, bf16[256,128]{1,0:T(8,128)(2,1)S(1)} %join.1.refs_0_.refs_2_, bf16[256,128]{1,0:T(8,128)(2,1)S(1)} %collective-permute-done.4.refs_1_, ...), custom_call_target="tpu_custom_call" | custom-call | flops 134217728 | bytes 16777216 | tf_op jit(solution)/shard_map/paged_attention/pallas_call | solution.py:560
  35.2 1.6 %collective-permute-start.7 = (bf16[2,176,128]{2,1,0:T(8,128)(2,1)S(1)}, bf16[2,176,128]{2,1,0:T(8,128)(2,1)S(1)}, u32[]{:S(2)}, u32[]{:S(2)}) collective-permute-start(bf16[2,176,128]{2,1,0:T(8,128)(2,1)S(1)} %get-tuple-element.36), channel_id=1, source_target_pairs={{0,12},{4,8},{8,4},{12,0},{16,28},{20,24},{24,20},{28,16},{1,13},{... | collective-permute-start | bytes 270344 | tf_op jit(solution)/shard_map/ppermute | solution.py:22
  36.8 1.2 %collective-permute-start.8 = (bf16[2,176,128]{2,1,0:T(8,128)(2,1)S(1)}, bf16[2,176,128]{2,1,0:T(8,128)(2,1)S(1)}, u32[]{:S(2)}, u32[]{:S(2)}) collective-permute-start(bf16[2,176,128]{2,1,0:T(8,128)(2,1)S(1)} %get-tuple-element.37), channel_id=1, source_target_pairs={{0,4},{4,0},{8,12},{12,8},{16,20},{20,16},{24,28},{28,24},{1,5},{5... | collective-permute-start | bytes 270344 | tf_op jit(solution)/shard_map/ppermute | solution.py:22
  38.8 2.3 %collective-permute-done.7.refs_1_ = bf16[2,176,128]{2,1,0:T(8,128)(2,1)S(1)} collective-permute-done((bf16[2,176,128]{2,1,0:T(8,128)(2,1)S(1)}, bf16[2,176,128]{2,1,0:T(8,128)(2,1)S(1)}, u32[]{:S(2)}, u32[]{:S(2)}) %collective-permute-start.7) | collective-permute-done | bytes 90144 | tf_op jit(solution)/shard_map/ppermute | solution.py:22
  41.0 0.9 %collective-permute-done.8.refs_2_ = bf16[2,176,128]{2,1,0:T(8,128)(2,1)S(1)} collective-permute-done((bf16[2,176,128]{2,1,0:T(8,128)(2,1)S(1)}, bf16[2,176,128]{2,1,0:T(8,128)(2,1)S(1)}, u32[]{:S(2)}, u32[]{:S(2)}) %collective-permute-start.8) | collective-permute-done | bytes 90144 | tf_op jit(solution)/shard_map/ppermute | solution.py:22
  43.0 2.3 %collective-permute-start.10 = (bf16[2,176,128]{2,1,0:T(8,128)(2,1)S(1)}, bf16[2,176,128]{2,1,0:T(8,128)(2,1)S(1)}, u32[]{:S(2)}, u32[]{:S(2)}) collective-permute-start(bf16[2,176,128]{2,1,0:T(8,128)(2,1)S(1)} %combine.1.refs_0_), channel_id=1, source_target_pairs={{0,16},{4,20},{8,24},{12,28},{16,0},{20,4},{24,8},{28,12},{1,17},{... | collective-permute-start | bytes 270344 | tf_op jit(solution)/shard_map/ppermute | solution.py:22
  45.3 4.2 %collective-permute-done.10.refs_1_ = bf16[2,176,128]{2,1,0:T(8,128)(2,1)S(1)} collective-permute-done((bf16[2,176,128]{2,1,0:T(8,128)(2,1)S(1)}, bf16[2,176,128]{2,1,0:T(8,128)(2,1)S(1)}, u32[]{:S(2)}, u32[]{:S(2)}) %collective-permute-start.10) | collective-permute-done | bytes 90144 | tf_op jit(solution)/shard_map/ppermute | solution.py:22
  50.4 1.5 %collective-permute-start.12 = (bf16[16,2048]{1,0:T(8,128)(2,1)S(1)}, bf16[16,2048]{1,0:T(8,128)(2,1)S(1)}, u32[]{:S(2)}, u32[]{:S(2)}) collective-permute-start(bf16[16,2048]{1,0:T(8,128)(2,1)S(1)} %finish.1.refs_0_), channel_id=1, source_target_pairs={{0,4},{4,0},{8,12},{12,8},{16,20},{20,16},{24,28},{28,24},{1,5},{5... | collective-permute-start | bytes 196616 | tf_op jit(solution)/shard_map/ppermute | solution.py:22
  51.9 1.6 %collective-permute-start.13 = (bf16[16,2048]{1,0:T(8,128)(2,1)S(1)}, bf16[16,2048]{1,0:T(8,128)(2,1)S(1)}, u32[]{:S(2)}, u32[]{:S(2)}) collective-permute-start(bf16[16,2048]{1,0:T(8,128)(2,1)S(1)} %finish.1.refs_0_), channel_id=1, source_target_pairs={{0,8},{4,12},{8,0},{12,4},{16,24},{20,28},{24,16},{28,20},{1,9},{5... | collective-permute-start | bytes 196616 | tf_op jit(solution)/shard_map/ppermute | solution.py:22
  53.5 1.8 %collective-permute-done.11.refs_1_ = bf16[16,2048]{1,0:T(8,128)(2,1)S(1)} collective-permute-done((bf16[16,2048]{1,0:T(8,128)(2,1)S(1)}, bf16[16,2048]{1,0:T(8,128)(2,1)S(1)}, u32[]{:S(2)}, u32[]{:S(2)}) %collective-permute-start.11) | collective-permute-done | bytes 65568 | tf_op jit(solution)/shard_map/ppermute | solution.py:22
  56.2 0.9 %project_out.1 = bf16[64,1024]{1,0:T(8,128)(2,1)S(1)} custom-call(bf16[16,2048]{1,0:T(8,128)(2,1)S(1)} %finish.1.refs_0_, bf16[16,2048]{1,0:T(8,128)(2,1)S(1)} %collective-permute-done.11.refs_1_, bf16[16,2048]{1,0:T(8,128)(2,1)S(1)} %collective-permute-done.12.refs_2_, bf16[16,2048]{1,0:T(8,128)(2,1)S(1)} %collective-permute-done.13.refs_3_, ...), custom_call_target="tpu_custom_call" | custom-call | tf_op jit(solution)/shard_map/project_out/pallas_call | solution.py:610
  57.0 1.6 %collective-permute-start.14 = (bf16[64,1024]{1,0:T(8,128)(2,1)S(1)}, bf16[64,1024]{1,0:T(8,128)(2,1)S(1)}, u32[]{:S(2)}, u32[]{:S(2)}) collective-permute-start(bf16[64,1024]{1,0:T(8,128)(2,1)S(1)} %project_out.1), channel_id=1, source_target_pairs={{0,2},{1,3},{2,0},{3,1},{4,6},{5,7},{6,4},{7,5},{8,10},{9,11},{10,... | collective-permute-start | bytes 393224 | tf_op jit(solution)/shard_map/ppermute | solution.py:22
  58.6 3.5 %collective-permute-done.14 = bf16[64,1024]{1,0:T(8,128)(2,1)S(1)} collective-permute-done((bf16[64,1024]{1,0:T(8,128)(2,1)S(1)}, bf16[64,1024]{1,0:T(8,128)(2,1)S(1)}, u32[]{:S(2)}, u32[]{:S(2)}) %collective-permute-start.14) | collective-permute-done | bytes 131104 | tf_op jit(solution)/shard_map/ppermute | solution.py:22
  62.2 1.5 %collective-permute-done.15 = f32[64,1024]{1,0:T(8,128)S(1)} collective-permute-done((f32[64,1024]{1,0:T(8,128)S(1)}, f32[64,1024]{1,0:T(8,128)S(1)}, u32[]{:S(2)}, u32[]{:S(2)}) %collective-permute-start.15) | collective-permute-done | bytes 262176 | tf_op jit(solution)/shard_map/ppermute | solution.py:22
  (40 shorter events, 9.1 us)
Async XLA Ops:
  3.6 8.9 %collective-permute-start = (f32[2,8,2048]{2,1,0:T(8,128)S(1)}, f32[2,8,2048]{2,1,0:T(8,128)S(1)}, u32[]{:S(2)}, u32[]{:S(2)}) collective-permute-start(f32[2,8,2048]{2,1,0:T(8,128)S(1)} %get-tuple-element.23), channel_id=1, source_target_pairs={{0,12},{4,8},{8,4},{12,0},{16,28},{20,24},{24,20},{28,16},{1,13},{... | collective-permute-start | bytes 393224 | tf_op jit(solution)/shard_map/ppermute | solution.py:22
  7.6 6.3 %collective-permute-start.1 = (f32[2,8,2048]{2,1,0:T(8,128)S(1)}, f32[2,8,2048]{2,1,0:T(8,128)S(1)}, u32[]{:S(2)}, u32[]{:S(2)}) collective-permute-start(f32[2,8,2048]{2,1,0:T(8,128)S(1)} %get-tuple-element.24), channel_id=1, source_target_pairs={{0,4},{4,0},{8,12},{12,8},{16,20},{20,16},{24,28},{28,24},{1,5},{5... | collective-permute-start | bytes 393224 | tf_op jit(solution)/shard_map/ppermute | solution.py:22
  8.1 6.0 %collective-permute-start.2 = (f32[2,8,2048]{2,1,0:T(8,128)S(1)}, f32[2,8,2048]{2,1,0:T(8,128)S(1)}, u32[]{:S(2)}, u32[]{:S(2)}) collective-permute-start(f32[2,8,2048]{2,1,0:T(8,128)S(1)} %get-tuple-element.25), channel_id=1, source_target_pairs={{0,8},{4,12},{8,0},{12,4},{16,24},{20,28},{24,16},{28,20},{1,9},{5... | collective-permute-start | bytes 393224 | tf_op jit(solution)/shard_map/ppermute | solution.py:22
  8.3 0.7 %copy-start.1 = (f32[128,2]{0,1:T(2,128)S(1)}, f32[128,2]{0,1:T(2,128)}, u32[]{:S(2)}) copy-start(f32[128,2]{0,1:T(2,128)} %param.17) | copy-start | bytes 3076
  9.0 0.7 %copy-start.2 = (f32[128,2]{0,1:T(2,128)S(1)}, f32[128,2]{0,1:T(2,128)}, u32[]{:S(2)}) copy-start(f32[128,2]{0,1:T(2,128)} %param.18) | copy-start | bytes 3076
  9.6 0.7 %copy-start.3 = (s32[64]{0:T(128)S(1)}, s32[64]{0:T(128)}, u32[]{:S(2)}) copy-start(s32[64]{0:T(128)} %counts.1) | copy-start | bytes 772
  14.1 15.8 %slice-start = ((s8[8388608]{0:T(1024)(128)(4,1)}), s8[4194304]{0:T(1024)(128)(4,1)S(1)}, s32[]{:S(2)}) async-start(s8[8388608]{0:T(1024)(128)(4,1)} %bitcast.4), calls=%async_computation | async-start | bytes 8388608
  14.1 15.8 %slice-start.2 = ((s8[8388608]{0:T(1024)(128)(4,1)}), s8[4194304]{0:T(1024)(128)(4,1)S(1)}, s32[]{:S(2)}) async-start(s8[8388608]{0:T(1024)(128)(4,1)} %bitcast.6), calls=%async_computation.2 | async-start | bytes 8388608
  14.2 15.7 %slice-start.1 = ((s8[8388608]{0:T(1024)(128)(4,1)}), s8[4194304]{0:T(1024)(128)(4,1)S(1)}, s32[]{:S(2)}) async-start(s8[8388608]{0:T(1024)(128)(4,1)} %bitcast.4), calls=%async_computation.1 | async-start | bytes 8388608
  14.2 15.7 %slice-start.3 = ((s8[8388608]{0:T(1024)(128)(4,1)}), s8[4194304]{0:T(1024)(128)(4,1)S(1)}, s32[]{:S(2)}) async-start(s8[8388608]{0:T(1024)(128)(4,1)} %bitcast.6), calls=%async_computation.3 | async-start | bytes 8388608
  14.2 9.1 %collective-permute-start.3 = (f32[2,8,2048]{2,1,0:T(8,128)S(1)}, f32[2,8,2048]{2,1,0:T(8,128)S(1)}, u32[]{:S(2)}, u32[]{:S(2)}) collective-permute-start(f32[2,8,2048]{2,1,0:T(8,128)S(1)} %add_add_fusion.refs_0_), channel_id=1, source_target_pairs={{0,16},{4,20},{8,24},{12,28},{16,0},{20,4},{24,8},{28,12},{1,17},{... | collective-permute-start | bytes 393224 | tf_op jit(solution)/shard_map/ppermute | solution.py:22
  23.3 5.5 %collective-permute-start.4 = (bf16[256,128]{1,0:T(8,128)(2,1)S(1)}, bf16[256,128]{1,0:T(8,128)(2,1)S(1)}, u32[]{:S(2)}, u32[]{:S(2)}) collective-permute-start(bf16[256,128]{1,0:T(8,128)(2,1)S(1)} %join.1.refs_0_.refs_2_), channel_id=1, source_target_pairs={{0,12},{4,8},{8,4},{12,0},{16,28},{20,24},{24,20},{28,16},{1,13},{... | collective-permute-start | bytes 196616 | tf_op jit(solution)/shard_map/ppermute | solution.py:22
  23.7 5.1 %collective-permute-start.5 = (bf16[256,128]{1,0:T(8,128)(2,1)S(1)}, bf16[256,128]{1,0:T(8,128)(2,1)S(1)}, u32[]{:S(2)}, u32[]{:S(2)}) collective-permute-start(bf16[256,128]{1,0:T(8,128)(2,1)S(1)} %join.1.refs_0_.refs_2_), channel_id=1, source_target_pairs={{0,4},{4,0},{8,12},{12,8},{16,20},{20,16},{24,28},{28,24},{1,5},{5... | collective-permute-start | bytes 196616 | tf_op jit(solution)/shard_map/ppermute | solution.py:22
  25.6 4.3 %collective-permute-start.6 = (bf16[256,128]{1,0:T(8,128)(2,1)S(1)}, bf16[256,128]{1,0:T(8,128)(2,1)S(1)}, u32[]{:S(2)}, u32[]{:S(2)}) collective-permute-start(bf16[256,128]{1,0:T(8,128)(2,1)S(1)} %join.1.refs_0_.refs_2_), channel_id=1, source_target_pairs={{0,8},{4,12},{8,0},{12,4},{16,24},{20,28},{24,16},{28,20},{1,9},{5... | collective-permute-start | bytes 196616 | tf_op jit(solution)/shard_map/ppermute | solution.py:22
  29.9 26.3 %copy-start = (bf16[2048,1024]{1,0:T(8,128)(2,1)S(1)}, bf16[2048,1024]{1,0:T(8,128)(2,1)}, u32[]{:S(2)}) copy-start(bf16[2048,1024]{1,0:T(8,128)(2,1)} %refs_4_.1) | copy-start | bytes 12582916
  35.2 5.8 %collective-permute-start.7 = (bf16[2,176,128]{2,1,0:T(8,128)(2,1)S(1)}, bf16[2,176,128]{2,1,0:T(8,128)(2,1)S(1)}, u32[]{:S(2)}, u32[]{:S(2)}) collective-permute-start(bf16[2,176,128]{2,1,0:T(8,128)(2,1)S(1)} %get-tuple-element.36), channel_id=1, source_target_pairs={{0,12},{4,8},{8,4},{12,0},{16,28},{20,24},{24,20},{28,16},{1,13},{... | collective-permute-start | bytes 270344 | tf_op jit(solution)/shard_map/ppermute | solution.py:22
  36.8 5.1 %collective-permute-start.8 = (bf16[2,176,128]{2,1,0:T(8,128)(2,1)S(1)}, bf16[2,176,128]{2,1,0:T(8,128)(2,1)S(1)}, u32[]{:S(2)}, u32[]{:S(2)}) collective-permute-start(bf16[2,176,128]{2,1,0:T(8,128)(2,1)S(1)} %get-tuple-element.37), channel_id=1, source_target_pairs={{0,4},{4,0},{8,12},{12,8},{16,20},{20,16},{24,28},{28,24},{1,5},{5... | collective-permute-start | bytes 270344 | tf_op jit(solution)/shard_map/ppermute | solution.py:22
  38.0 4.5 %collective-permute-start.9 = (bf16[2,176,128]{2,1,0:T(8,128)(2,1)S(1)}, bf16[2,176,128]{2,1,0:T(8,128)(2,1)S(1)}, u32[]{:S(2)}, u32[]{:S(2)}) collective-permute-start(bf16[2,176,128]{2,1,0:T(8,128)(2,1)S(1)} %get-tuple-element.38), channel_id=1, source_target_pairs={{0,8},{4,12},{8,0},{12,4},{16,24},{20,28},{24,16},{28,20},{1,9},{5... | collective-permute-start | bytes 270344 | tf_op jit(solution)/shard_map/ppermute | solution.py:22
  43.0 6.5 %collective-permute-start.10 = (bf16[2,176,128]{2,1,0:T(8,128)(2,1)S(1)}, bf16[2,176,128]{2,1,0:T(8,128)(2,1)S(1)}, u32[]{:S(2)}, u32[]{:S(2)}) collective-permute-start(bf16[2,176,128]{2,1,0:T(8,128)(2,1)S(1)} %combine.1.refs_0_), channel_id=1, source_target_pairs={{0,16},{4,20},{8,24},{12,28},{16,0},{20,4},{24,8},{28,12},{1,17},{... | collective-permute-start | bytes 270344 | tf_op jit(solution)/shard_map/ppermute | solution.py:22
  50.0 5.3 %collective-permute-start.11 = (bf16[16,2048]{1,0:T(8,128)(2,1)S(1)}, bf16[16,2048]{1,0:T(8,128)(2,1)S(1)}, u32[]{:S(2)}, u32[]{:S(2)}) collective-permute-start(bf16[16,2048]{1,0:T(8,128)(2,1)S(1)} %finish.1.refs_0_), channel_id=1, source_target_pairs={{0,12},{4,8},{8,4},{12,0},{16,28},{20,24},{24,20},{28,16},{1,13},{... | collective-permute-start | bytes 196616 | tf_op jit(solution)/shard_map/ppermute | solution.py:22
  50.4 5.0 %collective-permute-start.12 = (bf16[16,2048]{1,0:T(8,128)(2,1)S(1)}, bf16[16,2048]{1,0:T(8,128)(2,1)S(1)}, u32[]{:S(2)}, u32[]{:S(2)}) collective-permute-start(bf16[16,2048]{1,0:T(8,128)(2,1)S(1)} %finish.1.refs_0_), channel_id=1, source_target_pairs={{0,4},{4,0},{8,12},{12,8},{16,20},{20,16},{24,28},{28,24},{1,5},{5... | collective-permute-start | bytes 196616 | tf_op jit(solution)/shard_map/ppermute | solution.py:22
  51.9 4.3 %collective-permute-start.13 = (bf16[16,2048]{1,0:T(8,128)(2,1)S(1)}, bf16[16,2048]{1,0:T(8,128)(2,1)S(1)}, u32[]{:S(2)}, u32[]{:S(2)}) collective-permute-start(bf16[16,2048]{1,0:T(8,128)(2,1)S(1)} %finish.1.refs_0_), channel_id=1, source_target_pairs={{0,8},{4,12},{8,0},{12,4},{16,24},{20,28},{24,16},{28,20},{1,9},{5... | collective-permute-start | bytes 196616 | tf_op jit(solution)/shard_map/ppermute | solution.py:22
  57.0 5.0 %collective-permute-start.14 = (bf16[64,1024]{1,0:T(8,128)(2,1)S(1)}, bf16[64,1024]{1,0:T(8,128)(2,1)S(1)}, u32[]{:S(2)}, u32[]{:S(2)}) collective-permute-start(bf16[64,1024]{1,0:T(8,128)(2,1)S(1)} %project_out.1), channel_id=1, source_target_pairs={{0,2},{1,3},{2,0},{3,1},{4,6},{5,7},{6,4},{7,5},{8,10},{9,11},{10,... | collective-permute-start | bytes 393224 | tf_op jit(solution)/shard_map/ppermute | solution.py:22
  62.1 1.6 %collective-permute-start.15 = (f32[64,1024]{1,0:T(8,128)S(1)}, f32[64,1024]{1,0:T(8,128)S(1)}, u32[]{:S(2)}, u32[]{:S(2)}) collective-permute-start(f32[64,1024]{1,0:T(8,128)S(1)} %convert_add_fusion), channel_id=1, source_target_pairs={{0,1},{1,0},{2,3},{3,2},{4,5},{5,4},{6,7},{7,6},{8,9},{9,8},{10,11... | collective-permute-start | bytes 786440 | tf_op jit(solution)/shard_map/ppermute | solution.py:22
  (2 other events, 1.3 us)

commit v15 on v14

--- a/solution.py
+++ b/solution.py
@@ -263,7 +263,7 @@
     group = heads // 2
     chunks = slots // CHUNK
     blocks = outs[0].shape[0]
-    lag = 4
+    lag = 2
 
     for d, part in enumerate(in_order(queries)):
         rows = part[...]
@@ -618,13 +618,10 @@
     )(*gather_relative(my_context, "seq", seq_size), w_out)
     mask = head_size // 2
     while mask:
-        if mask > 1:
-            if total.dtype != jnp.bfloat16:
-                total = lax.reduce_precision(total, 8, 7).astype(jnp.bfloat16)
-            other = swap(total, "head", head_size, mask)
-            total = total.astype(jnp.float32) + other.astype(jnp.float32)
-        else:
-            total = total + swap(total, "head", head_size, mask)
+        if total.dtype != jnp.bfloat16:
+            total = lax.reduce_precision(total, 8, 7).astype(jnp.bfloat16)
+        other = swap(total, "head", head_size, mask)
+        total = total.astype(jnp.float32) + other.astype(jnp.float32)
         mask //= 2
     return total.astype(jnp.bfloat16)
 

time: 64.6 us -> 66.3 us (1.026)
  Pallas kernels: 11.6 us -> 13.6 us
    pallas_call x1, Pallas kernels: 5.28 us -> 7.24 us  [body(): pl.pallas_call(functools.partial(attention_kernel, ways, mine), out_shape...]
where the time goes in v15:
time: 66.3 us; the launch traced here: 66.2 us
  waiting for transfers between devices  26.4 us (40%)
  starting transfers between devices  21.9 us (33%)
  Pallas kernels  13.6 us (21%)
  local copies, waits for them, and re-layouts  3.35 us (5%)
  other arithmetic  0.77 us (1%)
    ppermute x16, waiting for transfers between devices, swap(): return lax.ppermute(x, axis, [(j, j ^ mask) for j in range(n)])  26.4 us
    ppermute x16, starting transfers between devices, swap(): return lax.ppermute(x, axis, [(j, j ^ mask) for j in range(n)])  21.9 us
    pallas_call x1, Pallas kernels, body(): pl.pallas_call(functools.partial(attention_kernel, ways, mine), out_shape...  7.24 us
    pallas_call x1, Pallas kernels, body(): pl.pallas_call(functools.partial(project_kernel, ways), out_shape=[part_s...  3.59 us
    unnamed x20, local copies, waits for them, and re-layouts  3.35 us
  transfers between devices with their start and end apart: 16, of which 14 were waited for; matrix products, arithmetic and copies ran while one was open for 0% of the time, Pallas kernels for 1%

profile of v15, /device:TPU:0, one launch (start us, length us, event | category | flops | bytes accessed | tf_op | source)
XLA Modules:
  0.0 66.2 jit_solution(3506499301347765987)
XLA Ops:
  0.0 3.6 %project.1 = (f32[2,8,2048]{2,1,0:T(8,128)S(1)}, f32[2,8,2048]{2,1,0:T(8,128)S(1)}, f32[2,8,2048]{2,1,0:T(8,128)S(1)}, f32[2,8,2048]{2,1,0:T(8,128)S(1)}, f32[64,512]{1,0:T(8,128)S(1)}) custom-call(bf16[64,1024]{1,0:T(8,128)(2,1)} %hidden.1, bf16[1024,2048]{1,0:T(8,128)(2,1)} %w_query.1, bf16[1024,512]{1,0:T(8,128)(2,1)} %w_keyval.1), custom_call_target="tpu_custom_call" | custom-call | tf_op jit(solution)/shard_map/project/pallas_call | solution.py:529
  3.6 4.0 %collective-permute-start = (f32[2,8,2048]{2,1,0:T(8,128)S(1)}, f32[2,8,2048]{2,1,0:T(8,128)S(1)}, u32[]{:S(2)}, u32[]{:S(2)}) collective-permute-start(f32[2,8,2048]{2,1,0:T(8,128)S(1)} %get-tuple-element.23), channel_id=1, source_target_pairs={{0,12},{4,8},{8,4},{12,0},{16,28},{20,24},{24,20},{28,16},{1,13},{... | collective-permute-start | bytes 393224 | tf_op jit(solution)/shard_map/ppermute | solution.py:22
  11.6 0.9 %page_table.1 = (f32[64,128]{1,0:T(8,128)S(1)}, s32[1,128]{1,0:T(1,128)S(1)}) custom-call(s32[64]{0:T(128)S(1)} %copy-done.3, s32[64]{0:T(128)S(1)} %copy-done.4, s32[1,128]{1,0:T(1,128)S(1)} %bitcast.11, f32[2,128]{1,0:T(2,128)S(1)} %bitcast.8, f32[2,128]{1,0:T(2,128)S(1)} %bitcast.9), custom_call_target="tpu_custom_call" | custom-call | tf_op jit(solution)/shard_map/page_table/pallas_call | solution.py:513
  12.5 1.5 %collective-permute-done.1 = f32[2,8,2048]{2,1,0:T(8,128)S(1)} collective-permute-done((f32[2,8,2048]{2,1,0:T(8,128)S(1)}, f32[2,8,2048]{2,1,0:T(8,128)S(1)}, u32[]{:S(2)}, u32[]{:S(2)}) %collective-permute-start.1) | collective-permute-done | bytes 131104 | tf_op jit(solution)/shard_map/ppermute | solution.py:22
  14.2 2.7 %collective-permute-start.3 = (f32[2,8,2048]{2,1,0:T(8,128)S(1)}, f32[2,8,2048]{2,1,0:T(8,128)S(1)}, u32[]{:S(2)}, u32[]{:S(2)}) collective-permute-start(f32[2,8,2048]{2,1,0:T(8,128)S(1)} %add_add_fusion.refs_0_), channel_id=1, source_target_pairs={{0,16},{4,20},{8,24},{12,28},{16,0},{20,4},{24,8},{28,12},{1,17},{... | collective-permute-start | bytes 393224 | tf_op jit(solution)/shard_map/ppermute | solution.py:22
  16.8 6.4 %collective-permute-done.3.refs_1_ = f32[2,8,2048]{2,1,0:T(8,128)S(1)} collective-permute-done((f32[2,8,2048]{2,1,0:T(8,128)S(1)}, f32[2,8,2048]{2,1,0:T(8,128)S(1)}, u32[]{:S(2)}, u32[]{:S(2)}) %collective-permute-start.3) | collective-permute-done | bytes 131104 | tf_op jit(solution)/shard_map/ppermute | solution.py:22
  23.7 1.9 %collective-permute-start.5 = (bf16[256,128]{1,0:T(8,128)(2,1)S(1)}, bf16[256,128]{1,0:T(8,128)(2,1)S(1)}, u32[]{:S(2)}, u32[]{:S(2)}) collective-permute-start(bf16[256,128]{1,0:T(8,128)(2,1)S(1)} %join.1.refs_0_.refs_2_), channel_id=1, source_target_pairs={{0,4},{4,0},{8,12},{12,8},{16,20},{20,16},{24,28},{28,24},{1,5},{5... | collective-permute-start | bytes 196616 | tf_op jit(solution)/shard_map/ppermute | solution.py:22
  25.6 1.3 %collective-permute-start.6 = (bf16[256,128]{1,0:T(8,128)(2,1)S(1)}, bf16[256,128]{1,0:T(8,128)(2,1)S(1)}, u32[]{:S(2)}, u32[]{:S(2)}) collective-permute-start(bf16[256,128]{1,0:T(8,128)(2,1)S(1)} %join.1.refs_0_.refs_2_), channel_id=1, source_target_pairs={{0,8},{4,12},{8,0},{12,4},{16,24},{20,28},{24,16},{28,20},{1,9},{5... | collective-permute-start | bytes 196616 | tf_op jit(solution)/shard_map/ppermute | solution.py:22
  26.9 1.9 %collective-permute-done.4.refs_1_ = bf16[256,128]{1,0:T(8,128)(2,1)S(1)} collective-permute-done((bf16[256,128]{1,0:T(8,128)(2,1)S(1)}, bf16[256,128]{1,0:T(8,128)(2,1)S(1)}, u32[]{:S(2)}, u32[]{:S(2)}) %collective-permute-start.4) | collective-permute-done | bytes 65568 | tf_op jit(solution)/shard_map/ppermute | solution.py:22
  28.8 1.1 %collective-permute-done.6.refs_3_ = bf16[256,128]{1,0:T(8,128)(2,1)S(1)} collective-permute-done((bf16[256,128]{1,0:T(8,128)(2,1)S(1)}, bf16[256,128]{1,0:T(8,128)(2,1)S(1)}, u32[]{:S(2)}, u32[]{:S(2)}) %collective-permute-start.6) | collective-permute-done | bytes 65568 | tf_op jit(solution)/shard_map/ppermute | solution.py:22
  29.9 7.2 %paged_attention.1 = (bf16[2,176,128]{2,1,0:T(8,128)(2,1)S(1)}, bf16[2,176,128]{2,1,0:T(8,128)(2,1)S(1)}, bf16[2,176,128]{2,1,0:T(8,128)(2,1)S(1)}, bf16[2,176,128]{2,1,0:T(8,128)(2,1)S(1)}) custom-call(s32[128]{0:T(128)S(1)} %bitcast.10, bf16[256,128]{1,0:T(8,128)(2,1)S(1)} %join.1.refs_0_.refs_2_, bf16[256,128]{1,0:T(8,128)(2,1)S(1)} %collective-permute-done.4.refs_1_, ...), custom_call_target="tpu_custom_call" | custom-call | flops 134217728 | bytes 16777216 | tf_op jit(solution)/shard_map/paged_attention/pallas_call | solution.py:560
  37.2 1.6 %collective-permute-start.7 = (bf16[2,176,128]{2,1,0:T(8,128)(2,1)S(1)}, bf16[2,176,128]{2,1,0:T(8,128)(2,1)S(1)}, u32[]{:S(2)}, u32[]{:S(2)}) collective-permute-start(bf16[2,176,128]{2,1,0:T(8,128)(2,1)S(1)} %get-tuple-element.36), channel_id=1, source_target_pairs={{0,12},{4,8},{8,4},{12,0},{16,28},{20,24},{24,20},{28,16},{1,13},{... | collective-permute-start | bytes 270344 | tf_op jit(solution)/shard_map/ppermute | solution.py:22
  38.8 1.2 %collective-permute-start.8 = (bf16[2,176,128]{2,1,0:T(8,128)(2,1)S(1)}, bf16[2,176,128]{2,1,0:T(8,128)(2,1)S(1)}, u32[]{:S(2)}, u32[]{:S(2)}) collective-permute-start(bf16[2,176,128]{2,1,0:T(8,128)(2,1)S(1)} %get-tuple-element.37), channel_id=1, source_target_pairs={{0,4},{4,0},{8,12},{12,8},{16,20},{20,16},{24,28},{28,24},{1,5},{5... | collective-permute-start | bytes 270344 | tf_op jit(solution)/shard_map/ppermute | solution.py:22
  40.7 2.2 %collective-permute-done.7.refs_1_ = bf16[2,176,128]{2,1,0:T(8,128)(2,1)S(1)} collective-permute-done((bf16[2,176,128]{2,1,0:T(8,128)(2,1)S(1)}, bf16[2,176,128]{2,1,0:T(8,128)(2,1)S(1)}, u32[]{:S(2)}, u32[]{:S(2)}) %collective-permute-start.7) | collective-permute-done | bytes 90144 | tf_op jit(solution)/shard_map/ppermute | solution.py:22
  43.0 0.9 %collective-permute-done.8.refs_2_ = bf16[2,176,128]{2,1,0:T(8,128)(2,1)S(1)} collective-permute-done((bf16[2,176,128]{2,1,0:T(8,128)(2,1)S(1)}, bf16[2,176,128]{2,1,0:T(8,128)(2,1)S(1)}, u32[]{:S(2)}, u32[]{:S(2)}) %collective-permute-start.8) | collective-permute-done | bytes 90144 | tf_op jit(solution)/shard_map/ppermute | solution.py:22
  45.0 2.3 %collective-permute-start.10 = (bf16[2,176,128]{2,1,0:T(8,128)(2,1)S(1)}, bf16[2,176,128]{2,1,0:T(8,128)(2,1)S(1)}, u32[]{:S(2)}, u32[]{:S(2)}) collective-permute-start(bf16[2,176,128]{2,1,0:T(8,128)(2,1)S(1)} %combine.1.refs_0_), channel_id=1, source_target_pairs={{0,16},{4,20},{8,24},{12,28},{16,0},{20,4},{24,8},{28,12},{1,17},{... | collective-permute-start | bytes 270344 | tf_op jit(solution)/shard_map/ppermute | solution.py:22
  47.2 4.2 %collective-permute-done.10.refs_1_ = bf16[2,176,128]{2,1,0:T(8,128)(2,1)S(1)} collective-permute-done((bf16[2,176,128]{2,1,0:T(8,128)(2,1)S(1)}, bf16[2,176,128]{2,1,0:T(8,128)(2,1)S(1)}, u32[]{:S(2)}, u32[]{:S(2)}) %collective-permute-start.10) | collective-permute-done | bytes 90144 | tf_op jit(solution)/shard_map/ppermute | solution.py:22
  52.4 1.5 %collective-permute-start.12 = (bf16[16,2048]{1,0:T(8,128)(2,1)S(1)}, bf16[16,2048]{1,0:T(8,128)(2,1)S(1)}, u32[]{:S(2)}, u32[]{:S(2)}) collective-permute-start(bf16[16,2048]{1,0:T(8,128)(2,1)S(1)} %finish.1.refs_0_), channel_id=1, source_target_pairs={{0,4},{4,0},{8,12},{12,8},{16,20},{20,16},{24,28},{28,24},{1,5},{5... | collective-permute-start | bytes 196616 | tf_op jit(solution)/shard_map/ppermute | solution.py:22
  53.8 1.6 %collective-permute-start.13 = (bf16[16,2048]{1,0:T(8,128)(2,1)S(1)}, bf16[16,2048]{1,0:T(8,128)(2,1)S(1)}, u32[]{:S(2)}, u32[]{:S(2)}) collective-permute-start(bf16[16,2048]{1,0:T(8,128)(2,1)S(1)} %finish.1.refs_0_), channel_id=1, source_target_pairs={{0,8},{4,12},{8,0},{12,4},{16,24},{20,28},{24,16},{28,20},{1,9},{5... | collective-permute-start | bytes 196616 | tf_op jit(solution)/shard_map/ppermute | solution.py:22
  55.5 1.8 %collective-permute-done.11.refs_1_ = bf16[16,2048]{1,0:T(8,128)(2,1)S(1)} collective-permute-done((bf16[16,2048]{1,0:T(8,128)(2,1)S(1)}, bf16[16,2048]{1,0:T(8,128)(2,1)S(1)}, u32[]{:S(2)}, u32[]{:S(2)}) %collective-permute-start.11) | collective-permute-done | bytes 65568 | tf_op jit(solution)/shard_map/ppermute | solution.py:22
  58.1 0.9 %project_out.1 = bf16[64,1024]{1,0:T(8,128)(2,1)S(1)} custom-call(bf16[16,2048]{1,0:T(8,128)(2,1)S(1)} %finish.1.refs_0_, bf16[16,2048]{1,0:T(8,128)(2,1)S(1)} %collective-permute-done.11.refs_1_, bf16[16,2048]{1,0:T(8,128)(2,1)S(1)} %collective-permute-done.12.refs_2_, bf16[16,2048]{1,0:T(8,128)(2,1)S(1)} %collective-permute-done.13.refs_3_, ...), custom_call_target="tpu_custom_call" | custom-call | tf_op jit(solution)/shard_map/project_out/pallas_call | solution.py:610
  59.0 1.6 %collective-permute-start.14 = (bf16[64,1024]{1,0:T(8,128)(2,1)S(1)}, bf16[64,1024]{1,0:T(8,128)(2,1)S(1)}, u32[]{:S(2)}, u32[]{:S(2)}) collective-permute-start(bf16[64,1024]{1,0:T(8,128)(2,1)S(1)} %project_out.1), channel_id=1, source_target_pairs={{0,2},{1,3},{2,0},{3,1},{4,6},{5,7},{6,4},{7,5},{8,10},{9,11},{10,... | collective-permute-start | bytes 393224 | tf_op jit(solution)/shard_map/ppermute | solution.py:22
  60.5 3.5 %collective-permute-done.14 = bf16[64,1024]{1,0:T(8,128)(2,1)S(1)} collective-permute-done((bf16[64,1024]{1,0:T(8,128)(2,1)S(1)}, bf16[64,1024]{1,0:T(8,128)(2,1)S(1)}, u32[]{:S(2)}, u32[]{:S(2)}) %collective-permute-start.14) | collective-permute-done | bytes 131104 | tf_op jit(solution)/shard_map/ppermute | solution.py:22
  64.1 1.3 %collective-permute-done.15 = bf16[64,1024]{1,0:T(8,128)(2,1)S(1)} collective-permute-done((bf16[64,1024]{1,0:T(8,128)(2,1)S(1)}, bf16[64,1024]{1,0:T(8,128)(2,1)S(1)}, u32[]{:S(2)}, u32[]{:S(2)}) %collective-permute-start.15) | collective-permute-done | bytes 131104 | tf_op jit(solution)/shard_map/ppermute | solution.py:22
  (40 shorter events, 9.0 us)
Async XLA Ops:
  3.6 8.9 %collective-permute-start = (f32[2,8,2048]{2,1,0:T(8,128)S(1)}, f32[2,8,2048]{2,1,0:T(8,128)S(1)}, u32[]{:S(2)}, u32[]{:S(2)}) collective-permute-start(f32[2,8,2048]{2,1,0:T(8,128)S(1)} %get-tuple-element.23), channel_id=1, source_target_pairs={{0,12},{4,8},{8,4},{12,0},{16,28},{20,24},{24,20},{28,16},{1,13},{... | collective-permute-start | bytes 393224 | tf_op jit(solution)/shard_map/ppermute | solution.py:22
  7.6 6.3 %collective-permute-start.1 = (f32[2,8,2048]{2,1,0:T(8,128)S(1)}, f32[2,8,2048]{2,1,0:T(8,128)S(1)}, u32[]{:S(2)}, u32[]{:S(2)}) collective-permute-start(f32[2,8,2048]{2,1,0:T(8,128)S(1)} %get-tuple-element.24), channel_id=1, source_target_pairs={{0,4},{4,0},{8,12},{12,8},{16,20},{20,16},{24,28},{28,24},{1,5},{5... | collective-permute-start | bytes 393224 | tf_op jit(solution)/shard_map/ppermute | solution.py:22
  8.1 6.0 %collective-permute-start.2 = (f32[2,8,2048]{2,1,0:T(8,128)S(1)}, f32[2,8,2048]{2,1,0:T(8,128)S(1)}, u32[]{:S(2)}, u32[]{:S(2)}) collective-permute-start(f32[2,8,2048]{2,1,0:T(8,128)S(1)} %get-tuple-element.25), channel_id=1, source_target_pairs={{0,8},{4,12},{8,0},{12,4},{16,24},{20,28},{24,16},{28,20},{1,9},{5... | collective-permute-start | bytes 393224 | tf_op jit(solution)/shard_map/ppermute | solution.py:22
  8.3 0.7 %copy-start.1 = (f32[128,2]{0,1:T(2,128)S(1)}, f32[128,2]{0,1:T(2,128)}, u32[]{:S(2)}) copy-start(f32[128,2]{0,1:T(2,128)} %param.17) | copy-start | bytes 3076
  9.0 0.7 %copy-start.2 = (f32[128,2]{0,1:T(2,128)S(1)}, f32[128,2]{0,1:T(2,128)}, u32[]{:S(2)}) copy-start(f32[128,2]{0,1:T(2,128)} %param.18) | copy-start | bytes 3076
  9.6 0.7 copy-start.3
  14.1 15.8 %slice-start = ((s8[8388608]{0:T(1024)(128)(4,1)}), s8[4194304]{0:T(1024)(128)(4,1)S(1)}, s32[]{:S(2)}) async-start(s8[8388608]{0:T(1024)(128)(4,1)} %bitcast.4), calls=%async_computation | async-start | bytes 8388608
  14.1 15.8 %slice-start.2 = ((s8[8388608]{0:T(1024)(128)(4,1)}), s8[4194304]{0:T(1024)(128)(4,1)S(1)}, s32[]{:S(2)}) async-start(s8[8388608]{0:T(1024)(128)(4,1)} %bitcast.6), calls=%async_computation.2 | async-start | bytes 8388608
  14.2 15.7 %slice-start.1 = ((s8[8388608]{0:T(1024)(128)(4,1)}), s8[4194304]{0:T(1024)(128)(4,1)S(1)}, s32[]{:S(2)}) async-start(s8[8388608]{0:T(1024)(128)(4,1)} %bitcast.4), calls=%async_computation.1 | async-start | bytes 8388608
  14.2 15.7 %slice-start.3 = ((s8[8388608]{0:T(1024)(128)(4,1)}), s8[4194304]{0:T(1024)(128)(4,1)S(1)}, s32[]{:S(2)}) async-start(s8[8388608]{0:T(1024)(128)(4,1)} %bitcast.6), calls=%async_computation.3 | async-start | bytes 8388608
  14.2 9.1 %collective-permute-start.3 = (f32[2,8,2048]{2,1,0:T(8,128)S(1)}, f32[2,8,2048]{2,1,0:T(8,128)S(1)}, u32[]{:S(2)}, u32[]{:S(2)}) collective-permute-start(f32[2,8,2048]{2,1,0:T(8,128)S(1)} %add_add_fusion.refs_0_), channel_id=1, source_target_pairs={{0,16},{4,20},{8,24},{12,28},{16,0},{20,4},{24,8},{28,12},{1,17},{... | collective-permute-start | bytes 393224 | tf_op jit(solution)/shard_map/ppermute | solution.py:22
  23.3 5.5 %collective-permute-start.4 = (bf16[256,128]{1,0:T(8,128)(2,1)S(1)}, bf16[256,128]{1,0:T(8,128)(2,1)S(1)}, u32[]{:S(2)}, u32[]{:S(2)}) collective-permute-start(bf16[256,128]{1,0:T(8,128)(2,1)S(1)} %join.1.refs_0_.refs_2_), channel_id=1, source_target_pairs={{0,12},{4,8},{8,4},{12,0},{16,28},{20,24},{24,20},{28,16},{1,13},{... | collective-permute-start | bytes 196616 | tf_op jit(solution)/shard_map/ppermute | solution.py:22
  23.7 5.1 %collective-permute-start.5 = (bf16[256,128]{1,0:T(8,128)(2,1)S(1)}, bf16[256,128]{1,0:T(8,128)(2,1)S(1)}, u32[]{:S(2)}, u32[]{:S(2)}) collective-permute-start(bf16[256,128]{1,0:T(8,128)(2,1)S(1)} %join.1.refs_0_.refs_2_), channel_id=1, source_target_pairs={{0,4},{4,0},{8,12},{12,8},{16,20},{20,16},{24,28},{28,24},{1,5},{5... | collective-permute-start | bytes 196616 | tf_op jit(solution)/shard_map/ppermute | solution.py:22
  25.6 4.3 %collective-permute-start.6 = (bf16[256,128]{1,0:T(8,128)(2,1)S(1)}, bf16[256,128]{1,0:T(8,128)(2,1)S(1)}, u32[]{:S(2)}, u32[]{:S(2)}) collective-permute-start(bf16[256,128]{1,0:T(8,128)(2,1)S(1)} %join.1.refs_0_.refs_2_), channel_id=1, source_target_pairs={{0,8},{4,12},{8,0},{12,4},{16,24},{20,28},{24,16},{28,20},{1,9},{5... | collective-permute-start | bytes 196616 | tf_op jit(solution)/shard_map/ppermute | solution.py:22
  29.9 28.2 %copy-start = (bf16[2048,1024]{1,0:T(8,128)(2,1)S(1)}, bf16[2048,1024]{1,0:T(8,128)(2,1)}, u32[]{:S(2)}) copy-start(bf16[2048,1024]{1,0:T(8,128)(2,1)} %refs_4_.1) | copy-start | bytes 12582916
  37.2 5.8 %collective-permute-start.7 = (bf16[2,176,128]{2,1,0:T(8,128)(2,1)S(1)}, bf16[2,176,128]{2,1,0:T(8,128)(2,1)S(1)}, u32[]{:S(2)}, u32[]{:S(2)}) collective-permute-start(bf16[2,176,128]{2,1,0:T(8,128)(2,1)S(1)} %get-tuple-element.36), channel_id=1, source_target_pairs={{0,12},{4,8},{8,4},{12,0},{16,28},{20,24},{24,20},{28,16},{1,13},{... | collective-permute-start | bytes 270344 | tf_op jit(solution)/shard_map/ppermute | solution.py:22
  38.8 5.1 %collective-permute-start.8 = (bf16[2,176,128]{2,1,0:T(8,128)(2,1)S(1)}, bf16[2,176,128]{2,1,0:T(8,128)(2,1)S(1)}, u32[]{:S(2)}, u32[]{:S(2)}) collective-permute-start(bf16[2,176,128]{2,1,0:T(8,128)(2,1)S(1)} %get-tuple-element.37), channel_id=1, source_target_pairs={{0,4},{4,0},{8,12},{12,8},{16,20},{20,16},{24,28},{28,24},{1,5},{5... | collective-permute-start | bytes 270344 | tf_op jit(solution)/shard_map/ppermute | solution.py:22
  40.0 4.5 %collective-permute-start.9 = (bf16[2,176,128]{2,1,0:T(8,128)(2,1)S(1)}, bf16[2,176,128]{2,1,0:T(8,128)(2,1)S(1)}, u32[]{:S(2)}, u32[]{:S(2)}) collective-permute-start(bf16[2,176,128]{2,1,0:T(8,128)(2,1)S(1)} %get-tuple-element.38), channel_id=1, source_target_pairs={{0,8},{4,12},{8,0},{12,4},{16,24},{20,28},{24,16},{28,20},{1,9},{5... | collective-permute-start | bytes 270344 | tf_op jit(solution)/shard_map/ppermute | solution.py:22
  45.0 6.5 %collective-permute-start.10 = (bf16[2,176,128]{2,1,0:T(8,128)(2,1)S(1)}, bf16[2,176,128]{2,1,0:T(8,128)(2,1)S(1)}, u32[]{:S(2)}, u32[]{:S(2)}) collective-permute-start(bf16[2,176,128]{2,1,0:T(8,128)(2,1)S(1)} %combine.1.refs_0_), channel_id=1, source_target_pairs={{0,16},{4,20},{8,24},{12,28},{16,0},{20,4},{24,8},{28,12},{1,17},{... | collective-permute-start | bytes 270344 | tf_op jit(solution)/shard_map/ppermute | solution.py:22
  51.9 5.3 %collective-permute-start.11 = (bf16[16,2048]{1,0:T(8,128)(2,1)S(1)}, bf16[16,2048]{1,0:T(8,128)(2,1)S(1)}, u32[]{:S(2)}, u32[]{:S(2)}) collective-permute-start(bf16[16,2048]{1,0:T(8,128)(2,1)S(1)} %finish.1.refs_0_), channel_id=1, source_target_pairs={{0,12},{4,8},{8,4},{12,0},{16,28},{20,24},{24,20},{28,16},{1,13},{... | collective-permute-start | bytes 196616 | tf_op jit(solution)/shard_map/ppermute | solution.py:22
  52.4 5.0 %collective-permute-start.12 = (bf16[16,2048]{1,0:T(8,128)(2,1)S(1)}, bf16[16,2048]{1,0:T(8,128)(2,1)S(1)}, u32[]{:S(2)}, u32[]{:S(2)}) collective-permute-start(bf16[16,2048]{1,0:T(8,128)(2,1)S(1)} %finish.1.refs_0_), channel_id=1, source_target_pairs={{0,4},{4,0},{8,12},{12,8},{16,20},{20,16},{24,28},{28,24},{1,5},{5... | collective-permute-start | bytes 196616 | tf_op jit(solution)/shard_map/ppermute | solution.py:22
  53.8 4.3 %collective-permute-start.13 = (bf16[16,2048]{1,0:T(8,128)(2,1)S(1)}, bf16[16,2048]{1,0:T(8,128)(2,1)S(1)}, u32[]{:S(2)}, u32[]{:S(2)}) collective-permute-start(bf16[16,2048]{1,0:T(8,128)(2,1)S(1)} %finish.1.refs_0_), channel_id=1, source_target_pairs={{0,8},{4,12},{8,0},{12,4},{16,24},{20,28},{24,16},{28,20},{1,9},{5... | collective-permute-start | bytes 196616 | tf_op jit(solution)/shard_map/ppermute | solution.py:22
  59.0 5.0 %collective-permute-start.14 = (bf16[64,1024]{1,0:T(8,128)(2,1)S(1)}, bf16[64,1024]{1,0:T(8,128)(2,1)S(1)}, u32[]{:S(2)}, u32[]{:S(2)}) collective-permute-start(bf16[64,1024]{1,0:T(8,128)(2,1)S(1)} %project_out.1), channel_id=1, source_target_pairs={{0,2},{1,3},{2,0},{3,1},{4,6},{5,7},{6,4},{7,5},{8,10},{9,11},{10,... | collective-permute-start | bytes 393224 | tf_op jit(solution)/shard_map/ppermute | solution.py:22
  64.1 1.4 %collective-permute-start.15 = (bf16[64,1024]{1,0:T(8,128)(2,1)S(1)}, bf16[64,1024]{1,0:T(8,128)(2,1)S(1)}, u32[]{:S(2)}, u32[]{:S(2)}) collective-permute-start(bf16[64,1024]{1,0:T(8,128)(2,1)S(1)} %reduce-precision_convert_fusion), channel_id=1, source_target_pairs={{0,1},{1,0},{2,3},{3,2},{4,5},{5,4},{6,7},{7,6},{8,9},{9,8},{10,11... | collective-permute-start | bytes 393224 | tf_op jit(solution)/shard_map/ppermute | solution.py:22
  (2 other events, 1.3 us)

commit v16 on v14

--- a/solution.py
+++ b/solution.py
@@ -263,7 +263,7 @@
     group = heads // 2
     chunks = slots // CHUNK
     blocks = outs[0].shape[0]
-    lag = 4
+    lag = 8
 
     for d, part in enumerate(in_order(queries)):
         rows = part[...]

time: 64.6 us -> 64.4 us (level)
  no operation moved by 1% of the time
where the time goes in v16:
time: 64.4 us; the launch traced here: 64.2 us
  waiting for transfers between devices  26.7 us (41%)
  starting transfers between devices  21.9 us (34%)
  Pallas kernels  11.4 us (18%)
  local copies, waits for them, and re-layouts  3.35 us (5%)
  other arithmetic  0.78 us (1%)
    ppermute x16, waiting for transfers between devices, swap(): return lax.ppermute(x, axis, [(j, j ^ mask) for j in range(n)])  26.7 us
    ppermute x16, starting transfers between devices, swap(): return lax.ppermute(x, axis, [(j, j ^ mask) for j in range(n)])  21.9 us
    pallas_call x1, Pallas kernels, body(): pl.pallas_call(functools.partial(attention_kernel, ways, mine), out_shape...  5.1 us
    pallas_call x1, Pallas kernels, body(): pl.pallas_call(functools.partial(project_kernel, ways), out_shape=[part_s...  3.59 us
    unnamed x20, local copies, waits for them, and re-layouts  3.35 us
  transfers between devices with their start and end apart: 16, of which 14 were waited for; matrix products, arithmetic and copies ran while one was open for 0% of the time, Pallas kernels for 1%

profile of v16, /device:TPU:0, one launch (start us, length us, event | category | flops | bytes accessed | tf_op | source)
XLA Modules:
  0.0 64.2 jit_solution(8875123169006625126)
XLA Ops:
  0.0 3.6 %project.1 = (f32[2,8,2048]{2,1,0:T(8,128)S(1)}, f32[2,8,2048]{2,1,0:T(8,128)S(1)}, f32[2,8,2048]{2,1,0:T(8,128)S(1)}, f32[2,8,2048]{2,1,0:T(8,128)S(1)}, f32[64,512]{1,0:T(8,128)S(1)}) custom-call(bf16[64,1024]{1,0:T(8,128)(2,1)} %hidden.1, bf16[1024,2048]{1,0:T(8,128)(2,1)} %w_query.1, bf16[1024,512]{1,0:T(8,128)(2,1)} %w_keyval.1), custom_call_target="tpu_custom_call" | custom-call | tf_op jit(solution)/shard_map/project/pallas_call | solution.py:529
  3.6 4.0 %collective-permute-start = (f32[2,8,2048]{2,1,0:T(8,128)S(1)}, f32[2,8,2048]{2,1,0:T(8,128)S(1)}, u32[]{:S(2)}, u32[]{:S(2)}) collective-permute-start(f32[2,8,2048]{2,1,0:T(8,128)S(1)} %get-tuple-element.23), channel_id=1, source_target_pairs={{0,12},{4,8},{8,4},{12,0},{16,28},{20,24},{24,20},{28,16},{1,13},{... | collective-permute-start | bytes 393224 | tf_op jit(solution)/shard_map/ppermute | solution.py:22
  11.6 0.9 %page_table.1 = (f32[64,128]{1,0:T(8,128)S(1)}, s32[1,128]{1,0:T(1,128)S(1)}) custom-call(s32[64]{0:T(128)S(1)} %copy-done.3, s32[64]{0:T(128)S(1)} %copy-done.4, s32[1,128]{1,0:T(1,128)S(1)} %bitcast.11, f32[2,128]{1,0:T(2,128)S(1)} %bitcast.8, f32[2,128]{1,0:T(2,128)S(1)} %bitcast.9), custom_call_target="tpu_custom_call" | custom-call | tf_op jit(solution)/shard_map/page_table/pallas_call | solution.py:513
  12.5 1.5 %collective-permute-done.1 = f32[2,8,2048]{2,1,0:T(8,128)S(1)} collective-permute-done((f32[2,8,2048]{2,1,0:T(8,128)S(1)}, f32[2,8,2048]{2,1,0:T(8,128)S(1)}, u32[]{:S(2)}, u32[]{:S(2)}) %collective-permute-start.1) | collective-permute-done | bytes 131104 | tf_op jit(solution)/shard_map/ppermute | solution.py:22
  14.2 2.7 %collective-permute-start.3 = (f32[2,8,2048]{2,1,0:T(8,128)S(1)}, f32[2,8,2048]{2,1,0:T(8,128)S(1)}, u32[]{:S(2)}, u32[]{:S(2)}) collective-permute-start(f32[2,8,2048]{2,1,0:T(8,128)S(1)} %add_add_fusion.refs_0_), channel_id=1, source_target_pairs={{0,16},{4,20},{8,24},{12,28},{16,0},{20,4},{24,8},{28,12},{1,17},{... | collective-permute-start | bytes 393224 | tf_op jit(solution)/shard_map/ppermute | solution.py:22
  16.8 6.4 %collective-permute-done.3.refs_1_ = f32[2,8,2048]{2,1,0:T(8,128)S(1)} collective-permute-done((f32[2,8,2048]{2,1,0:T(8,128)S(1)}, f32[2,8,2048]{2,1,0:T(8,128)S(1)}, u32[]{:S(2)}, u32[]{:S(2)}) %collective-permute-start.3) | collective-permute-done | bytes 131104 | tf_op jit(solution)/shard_map/ppermute | solution.py:22
  23.7 1.9 %collective-permute-start.5 = (bf16[256,128]{1,0:T(8,128)(2,1)S(1)}, bf16[256,128]{1,0:T(8,128)(2,1)S(1)}, u32[]{:S(2)}, u32[]{:S(2)}) collective-permute-start(bf16[256,128]{1,0:T(8,128)(2,1)S(1)} %join.1.refs_0_.refs_2_), channel_id=1, source_target_pairs={{0,4},{4,0},{8,12},{12,8},{16,20},{20,16},{24,28},{28,24},{1,5},{5... | collective-permute-start | bytes 196616 | tf_op jit(solution)/shard_map/ppermute | solution.py:22
  25.6 1.3 %collective-permute-start.6 = (bf16[256,128]{1,0:T(8,128)(2,1)S(1)}, bf16[256,128]{1,0:T(8,128)(2,1)S(1)}, u32[]{:S(2)}, u32[]{:S(2)}) collective-permute-start(bf16[256,128]{1,0:T(8,128)(2,1)S(1)} %join.1.refs_0_.refs_2_), channel_id=1, source_target_pairs={{0,8},{4,12},{8,0},{12,4},{16,24},{20,28},{24,16},{28,20},{1,9},{5... | collective-permute-start | bytes 196616 | tf_op jit(solution)/shard_map/ppermute | solution.py:22
  26.9 1.9 %collective-permute-done.4.refs_1_ = bf16[256,128]{1,0:T(8,128)(2,1)S(1)} collective-permute-done((bf16[256,128]{1,0:T(8,128)(2,1)S(1)}, bf16[256,128]{1,0:T(8,128)(2,1)S(1)}, u32[]{:S(2)}, u32[]{:S(2)}) %collective-permute-start.4) | collective-permute-done | bytes 65568 | tf_op jit(solution)/shard_map/ppermute | solution.py:22
  28.8 1.1 %collective-permute-done.6.refs_3_ = bf16[256,128]{1,0:T(8,128)(2,1)S(1)} collective-permute-done((bf16[256,128]{1,0:T(8,128)(2,1)S(1)}, bf16[256,128]{1,0:T(8,128)(2,1)S(1)}, u32[]{:S(2)}, u32[]{:S(2)}) %collective-permute-start.6) | collective-permute-done | bytes 65568 | tf_op jit(solution)/shard_map/ppermute | solution.py:22
  29.9 5.1 %paged_attention.1 = (bf16[2,176,128]{2,1,0:T(8,128)(2,1)S(1)}, bf16[2,176,128]{2,1,0:T(8,128)(2,1)S(1)}, bf16[2,176,128]{2,1,0:T(8,128)(2,1)S(1)}, bf16[2,176,128]{2,1,0:T(8,128)(2,1)S(1)}) custom-call(s32[128]{0:T(128)S(1)} %bitcast.10, bf16[256,128]{1,0:T(8,128)(2,1)S(1)} %join.1.refs_0_.refs_2_, bf16[256,128]{1,0:T(8,128)(2,1)S(1)} %collective-permute-done.4.refs_1_, ...), custom_call_target="tpu_custom_call" | custom-call | flops 134217728 | bytes 16777216 | tf_op jit(solution)/shard_map/paged_attention/pallas_call | solution.py:560
  35.0 1.6 %collective-permute-start.7 = (bf16[2,176,128]{2,1,0:T(8,128)(2,1)S(1)}, bf16[2,176,128]{2,1,0:T(8,128)(2,1)S(1)}, u32[]{:S(2)}, u32[]{:S(2)}) collective-permute-start(bf16[2,176,128]{2,1,0:T(8,128)(2,1)S(1)} %get-tuple-element.36), channel_id=1, source_target_pairs={{0,12},{4,8},{8,4},{12,0},{16,28},{20,24},{24,20},{28,16},{1,13},{... | collective-permute-start | bytes 270344 | tf_op jit(solution)/shard_map/ppermute | solution.py:22
  36.6 1.2 %collective-permute-start.8 = (bf16[2,176,128]{2,1,0:T(8,128)(2,1)S(1)}, bf16[2,176,128]{2,1,0:T(8,128)(2,1)S(1)}, u32[]{:S(2)}, u32[]{:S(2)}) collective-permute-start(bf16[2,176,128]{2,1,0:T(8,128)(2,1)S(1)} %get-tuple-element.37), channel_id=1, source_target_pairs={{0,4},{4,0},{8,12},{12,8},{16,20},{20,16},{24,28},{28,24},{1,5},{5... | collective-permute-start | bytes 270344 | tf_op jit(solution)/shard_map/ppermute | solution.py:22
  38.6 2.3 %collective-permute-done.7.refs_1_ = bf16[2,176,128]{2,1,0:T(8,128)(2,1)S(1)} collective-permute-done((bf16[2,176,128]{2,1,0:T(8,128)(2,1)S(1)}, bf16[2,176,128]{2,1,0:T(8,128)(2,1)S(1)}, u32[]{:S(2)}, u32[]{:S(2)}) %collective-permute-start.7) | collective-permute-done | bytes 90144 | tf_op jit(solution)/shard_map/ppermute | solution.py:22
  40.8 0.9 %collective-permute-done.8.refs_2_ = bf16[2,176,128]{2,1,0:T(8,128)(2,1)S(1)} collective-permute-done((bf16[2,176,128]{2,1,0:T(8,128)(2,1)S(1)}, bf16[2,176,128]{2,1,0:T(8,128)(2,1)S(1)}, u32[]{:S(2)}, u32[]{:S(2)}) %collective-permute-start.8) | collective-permute-done | bytes 90144 | tf_op jit(solution)/shard_map/ppermute | solution.py:22
  42.8 2.3 %collective-permute-start.10 = (bf16[2,176,128]{2,1,0:T(8,128)(2,1)S(1)}, bf16[2,176,128]{2,1,0:T(8,128)(2,1)S(1)}, u32[]{:S(2)}, u32[]{:S(2)}) collective-permute-start(bf16[2,176,128]{2,1,0:T(8,128)(2,1)S(1)} %combine.1.refs_0_), channel_id=1, source_target_pairs={{0,16},{4,20},{8,24},{12,28},{16,0},{20,4},{24,8},{28,12},{1,17},{... | collective-permute-start | bytes 270344 | tf_op jit(solution)/shard_map/ppermute | solution.py:22
  45.1 4.2 %collective-permute-done.10.refs_1_ = bf16[2,176,128]{2,1,0:T(8,128)(2,1)S(1)} collective-permute-done((bf16[2,176,128]{2,1,0:T(8,128)(2,1)S(1)}, bf16[2,176,128]{2,1,0:T(8,128)(2,1)S(1)}, u32[]{:S(2)}, u32[]{:S(2)}) %collective-permute-start.10) | collective-permute-done | bytes 90144 | tf_op jit(solution)/shard_map/ppermute | solution.py:22
  50.2 1.5 %collective-permute-start.12 = (bf16[16,2048]{1,0:T(8,128)(2,1)S(1)}, bf16[16,2048]{1,0:T(8,128)(2,1)S(1)}, u32[]{:S(2)}, u32[]{:S(2)}) collective-permute-start(bf16[16,2048]{1,0:T(8,128)(2,1)S(1)} %finish.1.refs_0_), channel_id=1, source_target_pairs={{0,4},{4,0},{8,12},{12,8},{16,20},{20,16},{24,28},{28,24},{1,5},{5... | collective-permute-start | bytes 196616 | tf_op jit(solution)/shard_map/ppermute | solution.py:22
  51.7 1.6 %collective-permute-start.13 = (bf16[16,2048]{1,0:T(8,128)(2,1)S(1)}, bf16[16,2048]{1,0:T(8,128)(2,1)S(1)}, u32[]{:S(2)}, u32[]{:S(2)}) collective-permute-start(bf16[16,2048]{1,0:T(8,128)(2,1)S(1)} %finish.1.refs_0_), channel_id=1, source_target_pairs={{0,8},{4,12},{8,0},{12,4},{16,24},{20,28},{24,16},{28,20},{1,9},{5... | collective-permute-start | bytes 196616 | tf_op jit(solution)/shard_map/ppermute | solution.py:22
  53.3 1.8 %collective-permute-done.11.refs_1_ = bf16[16,2048]{1,0:T(8,128)(2,1)S(1)} collective-permute-done((bf16[16,2048]{1,0:T(8,128)(2,1)S(1)}, bf16[16,2048]{1,0:T(8,128)(2,1)S(1)}, u32[]{:S(2)}, u32[]{:S(2)}) %collective-permute-start.11) | collective-permute-done | bytes 65568 | tf_op jit(solution)/shard_map/ppermute | solution.py:22
  56.0 0.9 %project_out.1 = bf16[64,1024]{1,0:T(8,128)(2,1)S(1)} custom-call(bf16[16,2048]{1,0:T(8,128)(2,1)S(1)} %finish.1.refs_0_, bf16[16,2048]{1,0:T(8,128)(2,1)S(1)} %collective-permute-done.11.refs_1_, bf16[16,2048]{1,0:T(8,128)(2,1)S(1)} %collective-permute-done.12.refs_2_, bf16[16,2048]{1,0:T(8,128)(2,1)S(1)} %collective-permute-done.13.refs_3_, ...), custom_call_target="tpu_custom_call" | custom-call | tf_op jit(solution)/shard_map/project_out/pallas_call | solution.py:610
  56.9 1.6 %collective-permute-start.14 = (bf16[64,1024]{1,0:T(8,128)(2,1)S(1)}, bf16[64,1024]{1,0:T(8,128)(2,1)S(1)}, u32[]{:S(2)}, u32[]{:S(2)}) collective-permute-start(bf16[64,1024]{1,0:T(8,128)(2,1)S(1)} %project_out.1), channel_id=1, source_target_pairs={{0,2},{1,3},{2,0},{3,1},{4,6},{5,7},{6,4},{7,5},{8,10},{9,11},{10,... | collective-permute-start | bytes 393224 | tf_op jit(solution)/shard_map/ppermute | solution.py:22
  58.4 3.5 %collective-permute-done.14 = bf16[64,1024]{1,0:T(8,128)(2,1)S(1)} collective-permute-done((bf16[64,1024]{1,0:T(8,128)(2,1)S(1)}, bf16[64,1024]{1,0:T(8,128)(2,1)S(1)}, u32[]{:S(2)}, u32[]{:S(2)}) %collective-permute-start.14) | collective-permute-done | bytes 131104 | tf_op jit(solution)/shard_map/ppermute | solution.py:22
  62.0 1.5 %collective-permute-done.15 = f32[64,1024]{1,0:T(8,128)S(1)} collective-permute-done((f32[64,1024]{1,0:T(8,128)S(1)}, f32[64,1024]{1,0:T(8,128)S(1)}, u32[]{:S(2)}, u32[]{:S(2)}) %collective-permute-start.15) | collective-permute-done | bytes 262176 | tf_op jit(solution)/shard_map/ppermute | solution.py:22
  (40 shorter events, 9.1 us)
Async XLA Ops:
  3.6 8.9 %collective-permute-start = (f32[2,8,2048]{2,1,0:T(8,128)S(1)}, f32[2,8,2048]{2,1,0:T(8,128)S(1)}, u32[]{:S(2)}, u32[]{:S(2)}) collective-permute-start(f32[2,8,2048]{2,1,0:T(8,128)S(1)} %get-tuple-element.23), channel_id=1, source_target_pairs={{0,12},{4,8},{8,4},{12,0},{16,28},{20,24},{24,20},{28,16},{1,13},{... | collective-permute-start | bytes 393224 | tf_op jit(solution)/shard_map/ppermute | solution.py:22
  7.6 6.3 %collective-permute-start.1 = (f32[2,8,2048]{2,1,0:T(8,128)S(1)}, f32[2,8,2048]{2,1,0:T(8,128)S(1)}, u32[]{:S(2)}, u32[]{:S(2)}) collective-permute-start(f32[2,8,2048]{2,1,0:T(8,128)S(1)} %get-tuple-element.24), channel_id=1, source_target_pairs={{0,4},{4,0},{8,12},{12,8},{16,20},{20,16},{24,28},{28,24},{1,5},{5... | collective-permute-start | bytes 393224 | tf_op jit(solution)/shard_map/ppermute | solution.py:22
  8.1 6.0 %collective-permute-start.2 = (f32[2,8,2048]{2,1,0:T(8,128)S(1)}, f32[2,8,2048]{2,1,0:T(8,128)S(1)}, u32[]{:S(2)}, u32[]{:S(2)}) collective-permute-start(f32[2,8,2048]{2,1,0:T(8,128)S(1)} %get-tuple-element.25), channel_id=1, source_target_pairs={{0,8},{4,12},{8,0},{12,4},{16,24},{20,28},{24,16},{28,20},{1,9},{5... | collective-permute-start | bytes 393224 | tf_op jit(solution)/shard_map/ppermute | solution.py:22
  8.3 0.7 %copy-start.1 = (f32[128,2]{0,1:T(2,128)S(1)}, f32[128,2]{0,1:T(2,128)}, u32[]{:S(2)}) copy-start(f32[128,2]{0,1:T(2,128)} %param.17) | copy-start | bytes 3076
  9.0 0.7 %copy-start.2 = (f32[128,2]{0,1:T(2,128)S(1)}, f32[128,2]{0,1:T(2,128)}, u32[]{:S(2)}) copy-start(f32[128,2]{0,1:T(2,128)} %param.18) | copy-start | bytes 3076
  9.6 0.7 %copy-start.3 = (s32[64]{0:T(128)S(1)}, s32[64]{0:T(128)}, u32[]{:S(2)}) copy-start(s32[64]{0:T(128)} %counts.1) | copy-start | bytes 772
  14.1 15.8 %slice-start = ((s8[8388608]{0:T(1024)(128)(4,1)}), s8[4194304]{0:T(1024)(128)(4,1)S(1)}, s32[]{:S(2)}) async-start(s8[8388608]{0:T(1024)(128)(4,1)} %bitcast.4), calls=%async_computation | async-start | bytes 8388608
  14.1 15.8 %slice-start.2 = ((s8[8388608]{0:T(1024)(128)(4,1)}), s8[4194304]{0:T(1024)(128)(4,1)S(1)}, s32[]{:S(2)}) async-start(s8[8388608]{0:T(1024)(128)(4,1)} %bitcast.6), calls=%async_computation.2 | async-start | bytes 8388608
  14.2 15.7 %slice-start.1 = ((s8[8388608]{0:T(1024)(128)(4,1)}), s8[4194304]{0:T(1024)(128)(4,1)S(1)}, s32[]{:S(2)}) async-start(s8[8388608]{0:T(1024)(128)(4,1)} %bitcast.4), calls=%async_computation.1 | async-start | bytes 8388608
  14.2 15.7 %slice-start.3 = ((s8[8388608]{0:T(1024)(128)(4,1)}), s8[4194304]{0:T(1024)(128)(4,1)S(1)}, s32[]{:S(2)}) async-start(s8[8388608]{0:T(1024)(128)(4,1)} %bitcast.6), calls=%async_computation.3 | async-start | bytes 8388608
  14.2 9.1 %collective-permute-start.3 = (f32[2,8,2048]{2,1,0:T(8,128)S(1)}, f32[2,8,2048]{2,1,0:T(8,128)S(1)}, u32[]{:S(2)}, u32[]{:S(2)}) collective-permute-start(f32[2,8,2048]{2,1,0:T(8,128)S(1)} %add_add_fusion.refs_0_), channel_id=1, source_target_pairs={{0,16},{4,20},{8,24},{12,28},{16,0},{20,4},{24,8},{28,12},{1,17},{... | collective-permute-start | bytes 393224 | tf_op jit(solution)/shard_map/ppermute | solution.py:22
  23.3 5.5 %collective-permute-start.4 = (bf16[256,128]{1,0:T(8,128)(2,1)S(1)}, bf16[256,128]{1,0:T(8,128)(2,1)S(1)}, u32[]{:S(2)}, u32[]{:S(2)}) collective-permute-start(bf16[256,128]{1,0:T(8,128)(2,1)S(1)} %join.1.refs_0_.refs_2_), channel_id=1, source_target_pairs={{0,12},{4,8},{8,4},{12,0},{16,28},{20,24},{24,20},{28,16},{1,13},{... | collective-permute-start | bytes 196616 | tf_op jit(solution)/shard_map/ppermute | solution.py:22
  23.7 5.1 %collective-permute-start.5 = (bf16[256,128]{1,0:T(8,128)(2,1)S(1)}, bf16[256,128]{1,0:T(8,128)(2,1)S(1)}, u32[]{:S(2)}, u32[]{:S(2)}) collective-permute-start(bf16[256,128]{1,0:T(8,128)(2,1)S(1)} %join.1.refs_0_.refs_2_), channel_id=1, source_target_pairs={{0,4},{4,0},{8,12},{12,8},{16,20},{20,16},{24,28},{28,24},{1,5},{5... | collective-permute-start | bytes 196616 | tf_op jit(solution)/shard_map/ppermute | solution.py:22
  25.6 4.3 %collective-permute-start.6 = (bf16[256,128]{1,0:T(8,128)(2,1)S(1)}, bf16[256,128]{1,0:T(8,128)(2,1)S(1)}, u32[]{:S(2)}, u32[]{:S(2)}) collective-permute-start(bf16[256,128]{1,0:T(8,128)(2,1)S(1)} %join.1.refs_0_.refs_2_), channel_id=1, source_target_pairs={{0,8},{4,12},{8,0},{12,4},{16,24},{20,28},{24,16},{28,20},{1,9},{5... | collective-permute-start | bytes 196616 | tf_op jit(solution)/shard_map/ppermute | solution.py:22
  29.9 26.1 %copy-start = (bf16[2048,1024]{1,0:T(8,128)(2,1)S(1)}, bf16[2048,1024]{1,0:T(8,128)(2,1)}, u32[]{:S(2)}) copy-start(bf16[2048,1024]{1,0:T(8,128)(2,1)} %refs_4_.1) | copy-start | bytes 12582916
  35.0 5.8 %collective-permute-start.7 = (bf16[2,176,128]{2,1,0:T(8,128)(2,1)S(1)}, bf16[2,176,128]{2,1,0:T(8,128)(2,1)S(1)}, u32[]{:S(2)}, u32[]{:S(2)}) collective-permute-start(bf16[2,176,128]{2,1,0:T(8,128)(2,1)S(1)} %get-tuple-element.36), channel_id=1, source_target_pairs={{0,12},{4,8},{8,4},{12,0},{16,28},{20,24},{24,20},{28,16},{1,13},{... | collective-permute-start | bytes 270344 | tf_op jit(solution)/shard_map/ppermute | solution.py:22
  36.6 5.1 %collective-permute-start.8 = (bf16[2,176,128]{2,1,0:T(8,128)(2,1)S(1)}, bf16[2,176,128]{2,1,0:T(8,128)(2,1)S(1)}, u32[]{:S(2)}, u32[]{:S(2)}) collective-permute-start(bf16[2,176,128]{2,1,0:T(8,128)(2,1)S(1)} %get-tuple-element.37), channel_id=1, source_target_pairs={{0,4},{4,0},{8,12},{12,8},{16,20},{20,16},{24,28},{28,24},{1,5},{5... | collective-permute-start | bytes 270344 | tf_op jit(solution)/shard_map/ppermute | solution.py:22
  37.8 4.5 %collective-permute-start.9 = (bf16[2,176,128]{2,1,0:T(8,128)(2,1)S(1)}, bf16[2,176,128]{2,1,0:T(8,128)(2,1)S(1)}, u32[]{:S(2)}, u32[]{:S(2)}) collective-permute-start(bf16[2,176,128]{2,1,0:T(8,128)(2,1)S(1)} %get-tuple-element.38), channel_id=1, source_target_pairs={{0,8},{4,12},{8,0},{12,4},{16,24},{20,28},{24,16},{28,20},{1,9},{5... | collective-permute-start | bytes 270344 | tf_op jit(solution)/shard_map/ppermute | solution.py:22
  42.8 6.5 %collective-permute-start.10 = (bf16[2,176,128]{2,1,0:T(8,128)(2,1)S(1)}, bf16[2,176,128]{2,1,0:T(8,128)(2,1)S(1)}, u32[]{:S(2)}, u32[]{:S(2)}) collective-permute-start(bf16[2,176,128]{2,1,0:T(8,128)(2,1)S(1)} %combine.1.refs_0_), channel_id=1, source_target_pairs={{0,16},{4,20},{8,24},{12,28},{16,0},{20,4},{24,8},{28,12},{1,17},{... | collective-permute-start | bytes 270344 | tf_op jit(solution)/shard_map/ppermute | solution.py:22
  49.8 5.3 %collective-permute-start.11 = (bf16[16,2048]{1,0:T(8,128)(2,1)S(1)}, bf16[16,2048]{1,0:T(8,128)(2,1)S(1)}, u32[]{:S(2)}, u32[]{:S(2)}) collective-permute-start(bf16[16,2048]{1,0:T(8,128)(2,1)S(1)} %finish.1.refs_0_), channel_id=1, source_target_pairs={{0,12},{4,8},{8,4},{12,0},{16,28},{20,24},{24,20},{28,16},{1,13},{... | collective-permute-start | bytes 196616 | tf_op jit(solution)/shard_map/ppermute | solution.py:22
  50.2 5.0 %collective-permute-start.12 = (bf16[16,2048]{1,0:T(8,128)(2,1)S(1)}, bf16[16,2048]{1,0:T(8,128)(2,1)S(1)}, u32[]{:S(2)}, u32[]{:S(2)}) collective-permute-start(bf16[16,2048]{1,0:T(8,128)(2,1)S(1)} %finish.1.refs_0_), channel_id=1, source_target_pairs={{0,4},{4,0},{8,12},{12,8},{16,20},{20,16},{24,28},{28,24},{1,5},{5... | collective-permute-start | bytes 196616 | tf_op jit(solution)/shard_map/ppermute | solution.py:22
  51.7 4.3 %collective-permute-start.13 = (bf16[16,2048]{1,0:T(8,128)(2,1)S(1)}, bf16[16,2048]{1,0:T(8,128)(2,1)S(1)}, u32[]{:S(2)}, u32[]{:S(2)}) collective-permute-start(bf16[16,2048]{1,0:T(8,128)(2,1)S(1)} %finish.1.refs_0_), channel_id=1, source_target_pairs={{0,8},{4,12},{8,0},{12,4},{16,24},{20,28},{24,16},{28,20},{1,9},{5... | collective-permute-start | bytes 196616 | tf_op jit(solution)/shard_map/ppermute | solution.py:22
  56.9 5.0 %collective-permute-start.14 = (bf16[64,1024]{1,0:T(8,128)(2,1)S(1)}, bf16[64,1024]{1,0:T(8,128)(2,1)S(1)}, u32[]{:S(2)}, u32[]{:S(2)}) collective-permute-start(bf16[64,1024]{1,0:T(8,128)(2,1)S(1)} %project_out.1), channel_id=1, source_target_pairs={{0,2},{1,3},{2,0},{3,1},{4,6},{5,7},{6,4},{7,5},{8,10},{9,11},{10,... | collective-permute-start | bytes 393224 | tf_op jit(solution)/shard_map/ppermute | solution.py:22
  61.9 1.6 %collective-permute-start.15 = (f32[64,1024]{1,0:T(8,128)S(1)}, f32[64,1024]{1,0:T(8,128)S(1)}, u32[]{:S(2)}, u32[]{:S(2)}) collective-permute-start(f32[64,1024]{1,0:T(8,128)S(1)} %convert_add_fusion), channel_id=1, source_target_pairs={{0,1},{1,0},{2,3},{3,2},{4,5},{5,4},{6,7},{7,6},{8,9},{9,8},{10,11... | collective-permute-start | bytes 786440 | tf_op jit(solution)/shard_map/ppermute | solution.py:22
  (2 other events, 1.3 us)

commit v17 on v16

--- a/solution.py
+++ b/solution.py
@@ -301,7 +301,9 @@
         score = every[:PAGE]
         for s in range(1, CHUNK):
             score = jnp.where(lane_slot == s, every[s * PAGE : (s + 1) * PAGE], score)
-        score = jnp.where(token < table(1, c), score * table(0, c), masked_low)
+        return jnp.where(token < table(1, c), score * table(0, c), masked_low)
+
+    def prob_chunk(c, score):
         top = jnp.max(score, axis=0, keepdims=True)
         page_max[pl.ds(c, 1), :] = top
         prob = jnp.exp(score - top).astype(jnp.bfloat16).astype(jnp.float32)
@@ -334,11 +336,14 @@
                 )
             )
 
+    held = {}
     for c in range(chunks + lag):
         if c >= lag:
             value_chunk(c - lag)
         if c < chunks:
-            score_chunk(c)
+            held[c] = score_chunk(c)
+        if 2 <= c < chunks + 2:
+            prob_chunk(c - 2, held.pop(c - 2))
 
     biggest, who = page_max[...], tables[3 * chunks :, :]
     best = biggest
@@ -355,11 +360,14 @@
 
     keep_max_row = lax.broadcasted_iota(jnp.int32, (PAGE, LANES), 0) % STAT < STAT // 2
 
-    for c in range(chunks):
+    def weigh_chunk(c):
         top = dev_max[pl.ds(c, 1), :]
         weight = jnp.exp(page_max[pl.ds(c, 1), :] - top)
         out_weight = jnp.broadcast_to(weight * table(2, c), (PAGE, LANES)).T
         stat = jnp.where(keep_max_row, top, weight * page_sum[pl.ds(c, 1), :]).T
+        return out_weight, stat
+
+    def total_chunk(c, out_weight, stat):
         for s in range(CHUNK):
             here = pl.ds(
                 pl.multiple_of((place_of[c * CHUNK + s] & 0xFFFF) * heads, heads), heads
@@ -371,6 +379,12 @@
             total_stat[turn, here, :] = jnp.where(
                 keep_max, stat[part], total_stat[turn, here, :] + stat[part]
             )
+
+    for c in range(chunks + 1):
+        if c < chunks:
+            held[c] = weigh_chunk(c)
+        if c >= 1:
+            total_chunk(c - 1, *held.pop(c - 1))
 
     lane = lax.broadcasted_iota(jnp.int32, (heads, LANES), 1)
     digit = place_of[0] >> 24

time: 64.4 us -> 64.4 us (level)
  no operation moved by 1% of the time
where the time goes in v17:
time: 64.4 us; the launch traced here: 64.2 us
  waiting for transfers between devices  26.7 us (41%)
  starting transfers between devices  21.9 us (34%)
  Pallas kernels  11.4 us (18%)
  local copies, waits for them, and re-layouts  3.35 us (5%)
  other arithmetic  0.78 us (1%)
    ppermute x16, waiting for transfers between devices, swap(): return lax.ppermute(x, axis, [(j, j ^ mask) for j in range(n)])  26.7 us
    ppermute x16, starting transfers between devices, swap(): return lax.ppermute(x, axis, [(j, j ^ mask) for j in range(n)])  21.9 us
    pallas_call x1, Pallas kernels, body(): pl.pallas_call(functools.partial(attention_kernel, ways, mine), out_shape...  5.09 us
    pallas_call x1, Pallas kernels, body(): pl.pallas_call(functools.partial(project_kernel, ways), out_shape=[part_s...  3.59 us
    unnamed x20, local copies, waits for them, and re-layouts  3.35 us
  transfers between devices with their start and end apart: 16, of which 14 were waited for; matrix products, arithmetic and copies ran while one was open for 0% of the time, Pallas kernels for 1%

profile of v17, /device:TPU:0, one launch (start us, length us, event | category | flops | bytes accessed | tf_op | source)
XLA Modules:
  0.0 64.2 jit_solution(8875123169006625126)
XLA Ops:
  0.0 3.6 %project.1 = (f32[2,8,2048]{2,1,0:T(8,128)S(1)}, f32[2,8,2048]{2,1,0:T(8,128)S(1)}, f32[2,8,2048]{2,1,0:T(8,128)S(1)}, f32[2,8,2048]{2,1,0:T(8,128)S(1)}, f32[64,512]{1,0:T(8,128)S(1)}) custom-call(bf16[64,1024]{1,0:T(8,128)(2,1)} %hidden.1, bf16[1024,2048]{1,0:T(8,128)(2,1)} %w_query.1, bf16[1024,512]{1,0:T(8,128)(2,1)} %w_keyval.1), custom_call_target="tpu_custom_call" | custom-call | tf_op jit(solution)/shard_map/project/pallas_call | solution.py:543
  3.6 4.0 %collective-permute-start = (f32[2,8,2048]{2,1,0:T(8,128)S(1)}, f32[2,8,2048]{2,1,0:T(8,128)S(1)}, u32[]{:S(2)}, u32[]{:S(2)}) collective-permute-start(f32[2,8,2048]{2,1,0:T(8,128)S(1)} %get-tuple-element.23), channel_id=1, source_target_pairs={{0,12},{4,8},{8,4},{12,0},{16,28},{20,24},{24,20},{28,16},{1,13},{... | collective-permute-start | bytes 393224 | tf_op jit(solution)/shard_map/ppermute | solution.py:22
  11.6 0.9 %page_table.1 = (f32[64,128]{1,0:T(8,128)S(1)}, s32[1,128]{1,0:T(1,128)S(1)}) custom-call(s32[64]{0:T(128)S(1)} %copy-done.3, s32[64]{0:T(128)S(1)} %copy-done.4, s32[1,128]{1,0:T(1,128)S(1)} %bitcast.11, f32[2,128]{1,0:T(2,128)S(1)} %bitcast.8, f32[2,128]{1,0:T(2,128)S(1)} %bitcast.9), custom_call_target="tpu_custom_call" | custom-call | tf_op jit(solution)/shard_map/page_table/pallas_call | solution.py:527
  12.5 1.5 %collective-permute-done.1 = f32[2,8,2048]{2,1,0:T(8,128)S(1)} collective-permute-done((f32[2,8,2048]{2,1,0:T(8,128)S(1)}, f32[2,8,2048]{2,1,0:T(8,128)S(1)}, u32[]{:S(2)}, u32[]{:S(2)}) %collective-permute-start.1) | collective-permute-done | bytes 131104 | tf_op jit(solution)/shard_map/ppermute | solution.py:22
  14.2 2.7 %collective-permute-start.3 = (f32[2,8,2048]{2,1,0:T(8,128)S(1)}, f32[2,8,2048]{2,1,0:T(8,128)S(1)}, u32[]{:S(2)}, u32[]{:S(2)}) collective-permute-start(f32[2,8,2048]{2,1,0:T(8,128)S(1)} %add_add_fusion.refs_0_), channel_id=1, source_target_pairs={{0,16},{4,20},{8,24},{12,28},{16,0},{20,4},{24,8},{28,12},{1,17},{... | collective-permute-start | bytes 393224 | tf_op jit(solution)/shard_map/ppermute | solution.py:22
  16.8 6.4 %collective-permute-done.3.refs_1_ = f32[2,8,2048]{2,1,0:T(8,128)S(1)} collective-permute-done((f32[2,8,2048]{2,1,0:T(8,128)S(1)}, f32[2,8,2048]{2,1,0:T(8,128)S(1)}, u32[]{:S(2)}, u32[]{:S(2)}) %collective-permute-start.3) | collective-permute-done | bytes 131104 | tf_op jit(solution)/shard_map/ppermute | solution.py:22
  23.7 1.9 %collective-permute-start.5 = (bf16[256,128]{1,0:T(8,128)(2,1)S(1)}, bf16[256,128]{1,0:T(8,128)(2,1)S(1)}, u32[]{:S(2)}, u32[]{:S(2)}) collective-permute-start(bf16[256,128]{1,0:T(8,128)(2,1)S(1)} %join.1.refs_0_.refs_2_), channel_id=1, source_target_pairs={{0,4},{4,0},{8,12},{12,8},{16,20},{20,16},{24,28},{28,24},{1,5},{5... | collective-permute-start | bytes 196616 | tf_op jit(solution)/shard_map/ppermute | solution.py:22
  25.6 1.3 %collective-permute-start.6 = (bf16[256,128]{1,0:T(8,128)(2,1)S(1)}, bf16[256,128]{1,0:T(8,128)(2,1)S(1)}, u32[]{:S(2)}, u32[]{:S(2)}) collective-permute-start(bf16[256,128]{1,0:T(8,128)(2,1)S(1)} %join.1.refs_0_.refs_2_), channel_id=1, source_target_pairs={{0,8},{4,12},{8,0},{12,4},{16,24},{20,28},{24,16},{28,20},{1,9},{5... | collective-permute-start | bytes 196616 | tf_op jit(solution)/shard_map/ppermute | solution.py:22
  26.9 1.9 %collective-permute-done.4.refs_1_ = bf16[256,128]{1,0:T(8,128)(2,1)S(1)} collective-permute-done((bf16[256,128]{1,0:T(8,128)(2,1)S(1)}, bf16[256,128]{1,0:T(8,128)(2,1)S(1)}, u32[]{:S(2)}, u32[]{:S(2)}) %collective-permute-start.4) | collective-permute-done | bytes 65568 | tf_op jit(solution)/shard_map/ppermute | solution.py:22
  28.8 1.1 %collective-permute-done.6.refs_3_ = bf16[256,128]{1,0:T(8,128)(2,1)S(1)} collective-permute-done((bf16[256,128]{1,0:T(8,128)(2,1)S(1)}, bf16[256,128]{1,0:T(8,128)(2,1)S(1)}, u32[]{:S(2)}, u32[]{:S(2)}) %collective-permute-start.6) | collective-permute-done | bytes 65568 | tf_op jit(solution)/shard_map/ppermute | solution.py:22
  29.9 5.1 %paged_attention.1 = (bf16[2,176,128]{2,1,0:T(8,128)(2,1)S(1)}, bf16[2,176,128]{2,1,0:T(8,128)(2,1)S(1)}, bf16[2,176,128]{2,1,0:T(8,128)(2,1)S(1)}, bf16[2,176,128]{2,1,0:T(8,128)(2,1)S(1)}) custom-call(s32[128]{0:T(128)S(1)} %bitcast.10, bf16[256,128]{1,0:T(8,128)(2,1)S(1)} %join.1.refs_0_.refs_2_, bf16[256,128]{1,0:T(8,128)(2,1)S(1)} %collective-permute-done.4.refs_1_, ...), custom_call_target="tpu_custom_call" | custom-call | flops 134217728 | bytes 16777216 | tf_op jit(solution)/shard_map/paged_attention/pallas_call | solution.py:574
  35.0 1.6 %collective-permute-start.7 = (bf16[2,176,128]{2,1,0:T(8,128)(2,1)S(1)}, bf16[2,176,128]{2,1,0:T(8,128)(2,1)S(1)}, u32[]{:S(2)}, u32[]{:S(2)}) collective-permute-start(bf16[2,176,128]{2,1,0:T(8,128)(2,1)S(1)} %get-tuple-element.36), channel_id=1, source_target_pairs={{0,12},{4,8},{8,4},{12,0},{16,28},{20,24},{24,20},{28,16},{1,13},{... | collective-permute-start | bytes 270344 | tf_op jit(solution)/shard_map/ppermute | solution.py:22
  36.6 1.2 %collective-permute-start.8 = (bf16[2,176,128]{2,1,0:T(8,128)(2,1)S(1)}, bf16[2,176,128]{2,1,0:T(8,128)(2,1)S(1)}, u32[]{:S(2)}, u32[]{:S(2)}) collective-permute-start(bf16[2,176,128]{2,1,0:T(8,128)(2,1)S(1)} %get-tuple-element.37), channel_id=1, source_target_pairs={{0,4},{4,0},{8,12},{12,8},{16,20},{20,16},{24,28},{28,24},{1,5},{5... | collective-permute-start | bytes 270344 | tf_op jit(solution)/shard_map/ppermute | solution.py:22
  38.6 2.3 %collective-permute-done.7.refs_1_ = bf16[2,176,128]{2,1,0:T(8,128)(2,1)S(1)} collective-permute-done((bf16[2,176,128]{2,1,0:T(8,128)(2,1)S(1)}, bf16[2,176,128]{2,1,0:T(8,128)(2,1)S(1)}, u32[]{:S(2)}, u32[]{:S(2)}) %collective-permute-start.7) | collective-permute-done | bytes 90144 | tf_op jit(solution)/shard_map/ppermute | solution.py:22
  40.8 0.9 %collective-permute-done.8.refs_2_ = bf16[2,176,128]{2,1,0:T(8,128)(2,1)S(1)} collective-permute-done((bf16[2,176,128]{2,1,0:T(8,128)(2,1)S(1)}, bf16[2,176,128]{2,1,0:T(8,128)(2,1)S(1)}, u32[]{:S(2)}, u32[]{:S(2)}) %collective-permute-start.8) | collective-permute-done | bytes 90144 | tf_op jit(solution)/shard_map/ppermute | solution.py:22
  42.8 2.3 %collective-permute-start.10 = (bf16[2,176,128]{2,1,0:T(8,128)(2,1)S(1)}, bf16[2,176,128]{2,1,0:T(8,128)(2,1)S(1)}, u32[]{:S(2)}, u32[]{:S(2)}) collective-permute-start(bf16[2,176,128]{2,1,0:T(8,128)(2,1)S(1)} %combine.1.refs_0_), channel_id=1, source_target_pairs={{0,16},{4,20},{8,24},{12,28},{16,0},{20,4},{24,8},{28,12},{1,17},{... | collective-permute-start | bytes 270344 | tf_op jit(solution)/shard_map/ppermute | solution.py:22
  45.1 4.2 %collective-permute-done.10.refs_1_ = bf16[2,176,128]{2,1,0:T(8,128)(2,1)S(1)} collective-permute-done((bf16[2,176,128]{2,1,0:T(8,128)(2,1)S(1)}, bf16[2,176,128]{2,1,0:T(8,128)(2,1)S(1)}, u32[]{:S(2)}, u32[]{:S(2)}) %collective-permute-start.10) | collective-permute-done | bytes 90144 | tf_op jit(solution)/shard_map/ppermute | solution.py:22
  50.2 1.5 %collective-permute-start.12 = (bf16[16,2048]{1,0:T(8,128)(2,1)S(1)}, bf16[16,2048]{1,0:T(8,128)(2,1)S(1)}, u32[]{:S(2)}, u32[]{:S(2)}) collective-permute-start(bf16[16,2048]{1,0:T(8,128)(2,1)S(1)} %finish.1.refs_0_), channel_id=1, source_target_pairs={{0,4},{4,0},{8,12},{12,8},{16,20},{20,16},{24,28},{28,24},{1,5},{5... | collective-permute-start | bytes 196616 | tf_op jit(solution)/shard_map/ppermute | solution.py:22
  51.7 1.6 %collective-permute-start.13 = (bf16[16,2048]{1,0:T(8,128)(2,1)S(1)}, bf16[16,2048]{1,0:T(8,128)(2,1)S(1)}, u32[]{:S(2)}, u32[]{:S(2)}) collective-permute-start(bf16[16,2048]{1,0:T(8,128)(2,1)S(1)} %finish.1.refs_0_), channel_id=1, source_target_pairs={{0,8},{4,12},{8,0},{12,4},{16,24},{20,28},{24,16},{28,20},{1,9},{5... | collective-permute-start | bytes 196616 | tf_op jit(solution)/shard_map/ppermute | solution.py:22
  53.3 1.8 %collective-permute-done.11.refs_1_ = bf16[16,2048]{1,0:T(8,128)(2,1)S(1)} collective-permute-done((bf16[16,2048]{1,0:T(8,128)(2,1)S(1)}, bf16[16,2048]{1,0:T(8,128)(2,1)S(1)}, u32[]{:S(2)}, u32[]{:S(2)}) %collective-permute-start.11) | collective-permute-done | bytes 65568 | tf_op jit(solution)/shard_map/ppermute | solution.py:22
  56.0 0.9 %project_out.1 = bf16[64,1024]{1,0:T(8,128)(2,1)S(1)} custom-call(bf16[16,2048]{1,0:T(8,128)(2,1)S(1)} %finish.1.refs_0_, bf16[16,2048]{1,0:T(8,128)(2,1)S(1)} %collective-permute-done.11.refs_1_, bf16[16,2048]{1,0:T(8,128)(2,1)S(1)} %collective-permute-done.12.refs_2_, bf16[16,2048]{1,0:T(8,128)(2,1)S(1)} %collective-permute-done.13.refs_3_, ...), custom_call_target="tpu_custom_call" | custom-call | tf_op jit(solution)/shard_map/project_out/pallas_call | solution.py:624
  56.9 1.6 %collective-permute-start.14 = (bf16[64,1024]{1,0:T(8,128)(2,1)S(1)}, bf16[64,1024]{1,0:T(8,128)(2,1)S(1)}, u32[]{:S(2)}, u32[]{:S(2)}) collective-permute-start(bf16[64,1024]{1,0:T(8,128)(2,1)S(1)} %project_out.1), channel_id=1, source_target_pairs={{0,2},{1,3},{2,0},{3,1},{4,6},{5,7},{6,4},{7,5},{8,10},{9,11},{10,... | collective-permute-start | bytes 393224 | tf_op jit(solution)/shard_map/ppermute | solution.py:22
  58.4 3.5 %collective-permute-done.14 = bf16[64,1024]{1,0:T(8,128)(2,1)S(1)} collective-permute-done((bf16[64,1024]{1,0:T(8,128)(2,1)S(1)}, bf16[64,1024]{1,0:T(8,128)(2,1)S(1)}, u32[]{:S(2)}, u32[]{:S(2)}) %collective-permute-start.14) | collective-permute-done | bytes 131104 | tf_op jit(solution)/shard_map/ppermute | solution.py:22
  62.0 1.5 %collective-permute-done.15 = f32[64,1024]{1,0:T(8,128)S(1)} collective-permute-done((f32[64,1024]{1,0:T(8,128)S(1)}, f32[64,1024]{1,0:T(8,128)S(1)}, u32[]{:S(2)}, u32[]{:S(2)}) %collective-permute-start.15) | collective-permute-done | bytes 262176 | tf_op jit(solution)/shard_map/ppermute | solution.py:22
  (40 shorter events, 9.1 us)
Async XLA Ops:
  3.6 8.9 %collective-permute-start = (f32[2,8,2048]{2,1,0:T(8,128)S(1)}, f32[2,8,2048]{2,1,0:T(8,128)S(1)}, u32[]{:S(2)}, u32[]{:S(2)}) collective-permute-start(f32[2,8,2048]{2,1,0:T(8,128)S(1)} %get-tuple-element.23), channel_id=1, source_target_pairs={{0,12},{4,8},{8,4},{12,0},{16,28},{20,24},{24,20},{28,16},{1,13},{... | collective-permute-start | bytes 393224 | tf_op jit(solution)/shard_map/ppermute | solution.py:22
  7.6 6.3 %collective-permute-start.1 = (f32[2,8,2048]{2,1,0:T(8,128)S(1)}, f32[2,8,2048]{2,1,0:T(8,128)S(1)}, u32[]{:S(2)}, u32[]{:S(2)}) collective-permute-start(f32[2,8,2048]{2,1,0:T(8,128)S(1)} %get-tuple-element.24), channel_id=1, source_target_pairs={{0,4},{4,0},{8,12},{12,8},{16,20},{20,16},{24,28},{28,24},{1,5},{5... | collective-permute-start | bytes 393224 | tf_op jit(solution)/shard_map/ppermute | solution.py:22
  8.1 6.0 %collective-permute-start.2 = (f32[2,8,2048]{2,1,0:T(8,128)S(1)}, f32[2,8,2048]{2,1,0:T(8,128)S(1)}, u32[]{:S(2)}, u32[]{:S(2)}) collective-permute-start(f32[2,8,2048]{2,1,0:T(8,128)S(1)} %get-tuple-element.25), channel_id=1, source_target_pairs={{0,8},{4,12},{8,0},{12,4},{16,24},{20,28},{24,16},{28,20},{1,9},{5... | collective-permute-start | bytes 393224 | tf_op jit(solution)/shard_map/ppermute | solution.py:22
  8.3 0.7 %copy-start.1 = (f32[128,2]{0,1:T(2,128)S(1)}, f32[128,2]{0,1:T(2,128)}, u32[]{:S(2)}) copy-start(f32[128,2]{0,1:T(2,128)} %param.17) | copy-start | bytes 3076
  9.0 0.7 %copy-start.2 = (f32[128,2]{0,1:T(2,128)S(1)}, f32[128,2]{0,1:T(2,128)}, u32[]{:S(2)}) copy-start(f32[128,2]{0,1:T(2,128)} %param.18) | copy-start | bytes 3076
  9.6 0.7 %copy-start.3 = (s32[64]{0:T(128)S(1)}, s32[64]{0:T(128)}, u32[]{:S(2)}) copy-start(s32[64]{0:T(128)} %counts.1) | copy-start | bytes 772
  14.1 15.8 %slice-start = ((s8[8388608]{0:T(1024)(128)(4,1)}), s8[4194304]{0:T(1024)(128)(4,1)S(1)}, s32[]{:S(2)}) async-start(s8[8388608]{0:T(1024)(128)(4,1)} %bitcast.4), calls=%async_computation | async-start | bytes 8388608
  14.1 15.8 %slice-start.2 = ((s8[8388608]{0:T(1024)(128)(4,1)}), s8[4194304]{0:T(1024)(128)(4,1)S(1)}, s32[]{:S(2)}) async-start(s8[8388608]{0:T(1024)(128)(4,1)} %bitcast.6), calls=%async_computation.2 | async-start | bytes 8388608
  14.2 15.7 %slice-start.1 = ((s8[8388608]{0:T(1024)(128)(4,1)}), s8[4194304]{0:T(1024)(128)(4,1)S(1)}, s32[]{:S(2)}) async-start(s8[8388608]{0:T(1024)(128)(4,1)} %bitcast.4), calls=%async_computation.1 | async-start | bytes 8388608
  14.2 15.7 %slice-start.3 = ((s8[8388608]{0:T(1024)(128)(4,1)}), s8[4194304]{0:T(1024)(128)(4,1)S(1)}, s32[]{:S(2)}) async-start(s8[8388608]{0:T(1024)(128)(4,1)} %bitcast.6), calls=%async_computation.3 | async-start | bytes 8388608
  14.2 9.1 %collective-permute-start.3 = (f32[2,8,2048]{2,1,0:T(8,128)S(1)}, f32[2,8,2048]{2,1,0:T(8,128)S(1)}, u32[]{:S(2)}, u32[]{:S(2)}) collective-permute-start(f32[2,8,2048]{2,1,0:T(8,128)S(1)} %add_add_fusion.refs_0_), channel_id=1, source_target_pairs={{0,16},{4,20},{8,24},{12,28},{16,0},{20,4},{24,8},{28,12},{1,17},{... | collective-permute-start | bytes 393224 | tf_op jit(solution)/shard_map/ppermute | solution.py:22
  23.3 5.5 %collective-permute-start.4 = (bf16[256,128]{1,0:T(8,128)(2,1)S(1)}, bf16[256,128]{1,0:T(8,128)(2,1)S(1)}, u32[]{:S(2)}, u32[]{:S(2)}) collective-permute-start(bf16[256,128]{1,0:T(8,128)(2,1)S(1)} %join.1.refs_0_.refs_2_), channel_id=1, source_target_pairs={{0,12},{4,8},{8,4},{12,0},{16,28},{20,24},{24,20},{28,16},{1,13},{... | collective-permute-start | bytes 196616 | tf_op jit(solution)/shard_map/ppermute | solution.py:22
  23.7 5.1 %collective-permute-start.5 = (bf16[256,128]{1,0:T(8,128)(2,1)S(1)}, bf16[256,128]{1,0:T(8,128)(2,1)S(1)}, u32[]{:S(2)}, u32[]{:S(2)}) collective-permute-start(bf16[256,128]{1,0:T(8,128)(2,1)S(1)} %join.1.refs_0_.refs_2_), channel_id=1, source_target_pairs={{0,4},{4,0},{8,12},{12,8},{16,20},{20,16},{24,28},{28,24},{1,5},{5... | collective-permute-start | bytes 196616 | tf_op jit(solution)/shard_map/ppermute | solution.py:22
  25.6 4.3 %collective-permute-start.6 = (bf16[256,128]{1,0:T(8,128)(2,1)S(1)}, bf16[256,128]{1,0:T(8,128)(2,1)S(1)}, u32[]{:S(2)}, u32[]{:S(2)}) collective-permute-start(bf16[256,128]{1,0:T(8,128)(2,1)S(1)} %join.1.refs_0_.refs_2_), channel_id=1, source_target_pairs={{0,8},{4,12},{8,0},{12,4},{16,24},{20,28},{24,16},{28,20},{1,9},{5... | collective-permute-start | bytes 196616 | tf_op jit(solution)/shard_map/ppermute | solution.py:22
  29.9 26.1 %copy-start = (bf16[2048,1024]{1,0:T(8,128)(2,1)S(1)}, bf16[2048,1024]{1,0:T(8,128)(2,1)}, u32[]{:S(2)}) copy-start(bf16[2048,1024]{1,0:T(8,128)(2,1)} %refs_4_.1) | copy-start | bytes 12582916
  35.0 5.8 %collective-permute-start.7 = (bf16[2,176,128]{2,1,0:T(8,128)(2,1)S(1)}, bf16[2,176,128]{2,1,0:T(8,128)(2,1)S(1)}, u32[]{:S(2)}, u32[]{:S(2)}) collective-permute-start(bf16[2,176,128]{2,1,0:T(8,128)(2,1)S(1)} %get-tuple-element.36), channel_id=1, source_target_pairs={{0,12},{4,8},{8,4},{12,0},{16,28},{20,24},{24,20},{28,16},{1,13},{... | collective-permute-start | bytes 270344 | tf_op jit(solution)/shard_map/ppermute | solution.py:22
  36.6 5.1 %collective-permute-start.8 = (bf16[2,176,128]{2,1,0:T(8,128)(2,1)S(1)}, bf16[2,176,128]{2,1,0:T(8,128)(2,1)S(1)}, u32[]{:S(2)}, u32[]{:S(2)}) collective-permute-start(bf16[2,176,128]{2,1,0:T(8,128)(2,1)S(1)} %get-tuple-element.37), channel_id=1, source_target_pairs={{0,4},{4,0},{8,12},{12,8},{16,20},{20,16},{24,28},{28,24},{1,5},{5... | collective-permute-start | bytes 270344 | tf_op jit(solution)/shard_map/ppermute | solution.py:22
  37.8 4.5 %collective-permute-start.9 = (bf16[2,176,128]{2,1,0:T(8,128)(2,1)S(1)}, bf16[2,176,128]{2,1,0:T(8,128)(2,1)S(1)}, u32[]{:S(2)}, u32[]{:S(2)}) collective-permute-start(bf16[2,176,128]{2,1,0:T(8,128)(2,1)S(1)} %get-tuple-element.38), channel_id=1, source_target_pairs={{0,8},{4,12},{8,0},{12,4},{16,24},{20,28},{24,16},{28,20},{1,9},{5... | collective-permute-start | bytes 270344 | tf_op jit(solution)/shard_map/ppermute | solution.py:22
  42.8 6.5 %collective-permute-start.10 = (bf16[2,176,128]{2,1,0:T(8,128)(2,1)S(1)}, bf16[2,176,128]{2,1,0:T(8,128)(2,1)S(1)}, u32[]{:S(2)}, u32[]{:S(2)}) collective-permute-start(bf16[2,176,128]{2,1,0:T(8,128)(2,1)S(1)} %combine.1.refs_0_), channel_id=1, source_target_pairs={{0,16},{4,20},{8,24},{12,28},{16,0},{20,4},{24,8},{28,12},{1,17},{... | collective-permute-start | bytes 270344 | tf_op jit(solution)/shard_map/ppermute | solution.py:22
  49.8 5.3 %collective-permute-start.11 = (bf16[16,2048]{1,0:T(8,128)(2,1)S(1)}, bf16[16,2048]{1,0:T(8,128)(2,1)S(1)}, u32[]{:S(2)}, u32[]{:S(2)}) collective-permute-start(bf16[16,2048]{1,0:T(8,128)(2,1)S(1)} %finish.1.refs_0_), channel_id=1, source_target_pairs={{0,12},{4,8},{8,4},{12,0},{16,28},{20,24},{24,20},{28,16},{1,13},{... | collective-permute-start | bytes 196616 | tf_op jit(solution)/shard_map/ppermute | solution.py:22
  50.2 5.0 %collective-permute-start.12 = (bf16[16,2048]{1,0:T(8,128)(2,1)S(1)}, bf16[16,2048]{1,0:T(8,128)(2,1)S(1)}, u32[]{:S(2)}, u32[]{:S(2)}) collective-permute-start(bf16[16,2048]{1,0:T(8,128)(2,1)S(1)} %finish.1.refs_0_), channel_id=1, source_target_pairs={{0,4},{4,0},{8,12},{12,8},{16,20},{20,16},{24,28},{28,24},{1,5},{5... | collective-permute-start | bytes 196616 | tf_op jit(solution)/shard_map/ppermute | solution.py:22
  51.7 4.3 %collective-permute-start.13 = (bf16[16,2048]{1,0:T(8,128)(2,1)S(1)}, bf16[16,2048]{1,0:T(8,128)(2,1)S(1)}, u32[]{:S(2)}, u32[]{:S(2)}) collective-permute-start(bf16[16,2048]{1,0:T(8,128)(2,1)S(1)} %finish.1.refs_0_), channel_id=1, source_target_pairs={{0,8},{4,12},{8,0},{12,4},{16,24},{20,28},{24,16},{28,20},{1,9},{5... | collective-permute-start | bytes 196616 | tf_op jit(solution)/shard_map/ppermute | solution.py:22
  56.9 5.0 %collective-permute-start.14 = (bf16[64,1024]{1,0:T(8,128)(2,1)S(1)}, bf16[64,1024]{1,0:T(8,128)(2,1)S(1)}, u32[]{:S(2)}, u32[]{:S(2)}) collective-permute-start(bf16[64,1024]{1,0:T(8,128)(2,1)S(1)} %project_out.1), channel_id=1, source_target_pairs={{0,2},{1,3},{2,0},{3,1},{4,6},{5,7},{6,4},{7,5},{8,10},{9,11},{10,... | collective-permute-start | bytes 393224 | tf_op jit(solution)/shard_map/ppermute | solution.py:22
  61.9 1.6 %collective-permute-start.15 = (f32[64,1024]{1,0:T(8,128)S(1)}, f32[64,1024]{1,0:T(8,128)S(1)}, u32[]{:S(2)}, u32[]{:S(2)}) collective-permute-start(f32[64,1024]{1,0:T(8,128)S(1)} %convert_add_fusion), channel_id=1, source_target_pairs={{0,1},{1,0},{2,3},{3,2},{4,5},{5,4},{6,7},{7,6},{8,9},{9,8},{10,11... | collective-permute-start | bytes 786440 | tf_op jit(solution)/shard_map/ppermute | solution.py:22
  (2 other events, 1.3 us)
